TPU v7x, 256 devices: a whole 4x4x8 slice. The times are simulated.
256 devices in a mesh: ctx: 16 (over x, z_hi), head: 16 (over y, z_lo, core).
Axes of the slice: x: 4, y: 4, z: 8 (z_hi: 4, z_lo: 2; z = z_hi * 2 + z_lo), core: 2. Of those that a mesh axis runs over, the one named last changes fastest.
Arguments:
- queries: bfloat16 [24576, 2048], P(('ctx', 'head')), may hold values from -8 to 8
- keys: bfloat16 [24576, 2048], P(('ctx', 'head')), may hold values from -8 to 8
- values: bfloat16 [24576, 2048], P(('ctx', 'head')), may hold values from -6 to 6
- kv_tiles: int32 [192, 96], replicated, may hold values from 0 to 191, as said below
- tile_count: int32 [192], replicated, may hold values from 24 to 96
- assign: int32 [192], replicated, may hold values from 0 to 191, as said below
Outputs:
- attended: bfloat16 [24576, 2048], P(('ctx', 'head'))
- slot_lse: float32 [16, 24576], P('head', 'ctx')
Inputs may be any that keep to these rules, and one draw needn't show every extreme that they name: `kv_tiles`: row t lists 96 distinct key tiles and its first entry is t; entries at positions tile_count[t] and later are not used. `assign`: A permutation of the 192 tiles: entry d * 12 + s names the tile that index d of ctx takes in its slot s. Tile t belongs to index t // 12 of ctx; at most 2 of one index's slots hold tiles of one owner.
All inputs are finite; a program needn't handle non-finite values.
Results may differ from a plain program's by a relative error of at most 0.0095.
Values may be sent and summed in bfloat16 or wider, within the bound.
No kernel may reach another device: no remote copies, remote signals or barrier semaphores. Data moves between devices by JAX's collectives and lax.ppermute only.
A program may use at most 128 MiB of HBM per device.

v0:
```python
import math

import jax
import jax.numpy as jnp
from jax import lax
from jax.sharding import PartitionSpec as P

HD = 128
BLK = 128


def table_rows(lookup_table, chosen_ids):
    matches = chosen_ids[:, None] == jnp.arange(lookup_table.shape[0], dtype=jnp.int32)[None, :]
    return jnp.sum(jnp.where(matches[:, :, None], lookup_table[None, :, :], 0), axis=1)


def place_rows(carry_state, piece, source_rows):
    piece_rows = piece.shape[0]
    inside = (source_rows >= 0) & (source_rows < piece_rows)
    picked = jnp.take(piece, jnp.clip(source_rows, 0, piece_rows - 1), axis=0)
    return jnp.where(inside[:, None], picked, carry_state)


def sparse_attend(query_tiles, tile_lists, tile_counts, key_rows, value_rows):
    slot_count, tile_rows, channels = query_tiles.shape
    head_count = channels // HD
    list_width = tile_lists.shape[1]
    key_tiles = key_rows.reshape(-1, tile_rows, channels)
    value_tiles = value_rows.reshape(-1, tile_rows, channels)
    group_size = math.gcd(slot_count, max(1, 512 // tile_rows))
    scaling = HD ** (-0.5)

    def one_group(packed):
        query_group, list_group, count_group = packed
        key_group = key_tiles[list_group].reshape(
            group_size, list_width * tile_rows, head_count, HD
        )
        value_group = value_tiles[list_group].reshape(
            group_size, list_width * tile_rows, head_count, HD
        )
        query_heads = query_group.reshape(group_size, tile_rows, head_count, HD)
        scores = (
            jnp.einsum(
                "gqhd,gkhd->ghqk", query_heads, key_group, preferred_element_type=jnp.float32
            )
            * scaling
        )
        usable = (jnp.arange(list_width * tile_rows, dtype=jnp.int32) // tile_rows)[
            None, :
        ] < count_group[:, None]
        usable = usable[:, None, None, :]
        rowmax = jnp.max(jnp.where(usable, scores, -jnp.inf), axis=-1)
        weights = jnp.where(usable, jnp.exp(scores - rowmax[..., None]), 0.0)
        totals = jnp.sum(weights, axis=-1)
        blended = jnp.einsum(
            "ghqk,gkhd->gqhd",
            weights.astype(jnp.bfloat16),
            value_group,
            preferred_element_type=jnp.float32,
        )
        blended = blended / jnp.transpose(totals, (0, 2, 1))[..., None]
        return (
            blended.astype(jnp.bfloat16).reshape(group_size, tile_rows, channels),
            rowmax + jnp.log(totals),
        )

    groups = slot_count // group_size
    blended_all, log_all = lax.map(
        one_group,
        (
            query_tiles.reshape(groups, group_size, tile_rows, channels),
            tile_lists.reshape(groups, group_size, list_width),
            tile_counts.reshape(groups, group_size),
        ),
    )
    log_totals = jnp.transpose(
        log_all.reshape(slot_count, head_count, tile_rows), (1, 0, 2)
    ).reshape(head_count, slot_count * tile_rows)
    return (blended_all.reshape(slot_count, tile_rows, channels), log_totals)


def on_device(queries, keys, values, kv_tiles, tile_count, assign):
    query_local, key_local, value_local = (
        lax.all_to_all(queries, "head", split_axis=1, concat_axis=0, tiled=True),
        lax.all_to_all(keys, "head", split_axis=1, concat_axis=0, tiled=True),
        lax.all_to_all(values, "head", split_axis=1, concat_axis=0, tiled=True),
    )
    token_rows, channels = query_local.shape
    slot_count = token_rows // BLK
    all_tiles = assign.shape[0]
    device_index = lax.axis_index("ctx")
    my_slots = lax.dynamic_slice_in_dim(assign, device_index * slot_count, slot_count)
    tile_lists = table_rows(kv_tiles, my_slots)
    tile_counts = table_rows(tile_count[:, None], my_slots)[:, 0]
    slot_ids = jnp.arange(slot_count, dtype=jnp.int32)
    within_ids = jnp.arange(BLK, dtype=jnp.int32)
    wanted_rows = (my_slots[:, None] * BLK + within_ids[None, :]).reshape(-1)
    empty_rows = jnp.zeros((slot_count * BLK, channels), jnp.bfloat16)
    taken = place_rows(
        empty_rows, lax.all_gather(query_local, "ctx", axis=0, tiled=True), wanted_rows
    )
    query_tiles = taken.reshape(slot_count, BLK, channels)
    key_rows, value_rows = (
        lax.all_gather(key_local, "ctx", axis=0, tiled=True),
        lax.all_gather(value_local, "ctx", axis=0, tiled=True),
    )
    processed, log_totals = sparse_attend(
        query_tiles, tile_lists, tile_counts, key_rows, value_rows
    )
    home_tiles = device_index * slot_count + slot_ids
    position_ids = jnp.arange(all_tiles, dtype=jnp.int32)
    holder = jnp.sum(
        jnp.where(assign[None, :] == home_tiles[:, None], position_ids[None, :], 0), axis=1
    )
    home_sources = (holder[:, None] * BLK + within_ids[None, :]).reshape(-1)
    empty_home = jnp.zeros((slot_count * BLK, channels), jnp.bfloat16)
    home_rows = place_rows(
        empty_home,
        lax.all_gather(processed.reshape(slot_count * BLK, channels), "ctx", axis=0, tiled=True),
        home_sources,
    )
    attended = lax.all_to_all(home_rows, "head", split_axis=0, concat_axis=1, tiled=True)
    return (attended, log_totals)


def solution(mesh):
    return jax.shard_map(
        on_device,
        mesh=mesh,
        in_specs=(
            P(("ctx", "head"), None),
            P(("ctx", "head"), None),
            P(("ctx", "head"), None),
            P(),
            P(),
            P(),
        ),
        out_specs=(P(("ctx", "head"), None), P("head", "ctx")),
        check_vma=False,
    )
```

profile of v0, /device:TPU:16, one launch (start us, length us, event | category | flops | bytes accessed | tf_op | source)
XLA Modules:
  0.0 646.4 jit_solution(7126691639268626963)
XLA Ops:
  8.2 12.9 %all_to_all.76 = bf16[96,16,128]{2,0,1:T(8,128)(2,1)} all-to-all(bf16[96,16,128]{2,0,1:T(8,128)(2,1)S(1)} %copy_bitcast_fusion.2), channel_id=1, replica_groups=mesh['ctx'=16,'head'=16] {'head'}, dimensions={1} | all-to-all | bytes 786432 | tf_op jit(solution)/shard_map/all_to_all | solution.py:84
  21.3 1.1 copy_bitcast_fusion.3
  22.3 12.7 %all_to_all.77 = bf16[96,16,128]{2,0,1:T(8,128)(2,1)} all-to-all(bf16[96,16,128]{2,0,1:T(8,128)(2,1)S(1)} %copy_bitcast_fusion.3), channel_id=1, replica_groups=mesh['ctx'=16,'head'=16] {'head'}, dimensions={1} | all-to-all | bytes 786432 | tf_op jit(solution)/shard_map/all_to_all | solution.py:86
  35.1 1.1 copy_bitcast_fusion.1
  36.2 20.4 %all_to_all.78 = bf16[96,16,128]{2,0,1:T(8,128)(2,1)} all-to-all(bf16[96,16,128]{2,0,1:T(8,128)(2,1)S(1)} %copy_bitcast_fusion.1), channel_id=1, replica_groups=mesh['ctx'=16,'head'=16] {'head'}, dimensions={1} | all-to-all | bytes 786432 | tf_op jit(solution)/shard_map/all_to_all | solution.py:85
  57.5 1.3 select_reduce_fusion.1
  58.8 1.1 fusion.30
  60.2 62.8 %all-gather.7.cloned.1.call-done = bf16[24576,128]{1,0:T(8,128)(2,1)} async-done(((bf16[1536,128]{1,0:T(8,128)(2,1)}), bf16[24576,128]{1,0:T(8,128)(2,1)}) %all-gather.7.cloned.1.call-update) | async-done | bytes 6291472 | tf_op jit(solution)/shard_map/all_gather | solution.py:100
  123.0 6.2 gather_fusion.2
  129.2 1.1 select_select_fusion.1
  130.2 90.8 %all-gather.5.cloned.1.call-done = bf16[24576,128]{1,0:T(8,128)(2,1)} async-done(((bf16[1536,128]{1,0:T(8,128)(2,1)}), bf16[24576,128]{1,0:T(8,128)(2,1)}) %all-gather.5.cloned.1.call-update) | async-done | bytes 6291472 | tf_op jit(solution)/shard_map/all_gather | solution.py:105
  221.1 98.1 %all-gather.9.cloned.1.call-done = bf16[24576,128]{1,0:T(8,128)(2,1)} async-done(((bf16[1536,128]{1,0:T(8,128)(2,1)}), bf16[24576,128]{1,0:T(8,128)(2,1)}) %all-gather.9.cloned.1.call-update) | async-done | bytes 6291472 | tf_op jit(solution)/shard_map/all_gather | solution.py:104
  319.2 204.4 %while.14 = (s32[]{:T(128)}, bf16[3,4,128,128]{3,2,1,0:T(8,128)(2,1)S(1)}, f32[3,4,1,128]{3,1,2,0:T(4,128)}, s32[3,4,96]{2,1,0:T(4,128)S(1)}, bf16[192,128,128]{...) while((s32[]{:T(128)}, ...), condition=%wide.region_6.8_spmd, body=%wide.region_3.7_spmd.sunk | while | flops 3290711552 | bytes 152108176 | solution.py:68
  319.3 14.2 %gather_fusion.1 = bf16[384,128,128]{2,1,0:T(8,128)(2,1)} fusion(bf16[192,128,128]{2,1,0:T(8,128)(2,1)} %get-tuple-element.206, s32[1024]{0:T(1024)S(1)} %pad_clamp_fusion.4), kind=kCustom, calls=%fused_computation.2.clone.1 | custom fusion | bytes 25167360 | tf_op jit(solution)/shard_map/while/body/eval_jaxpr/gather | solution.py:35
  333.6 12.8 %select_reduce_fusion.4 = (f32[4,128]{1,0:T(4,128)S(1)}, f32[4,128,12288]{2,1,0:T(8,128)}) fusion(pred[4,12288]{1,0:T(4,128)(4,1)S(1)} %broadcast_compare_fusion.2, bf16[4,12288,128]{2,1,0:T(8,128)(2,1)} %bitcast.97, bf16[3,4,128,128]{3,2,1,0:T(8,128)(2,1)S(1)} %get-tuple-element.205, s32[]{:T(128)} %get-tuple-element.190), kind=kOutput, calls=%fused_computation.5.clone.1 | convolution fusion | flops 1629486592 | bytes 37931012 | tf_op jit(solution)/shard_map/while/body/eval_jaxpr/gqhd,gkhd->ghqk/dot_general | solution.py:43
  346.5 11.6 %fusion.55 = f32[4,128]{1,0:T(4,128)S(1)} fusion(f32[4,128,12288]{2,1,0:T(8,128)} %get-tuple-element.179, f32[4,128]{1,0:T(4,128)S(1)} %get-tuple-element.180, pred[4,12288]{1,0:T(4,128)(4,1)S(1)} %broadcast_compare_fusion.2), kind=kLoop, calls=%fused_computation.6.clone.1 | loop fusion | flops 25165312 | bytes 25219072 | tf_op jit(solution)/shard_map/while/body/eval_jaxpr/reduce_sum | solution.py:54
  358.6 14.2 %gather_fusion = bf16[384,128,128]{2,1,0:T(8,128)(2,1)} fusion(bf16[192,128,128]{2,1,0:T(8,128)(2,1)} %get-tuple-element.203, s32[1024]{0:T(1024)S(1)} %pad_clamp_fusion.4), kind=kCustom, calls=%fused_computation.1.clone.1 | custom fusion | bytes 25167360 | tf_op jit(solution)/shard_map/while/body/eval_jaxpr/gather | solution.py:38
  372.8 14.4 %fusion.56 = bf16[1,4,128,128]{2,3,1,0:T(8,128)(2,1)S(1)} fusion(bf16[4,12288,128]{2,1,0:T(8,128)(2,1)} %bitcast.100, f32[4,128,12288]{2,1,0:T(8,128)} %get-tuple-element.179, f32[4,128]{1,0:T(4,128)S(1)} %get-tuple-element.180, pred[4,12288]{1,0:T(4,128)(4,1)S(1)} %broadcast_compare_fusion.2, f32[4,128]{1,0:T(4,128)S(1)} %fusion.55), kind=kOutput, calls=%fused_computation.16.clone.1 | convolution fusion | flops 1635909632 | bytes 37933056 | tf_op jit(solution)/shard_map/while/body/eval_jaxpr/ghqk,gkhd->gqhd/dot_general | solution.py:55
  387.5 14.2 %gather_fusion.1 = bf16[384,128,128]{2,1,0:T(8,128)(2,1)} fusion(bf16[192,128,128]{2,1,0:T(8,128)(2,1)} %get-tuple-element.206, s32[1024]{0:T(1024)S(1)} %pad_clamp_fusion.4), kind=kCustom, calls=%fused_computation.2.clone.1 | custom fusion | bytes 25167360 | tf_op jit(solution)/shard_map/while/body/eval_jaxpr/gather | solution.py:35
  401.8 12.8 %select_reduce_fusion.4 = (f32[4,128]{1,0:T(4,128)S(1)}, f32[4,128,12288]{2,1,0:T(8,128)}) fusion(pred[4,12288]{1,0:T(4,128)(4,1)S(1)} %broadcast_compare_fusion.2, bf16[4,12288,128]{2,1,0:T(8,128)(2,1)} %bitcast.97, bf16[3,4,128,128]{3,2,1,0:T(8,128)(2,1)S(1)} %get-tuple-element.205, s32[]{:T(128)} %get-tuple-element.190), kind=kOutput, calls=%fused_computation.5.clone.1 | convolution fusion | flops 1629486592 | bytes 37931012 | tf_op jit(solution)/shard_map/while/body/eval_jaxpr/gqhd,gkhd->ghqk/dot_general | solution.py:43
  414.6 11.6 %fusion.55 = f32[4,128]{1,0:T(4,128)S(1)} fusion(f32[4,128,12288]{2,1,0:T(8,128)} %get-tuple-element.179, f32[4,128]{1,0:T(4,128)S(1)} %get-tuple-element.180, pred[4,12288]{1,0:T(4,128)(4,1)S(1)} %broadcast_compare_fusion.2), kind=kLoop, calls=%fused_computation.6.clone.1 | loop fusion | flops 25165312 | bytes 25219072 | tf_op jit(solution)/shard_map/while/body/eval_jaxpr/reduce_sum | solution.py:54
  426.8 14.2 %gather_fusion = bf16[384,128,128]{2,1,0:T(8,128)(2,1)} fusion(bf16[192,128,128]{2,1,0:T(8,128)(2,1)} %get-tuple-element.203, s32[1024]{0:T(1024)S(1)} %pad_clamp_fusion.4), kind=kCustom, calls=%fused_computation.1.clone.1 | custom fusion | bytes 25167360 | tf_op jit(solution)/shard_map/while/body/eval_jaxpr/gather | solution.py:38
  440.9 14.4 %fusion.56 = bf16[1,4,128,128]{2,3,1,0:T(8,128)(2,1)S(1)} fusion(bf16[4,12288,128]{2,1,0:T(8,128)(2,1)} %bitcast.100, f32[4,128,12288]{2,1,0:T(8,128)} %get-tuple-element.179, f32[4,128]{1,0:T(4,128)S(1)} %get-tuple-element.180, pred[4,12288]{1,0:T(4,128)(4,1)S(1)} %broadcast_compare_fusion.2, f32[4,128]{1,0:T(4,128)S(1)} %fusion.55), kind=kOutput, calls=%fused_computation.16.clone.1 | convolution fusion | flops 1635909632 | bytes 37933056 | tf_op jit(solution)/shard_map/while/body/eval_jaxpr/ghqk,gkhd->gqhd/dot_general | solution.py:55
  455.6 14.2 %gather_fusion.1 = bf16[384,128,128]{2,1,0:T(8,128)(2,1)} fusion(bf16[192,128,128]{2,1,0:T(8,128)(2,1)} %get-tuple-element.206, s32[1024]{0:T(1024)S(1)} %pad_clamp_fusion.4), kind=kCustom, calls=%fused_computation.2.clone.1 | custom fusion | bytes 25167360 | tf_op jit(solution)/shard_map/while/body/eval_jaxpr/gather | solution.py:35
  469.9 12.8 %select_reduce_fusion.4 = (f32[4,128]{1,0:T(4,128)S(1)}, f32[4,128,12288]{2,1,0:T(8,128)}) fusion(pred[4,12288]{1,0:T(4,128)(4,1)S(1)} %broadcast_compare_fusion.2, bf16[4,12288,128]{2,1,0:T(8,128)(2,1)} %bitcast.97, bf16[3,4,128,128]{3,2,1,0:T(8,128)(2,1)S(1)} %get-tuple-element.205, s32[]{:T(128)} %get-tuple-element.190), kind=kOutput, calls=%fused_computation.5.clone.1 | convolution fusion | flops 1629486592 | bytes 37931012 | tf_op jit(solution)/shard_map/while/body/eval_jaxpr/gqhd,gkhd->ghqk/dot_general | solution.py:43
  482.8 11.6 %fusion.55 = f32[4,128]{1,0:T(4,128)S(1)} fusion(f32[4,128,12288]{2,1,0:T(8,128)} %get-tuple-element.179, f32[4,128]{1,0:T(4,128)S(1)} %get-tuple-element.180, pred[4,12288]{1,0:T(4,128)(4,1)S(1)} %broadcast_compare_fusion.2), kind=kLoop, calls=%fused_computation.6.clone.1 | loop fusion | flops 25165312 | bytes 25219072 | tf_op jit(solution)/shard_map/while/body/eval_jaxpr/reduce_sum | solution.py:54
  494.9 14.2 %gather_fusion = bf16[384,128,128]{2,1,0:T(8,128)(2,1)} fusion(bf16[192,128,128]{2,1,0:T(8,128)(2,1)} %get-tuple-element.203, s32[1024]{0:T(1024)S(1)} %pad_clamp_fusion.4), kind=kCustom, calls=%fused_computation.1.clone.1 | custom fusion | bytes 25167360 | tf_op jit(solution)/shard_map/while/body/eval_jaxpr/gather | solution.py:38
  509.1 14.4 %fusion.56 = bf16[1,4,128,128]{2,3,1,0:T(8,128)(2,1)S(1)} fusion(bf16[4,12288,128]{2,1,0:T(8,128)(2,1)} %bitcast.100, f32[4,128,12288]{2,1,0:T(8,128)} %get-tuple-element.179, f32[4,128]{1,0:T(4,128)S(1)} %get-tuple-element.180, pred[4,12288]{1,0:T(4,128)(4,1)S(1)} %broadcast_compare_fusion.2, f32[4,128]{1,0:T(4,128)S(1)} %fusion.55), kind=kOutput, calls=%fused_computation.16.clone.1 | convolution fusion | flops 1635909632 | bytes 37933056 | tf_op jit(solution)/shard_map/while/body/eval_jaxpr/ghqk,gkhd->gqhd/dot_general | solution.py:55
  524.9 95.3 %all-gather.11.cloned.1.call-done = bf16[24576,128]{1,0:T(8,128)(2,1)} async-done(((bf16[1536,128]{1,0:T(8,128)(2,1)}), bf16[24576,128]{1,0:T(8,128)(2,1)}) %all-gather.11.cloned.1.call-update) | async-done | bytes 6291472 | tf_op jit(solution)/shard_map/all_gather | solution.py:119
  620.2 6.2 gather_fusion.3
  626.4 1.1 select_select_fusion
  627.5 11.6 %all_to_all.79 = bf16[16,96,128]{2,1,0:T(8,128)(2,1)S(1)} all-to-all(bf16[16,96,128]{2,1,0:T(8,128)(2,1)S(1)} %bitcast.105), channel_id=1, replica_groups=mesh['ctx'=16,'head'=16] {'head'}, dimensions={0} | all-to-all | bytes 786432 | tf_op jit(solution)/shard_map/all_to_all | solution.py:122
  (62 shorter events, 7.3 us)
Async XLA Ops:
  7.2 1.0 copy-start
  7.2 115.8 %all-gather.7.cloned.1.call-start = ((), (), s32[]{:S(2)}) async-start(), calls=%async_computation.5 | async-start | bytes 6684672 | tf_op jit(solution)/shard_map/all_gather | solution.py:100
  21.2 199.9 %all-gather.5.cloned.1.call-start = ((), (), s32[]{:S(2)}) async-start(), calls=%async_computation.4 | async-start | bytes 6684672 | tf_op jit(solution)/shard_map/all_gather | solution.py:105
  35.0 284.2 %all-gather.9.cloned.1.call-start = ((), (), s32[]{:S(2)}) async-start(), calls=%async_computation.6 | async-start | bytes 6684672 | tf_op jit(solution)/shard_map/all_gather | solution.py:104
  56.6 563.6 %all-gather.11.cloned.1.call-start = ((), (), s32[]{:S(2)}) async-start(), calls=%async_computation.7 | async-start | bytes 6684672 | tf_op jit(solution)/shard_map/all_gather | solution.py:119
  319.2 205.2 %copy-start.3 = (s32[192]{0:T(256)S(1)}, s32[192]{0:T(256)}, u32[]{:S(2)}) copy-start(s32[192]{0:T(256)} %param.15) | copy-start | bytes 2308
  523.6 0.7 copy-start.2
  523.7 116.2 %copy-start.1 = (bf16[96,2048]{1,0:T(8,128)(2,1)S(1)}, bf16[96,2048]{1,0:T(8,128)(2,1)}, u32[]{:S(2)}) copy-start(bf16[96,2048]{1,0:T(8,128)(2,1)} %param.10) | copy-start | bytes 1179652
Sparse Core Ops, SparseCore 0:
  21.3 101.5 all-gather.6
  125.4 95.5 all-gather.4
  223.6 95.5 all-gather.8
  524.5 95.6 all-gather.10
where the time goes:
time: 650 us; the launch traced here: 646 us
  waiting for transfers between devices  347 us (53%)
  local copies, waits for them, and re-layouts  103 us (16%)
  matrix products  81.7 us (13%)
  blocking collectives  57.6 us (9%)
  other arithmetic  42.9 us (7%)
  between operations  13.9 us (2%)
    all_gather x1, waiting for transfers between devices, on_device(): lax.all_gather(key_local, 'ctx', axis=0, tiled=True)  98.1 us
    all_gather x1, waiting for transfers between devices, on_device(): lax.all_gather(processed.reshape(slot_count * BLK, channels), 'ctx', axis...  95.3 us
    all_gather x1, waiting for transfers between devices, on_device(): lax.all_gather(value_local, 'ctx', axis=0, tiled=True)  90.8 us
    all_gather x1, waiting for transfers between devices, on_device(): lax.all_gather(query_local, 'ctx', axis=0, tiled=True)  62.8 us
    dot_general x3, matrix products, one_group(): jnp.einsum('ghqk,gkhd->gqhd', weights.astype(jnp.bfloat16), value_group,...  43.1 us
    gather x3, local copies, waits for them, and re-layouts, one_group(): key_tiles[list_group]  42.5 us
    gather x3, local copies, waits for them, and re-layouts, one_group(): value_tiles[list_group]  42.5 us
    dot_general x3, matrix products, one_group(): jnp.einsum('gqhd,gkhd->ghqk', query_heads, key_group, preferred_element_t...  38.5 us
  transfers between devices with their start and end apart: 4, of which 4 were waited for; matrix products, arithmetic and copies ran while one was open for 2% of the time, Pallas kernels for 0%

commit v1 on v0

v1 whole, which is shorter than its diff:
```python
import jax
import jax.numpy as jnp
from jax import lax
from jax.experimental import pallas as pl
from jax.experimental.pallas import tpu as pltpu
from jax.sharding import PartitionSpec as P

HD = 128
BLK = 128
LIST = 96
RING = 4
OWN = 12
KEYS = RING * OWN
CHUNK = 4
ROWS = OWN + 1
NEG = -1e30
SCALE = HD**-0.5
LOG2E = 1.4426950408889634
VMEM = pl.BlockSpec(memory_space=pltpu.VMEM)
SMEM = pl.BlockSpec(memory_space=pltpu.SMEM)
ANY = pl.BlockSpec(memory_space=pl.ANY)
GROUP = ("zh", "zl", "core")


def shift(array, axis, by):
    return lax.ppermute(array, axis, [(i, (i + by) % RING) for i in range(RING)])


def prepare_kernel(got_ref, k_ref, qt_ref, vt_ref):
    for part in range(RING):
        q, k, v = (
            got_ref[4 * part : 4 * part + 4, which].reshape(3, BLK, HD) for which in range(3)
        )
        k_ref[3 * part : 3 * part + 3] = k
        for i in range(3):
            qt_ref[3 * part + i] = q[i].T
            vt_ref[3 * part + i] = v[i].T


def prepare(got):
    tiles = jax.ShapeDtypeStruct((OWN, BLK, HD), jnp.bfloat16)
    return pl.pallas_call(
        prepare_kernel,
        out_shape=(tiles, tiles, tiles),
        in_specs=[VMEM],
        out_specs=(VMEM, VMEM, VMEM),
        name="prepare",
    )(got)


def attend_kernel(lists, counts, qa, qb, *refs):
    k_in, v_in = refs[0:4], refs[4:8]
    oa, ob, lse_a, lse_b = refs[8:12]
    ks, vs, sems = refs[12:15]
    states = (refs[15:19], refs[19:23])
    queries = (qa, qb)
    copies = []
    for b in range(RING):
        span = pl.ds(b * OWN, OWN)
        copies.append(pltpu.make_async_copy(k_in[b], ks.at[span], sems.at[b]))
        copies.append(pltpu.make_async_copy(v_in[b], vs.at[span], sems.at[RING + b]))
    for copy in copies:
        copy.start()
    for s_ref, m_ref, l_ref, acc_ref in states:
        m_ref[...] = jnp.full(m_ref.shape, NEG, jnp.float32)
        l_ref[...] = jnp.zeros(l_ref.shape, jnp.float32)
        acc_ref[...] = jnp.zeros(acc_ref.shape, jnp.float32)

    def steps_of(stream, t):
        return jnp.maximum((counts[stream * ROWS + t] + CHUNK - 1) // CHUNK, 1)

    totals = [sum(steps_of(stream, t) for t in range(OWN)) for stream in range(2)]
    steps = jnp.maximum(totals[0], totals[1])

    def advance(stream, t, j):
        more = j + 1 < steps_of(stream, t)
        return jnp.where(more, t, jnp.minimum(t + 1, OWN)), jnp.where(more, j + 1, 0)

    def listed(stream, t, j):
        base = (stream * ROWS + t) * KEYS + j * CHUNK
        return [lists[base + u] for u in range(CHUNK)]

    def score(stream, t, j):
        s_ref = states[stream][0]
        qt = queries[stream][jnp.minimum(t, OWN - 1)]
        for u, tile in enumerate(listed(stream, t, j)):
            s_ref[u * BLK : (u + 1) * BLK] = jnp.dot(
                ks[tile], qt, preferred_element_type=jnp.float32
            )

    def blend(stream, t, j):
        s_ref, m_ref, l_ref, acc_ref = states[stream]
        left = counts[stream * ROWS + t] - j * CHUNK
        top = jnp.full((8, BLK), NEG, jnp.float32)
        for u in range(CHUNK):
            s = s_ref[u * BLK : (u + 1) * BLK]
            top = jnp.maximum(top, jnp.where(u < left, jnp.max(s.reshape(16, 8, BLK), axis=0), NEG))
        m_old = m_ref[t]
        m_new = jnp.maximum(m_old, jnp.max(top, axis=0, keepdims=True))
        alpha = jnp.exp2((m_old - m_new) * (SCALE * LOG2E))
        base = m_new * (SCALE * LOG2E)
        total = l_ref[t] * alpha
        weights = []
        for u in range(CHUNK):
            s = s_ref[u * BLK : (u + 1) * BLK] * (SCALE * LOG2E)
            w = jnp.exp2(s - jnp.where(u < left, base, -NEG))
            total = total + jnp.sum(w.reshape(16, 8, BLK), axis=0)
            weights.append(w.astype(jnp.bfloat16))
        m_ref[t] = m_new
        l_ref[t] = total
        vt = jnp.concatenate([vs[tile] for tile in listed(stream, t, j)], axis=1)
        acc_ref[t] = acc_ref[t] * alpha + jnp.dot(
            vt, jnp.concatenate(weights, axis=0), preferred_element_type=jnp.float32
        )

    for copy in copies:
        copy.wait()
    zero = jnp.int32(0)
    score(0, zero, zero)

    def step(_, carry):
        ta, ja, tb, jb = carry
        score(1, tb, jb)
        blend(0, ta, ja)
        ta, ja = advance(0, ta, ja)
        score(0, ta, ja)
        blend(1, tb, jb)
        tb, jb = advance(1, tb, jb)
        return ta, ja, tb, jb

    lax.fori_loop(0, steps, step, (zero, zero, zero, zero))

    for stream, (o_ref, lse_ref) in enumerate(((oa, lse_a), (ob, lse_b))):
        _, m_ref, l_ref, acc_ref = states[stream]

        def finish(t, _):
            total = jnp.sum(l_ref[t], axis=0, keepdims=True)
            some = total > 0.0
            safe = jnp.where(some, total, 1.0)
            o_ref[t] = (acc_ref[t] * jnp.where(some, 1.0 / safe, 0.0)).astype(jnp.bfloat16)
            lse_ref[t] = jnp.where(some, m_ref[t] * SCALE + jnp.log(safe), NEG)
            return 0

        lax.fori_loop(0, OWN, finish, 0)


def attend(lists, counts, qa, qb, keys, values):
    tiles = jax.ShapeDtypeStruct((OWN, HD, BLK), jnp.bfloat16)
    rows = jax.ShapeDtypeStruct((OWN, 1, BLK), jnp.float32)
    state = [
        pltpu.VMEM((CHUNK * BLK, BLK), jnp.float32),
        pltpu.VMEM((ROWS, 1, BLK), jnp.float32),
        pltpu.VMEM((ROWS, 8, BLK), jnp.float32),
        pltpu.VMEM((ROWS, HD, BLK), jnp.float32),
    ]
    return pl.pallas_call(
        attend_kernel,
        out_shape=(tiles, tiles, rows, rows),
        in_specs=[SMEM, SMEM, VMEM, VMEM] + [ANY] * 8,
        out_specs=(VMEM, VMEM, VMEM, VMEM),
        scratch_shapes=[
            pltpu.VMEM((KEYS, BLK, HD), jnp.bfloat16),
            pltpu.VMEM((KEYS, HD, BLK), jnp.bfloat16),
            pltpu.SemaphoreType.DMA((2 * RING,)),
        ]
        + state
        + state,
        compiler_params=pltpu.CompilerParams(vmem_limit_bytes=32 * 1024 * 1024),
        cost_estimate=pl.CostEstimate(
            flops=360 * 4 * BLK * BLK * HD, bytes_accessed=6 << 20, transcendentals=360 * BLK * BLK
        ),
        name="attend",
    )(lists, counts, qa, qb, *keys, *values)


def combine_kernel(*refs):
    outs, lses = refs[0:4], refs[4:8]
    o_ref, lse_ref = refs[8:10]
    for t in range(OWN):
        parts = [lse[t] for lse in lses]
        top = jnp.maximum(jnp.maximum(parts[0], parts[1]), jnp.maximum(parts[2], parts[3]))
        shares = [jnp.exp(part - top) for part in parts]
        total = (shares[0] + shares[1]) + (shares[2] + shares[3])
        lse_ref[t] = top + jnp.log(total)
        mixed = sum(o[t].astype(jnp.float32) * (w / total) for o, w in zip(outs, shares))
        o_ref[t] = mixed.T.astype(jnp.bfloat16)


def combine(outs, lses):
    return pl.pallas_call(
        combine_kernel,
        out_shape=(
            jax.ShapeDtypeStruct((OWN, BLK, HD), jnp.bfloat16),
            jax.ShapeDtypeStruct((OWN, 1, BLK), jnp.float32),
        ),
        in_specs=[VMEM] * 8,
        out_specs=(VMEM, VMEM),
        name="combine",
    )(*outs, *lses)


def key_lists(kv_tiles, tile_count, xi, yi):
    rows = lax.dynamic_slice_in_dim(kv_tiles, xi * KEYS, KEYS).reshape(RING, RING, 3, LIST)
    used = lax.dynamic_slice_in_dim(tile_count, xi * KEYS, KEYS).reshape(RING, RING, 3)
    rows = lax.dynamic_slice_in_dim(jnp.concatenate([rows, rows], axis=1), yi, RING, axis=1)
    used = lax.dynamic_slice_in_dim(jnp.concatenate([used, used], axis=1), yi, RING, axis=1)
    rows = jnp.transpose(rows, (1, 0, 2, 3)).reshape(KEYS, LIST)
    used = jnp.transpose(used, (1, 0, 2)).reshape(KEYS)
    here = (rows % OWN // 3 == yi) & (jnp.arange(LIST, dtype=jnp.int32)[None, :] < used[:, None])
    place = (rows // KEYS - xi) % RING * OWN + rows % KEYS // OWN * 3 + rows % 3
    before = jnp.arange(LIST)[:, None] < jnp.arange(LIST)[None, :]
    rank = jnp.dot(
        here.astype(jnp.bfloat16), before.astype(jnp.bfloat16), preferred_element_type=jnp.float32
    ).astype(jnp.int32)
    at = here[:, None, :] & (rank[:, None, :] == jnp.arange(KEYS, dtype=jnp.int32)[None, :, None])
    lists = jnp.sum(jnp.where(at, place[:, None, :], 0), axis=2)
    return lists, jnp.sum(here.astype(jnp.int32), axis=1)


def for_streams(lists, counts, first, second):
    picked, sizes = [], []
    for block in (first, second):
        picked += [lists[block * OWN : (block + 1) * OWN], jnp.zeros((1, KEYS), jnp.int32)]
        sizes += [counts[block * OWN : (block + 1) * OWN], jnp.zeros((1,), jnp.int32)]
    return jnp.concatenate(picked).reshape(-1), jnp.concatenate(sizes)


def on_device(queries, keys, values, kv_tiles, tile_count, assign):
    xi, yi = lax.axis_index("x"), lax.axis_index("y")
    sent = jnp.stack([a.reshape(96, 16, HD) for a in (queries, keys, values)])
    got = lax.all_to_all(
        jnp.transpose(sent, (2, 0, 1, 3)), GROUP, split_axis=0, concat_axis=0, tiled=True
    )
    k0, q0, v0 = prepare(got)
    k1, k3 = shift(k0, "x", -1), shift(k0, "x", 1)
    v1, v3 = shift(v0, "x", -1), shift(v0, "x", 1)
    q1, q3 = shift(q0, "y", -1), shift(q0, "y", 1)
    k2, v2 = shift(k3, "x", 1), shift(v1, "x", -1)
    half = OWN // 2
    q2 = jnp.concatenate([shift(q3[:half], "y", 1), shift(q1[half:], "y", -1)])
    lists, counts = key_lists(kv_tiles, tile_count, xi, yi)
    all_keys, all_values = (k0, k1, k2, k3), (v0, v1, v2, v3)
    o2, o1, e2, e1 = attend(*for_streams(lists, counts, 2, 1), q2, q1, all_keys, all_values)
    o3, o0, e3, e0 = attend(*for_streams(lists, counts, 3, 0), q3, q0, all_keys, all_values)
    outs = [o0, shift(o1, "y", 1), shift(o2, "y", 2), shift(o3, "y", -1)]
    lses = [e0, shift(e1, "y", 1), shift(e2, "y", 2), shift(e3, "y", -1)]
    blended, lse = combine(outs, lses)
    back = lax.all_to_all(
        blended.reshape(16, 96, HD), GROUP, split_axis=0, concat_axis=0, tiled=True
    )
    attended = jnp.transpose(back, (1, 0, 2)).reshape(96, 16 * HD)
    every = lax.all_gather(lse.reshape(OWN, BLK), ("x", "y"), axis=0, tiled=True)
    tiles = lax.dynamic_slice_in_dim(assign, (xi * RING + yi) * OWN, OWN)
    spots = tiles // KEYS * KEYS + tiles % OWN // 3 * OWN + tiles % KEYS // OWN * 3 + tiles % 3
    chosen = jnp.take(every, spots, axis=0).reshape(1, OWN * BLK)
    turned = [(b * RING + a, a * RING + b) for a in range(RING) for b in range(RING)]
    return attended, lax.ppermute(chosen, ("zh", "y"), turned)


def solution(mesh):
    split = jax.sharding.Mesh(
        mesh.devices.reshape(RING, RING, RING, 2, 2), ("x", "zh", "y", "zl", "core")
    )
    tokens = P(("x", "zh", "y", "zl", "core"), None)
    return jax.shard_map(
        on_device,
        mesh=split,
        in_specs=(tokens, tokens, tokens, P(), P(), P()),
        out_specs=(tokens, P(("y", "zl", "core"), ("x", "zh"))),
        check_vma=False,
    )
```

time: 650 us -> 199 us (0.31)
  waiting for transfers between devices: 347 us -> 54.9 us
  local copies, waits for them, and re-layouts: 103 us -> 9.22 us
  matrix products: 81.7 us -> 0.13 us
  Pallas kernels: 0 us -> 58.6 us
  starting transfers between devices: 0.16 us -> 46.9 us
  other arithmetic: 42.9 us -> 4.09 us
  blocking collectives: 57.6 us -> 23.5 us
  between operations: 13.9 us -> 1.02 us
    all_gather x4 -> x0, waiting for transfers between devices: 347 us -> none  [the longest x1 98.1 us: on_device(): lax.all_gather(key_local, 'ctx', axis=0, tiled=True)]
    gather x8 -> x1, local copies, waits for them, and re-layouts: 97.5 us -> 0.56 us  [on_device(): chosen = jnp.take(every, spots, axis=0).reshape(1, OWN * BLK)]
    dot_general x6 -> x1, matrix products: 81.7 us -> 0.13 us  [key_lists(): jnp.dot(here.astype(jnp.bfloat16), before.astype(jnp.bfloat16), preferred...]
    pallas_call x0 -> x4, Pallas kernels: none -> 58.6 us  [the longest x2 53.5 us: attend(): pl.pallas_call(attend_kernel, out_shape=(tiles, tiles, rows, rows), in_sp...]
    all_to_all x4 -> x0, blocking collectives: 57.6 us -> none  [the longest x1 20.4 us: on_device(): lax.all_to_all(keys, 'head', split_axis=1, concat_axis=0, tiled=True)]
    reduce_sum x6 -> x1, other arithmetic: 37.2 us -> 0.89 us  [key_lists(): lists = jnp.sum(jnp.where(at, place[:, None, :], 0), axis=2)]
    ppermute x0 -> x17, starting transfers between devices: none -> 34.6 us  [the longest x16 25.5 us: shift(): lax.ppermute(array, axis, [(i, (i + by) % RING) for i in range(RING)])]
    all_to_all x0 -> x2, waiting for transfers between devices: none -> 28 us  [the longest x1 28 us: on_device(): lax.all_to_all(jnp.transpose(sent, (2, 0, 1, 3)), GROUP, split_axis=0, co...]
  transfers between devices with their start and end apart: 4 -> 19, of which waited for: 4 -> 10; matrix products, arithmetic and copies ran while one was open for 2% -> 2% of each run, Pallas kernels for 0% -> 13%
where the time goes in v1:
time: 199 us; the launch traced here: 198 us
  Pallas kernels  58.6 us (29%)
  waiting for transfers between devices  54.9 us (28%)
  starting transfers between devices  46.9 us (24%)
  blocking collectives  23.5 us (12%)
  local copies, waits for them, and re-layouts  9.22 us (5%)
  other arithmetic  4.09 us (2%)
    pallas_call x2, Pallas kernels, attend(): pl.pallas_call(attend_kernel, out_shape=(tiles, tiles, rows, rows), in_sp...  53.5 us
    all_to_all x1, waiting for transfers between devices, on_device(): lax.all_to_all(jnp.transpose(sent, (2, 0, 1, 3)), GROUP, split_axis=0, co...  28 us
    ppermute x16, starting transfers between devices, shift(): lax.ppermute(array, axis, [(i, (i + by) % RING) for i in range(RING)])  25.5 us
    ppermute x16, waiting for transfers between devices, shift(): lax.ppermute(array, axis, [(i, (i + by) % RING) for i in range(RING)])  24.2 us
    all_gather x1, blocking collectives, on_device(): lax.all_gather(lse.reshape(OWN, BLK), ('x', 'y'), axis=0, tiled=True)  23.5 us
    ppermute x1, starting transfers between devices, on_device(): return (attended, lax.ppermute(chosen, ('zh', 'y'), turned))  9.16 us
    all_to_all x1, starting transfers between devices, on_device(): lax.all_to_all(jnp.transpose(sent, (2, 0, 1, 3)), GROUP, split_axis=0, co...  8.7 us
    unnamed x39, local copies, waits for them, and re-layouts  6.42 us
  transfers between devices with their start and end apart: 19, of which 10 were waited for; matrix products, arithmetic and copies ran while one was open for 2% of the time, Pallas kernels for 13%

profile of v1, /device:TPU:16, one launch (start us, length us, event | category | flops | bytes accessed | tf_op | source)
XLA Modules:
  0.0 198.3 jit_solution(6388507061346056485)
XLA Ops:
  0.7 1.1 copy.52
  3.0 1.2 maximum_bitcast_fusion
  4.1 8.7 %all-to-all-start = ((bf16[16,3,96,128]{3,2,1,0:T(8,128)(2,1)}), bf16[16,3,96,128]{3,2,1,0:T(8,128)(2,1)S(1)}, u32[]{:S(2)}, u32[]{:S(2)}) async-start(bf16[16,3,96,128]{3,2,1,0:T(8,128)(2,1)} %maximum_bitcast_fusion), calls=%async_computation | async-start | bytes 2359296 | tf_op jit(solution)/shard_map/all_to_all | solution.py:231
  14.3 28.0 %all-to-all-done.got_ref = bf16[16,3,96,128]{3,2,1,0:T(8,128)(2,1)S(1)} async-done(((bf16[16,3,96,128]{3,2,1,0:T(8,128)(2,1)}), bf16[16,3,96,128]{3,2,1,0:T(8,128)(2,1)S(1)}, u32[]{:S(2)}, u32[]{:S(2)}) %all-to-all-start) | async-done | bytes 1179680 | tf_op jit(solution)/shard_map/all_to_all | solution.py:231
  42.3 1.0 copy-done.6
  43.3 2.5 %prepare.1 = (bf16[12,128,128]{2,1,0:T(8,128)(2,1)}, bf16[12,128,128]{2,1,0:T(8,128)(2,1)}, bf16[12,128,128]{2,1,0:T(8,128)(2,1)}) custom-call(bf16[16,3,96,128]{3,2,1,0:T(8,128)(2,1)} %copy-done.6), custom_call_target="tpu_custom_call" | custom-call | tf_op jit(solution)/shard_map/prepare/pallas_call | solution.py:42
  46.4 0.9 select_reduce_fusion
  47.3 1.7 collective-permute-start
  49.0 1.5 collective-permute-start.2
  50.5 1.7 collective-permute-start.4
  52.2 5.3 %collective-permute-done.8.qb = bf16[12,128,128]{2,1,0:T(8,128)(2,1)S(1)} collective-permute-done((bf16[12,128,128]{2,1,0:T(8,128)(2,1)}, bf16[12,128,128]{2,1,0:T(8,128)(2,1)S(1)}, u32[]{:S(2)}, u32[]{:S(2)}) %collective-permute-start.8) | collective-permute-done | bytes 393248 | tf_op jit(solution)/shard_map/ppermute | solution.py:26
  58.1 2.8 %collective-permute-start.1 = (bf16[12,128,128]{2,1,0:T(8,128)(2,1)}, bf16[12,128,128]{2,1,0:T(8,128)(2,1)S(1)}, u32[]{:S(2)}, u32[]{:S(2)}) collective-permute-start(bf16[12,128,128]{2,1,0:T(8,128)(2,1)} %get-tuple-element.16.refs_0_), channel_id=1, source_target_pairs={{0,192},{64,0},{128,64},{192,128},{1,193},{65,1},{129,65},{193,129... | collective-permute-start | bytes 1179656 | tf_op jit(solution)/shard_map/ppermute | solution.py:26
  60.9 1.5 collective-permute-done.2.refs_3_
  62.7 3.0 %collective-permute-start.5 = (bf16[12,128,128]{2,1,0:T(8,128)(2,1)S(1)}, bf16[12,128,128]{2,1,0:T(8,128)(2,1)}, u32[]{:S(2)}, u32[]{:S(2)}) collective-permute-start(bf16[12,128,128]{2,1,0:T(8,128)(2,1)S(1)} %collective-permute-done.4.refs_5_), channel_id=1, source_target_pairs={{0,192},{64,0},{128,64},{192,128},{1,193},{65,1},{129,65},{193,129... | collective-permute-start | bytes 1179656 | tf_op jit(solution)/shard_map/ppermute | solution.py:26
  66.2 2.7 %collective-permute-start.7 = (bf16[6,128,128]{2,1,0:T(8,128)(2,1)S(1)}, bf16[6,128,128]{2,1,0:T(8,128)(2,1)S(1)}, u32[]{:S(2)}, u32[]{:S(2)}) collective-permute-start(bf16[6,128,128]{2,1,0:T(8,128)(2,1)S(1)} %slice.66), channel_id=1, source_target_pairs={{0,4},{4,8},{8,12},{12,0},{1,5},{5,9},{9,13},{13,1},{2,6},{6,10},{... | collective-permute-start | bytes 589832 | tf_op jit(solution)/shard_map/ppermute | solution.py:26
  69.0 4.0 %collective-permute-done.7 = bf16[6,128,128]{2,1,0:T(8,128)(2,1)S(1)} collective-permute-done((bf16[6,128,128]{2,1,0:T(8,128)(2,1)S(1)}, bf16[6,128,128]{2,1,0:T(8,128)(2,1)S(1)}, u32[]{:S(2)}, u32[]{:S(2)}) %collective-permute-start.7) | collective-permute-done | bytes 196640 | tf_op jit(solution)/shard_map/ppermute | solution.py:26
  73.0 1.0 pad_maximum_fusion.qa
  74.2 7.6 %collective-permute-done.3.refs_2_ = bf16[12,128,128]{2,1,0:T(8,128)(2,1)} collective-permute-done((bf16[12,128,128]{2,1,0:T(8,128)(2,1)S(1)}, bf16[12,128,128]{2,1,0:T(8,128)(2,1)}, u32[]{:S(2)}, u32[]{:S(2)}) %collective-permute-start.3) | collective-permute-done | bytes 393248 | tf_op jit(solution)/shard_map/ppermute | solution.py:26
  81.9 26.8 %attend.3 = (bf16[12,128,128]{2,1,0:T(8,128)(2,1)S(1)}, bf16[12,128,128]{2,1,0:T(8,128)(2,1)S(1)}, f32[12,1,128]{2,1,0:T(1,128)S(1)}, f32[12,1,128]{2,1,0:T(1,128)S(1)}) custom-call(s32[1248]{0:T(1024)S(1)} %reshape.176.lists, s32[26]{0:T(128)S(1)} %pad_add_fusion.4.counts, bf16[12,128,128]{2,1,0:T(8,128)(2,1)S(1)} %pad_maximum_fusion.qa, ...), custom_call_target="tpu_custom_call" | custom-call | flops 3019898880 | bytes 6291456 | tf_op jit(solution)/shard_map/attend/pallas_call | solution.py:156
  108.8 5.7 %collective-permute-start.11 = (bf16[12,128,128]{2,1,0:T(8,128)(2,1)S(1)}, bf16[12,128,128]{2,1,0:T(8,128)(2,1)S(1)}, u32[]{:S(2)}, u32[]{:S(2)}) collective-permute-start(bf16[12,128,128]{2,1,0:T(8,128)(2,1)S(1)} %get-tuple-element.20), channel_id=1, source_target_pairs={{0,8},{4,12},{8,0},{12,4},{1,9},{5,13},{9,1},{13,5},{2,10},{6,14},... | collective-permute-start | bytes 1179656 | tf_op jit(solution)/shard_map/ppermute | solution.py:26
  114.5 26.7 %attend.2 = (bf16[12,128,128]{2,1,0:T(8,128)(2,1)S(1)}, bf16[12,128,128]{2,1,0:T(8,128)(2,1)S(1)}, f32[12,1,128]{2,1,0:T(1,128)S(1)}, f32[12,1,128]{2,1,0:T(1,128)S(1)}) custom-call(s32[1248]{0:T(1024)S(1)} %reshape.175.lists, s32[26]{0:T(128)S(1)} %pad_add_fusion.5.counts, bf16[12,128,128]{2,1,0:T(8,128)(2,1)S(1)} %collective-permute-done.qa, ...), custom_call_target="tpu_custom_call" | custom-call | flops 3019898880 | bytes 6291456 | tf_op jit(solution)/shard_map/attend/pallas_call | solution.py:156
  142.5 2.4 %collective-permute-start.12 = (bf16[12,128,128]{2,1,0:T(8,128)(2,1)S(1)}, bf16[12,128,128]{2,1,0:T(8,128)(2,1)S(1)}, u32[]{:S(2)}, u32[]{:S(2)}) collective-permute-start(bf16[12,128,128]{2,1,0:T(8,128)(2,1)S(1)} %get-tuple-element.21), channel_id=1, source_target_pairs={{0,12},{4,0},{8,4},{12,8},{1,13},{5,1},{9,5},{13,9},{2,14},{6,2},{... | collective-permute-start | bytes 1179656 | tf_op jit(solution)/shard_map/ppermute | solution.py:26
  144.9 1.9 collective-permute-start.14
  146.7 1.7 collective-permute-done.13.refs_5_
  148.5 0.9 collective-permute-start.15
  150.0 3.1 %collective-permute-done.15.refs_7_ = f32[12,1,128]{2,1,0:T(1,128)S(1)} collective-permute-done((f32[12,1,128]{2,1,0:T(1,128)S(1)}, f32[12,1,128]{2,1,0:T(1,128)S(1)}, u32[]{:S(2)}, u32[]{:S(2)}) %collective-permute-start.15) | collective-permute-done | bytes 6176 | tf_op jit(solution)/shard_map/ppermute | solution.py:26
  154.6 2.6 %combine.1 = (bf16[12,128,128]{2,1,0:T(8,128)(2,1)}, f32[12,1,128]{2,1,0:T(1,128)}) custom-call(bf16[12,128,128]{2,1,0:T(8,128)(2,1)} %copy-done.1, bf16[12,128,128]{2,1,0:T(8,128)(2,1)} %copy-done.9, bf16[12,128,128]{2,1,0:T(8,128)(2,1)} %copy-done.10, bf16[12,128,128]{2,1,0:T(8,128)(2,1)} %copy-done.11, f32[12,1,128]{2,1,0:T(1,128)} %copy-done.2, ...), custom_call_target="tpu_custom_call" | custom-call | tf_op jit(solution)/shard_map/combine/pallas_call | solution.py:190
  157.2 3.6 %all-to-all-start.1 = ((bf16[16,96,128]{2,1,0:T(8,128)(2,1)}), bf16[16,96,128]{2,1,0:T(8,128)(2,1)S(1)}, u32[]{:S(2)}, u32[]{:S(2)}) async-start(bf16[16,96,128]{2,1,0:T(8,128)(2,1)} %bitcast.47), calls=%async_computation.1 | async-start | bytes 786432 | tf_op jit(solution)/shard_map/all_to_all | solution.py:248
  160.9 23.5 %all-gather = f32[192,1,128]{2,1,0:T(1,128)S(1)} all-gather(f32[12,1,128]{2,1,0:T(1,128)} %get-tuple-element.27), channel_id=2, replica_groups=mesh['x'=4,'zh'=4,'y'=4,'zl'=2,'core'=2] {'x','y'}, dimensions={0}, use_global_device_ids=true | all-gather | bytes 104448 | tf_op jit(solution)/shard_map/all_gather | solution.py:252
  185.1 9.2 %collective-permute-start.16 = (f32[1,1536]{1,0:T(1,128)S(1)}, f32[1,1536]{1,0:T(1,128)S(1)}, u32[]{:S(2)}, u32[]{:S(2)}) collective-permute-start(f32[1,1536]{1,0:T(1,128)S(1)} %bitcast.50), channel_id=1, source_target_pairs={{0,0},{16,4},{32,8},{48,12},{4,16},{20,20},{36,24},{52,28},{8,32},... | collective-permute-start | bytes 18440 | tf_op jit(solution)/shard_map/ppermute | solution.py:257
  194.3 2.7 %collective-permute-done.16 = f32[1,1536]{1,0:T(1,128)S(1)} collective-permute-done((f32[1,1536]{1,0:T(1,128)S(1)}, f32[1,1536]{1,0:T(1,128)S(1)}, u32[]{:S(2)}, u32[]{:S(2)}) %collective-permute-start.16) | collective-permute-done | bytes 6176 | tf_op jit(solution)/shard_map/ppermute | solution.py:257
  197.0 0.8 copy_bitcast_fusion
  (99 shorter events, 9.7 us)
Async XLA Ops:
  0.6 12.2 %copy-start = (s32[192,96]{1,0:T(8,128)S(1)}, s32[192,96]{1,0:T(8,128)}, u32[]{:S(2)}) copy-start(s32[192,96]{1,0:T(8,128)} %param.9) | copy-start | bytes 221188
  0.6 1.3 copy-start.7
  1.8 1.0 copy-start.8
  4.1 8.8 %copy-start.16 = (s32[192]{0:T(256)S(1)}, s32[192]{0:T(256)}, u32[]{:S(2)}) copy-start(s32[192]{0:T(256)} %param.10) | copy-start | bytes 2308
  4.1 38.2 %all-to-all-start = ((bf16[16,3,96,128]{3,2,1,0:T(8,128)(2,1)}), bf16[16,3,96,128]{3,2,1,0:T(8,128)(2,1)S(1)}, u32[]{:S(2)}, u32[]{:S(2)}) async-start(bf16[16,3,96,128]{3,2,1,0:T(8,128)(2,1)} %maximum_bitcast_fusion), calls=%async_computation | async-start | bytes 2359296 | tf_op jit(solution)/shard_map/all_to_all | solution.py:231
  42.3 1.0 copy-start.6
  45.8 36.0 %copy-start.3 = (bf16[12,128,128]{2,1,0:T(8,128)(2,1)S(1)}, bf16[12,128,128]{2,1,0:T(8,128)(2,1)}, u32[]{:S(2)}) copy-start(bf16[12,128,128]{2,1,0:T(8,128)(2,1)} %get-tuple-element.16.refs_0_) | copy-start | bytes 1179652
  45.8 36.0 %copy-start.5 = (bf16[12,128,128]{2,1,0:T(8,128)(2,1)S(1)}, bf16[12,128,128]{2,1,0:T(8,128)(2,1)}, u32[]{:S(2)}) copy-start(bf16[12,128,128]{2,1,0:T(8,128)(2,1)} %get-tuple-element.17.refs_4_) | copy-start | bytes 1179652
  45.8 11.7 %collective-permute-start.8 = (bf16[12,128,128]{2,1,0:T(8,128)(2,1)}, bf16[12,128,128]{2,1,0:T(8,128)(2,1)S(1)}, u32[]{:S(2)}, u32[]{:S(2)}) collective-permute-start(bf16[12,128,128]{2,1,0:T(8,128)(2,1)} %get-tuple-element.15.qb), channel_id=1, source_target_pairs={{0,12},{4,0},{8,4},{12,8},{1,13},{5,1},{9,5},{13,9},{2,14},{6,2},{... | collective-permute-start | bytes 1179656 | tf_op jit(solution)/shard_map/ppermute | solution.py:26
  47.3 13.5 %collective-permute-start = (bf16[12,128,128]{2,1,0:T(8,128)(2,1)}, bf16[12,128,128]{2,1,0:T(8,128)(2,1)S(1)}, u32[]{:S(2)}, u32[]{:S(2)}) collective-permute-start(bf16[12,128,128]{2,1,0:T(8,128)(2,1)} %get-tuple-element.15.qb), channel_id=1, source_target_pairs={{0,4},{4,8},{8,12},{12,0},{1,5},{5,9},{9,13},{13,1},{2,6},{6,10},{... | collective-permute-start | bytes 1179656 | tf_op jit(solution)/shard_map/ppermute | solution.py:26
  49.0 13.4 %collective-permute-start.2 = (bf16[12,128,128]{2,1,0:T(8,128)(2,1)}, bf16[12,128,128]{2,1,0:T(8,128)(2,1)S(1)}, u32[]{:S(2)}, u32[]{:S(2)}) collective-permute-start(bf16[12,128,128]{2,1,0:T(8,128)(2,1)} %get-tuple-element.16.refs_0_), channel_id=1, source_target_pairs={{0,64},{64,128},{128,192},{192,0},{1,65},{65,129},{129,193},{193,1... | collective-permute-start | bytes 1179656 | tf_op jit(solution)/shard_map/ppermute | solution.py:26
  50.5 12.2 %collective-permute-start.4 = (bf16[12,128,128]{2,1,0:T(8,128)(2,1)}, bf16[12,128,128]{2,1,0:T(8,128)(2,1)S(1)}, u32[]{:S(2)}, u32[]{:S(2)}) collective-permute-start(bf16[12,128,128]{2,1,0:T(8,128)(2,1)} %get-tuple-element.17.refs_4_), channel_id=1, source_target_pairs={{0,192},{64,0},{128,64},{192,128},{1,193},{65,1},{129,65},{193,129... | collective-permute-start | bytes 1179656 | tf_op jit(solution)/shard_map/ppermute | solution.py:26
  57.6 8.6 %collective-permute-start.9 = (bf16[6,128,128]{2,1,0:T(8,128)(2,1)S(1)}, bf16[6,128,128]{2,1,0:T(8,128)(2,1)}, u32[]{:S(2)}, u32[]{:S(2)}) collective-permute-start(bf16[6,128,128]{2,1,0:T(8,128)(2,1)S(1)} %slice.67), channel_id=1, source_target_pairs={{0,12},{4,0},{8,4},{12,8},{1,13},{5,1},{9,5},{13,9},{2,14},{6,2},{... | collective-permute-start | bytes 589832 | tf_op jit(solution)/shard_map/ppermute | solution.py:26
  58.1 15.9 %collective-permute-start.1 = (bf16[12,128,128]{2,1,0:T(8,128)(2,1)}, bf16[12,128,128]{2,1,0:T(8,128)(2,1)S(1)}, u32[]{:S(2)}, u32[]{:S(2)}) collective-permute-start(bf16[12,128,128]{2,1,0:T(8,128)(2,1)} %get-tuple-element.16.refs_0_), channel_id=1, source_target_pairs={{0,192},{64,0},{128,64},{192,128},{1,193},{65,1},{129,65},{193,129... | collective-permute-start | bytes 1179656 | tf_op jit(solution)/shard_map/ppermute | solution.py:26
  60.9 13.4 %collective-permute-start.6 = (bf16[12,128,128]{2,1,0:T(8,128)(2,1)}, bf16[12,128,128]{2,1,0:T(8,128)(2,1)S(1)}, u32[]{:S(2)}, u32[]{:S(2)}) collective-permute-start(bf16[12,128,128]{2,1,0:T(8,128)(2,1)} %get-tuple-element.17.refs_4_), channel_id=1, source_target_pairs={{0,64},{64,128},{128,192},{192,0},{1,65},{65,129},{129,193},{193,1... | collective-permute-start | bytes 1179656 | tf_op jit(solution)/shard_map/ppermute | solution.py:26
  62.4 19.5 %collective-permute-start.3 = (bf16[12,128,128]{2,1,0:T(8,128)(2,1)S(1)}, bf16[12,128,128]{2,1,0:T(8,128)(2,1)}, u32[]{:S(2)}, u32[]{:S(2)}) collective-permute-start(bf16[12,128,128]{2,1,0:T(8,128)(2,1)S(1)} %collective-permute-done.2.refs_3_), channel_id=1, source_target_pairs={{0,64},{64,128},{128,192},{192,0},{1,65},{65,129},{129,193},{193,1... | collective-permute-start | bytes 1179656 | tf_op jit(solution)/shard_map/ppermute | solution.py:26
  62.7 19.2 %collective-permute-start.5 = (bf16[12,128,128]{2,1,0:T(8,128)(2,1)S(1)}, bf16[12,128,128]{2,1,0:T(8,128)(2,1)}, u32[]{:S(2)}, u32[]{:S(2)}) collective-permute-start(bf16[12,128,128]{2,1,0:T(8,128)(2,1)S(1)} %collective-permute-done.4.refs_5_), channel_id=1, source_target_pairs={{0,192},{64,0},{128,64},{192,128},{1,193},{65,1},{129,65},{193,129... | collective-permute-start | bytes 1179656 | tf_op jit(solution)/shard_map/ppermute | solution.py:26
  66.2 6.9 %collective-permute-start.7 = (bf16[6,128,128]{2,1,0:T(8,128)(2,1)S(1)}, bf16[6,128,128]{2,1,0:T(8,128)(2,1)S(1)}, u32[]{:S(2)}, u32[]{:S(2)}) collective-permute-start(bf16[6,128,128]{2,1,0:T(8,128)(2,1)S(1)} %slice.66), channel_id=1, source_target_pairs={{0,4},{4,8},{8,12},{12,0},{1,5},{5,9},{9,13},{13,1},{2,6},{6,10},{... | collective-permute-start | bytes 589832 | tf_op jit(solution)/shard_map/ppermute | solution.py:26
  74.0 40.5 %copy-start.4 = (bf16[12,128,128]{2,1,0:T(8,128)(2,1)S(1)}, bf16[12,128,128]{2,1,0:T(8,128)(2,1)}, u32[]{:S(2)}) copy-start(bf16[12,128,128]{2,1,0:T(8,128)(2,1)} %get-tuple-element.15.qb) | copy-start | bytes 1179652
  108.7 44.4 %collective-permute-start.10 = (bf16[12,128,128]{2,1,0:T(8,128)(2,1)S(1)}, bf16[12,128,128]{2,1,0:T(8,128)(2,1)S(1)}, u32[]{:S(2)}, u32[]{:S(2)}) collective-permute-start(bf16[12,128,128]{2,1,0:T(8,128)(2,1)S(1)} %get-tuple-element.19), channel_id=1, source_target_pairs={{0,4},{4,8},{8,12},{12,0},{1,5},{5,9},{9,13},{13,1},{2,6},{6,10},{... | collective-permute-start | bytes 1179656 | tf_op jit(solution)/shard_map/ppermute | solution.py:26
  108.8 44.3 %collective-permute-start.11 = (bf16[12,128,128]{2,1,0:T(8,128)(2,1)S(1)}, bf16[12,128,128]{2,1,0:T(8,128)(2,1)S(1)}, u32[]{:S(2)}, u32[]{:S(2)}) collective-permute-start(bf16[12,128,128]{2,1,0:T(8,128)(2,1)S(1)} %get-tuple-element.20), channel_id=1, source_target_pairs={{0,8},{4,12},{8,0},{12,4},{1,9},{5,13},{9,1},{13,5},{2,10},{6,14},... | collective-permute-start | bytes 1179656 | tf_op jit(solution)/shard_map/ppermute | solution.py:26
  142.5 10.7 %collective-permute-start.12 = (bf16[12,128,128]{2,1,0:T(8,128)(2,1)S(1)}, bf16[12,128,128]{2,1,0:T(8,128)(2,1)S(1)}, u32[]{:S(2)}, u32[]{:S(2)}) collective-permute-start(bf16[12,128,128]{2,1,0:T(8,128)(2,1)S(1)} %get-tuple-element.21), channel_id=1, source_target_pairs={{0,12},{4,0},{8,4},{12,8},{1,13},{5,1},{9,5},{13,9},{2,14},{6,2},{... | collective-permute-start | bytes 1179656 | tf_op jit(solution)/shard_map/ppermute | solution.py:26
  144.9 3.6 %collective-permute-start.13 = (f32[12,1,128]{2,1,0:T(1,128)S(1)}, f32[12,1,128]{2,1,0:T(1,128)S(1)}, u32[]{:S(2)}, u32[]{:S(2)}) collective-permute-start(f32[12,1,128]{2,1,0:T(1,128)S(1)} %get-tuple-element.23), channel_id=1, source_target_pairs={{0,4},{4,8},{8,12},{12,0},{1,5},{5,9},{9,13},{13,1},{2,6},{6,10},{... | collective-permute-start | bytes 18440 | tf_op jit(solution)/shard_map/ppermute | solution.py:26
  144.9 5.1 %collective-permute-start.14 = (f32[12,1,128]{2,1,0:T(1,128)S(1)}, f32[12,1,128]{2,1,0:T(1,128)S(1)}, u32[]{:S(2)}, u32[]{:S(2)}) collective-permute-start(f32[12,1,128]{2,1,0:T(1,128)S(1)} %get-tuple-element.24), channel_id=1, source_target_pairs={{0,8},{4,12},{8,0},{12,4},{1,9},{5,13},{9,1},{13,5},{2,10},{6,14},... | collective-permute-start | bytes 18440 | tf_op jit(solution)/shard_map/ppermute | solution.py:26
  148.5 5.6 %copy-start.12 = (f32[12,1,128]{2,1,0:T(1,128)}, f32[12,1,128]{2,1,0:T(1,128)S(1)}, u32[]{:S(2)}) copy-start(f32[12,1,128]{2,1,0:T(1,128)S(1)} %collective-permute-done.13.refs_5_) | copy-start | bytes 18436
  148.5 4.7 %collective-permute-start.15 = (f32[12,1,128]{2,1,0:T(1,128)S(1)}, f32[12,1,128]{2,1,0:T(1,128)S(1)}, u32[]{:S(2)}, u32[]{:S(2)}) collective-permute-start(f32[12,1,128]{2,1,0:T(1,128)S(1)} %get-tuple-element.25), channel_id=1, source_target_pairs={{0,12},{4,0},{8,4},{12,8},{1,13},{5,1},{9,5},{13,9},{2,14},{6,2},{... | collective-permute-start | bytes 18440 | tf_op jit(solution)/shard_map/ppermute | solution.py:26
  150.0 4.1 %copy-start.13 = (f32[12,1,128]{2,1,0:T(1,128)}, f32[12,1,128]{2,1,0:T(1,128)S(1)}, u32[]{:S(2)}) copy-start(f32[12,1,128]{2,1,0:T(1,128)S(1)} %collective-permute-done.14.refs_6_) | copy-start | bytes 18436
  153.1 0.9 copy-start.14
  153.2 0.9 copy-start.10
  154.6 6.2 %copy-start.15 = (s32[192]{0:T(256)S(1)}, s32[192]{0:T(256)}, u32[]{:S(2)}) copy-start(s32[192]{0:T(256)} %param.11) | copy-start | bytes 2308
  157.2 39.7 %all-to-all-start.1 = ((bf16[16,96,128]{2,1,0:T(8,128)(2,1)}), bf16[16,96,128]{2,1,0:T(8,128)(2,1)S(1)}, u32[]{:S(2)}, u32[]{:S(2)}) async-start(bf16[16,96,128]{2,1,0:T(8,128)(2,1)} %bitcast.47), calls=%async_computation.1 | async-start | bytes 786432 | tf_op jit(solution)/shard_map/all_to_all | solution.py:248
  185.1 11.8 %collective-permute-start.16 = (f32[1,1536]{1,0:T(1,128)S(1)}, f32[1,1536]{1,0:T(1,128)S(1)}, u32[]{:S(2)}, u32[]{:S(2)}) collective-permute-start(f32[1,1536]{1,0:T(1,128)S(1)} %bitcast.50), channel_id=1, source_target_pairs={{0,0},{16,4},{32,8},{48,12},{4,16},{20,20},{36,24},{52,28},{8,32},... | collective-permute-start | bytes 18440 | tf_op jit(solution)/shard_map/ppermute | solution.py:257
  (4 other events, 2.8 us)

commit v2 on v1

v2 whole, which is shorter than its diff:
```python
import functools

import jax
import jax.numpy as jnp
from jax import lax
from jax.experimental import pallas as pl
from jax.experimental.pallas import tpu as pltpu
from jax.sharding import PartitionSpec as P

HD = 128
BLK = 128
LIST = 96
RING = 4
OWN = 12
KEYS = RING * OWN
CHUNK = 4
WIDTH = 4
PAD = 16
NEG = -1e30
SCALE = HD**-0.5
LOG2E = 1.4426950408889634
VMEM = pl.BlockSpec(memory_space=pltpu.VMEM)
SMEM = pl.BlockSpec(memory_space=pltpu.SMEM)
ANY = pl.BlockSpec(memory_space=pl.ANY)
GROUP = ("zh", "zl", "core")


def shift(array, axis, by):
    return lax.ppermute(array, axis, [(i, (i + by) % RING) for i in range(RING)])


def prepare_kernel(got_ref, kv_ref):
    for part in range(RING):
        k, v = (
            got_ref[4 * part : 4 * part + 4, which].reshape(3, BLK, HD) for which in range(2)
        )
        kv_ref[0, 3 * part : 3 * part + 3] = k
        for i in range(3):
            kv_ref[1, 3 * part + i] = v[i].T


def prepare(got):
    return pl.pallas_call(
        prepare_kernel,
        out_shape=jax.ShapeDtypeStruct((2, OWN, BLK, HD), jnp.bfloat16),
        in_specs=[VMEM],
        out_specs=VMEM,
        name="prepare",
    )(got)


def attend_kernel(blocks, lists, counts, *refs):
    tiles = blocks * OWN
    q_in, refs = refs[:blocks], refs[blocks:]
    kv0, kv1, kv3, k2, v2 = refs[:5]
    refs = refs[5:]
    o_out, refs = refs[:blocks], refs[blocks:]
    qs, ks, vs, sems, m_ref, l_ref, acc_ref = refs[:7]
    s_refs, top_refs = refs[7 : 7 + WIDTH], refs[7 + WIDTH :]
    moves = [(q, qs, b) for b, q in enumerate(q_in)]
    for b, (k, v) in enumerate(
        ((kv0.at[0], kv0.at[1]), (kv1.at[0], kv1.at[1]), (k2, v2), (kv3.at[0], kv3.at[1]))
    ):
        moves += [(k, ks, b), (v, vs, b)]
    copies = [
        pltpu.make_async_copy(source, held.at[pl.ds(b * OWN, OWN)], sems.at[i])
        for i, (source, held, b) in enumerate(moves)
    ]
    for copy in copies:
        copy.start()
    m_ref[...] = jnp.full(m_ref.shape, NEG, jnp.float32)
    l_ref[...] = jnp.zeros(l_ref.shape, jnp.float32)
    acc_ref[...] = jnp.zeros(acc_ref.shape, jnp.float32)

    def steps_of(t):
        return jnp.maximum((counts[t] + CHUNK - 1) // CHUNK, 1)

    items = lax.fori_loop(0, tiles, lambda t, n: n + steps_of(t), jnp.int32(0))

    def advance(t, j):
        more = j + 1 < steps_of(t)
        return jnp.where(more, t, jnp.minimum(t + 1, tiles)), jnp.where(more, j + 1, 0)

    def listed(t, j):
        base = t * KEYS + j * CHUNK
        return [lists[base + u] for u in range(CHUNK)]

    def score(lane, t, j):
        left = counts[t] - j * CHUNK
        s = lax.dot_general(
            jnp.concatenate([ks[tile] for tile in listed(t, j)], axis=0),
            qs[jnp.minimum(t, tiles - 1)],
            (((1,), (1,)), ((), ())),
            preferred_element_type=jnp.float32,
        )
        s_refs[lane][...] = s
        top = jnp.full((8, BLK), NEG, jnp.float32)
        for u in range(CHUNK):
            part = jnp.max(s[u * BLK : (u + 1) * BLK].reshape(16, 8, BLK), axis=0)
            top = jnp.maximum(top, jnp.where(u < left, part, NEG))
        top_refs[lane][...] = jnp.max(top, axis=0, keepdims=True)

    def blend(lane, t, j):
        left = counts[t] - j * CHUNK
        m_old = m_ref[t]
        m_new = jnp.maximum(m_old, top_refs[lane][...])
        m_ref[t] = m_new
        alpha = jnp.exp2((m_old - m_new) * (SCALE * LOG2E))
        base = m_new * (SCALE * LOG2E)
        total = jnp.zeros((8, BLK), jnp.float32)
        weights = []
        for u in range(CHUNK):
            s = s_refs[lane][u * BLK : (u + 1) * BLK] * (SCALE * LOG2E)
            w = jnp.exp2(s - jnp.where(u < left, base, -NEG))
            total = total + jnp.sum(w.reshape(16, 8, BLK), axis=0)
            weights.append(w.astype(jnp.bfloat16))
        vt = jnp.concatenate([vs[tile] for tile in listed(t, j)], axis=1)
        mixed = jnp.dot(vt, jnp.concatenate(weights, axis=0), preferred_element_type=jnp.float32)
        l_ref[t] = l_ref[t] * alpha + total
        acc_ref[t] = acc_ref[t] * alpha + mixed

    def following(t, j):
        group = []
        for _ in range(WIDTH):
            t, j = advance(t, j)
            group += [t, j]
        return tuple(group)

    for copy in copies:
        copy.wait()
    first = [jnp.int32(0), jnp.int32(0)]
    for _ in range(WIDTH - 1):
        first += advance(*first[-2:])
    for lane in range(WIDTH):
        score(lane, first[2 * lane], first[2 * lane + 1])

    def step(_, now):
        later = following(*now[-2:])
        for lane in range(WIDTH):
            blend(lane, now[2 * lane], now[2 * lane + 1])
            score(lane, later[2 * lane], later[2 * lane + 1])
        return later

    lax.fori_loop(0, (items + WIDTH - 1) // WIDTH, step, tuple(first))

    for b in range(blocks):

        def finish(i, _):
            for u in range(4):
                t = i * 4 + u
                total = jnp.sum(l_ref[b * OWN + t], axis=0, keepdims=True)
                some = total > 0.0
                safe = jnp.where(some, total, 1.0)
                share = jnp.where(some, 1.0 / safe, 0.0)
                lse = jnp.where(some, m_ref[b * OWN + t] * SCALE + jnp.log(safe), NEG)
                high = lse.astype(jnp.bfloat16)
                middle = (lse - high.astype(jnp.float32)).astype(jnp.bfloat16)
                low = (lse - high.astype(jnp.float32) - middle.astype(jnp.float32)).astype(
                    jnp.bfloat16
                )
                o_out[b][t, :HD] = (acc_ref[b * OWN + t] * share).astype(jnp.bfloat16)
                o_out[b][t, HD:] = jnp.concatenate(
                    [high, middle, low, jnp.zeros((PAD - 3, BLK), jnp.bfloat16)], axis=0
                )
            return 0

        lax.fori_loop(0, OWN // 4, finish, 0)


def attend(lists, counts, queries, kv):
    blocks = len(queries)
    tiles = jax.ShapeDtypeStruct((OWN, HD + PAD, BLK), jnp.bfloat16)
    slots = blocks * OWN + 1
    pairs = blocks * OWN * 15
    return pl.pallas_call(
        functools.partial(attend_kernel, blocks),
        out_shape=(tiles,) * blocks,
        in_specs=[SMEM, SMEM] + [ANY] * (blocks + 5),
        out_specs=(VMEM,) * blocks,
        scratch_shapes=[
            pltpu.VMEM((blocks * OWN, BLK, HD), jnp.bfloat16),
            pltpu.VMEM((KEYS, BLK, HD), jnp.bfloat16),
            pltpu.VMEM((KEYS, HD, BLK), jnp.bfloat16),
            pltpu.SemaphoreType.DMA((blocks + 2 * RING,)),
            pltpu.VMEM((slots, 1, BLK), jnp.float32),
            pltpu.VMEM((slots, 8, BLK), jnp.float32),
            pltpu.VMEM((slots, HD, BLK), jnp.float32),
        ]
        + [pltpu.VMEM((CHUNK * BLK, BLK), jnp.float32)] * WIDTH
        + [pltpu.VMEM((1, BLK), jnp.float32)] * WIDTH,
        compiler_params=pltpu.CompilerParams(vmem_limit_bytes=32 * 1024 * 1024),
        cost_estimate=pl.CostEstimate(
            flops=pairs * 4 * BLK * BLK * HD,
            bytes_accessed=5 << 20,
            transcendentals=pairs * BLK * BLK,
        ),
        name="attend",
    )(lists, counts, *queries, *kv)


def combine_kernel(*refs):
    outs, (o_ref, lse_ref) = refs[:RING], refs[RING:]
    for t in range(OWN):
        parts = []
        for o in outs:
            split = o[t, HD:].astype(jnp.float32)
            parts.append(split[0:1] + split[1:2] + split[2:3])
        top = jnp.maximum(jnp.maximum(parts[0], parts[1]), jnp.maximum(parts[2], parts[3]))
        shares = [jnp.exp(part - top) for part in parts]
        total = (shares[0] + shares[1]) + (shares[2] + shares[3])
        lse_ref[t : t + 1] = top + jnp.log(total)
        mixed = sum(o[t, :HD].astype(jnp.float32) * (w / total) for o, w in zip(outs, shares))
        o_ref[t] = mixed.T.astype(jnp.bfloat16)


def combine(outs):
    return pl.pallas_call(
        combine_kernel,
        out_shape=(
            jax.ShapeDtypeStruct((OWN, BLK, HD), jnp.bfloat16),
            jax.ShapeDtypeStruct((OWN, BLK), jnp.float32),
        ),
        in_specs=[VMEM] * RING,
        out_specs=(VMEM, VMEM),
        name="combine",
    )(*outs)


def key_lists(kv_tiles, tile_count, xi, yi):
    rows = lax.dynamic_slice_in_dim(kv_tiles, xi * KEYS, KEYS).reshape(RING, RING, 3, LIST)
    used = lax.dynamic_slice_in_dim(tile_count, xi * KEYS, KEYS).reshape(RING, RING, 3)
    rows = lax.dynamic_slice_in_dim(jnp.concatenate([rows, rows], axis=1), yi, RING, axis=1)
    used = lax.dynamic_slice_in_dim(jnp.concatenate([used, used], axis=1), yi, RING, axis=1)
    rows = jnp.transpose(rows, (1, 0, 2, 3)).reshape(KEYS, LIST)
    used = jnp.transpose(used, (1, 0, 2)).reshape(KEYS)
    here = (rows % OWN // 3 == yi) & (jnp.arange(LIST, dtype=jnp.int32)[None, :] < used[:, None])
    place = (rows // KEYS - xi) % RING * OWN + rows % KEYS // OWN * 3 + rows % 3
    before = jnp.arange(LIST)[:, None] < jnp.arange(LIST)[None, :]
    rank = jnp.dot(
        here.astype(jnp.bfloat16), before.astype(jnp.bfloat16), preferred_element_type=jnp.float32
    ).astype(jnp.int32)
    at = here[:, None, :] & (rank[:, None, :] == jnp.arange(KEYS, dtype=jnp.int32)[None, :, None])
    lists = jnp.sum(jnp.where(at, place[:, None, :], 0), axis=2)
    return lists, jnp.sum(here.astype(jnp.int32), axis=1)


def for_blocks(lists, counts, blocks):
    picked = [lists[b * OWN : (b + 1) * OWN] for b in blocks] + [jnp.zeros((1, KEYS), jnp.int32)]
    sizes = [counts[b * OWN : (b + 1) * OWN] for b in blocks] + [jnp.zeros((1,), jnp.int32)]
    return jnp.concatenate(picked).reshape(-1), jnp.concatenate(sizes)


def exchange(array):
    return lax.all_to_all(array, GROUP, split_axis=0, concat_axis=0, tiled=True)


def on_device(queries, keys, values, kv_tiles, tile_count, assign):
    xi, yi = lax.axis_index("x"), lax.axis_index("y")
    sent = jnp.stack([a.reshape(96, 16, HD) for a in (keys, values)])
    kv0 = prepare(exchange(jnp.transpose(sent, (2, 0, 1, 3))))
    kv1, kv3 = shift(kv0, "x", -1), shift(kv0, "x", 1)
    queries, kv0 = lax.optimization_barrier((queries, kv0))
    q0 = exchange(jnp.transpose(queries.reshape(96, 16, HD), (1, 0, 2))).reshape(OWN, BLK, HD)
    k2, v2 = shift(kv3[0], "x", 1), shift(kv1[1], "x", -1)
    q1, q3 = shift(q0, "y", -1), shift(q0, "y", 1)
    half = OWN // 2
    q2 = jnp.concatenate([shift(q3[:half], "y", 1), shift(q1[half:], "y", -1)])
    lists, counts = key_lists(kv_tiles, tile_count, xi, yi)
    kv = (kv0, kv1, kv3, k2, v2)
    (o2,) = attend(*for_blocks(lists, counts, (2,)), (q2,), kv)
    o1, o3 = attend(*for_blocks(lists, counts, (1, 3)), (q1, q3), kv)
    (o0,) = attend(*for_blocks(lists, counts, (0,)), (q0,), kv)
    blended, lse = combine((o0, shift(o1, "y", 1), shift(o2, "y", 2), shift(o3, "y", -1)))
    back = exchange(blended.reshape(16, 96, HD))
    attended = jnp.transpose(back, (1, 0, 2)).reshape(96, 16 * HD)
    every = lax.all_to_all(
        jnp.broadcast_to(lse[None], (RING * RING, OWN, BLK)),
        ("x", "y"),
        split_axis=0,
        concat_axis=0,
        tiled=True,
    ).reshape(-1, BLK)
    tiles = lax.dynamic_slice_in_dim(assign, (xi * RING + yi) * OWN, OWN)
    spots = tiles // KEYS * KEYS + tiles % OWN // 3 * OWN + tiles % KEYS // OWN * 3 + tiles % 3
    chosen = jnp.take(every, spots, axis=0).reshape(1, OWN * BLK)
    turned = [(b * RING + a, a * RING + b) for a in range(RING) for b in range(RING)]
    return attended, lax.ppermute(chosen, ("zh", "y"), turned)


def solution(mesh):
    split = jax.sharding.Mesh(
        mesh.devices.reshape(RING, RING, RING, 2, 2), ("x", "zh", "y", "zl", "core")
    )
    tokens = P(("x", "zh", "y", "zl", "core"), None)
    return jax.shard_map(
        on_device,
        mesh=split,
        in_specs=(tokens, tokens, tokens, P(), P(), P()),
        out_specs=(tokens, P(("y", "zl", "core"), ("x", "zh"))),
        check_vma=False,
    )
```

time: 199 us -> 162 us (0.81)
  waiting for transfers between devices: 54.9 us -> 35.9 us
  Pallas kernels: 58.6 us -> 42.4 us
  blocking collectives: 23.5 us -> 12.5 us
  local copies, waits for them, and re-layouts: 9.22 us -> 16.6 us
    all_gather x1 -> x0, blocking collectives: 23.5 us -> none  [on_device(): lax.all_gather(lse.reshape(OWN, BLK), ('x', 'y'), axis=0, tiled=True)]
    ppermute x16 -> x11, waiting for transfers between devices: 24.2 us -> 2.08 us  [shift(): lax.ppermute(array, axis, [(i, (i + by) % RING) for i in range(RING)])]
    pallas_call x3 -> x4, Pallas kernels: 56 us -> 39.7 us  [the longest x3 37.5 us: attend(): pl.pallas_call(functools.partial(attend_kernel, blocks), out_shape=(tiles...]
    all_to_all x0 -> x1, blocking collectives: none -> 12.5 us  [on_device(): lax.all_to_all(jnp.broadcast_to(lse[None], (RING * RING, OWN, BLK)), ('x'...]
    ppermute x16 -> x11, starting transfers between devices: 25.5 us -> 16.1 us  [shift(): lax.ppermute(array, axis, [(i, (i + by) % RING) for i in range(RING)])]
    all_to_all x2 -> x3, starting transfers between devices: 12.3 us -> 20.1 us  [exchange(): return lax.all_to_all(array, GROUP, split_axis=0, concat_axis=0, tiled=True)]
    ppermute x1, waiting for transfers between devices: 2.66 us -> 7.05 us  [on_device(): return (attended, lax.ppermute(chosen, ('zh', 'y'), turned))]
    slice x6, local copies, waits for them, and re-layouts: 0.34 us -> 4.52 us  [the longest x5 3.93 us: for_blocks(): counts[b * OWN:(b + 1) * OWN]]
  transfers between devices with their start and end apart: 19 -> 15, of which waited for: 10 -> 4; matrix products, arithmetic and copies ran while one was open for 2% -> 10% of each run, Pallas kernels for 13% -> 24%
where the time goes in v2:
time: 162 us; the launch traced here: 160 us
  starting transfers between devices  45.4 us (28%)
  Pallas kernels  42.4 us (26%)
  waiting for transfers between devices  35.9 us (22%)
  local copies, waits for them, and re-layouts  16.6 us (10%)
  blocking collectives  12.5 us (8%)
  other arithmetic  5.82 us (4%)
    pallas_call x3, Pallas kernels, attend(): pl.pallas_call(functools.partial(attend_kernel, blocks), out_shape=(tiles...  37.5 us
    all_to_all x3, waiting for transfers between devices, exchange(): return lax.all_to_all(array, GROUP, split_axis=0, concat_axis=0, tiled=True)  26.8 us
    all_to_all x3, starting transfers between devices, exchange(): return lax.all_to_all(array, GROUP, split_axis=0, concat_axis=0, tiled=True)  20.1 us
    ppermute x11, starting transfers between devices, shift(): lax.ppermute(array, axis, [(i, (i + by) % RING) for i in range(RING)])  16.1 us
    all_to_all x1, blocking collectives, on_device(): lax.all_to_all(jnp.broadcast_to(lse[None], (RING * RING, OWN, BLK)), ('x'...  12.5 us
    ppermute x1, starting transfers between devices, on_device(): return (attended, lax.ppermute(chosen, ('zh', 'y'), turned))  9.18 us
    ppermute x1, waiting for transfers between devices, on_device(): return (attended, lax.ppermute(chosen, ('zh', 'y'), turned))  7.05 us
    slice x5, local copies, waits for them, and re-layouts, for_blocks(): counts[b * OWN:(b + 1) * OWN]  3.93 us
  transfers between devices with their start and end apart: 15, of which 4 were waited for; matrix products, arithmetic and copies ran while one was open for 10% of the time, Pallas kernels for 24%

profile of v2, /device:TPU:16, one launch (start us, length us, event | category | flops | bytes accessed | tf_op | source)
XLA Modules:
  0.0 159.7 jit_solution(14795535167873015164)
XLA Ops:
  0.7 1.1 copy.52
  2.1 1.0 maximum_bitcast_fusion
  3.1 8.7 %all-to-all-start = ((bf16[16,2,96,128]{3,2,1,0:T(8,128)(2,1)}), bf16[16,2,96,128]{3,2,1,0:T(8,128)(2,1)S(1)}, u32[]{:S(2)}, u32[]{:S(2)}) async-start(bf16[16,2,96,128]{3,2,1,0:T(8,128)(2,1)} %maximum_bitcast_fusion), calls=%async_computation | async-start | bytes 1572864 | tf_op jit(solution)/shard_map/all_to_all | solution.py:254
  14.0 18.5 %all-to-all-done.got_ref = bf16[16,2,96,128]{3,2,1,0:T(8,128)(2,1)S(1)} async-done(((bf16[16,2,96,128]{3,2,1,0:T(8,128)(2,1)}), bf16[16,2,96,128]{3,2,1,0:T(8,128)(2,1)S(1)}, u32[]{:S(2)}, u32[]{:S(2)}) %all-to-all-start) | async-done | bytes 786464 | tf_op jit(solution)/shard_map/all_to_all | solution.py:254
  32.5 0.9 copy-done.3
  33.4 2.2 %prepare.1.refs_1_.refs_2_ = bf16[2,12,128,128]{3,2,1,0:T(8,128)(2,1)} custom-call(bf16[16,2,96,128]{3,2,1,0:T(8,128)(2,1)} %copy-done.3), custom_call_target="tpu_custom_call" | custom-call | tf_op jit(solution)/shard_map/prepare/pallas_call | solution.py:43
  35.6 1.5 collective-permute-start.1
  37.1 0.8 bitcast_bitcast_fusion
  37.9 5.1 %all-to-all-start.1 = ((bf16[16,96,128]{2,1,0:T(8,128)(2,1)}), bf16[16,96,128]{2,1,0:T(8,128)(2,1)S(1)}, u32[]{:S(2)}, u32[]{:S(2)}) async-start(bf16[16,96,128]{2,1,0:T(8,128)(2,1)} %bitcast_bitcast_fusion), calls=%async_computation.1 | async-start | bytes 786432 | tf_op jit(solution)/shard_map/all_to_all | solution.py:254
  43.2 1.8 %collective-permute-start = (bf16[2,12,128,128]{3,2,1,0:T(8,128)(2,1)S(1)}, bf16[2,12,128,128]{3,2,1,0:T(8,128)(2,1)S(1)}, u32[]{:S(2)}, u32[]{:S(2)}) collective-permute-start(bf16[2,12,128,128]{3,2,1,0:T(8,128)(2,1)S(1)} %copy-done.1), channel_id=1, source_target_pairs={{0,192},{64,0},{128,64},{192,128},{1,193},{65,1},{129,65},{193,129... | collective-permute-start | bytes 2359304 | tf_op jit(solution)/shard_map/ppermute | solution.py:29
  45.0 0.9 select_reduce_fusion
  48.5 8.3 %all-to-all-done.1 = bf16[16,96,128]{2,1,0:T(8,128)(2,1)S(1)} async-done(((bf16[16,96,128]{2,1,0:T(8,128)(2,1)}), bf16[16,96,128]{2,1,0:T(8,128)(2,1)S(1)}, u32[]{:S(2)}, u32[]{:S(2)}) %all-to-all-start.1) | async-done | bytes 393248 | tf_op jit(solution)/shard_map/all_to_all | solution.py:254
  56.8 1.3 collective-permute-start.5
  59.6 1.5 collective-permute-start.2
  61.1 2.1 %collective-permute-done.refs_2_.refs_3_ = bf16[2,12,128,128]{3,2,1,0:T(8,128)(2,1)S(1)} collective-permute-done((bf16[2,12,128,128]{3,2,1,0:T(8,128)(2,1)S(1)}, bf16[2,12,128,128]{3,2,1,0:T(8,128)(2,1)S(1)}, u32[]{:S(2)}, u32[]{:S(2)}) %collective-permute-start) | collective-permute-done | bytes 786464 | tf_op jit(solution)/shard_map/ppermute | solution.py:29
  63.9 3.0 %collective-permute-start.3 = (bf16[12,128,128]{2,1,0:T(8,128)(2,1)}, bf16[12,128,128]{2,1,0:T(8,128)(2,1)}, u32[]{:S(2)}, u32[]{:S(2)}) collective-permute-start(bf16[12,128,128]{2,1,0:T(8,128)(2,1)} %slice_bitcast_fusion), channel_id=1, source_target_pairs={{0,192},{64,0},{128,64},{192,128},{1,193},{65,1},{129,65},{193,129... | collective-permute-start | bytes 1179656 | tf_op jit(solution)/shard_map/ppermute | solution.py:29
  67.5 0.8 reshape.188.lists
  68.3 1.2 slice.57
  69.6 1.3 slice.59
  72.4 1.4 collective-permute-start.7
  73.8 0.9 slice.78
  74.7 0.8 collective-permute-start.8
  75.5 18.3 %attend.4 = (bf16[12,144,128]{2,1,0:T(8,128)(2,1)}, bf16[12,144,128]{2,1,0:T(8,128)(2,1)}) custom-call(s32[1200]{0:T(1024)S(1)} %reshape.188.lists, s32[25]{0:T(128)S(1)} %pad_add_fusion.2.counts, bf16[12,128,128]{2,1,0:T(8,128)(2,1)} %collective-permute-done.4.refs_0_, bf16[12,128,128]{2,1,0:T(8,128)(2,1)S(1)} %collective-permute-done.5.refs_1_, ...), custom_call_target="tpu_custom_call" | custom-call | flops 3019898880 | bytes 5242880 | tf_op jit(solution)/shard_map/attend/pallas_call | solution.py:175
  94.0 2.0 %collective-permute-start.6 = (bf16[12,144,128]{2,1,0:T(8,128)(2,1)}, bf16[12,144,128]{2,1,0:T(8,128)(2,1)}, u32[]{:S(2)}, u32[]{:S(2)}) collective-permute-start(bf16[12,144,128]{2,1,0:T(8,128)(2,1)} %get-tuple-element.10), channel_id=1, source_target_pairs={{0,4},{4,8},{8,12},{12,0},{1,5},{5,9},{9,13},{13,1},{2,6},{6,10},{... | collective-permute-start | bytes 1327112 | tf_op jit(solution)/shard_map/ppermute | solution.py:29
  96.0 9.7 %attend.5 = bf16[12,144,128]{2,1,0:T(8,128)(2,1)} custom-call(s32[624]{0:T(1024)S(1)} %reshape.189.lists, s32[13]{0:T(128)S(1)} %pad_add_fusion.counts, bf16[12,128,128]{2,1,0:T(8,128)(2,1)S(1)} %pad_maximum_fusion.refs_0_, bf16[2,12,128,128]{3,2,1,0:T(8,128)(2,1)S(1)} %copy-done.1, bf16[2,12,128,128]{3,2,1,0:T(8,128)(2,1)S(1)} %collective-permute-done.refs_2_.refs_3_, ...), custom_call_target="tpu_custom_call" | custom-call | flops 1509949440 | bytes 5242880 | tf_op jit(solution)/shard_map/attend/pallas_call | solution.py:175
  105.8 2.1 %collective-permute-start.9 = (bf16[12,144,128]{2,1,0:T(8,128)(2,1)}, bf16[12,144,128]{2,1,0:T(8,128)(2,1)}, u32[]{:S(2)}, u32[]{:S(2)}) collective-permute-start(bf16[12,144,128]{2,1,0:T(8,128)(2,1)} %attend.5), channel_id=1, source_target_pairs={{0,8},{4,12},{8,0},{12,4},{1,9},{5,13},{9,1},{13,5},{2,10},{6,14},... | collective-permute-start | bytes 1327112 | tf_op jit(solution)/shard_map/ppermute | solution.py:29
  108.9 9.5 %attend.3.refs_0_ = bf16[12,144,128]{2,1,0:T(8,128)(2,1)S(1)} custom-call(s32[624]{0:T(1024)S(1)} %reshape.185.lists, s32[13]{0:T(128)S(1)} %pad_add_fusion.1.counts, bf16[12,128,128]{2,1,0:T(8,128)(2,1)S(1)} %bitcast.52, bf16[2,12,128,128]{3,2,1,0:T(8,128)(2,1)S(1)} %copy-done.1, bf16[2,12,128,128]{3,2,1,0:T(8,128)(2,1)S(1)} %collective-permute-done.refs_2_.refs_3_, ...), custom_call_target="tpu_custom_call" | custom-call | flops 1509949440 | bytes 5242880 | tf_op jit(solution)/shard_map/attend/pallas_call | solution.py:175
  119.2 2.6 %combine.1 = (bf16[12,128,128]{2,1,0:T(8,128)(2,1)}, f32[12,128]{1,0:T(8,128)}) custom-call(bf16[12,144,128]{2,1,0:T(8,128)(2,1)} %copy-done.2, bf16[12,144,128]{2,1,0:T(8,128)(2,1)} %collective-permute-done.6.refs_1_, bf16[12,144,128]{2,1,0:T(8,128)(2,1)} %collective-permute-done.9.refs_2_, bf16[12,144,128]{2,1,0:T(8,128)(2,1)} %collective-permute-done.10.refs_3_), custom_call_target="tpu_custom_call" | custom-call | tf_op jit(solution)/shard_map/combine/pallas_call | solution.py:217
  122.5 12.5 %all_to_all.20 = f32[16,12,128]{2,1,0:T(8,128)S(1)} all-to-all(f32[16,12,128]{2,1,0:T(8,128)S(1)} %broadcast_in_dim.40), channel_id=1, replica_groups=mesh['x'=4,'zh'=4,'y'=4,'zl'=2,'core'=2] {'x','y'}, dimensions={0} | all-to-all | bytes 196608 | tf_op jit(solution)/shard_map/all_to_all | solution.py:276
  135.1 6.3 %all-to-all-start.2 = ((bf16[16,96,128]{2,1,0:T(8,128)(2,1)}), bf16[16,96,128]{2,1,0:T(8,128)(2,1)S(1)}, u32[]{:S(2)}, u32[]{:S(2)}) async-start(bf16[16,96,128]{2,1,0:T(8,128)(2,1)} %bitcast.57), calls=%async_computation.2 | async-start | bytes 786432 | tf_op jit(solution)/shard_map/all_to_all | solution.py:254
  142.1 9.2 %collective-permute-start.11 = (f32[1,1536]{1,0:T(1,128)S(1)}, f32[1,1536]{1,0:T(1,128)S(1)}, u32[]{:S(2)}, u32[]{:S(2)}) collective-permute-start(f32[1,1536]{1,0:T(1,128)S(1)} %bitcast.59), channel_id=1, source_target_pairs={{0,0},{16,4},{32,8},{48,12},{4,16},{20,20},{36,24},{52,28},{8,32},... | collective-permute-start | bytes 18440 | tf_op jit(solution)/shard_map/ppermute | solution.py:287
  151.3 7.0 %collective-permute-done.11 = f32[1,1536]{1,0:T(1,128)S(1)} collective-permute-done((f32[1,1536]{1,0:T(1,128)S(1)}, f32[1,1536]{1,0:T(1,128)S(1)}, u32[]{:S(2)}, u32[]{:S(2)}) %collective-permute-start.11) | collective-permute-done | bytes 6176 | tf_op jit(solution)/shard_map/ppermute | solution.py:287
  (87 shorter events, 14.4 us)
Async XLA Ops:
  0.6 36.5 %copy-start = (bf16[96,2048]{1,0:T(8,128)(2,1)S(1)}, bf16[96,2048]{1,0:T(8,128)(2,1)}, u32[]{:S(2)}) copy-start(bf16[96,2048]{1,0:T(8,128)(2,1)} %param.6) | copy-start | bytes 1179652
  0.6 1.3 copy-start.4
  3.1 9.5 %copy-start.10 = (s32[192]{0:T(256)S(1)}, s32[192]{0:T(256)}, u32[]{:S(2)}) copy-start(s32[192]{0:T(256)} %param.10) | copy-start | bytes 2308
  3.1 29.4 %all-to-all-start = ((bf16[16,2,96,128]{3,2,1,0:T(8,128)(2,1)}), bf16[16,2,96,128]{3,2,1,0:T(8,128)(2,1)S(1)}, u32[]{:S(2)}, u32[]{:S(2)}) async-start(bf16[16,2,96,128]{3,2,1,0:T(8,128)(2,1)} %maximum_bitcast_fusion), calls=%async_computation | async-start | bytes 1572864 | tf_op jit(solution)/shard_map/all_to_all | solution.py:254
  32.5 0.9 copy-start.3
  35.6 7.6 %copy-start.1 = (bf16[2,12,128,128]{3,2,1,0:T(8,128)(2,1)S(1)}, bf16[2,12,128,128]{3,2,1,0:T(8,128)(2,1)}, u32[]{:S(2)}) copy-start(bf16[2,12,128,128]{3,2,1,0:T(8,128)(2,1)} %prepare.1.refs_1_.refs_2_) | copy-start | bytes 2359300
  35.6 23.2 %collective-permute-start.1 = (bf16[2,12,128,128]{3,2,1,0:T(8,128)(2,1)}, bf16[2,12,128,128]{3,2,1,0:T(8,128)(2,1)S(1)}, u32[]{:S(2)}, u32[]{:S(2)}) collective-permute-start(bf16[2,12,128,128]{3,2,1,0:T(8,128)(2,1)} %prepare.1.refs_1_.refs_2_), channel_id=1, source_target_pairs={{0,64},{64,128},{128,192},{192,0},{1,65},{65,129},{129,193},{193,1... | collective-permute-start | bytes 2359304 | tf_op jit(solution)/shard_map/ppermute | solution.py:29
  37.9 18.8 %all-to-all-start.1 = ((bf16[16,96,128]{2,1,0:T(8,128)(2,1)}), bf16[16,96,128]{2,1,0:T(8,128)(2,1)S(1)}, u32[]{:S(2)}, u32[]{:S(2)}) async-start(bf16[16,96,128]{2,1,0:T(8,128)(2,1)} %bitcast_bitcast_fusion), calls=%async_computation.1 | async-start | bytes 786432 | tf_op jit(solution)/shard_map/all_to_all | solution.py:254
  43.2 19.9 %collective-permute-start = (bf16[2,12,128,128]{3,2,1,0:T(8,128)(2,1)S(1)}, bf16[2,12,128,128]{3,2,1,0:T(8,128)(2,1)S(1)}, u32[]{:S(2)}, u32[]{:S(2)}) collective-permute-start(bf16[2,12,128,128]{3,2,1,0:T(8,128)(2,1)S(1)} %copy-done.1), channel_id=1, source_target_pairs={{0,192},{64,0},{128,64},{192,128},{1,193},{65,1},{129,65},{193,129... | collective-permute-start | bytes 2359304 | tf_op jit(solution)/shard_map/ppermute | solution.py:29
  45.9 0.6 copy-start.5
  56.8 10.1 %copy-start.6 = (s32[12,48]{1,0:T(8,128)S(1)}, s32[12,48]{1,0:T(8,128)}, u32[]{:S(2)}) copy-start(s32[12,48]{1,0:T(8,128)} %get-tuple-element.23) | copy-start | bytes 6916
  56.8 10.1 %copy-start.7 = (s32[25]{0:T(128)S(1)}, s32[25]{0:T(128)}, u32[]{:S(2)}) copy-start(s32[25]{0:T(128)} %pad.11.clone) | copy-start | bytes 304
  56.8 15.6 %collective-permute-start.5 = (bf16[12,128,128]{2,1,0:T(8,128)(2,1)S(1)}, bf16[12,128,128]{2,1,0:T(8,128)(2,1)S(1)}, u32[]{:S(2)}, u32[]{:S(2)}) collective-permute-start(bf16[12,128,128]{2,1,0:T(8,128)(2,1)S(1)} %bitcast.50), channel_id=1, source_target_pairs={{0,4},{4,8},{8,12},{12,0},{1,5},{5,9},{9,13},{13,1},{2,6},{6,10},{... | collective-permute-start | bytes 1179656 | tf_op jit(solution)/shard_map/ppermute | solution.py:29
  58.0 15.7 %collective-permute-start.4 = (bf16[12,128,128]{2,1,0:T(8,128)(2,1)S(1)}, bf16[12,128,128]{2,1,0:T(8,128)(2,1)}, u32[]{:S(2)}, u32[]{:S(2)}) collective-permute-start(bf16[12,128,128]{2,1,0:T(8,128)(2,1)S(1)} %bitcast.51), channel_id=1, source_target_pairs={{0,12},{4,0},{8,4},{12,8},{1,13},{5,1},{9,5},{13,9},{2,14},{6,2},{... | collective-permute-start | bytes 1179656 | tf_op jit(solution)/shard_map/ppermute | solution.py:29
  59.6 16.0 %collective-permute-start.2 = (bf16[12,128,128]{2,1,0:T(8,128)(2,1)}, bf16[12,128,128]{2,1,0:T(8,128)(2,1)}, u32[]{:S(2)}, u32[]{:S(2)}) collective-permute-start(bf16[12,128,128]{2,1,0:T(8,128)(2,1)} %slice_bitcast_fusion.1), channel_id=1, source_target_pairs={{0,64},{64,128},{128,192},{192,0},{1,65},{65,129},{129,193},{193,1... | collective-permute-start | bytes 1179656 | tf_op jit(solution)/shard_map/ppermute | solution.py:29
  63.9 11.7 %collective-permute-start.3 = (bf16[12,128,128]{2,1,0:T(8,128)(2,1)}, bf16[12,128,128]{2,1,0:T(8,128)(2,1)}, u32[]{:S(2)}, u32[]{:S(2)}) collective-permute-start(bf16[12,128,128]{2,1,0:T(8,128)(2,1)} %slice_bitcast_fusion), channel_id=1, source_target_pairs={{0,192},{64,0},{128,64},{192,128},{1,193},{65,1},{129,65},{193,129... | collective-permute-start | bytes 1179656 | tf_op jit(solution)/shard_map/ppermute | solution.py:29
  72.4 23.6 %collective-permute-start.7 = (bf16[6,128,128]{2,1,0:T(8,128)(2,1)S(1)}, bf16[6,128,128]{2,1,0:T(8,128)(2,1)S(1)}, u32[]{:S(2)}, u32[]{:S(2)}) collective-permute-start(bf16[6,128,128]{2,1,0:T(8,128)(2,1)S(1)} %slice.77), channel_id=1, source_target_pairs={{0,4},{4,8},{8,12},{12,0},{1,5},{5,9},{9,13},{13,1},{2,6},{6,10},{... | collective-permute-start | bytes 589832 | tf_op jit(solution)/shard_map/ppermute | solution.py:29
  74.7 21.3 %collective-permute-start.8 = (bf16[6,128,128]{2,1,0:T(8,128)(2,1)S(1)}, bf16[6,128,128]{2,1,0:T(8,128)(2,1)S(1)}, u32[]{:S(2)}, u32[]{:S(2)}) collective-permute-start(bf16[6,128,128]{2,1,0:T(8,128)(2,1)S(1)} %slice.78), channel_id=1, source_target_pairs={{0,12},{4,0},{8,4},{12,8},{1,13},{5,1},{9,5},{13,9},{2,14},{6,2},{... | collective-permute-start | bytes 589832 | tf_op jit(solution)/shard_map/ppermute | solution.py:29
  93.9 25.3 %collective-permute-start.10 = (bf16[12,144,128]{2,1,0:T(8,128)(2,1)}, bf16[12,144,128]{2,1,0:T(8,128)(2,1)}, u32[]{:S(2)}, u32[]{:S(2)}) collective-permute-start(bf16[12,144,128]{2,1,0:T(8,128)(2,1)} %get-tuple-element.11), channel_id=1, source_target_pairs={{0,12},{4,0},{8,4},{12,8},{1,13},{5,1},{9,5},{13,9},{2,14},{6,2},{... | collective-permute-start | bytes 1327112 | tf_op jit(solution)/shard_map/ppermute | solution.py:29
  94.0 25.2 %collective-permute-start.6 = (bf16[12,144,128]{2,1,0:T(8,128)(2,1)}, bf16[12,144,128]{2,1,0:T(8,128)(2,1)}, u32[]{:S(2)}, u32[]{:S(2)}) collective-permute-start(bf16[12,144,128]{2,1,0:T(8,128)(2,1)} %get-tuple-element.10), channel_id=1, source_target_pairs={{0,4},{4,8},{8,12},{12,0},{1,5},{5,9},{9,13},{13,1},{2,6},{6,10},{... | collective-permute-start | bytes 1327112 | tf_op jit(solution)/shard_map/ppermute | solution.py:29
  96.0 11.9 %copy-start.8 = (pred[13]{0:T(512)(128)(4,1)S(1)}, pred[13]{0:T(512)(128)(4,1)}, u32[]{:S(2)}) copy-start(pred[13]{0:T(512)(128)(4,1)} %constant.99.clone.1) | copy-start | bytes 43
  105.8 13.4 %collective-permute-start.9 = (bf16[12,144,128]{2,1,0:T(8,128)(2,1)}, bf16[12,144,128]{2,1,0:T(8,128)(2,1)}, u32[]{:S(2)}, u32[]{:S(2)}) collective-permute-start(bf16[12,144,128]{2,1,0:T(8,128)(2,1)} %attend.5), channel_id=1, source_target_pairs={{0,8},{4,12},{8,0},{12,4},{1,9},{5,13},{9,1},{13,5},{2,10},{6,14},... | collective-permute-start | bytes 1327112 | tf_op jit(solution)/shard_map/ppermute | solution.py:29
  118.4 0.8 copy-start.2
  121.8 19.5 %copy-start.9 = (s32[192]{0:T(256)S(1)}, s32[192]{0:T(256)}, u32[]{:S(2)}) copy-start(s32[192]{0:T(256)} %param.11) | copy-start | bytes 2308
  135.1 23.3 %all-to-all-start.2 = ((bf16[16,96,128]{2,1,0:T(8,128)(2,1)}), bf16[16,96,128]{2,1,0:T(8,128)(2,1)S(1)}, u32[]{:S(2)}, u32[]{:S(2)}) async-start(bf16[16,96,128]{2,1,0:T(8,128)(2,1)} %bitcast.57), calls=%async_computation.2 | async-start | bytes 786432 | tf_op jit(solution)/shard_map/all_to_all | solution.py:254
  142.1 16.2 %collective-permute-start.11 = (f32[1,1536]{1,0:T(1,128)S(1)}, f32[1,1536]{1,0:T(1,128)S(1)}, u32[]{:S(2)}, u32[]{:S(2)}) collective-permute-start(f32[1,1536]{1,0:T(1,128)S(1)} %bitcast.59), channel_id=1, source_target_pairs={{0,0},{16,4},{32,8},{48,12},{4,16},{20,20},{36,24},{52,28},{8,32},... | collective-permute-start | bytes 18440 | tf_op jit(solution)/shard_map/ppermute | solution.py:287

commit v3 on v2

--- a/solution.py
+++ b/solution.py
@@ -49,59 +49,102 @@
     )(got)
 
 
-def attend_kernel(blocks, lists, counts, *refs):
-    tiles = blocks * OWN
-    q_in, refs = refs[:blocks], refs[blocks:]
-    kv0, kv1, kv3, k2, v2 = refs[:5]
-    refs = refs[5:]
-    o_out, refs = refs[:blocks], refs[blocks:]
-    qs, ks, vs, sems, m_ref, l_ref, acc_ref = refs[:7]
+def pack_kernel(kv0, kv1, kv3, ks, vs, sems):
+    copies = []
+    for b, kv in ((0, kv0), (1, kv1), (3, kv3)):
+        for which, held in enumerate((ks, vs)):
+            span = pl.ds(b * OWN, OWN)
+            copies.append(
+                pltpu.make_async_copy(kv.at[which], held.at[span], sems.at[len(copies)])
+            )
+    for copy in copies:
+        copy.start()
+    for copy in copies:
+        copy.wait()
+
+
+def pack(kv0, kv1, kv3):
+    tiles = jax.ShapeDtypeStruct((KEYS, BLK, HD), jnp.bfloat16)
+    return pl.pallas_call(
+        pack_kernel,
+        out_shape=(tiles, tiles),
+        in_specs=[VMEM] * 3,
+        out_specs=(VMEM, VMEM),
+        scratch_shapes=[pltpu.SemaphoreType.DMA((6,))],
+        name="pack",
+    )(kv0, kv1, kv3)
+
+
+def attend_kernel(blocks, last, lists, counts, *refs):
+    tiles = len(blocks) * OWN
+    queries, refs = refs[: len(blocks)], refs[len(blocks) :]
+    if last:
+        k2, v2, _, _, ks, vs = refs[:6]
+        o_out, refs = refs[6 : 6 + len(blocks)], refs[6 + len(blocks) :]
+    else:
+        ks, vs = refs[:2]
+        o_out, refs = refs[2 : 2 + len(blocks)], refs[2 + len(blocks) :]
+    sems, rows, sizes, qs, m_ref, l_ref, acc_ref = refs[:7]
     s_refs, top_refs = refs[7 : 7 + WIDTH], refs[7 + WIDTH :]
-    moves = [(q, qs, b) for b, q in enumerate(q_in)]
-    for b, (k, v) in enumerate(
-        ((kv0.at[0], kv0.at[1]), (kv1.at[0], kv1.at[1]), (k2, v2), (kv3.at[0], kv3.at[1]))
-    ):
-        moves += [(k, ks, b), (v, vs, b)]
+    moves = [(q, qs, b * OWN) for b, q in enumerate(queries)]
+    if last:
+        moves += [(k2, ks, 2 * OWN), (v2, vs, 2 * OWN)]
     copies = [
-        pltpu.make_async_copy(source, held.at[pl.ds(b * OWN, OWN)], sems.at[i])
-        for i, (source, held, b) in enumerate(moves)
+        pltpu.make_async_copy(source, held.at[pl.ds(at, OWN)], sems.at[i])
+        for i, (source, held, at) in enumerate(moves)
     ]
     for copy in copies:
         copy.start()
     m_ref[...] = jnp.full(m_ref.shape, NEG, jnp.float32)
     l_ref[...] = jnp.zeros(l_ref.shape, jnp.float32)
     acc_ref[...] = jnp.zeros(acc_ref.shape, jnp.float32)
-
-    def steps_of(t):
-        return jnp.maximum((counts[t] + CHUNK - 1) // CHUNK, 1)
-
-    items = lax.fori_loop(0, tiles, lambda t, n: n + steps_of(t), jnp.int32(0))
+    yi = lax.axis_index("y")
+    items = jnp.int32(0)
+    for b, block in enumerate(blocks):
+        owner = lax.rem(yi + block, RING) * 3
+        for t in range(OWN):
+            row = owner + (t // 3 * OWN + t % 3)
+            rows[b * OWN + t] = row
+            sizes[b * OWN + t] = counts[row]
+            items += jnp.maximum((counts[row] + CHUNK - 1) // CHUNK, 1)
+    rows[tiles] = 0
+    sizes[tiles] = 0
 
     def advance(t, j):
-        more = j + 1 < steps_of(t)
+        more = (j + 1) * CHUNK < sizes[t]
         return jnp.where(more, t, jnp.minimum(t + 1, tiles)), jnp.where(more, j + 1, 0)
 
     def listed(t, j):
-        base = t * KEYS + j * CHUNK
-        return [lists[base + u] for u in range(CHUNK)]
+        row = rows[t]
+        return [lists[row, j * CHUNK + u] for u in range(CHUNK)]
 
     def score(lane, t, j):
-        left = counts[t] - j * CHUNK
+        left = sizes[t] - j * CHUNK
+        tile = listed(t, j)
+        q = qs[jnp.minimum(t, tiles - 1)]
+        none = jnp.zeros_like(q)
+        twice = jnp.concatenate(
+            [jnp.concatenate([q, none], axis=1), jnp.concatenate([none, q], axis=1)], axis=0
+        )
+        pairs = [
+            jnp.concatenate([ks[tile[u]], ks[tile[u + 1]]], axis=1) for u in range(0, CHUNK, 2)
+        ]
         s = lax.dot_general(
-            jnp.concatenate([ks[tile] for tile in listed(t, j)], axis=0),
-            qs[jnp.minimum(t, tiles - 1)],
+            jnp.concatenate(pairs, axis=0),
+            twice,
             (((1,), (1,)), ((), ())),
             preferred_element_type=jnp.float32,
         )
         s_refs[lane][...] = s
         top = jnp.full((8, BLK), NEG, jnp.float32)
         for u in range(CHUNK):
-            part = jnp.max(s[u * BLK : (u + 1) * BLK].reshape(16, 8, BLK), axis=0)
+            part = s[u // 2 * BLK : (u // 2 + 1) * BLK, u % 2 * BLK : (u % 2 + 1) * BLK]
+            part = jnp.max(part.reshape(16, 8, BLK), axis=0)
             top = jnp.maximum(top, jnp.where(u < left, part, NEG))
         top_refs[lane][...] = jnp.max(top, axis=0, keepdims=True)
 
     def blend(lane, t, j):
-        left = counts[t] - j * CHUNK
+        left = sizes[t] - j * CHUNK
         m_old = m_ref[t]
         m_new = jnp.maximum(m_old, top_refs[lane][...])
         m_ref[t] = m_new
@@ -110,8 +153,8 @@
         total = jnp.zeros((8, BLK), jnp.float32)
         weights = []
         for u in range(CHUNK):
-            s = s_refs[lane][u * BLK : (u + 1) * BLK] * (SCALE * LOG2E)
-            w = jnp.exp2(s - jnp.where(u < left, base, -NEG))
+            s = s_refs[lane][u // 2 * BLK : (u // 2 + 1) * BLK, u % 2 * BLK : (u % 2 + 1) * BLK]
+            w = jnp.exp2(s * (SCALE * LOG2E) - jnp.where(u < left, base, -NEG))
             total = total + jnp.sum(w.reshape(16, 8, BLK), axis=0)
             weights.append(w.astype(jnp.bfloat16))
         vt = jnp.concatenate([vs[tile] for tile in listed(t, j)], axis=1)
@@ -143,7 +186,7 @@
 
     lax.fori_loop(0, (items + WIDTH - 1) // WIDTH, step, tuple(first))
 
-    for b in range(blocks):
+    for b in range(len(blocks)):
 
         def finish(i, _):
             for u in range(4):
@@ -167,26 +210,28 @@
         lax.fori_loop(0, OWN // 4, finish, 0)
 
 
-def attend(lists, counts, queries, kv):
-    blocks = len(queries)
+def attend(blocks, lists, counts, queries, keys, values, last=()):
     tiles = jax.ShapeDtypeStruct((OWN, HD + PAD, BLK), jnp.bfloat16)
-    slots = blocks * OWN + 1
-    pairs = blocks * OWN * 15
+    held = jax.ShapeDtypeStruct((KEYS, BLK, HD), jnp.bfloat16)
+    count = len(blocks)
+    slots = count * OWN + 1
+    pairs = count * OWN * 15
     return pl.pallas_call(
-        functools.partial(attend_kernel, blocks),
-        out_shape=(tiles,) * blocks,
-        in_specs=[SMEM, SMEM] + [ANY] * (blocks + 5),
-        out_specs=(VMEM,) * blocks,
+        functools.partial(attend_kernel, blocks, bool(last)),
+        out_shape=((held, held) if last else ()) + (tiles,) * count,
+        in_specs=[SMEM, SMEM] + [VMEM] * (count + len(last) + 2),
+        out_specs=(VMEM,) * (count + len(last)),
+        input_output_aliases={count + 4: 0, count + 5: 1} if last else {},
         scratch_shapes=[
-            pltpu.VMEM((blocks * OWN, BLK, HD), jnp.bfloat16),
-            pltpu.VMEM((KEYS, BLK, HD), jnp.bfloat16),
-            pltpu.VMEM((KEYS, HD, BLK), jnp.bfloat16),
-            pltpu.SemaphoreType.DMA((blocks + 2 * RING,)),
+            pltpu.SemaphoreType.DMA((count + len(last),)),
+            pltpu.SMEM((slots,), jnp.int32),
+            pltpu.SMEM((slots,), jnp.int32),
+            pltpu.VMEM((count * OWN, BLK, HD), jnp.bfloat16),
             pltpu.VMEM((slots, 1, BLK), jnp.float32),
             pltpu.VMEM((slots, 8, BLK), jnp.float32),
             pltpu.VMEM((slots, HD, BLK), jnp.float32),
         ]
-        + [pltpu.VMEM((CHUNK * BLK, BLK), jnp.float32)] * WIDTH
+        + [pltpu.VMEM((CHUNK // 2 * BLK, 2 * BLK), jnp.float32)] * WIDTH
         + [pltpu.VMEM((1, BLK), jnp.float32)] * WIDTH,
         compiler_params=pltpu.CompilerParams(vmem_limit_bytes=32 * 1024 * 1024),
         cost_estimate=pl.CostEstimate(
@@ -195,7 +240,7 @@
             transcendentals=pairs * BLK * BLK,
         ),
         name="attend",
-    )(lists, counts, *queries, *kv)
+    )(lists, counts, *queries, *last, keys, values)
 
 
 def combine_kernel(*refs):
@@ -227,12 +272,8 @@
 
 
 def key_lists(kv_tiles, tile_count, xi, yi):
-    rows = lax.dynamic_slice_in_dim(kv_tiles, xi * KEYS, KEYS).reshape(RING, RING, 3, LIST)
-    used = lax.dynamic_slice_in_dim(tile_count, xi * KEYS, KEYS).reshape(RING, RING, 3)
-    rows = lax.dynamic_slice_in_dim(jnp.concatenate([rows, rows], axis=1), yi, RING, axis=1)
-    used = lax.dynamic_slice_in_dim(jnp.concatenate([used, used], axis=1), yi, RING, axis=1)
-    rows = jnp.transpose(rows, (1, 0, 2, 3)).reshape(KEYS, LIST)
-    used = jnp.transpose(used, (1, 0, 2)).reshape(KEYS)
+    rows = lax.dynamic_slice_in_dim(kv_tiles, xi * KEYS, KEYS)
+    used = lax.dynamic_slice_in_dim(tile_count, xi * KEYS, KEYS)
     here = (rows % OWN // 3 == yi) & (jnp.arange(LIST, dtype=jnp.int32)[None, :] < used[:, None])
     place = (rows // KEYS - xi) % RING * OWN + rows % KEYS // OWN * 3 + rows % 3
     before = jnp.arange(LIST)[:, None] < jnp.arange(LIST)[None, :]
@@ -244,20 +285,17 @@
     return lists, jnp.sum(here.astype(jnp.int32), axis=1)
 
 
-def for_blocks(lists, counts, blocks):
-    picked = [lists[b * OWN : (b + 1) * OWN] for b in blocks] + [jnp.zeros((1, KEYS), jnp.int32)]
-    sizes = [counts[b * OWN : (b + 1) * OWN] for b in blocks] + [jnp.zeros((1,), jnp.int32)]
-    return jnp.concatenate(picked).reshape(-1), jnp.concatenate(sizes)
-
-
 def exchange(array):
     return lax.all_to_all(array, GROUP, split_axis=0, concat_axis=0, tiled=True)
 
 
 def on_device(queries, keys, values, kv_tiles, tile_count, assign):
     xi, yi = lax.axis_index("x"), lax.axis_index("y")
+    lists, counts = key_lists(kv_tiles, tile_count, xi, yi)
     sent = jnp.stack([a.reshape(96, 16, HD) for a in (keys, values)])
-    kv0 = prepare(exchange(jnp.transpose(sent, (2, 0, 1, 3))))
+    got = exchange(jnp.transpose(sent, (2, 0, 1, 3)))
+    got, lists, counts = lax.optimization_barrier((got, lists, counts))
+    kv0 = prepare(got)
     kv1, kv3 = shift(kv0, "x", -1), shift(kv0, "x", 1)
     queries, kv0 = lax.optimization_barrier((queries, kv0))
     q0 = exchange(jnp.transpose(queries.reshape(96, 16, HD), (1, 0, 2))).reshape(OWN, BLK, HD)
@@ -265,21 +303,16 @@
     q1, q3 = shift(q0, "y", -1), shift(q0, "y", 1)
     half = OWN // 2
     q2 = jnp.concatenate([shift(q3[:half], "y", 1), shift(q1[half:], "y", -1)])
-    lists, counts = key_lists(kv_tiles, tile_count, xi, yi)
-    kv = (kv0, kv1, kv3, k2, v2)
-    (o2,) = attend(*for_blocks(lists, counts, (2,)), (q2,), kv)
-    o1, o3 = attend(*for_blocks(lists, counts, (1, 3)), (q1, q3), kv)
-    (o0,) = attend(*for_blocks(lists, counts, (0,)), (q0,), kv)
+    some_keys, some_values = pack(kv0, kv1, kv3)
+    all_keys, all_values, o1, o3 = attend(
+        (1, 3), lists, counts, (q1, q3), some_keys, some_values, (k2, v2)
+    )
+    (o2,) = attend((2,), lists, counts, (q2,), all_keys, all_values)
+    (o0,) = attend((0,), lists, counts, (q0,), all_keys, all_values)
     blended, lse = combine((o0, shift(o1, "y", 1), shift(o2, "y", 2), shift(o3, "y", -1)))
     back = exchange(blended.reshape(16, 96, HD))
     attended = jnp.transpose(back, (1, 0, 2)).reshape(96, 16 * HD)
-    every = lax.all_to_all(
-        jnp.broadcast_to(lse[None], (RING * RING, OWN, BLK)),
-        ("x", "y"),
-        split_axis=0,
-        concat_axis=0,
-        tiled=True,
-    ).reshape(-1, BLK)
+    every = lax.all_gather(lax.all_gather(lse, "y"), "x").reshape(-1, BLK)
     tiles = lax.dynamic_slice_in_dim(assign, (xi * RING + yi) * OWN, OWN)
     spots = tiles // KEYS * KEYS + tiles % OWN // 3 * OWN + tiles % KEYS // OWN * 3 + tiles % 3
     chosen = jnp.take(every, spots, axis=0).reshape(1, OWN * BLK)

time: 162 us -> 169 us (1.043)
  blocking collectives: 12.5 us -> 30 us
  Pallas kernels: 42.4 us -> 37.7 us
  local copies, waits for them, and re-layouts: 16.6 us -> 12.3 us
  waiting for transfers between devices: 35.9 us -> 39.1 us
  other arithmetic: 5.82 us -> 3.03 us
    all_gather x0 -> x2, blocking collectives: none -> 30 us  [on_device(): every = lax.all_gather(lax.all_gather(lse, 'y'), 'x').reshape(-1, BLK)]
    all_to_all x1 -> x0, blocking collectives: 12.5 us -> none  [on_device(): lax.all_to_all(jnp.broadcast_to(lse[None], (RING * RING, OWN, BLK)), ('x'...]
    pallas_call x3 -> x4, Pallas kernels: 37.5 us -> 33 us  [the longest x3 28.5 us: attend(): pl.pallas_call(functools.partial(attend_kernel, blocks, bool(last)), out_...]
    slice x6 -> x0, local copies, waits for them, and re-layouts: 4.52 us -> none  [the longest x5 3.93 us: for_blocks(): counts[b * OWN:(b + 1) * OWN]]
    unnamed x26 -> x30, local copies, waits for them, and re-layouts: 3.54 us -> 8.02 us
    ppermute x1, waiting for transfers between devices: 7.05 us -> 2.58 us  [on_device(): return (attended, lax.ppermute(chosen, ('zh', 'y'), turned))]
    ppermute x11, waiting for transfers between devices: 2.08 us -> 6.02 us  [shift(): lax.ppermute(array, axis, [(i, (i + by) % RING) for i in range(RING)])]
    all_to_all x3, waiting for transfers between devices: 26.8 us -> 30.5 us  [exchange(): return lax.all_to_all(array, GROUP, split_axis=0, concat_axis=0, tiled=True)]
  transfers between devices with their start and end apart: 15 -> 15, of which waited for: 4 -> 6; matrix products, arithmetic and copies ran while one was open for 10% -> 3% of each run, Pallas kernels for 24% -> 20%
where the time goes in v3:
time: 169 us; the launch traced here: 168 us
  starting transfers between devices  44.8 us (27%)
  waiting for transfers between devices  39.1 us (23%)
  Pallas kernels  37.7 us (22%)
  blocking collectives  30 us (18%)
  local copies, waits for them, and re-layouts  12.3 us (7%)
  other arithmetic  3.03 us (2%)
    all_to_all x3, waiting for transfers between devices, exchange(): return lax.all_to_all(array, GROUP, split_axis=0, concat_axis=0, tiled=True)  30.5 us
    all_gather x2, blocking collectives, on_device(): every = lax.all_gather(lax.all_gather(lse, 'y'), 'x').reshape(-1, BLK)  30 us
    pallas_call x3, Pallas kernels, attend(): pl.pallas_call(functools.partial(attend_kernel, blocks, bool(last)), out_...  28.5 us
    all_to_all x3, starting transfers between devices, exchange(): return lax.all_to_all(array, GROUP, split_axis=0, concat_axis=0, tiled=True)  18.4 us
    ppermute x11, starting transfers between devices, shift(): lax.ppermute(array, axis, [(i, (i + by) % RING) for i in range(RING)])  17.1 us
    ppermute x1, starting transfers between devices, on_device(): return (attended, lax.ppermute(chosen, ('zh', 'y'), turned))  9.24 us
    unnamed x30, local copies, waits for them, and re-layouts  8.02 us
    ppermute x11, waiting for transfers between devices, shift(): lax.ppermute(array, axis, [(i, (i + by) % RING) for i in range(RING)])  6.02 us
  transfers between devices with their start and end apart: 15, of which 6 were waited for; matrix products, arithmetic and copies ran while one was open for 3% of the time, Pallas kernels for 20%

profile of v3, /device:TPU:16, one launch (start us, length us, event | category | flops | bytes accessed | tf_op | source)
XLA Modules:
  0.0 168.0 jit_solution(68864093240966389)
XLA Ops:
  0.7 1.1 copy.26
  2.1 1.0 maximum_bitcast_fusion
  3.1 8.7 %all-to-all-start = ((bf16[16,2,96,128]{3,2,1,0:T(8,128)(2,1)}), bf16[16,2,96,128]{3,2,1,0:T(8,128)(2,1)S(1)}, u32[]{:S(2)}, u32[]{:S(2)}) async-start(bf16[16,2,96,128]{3,2,1,0:T(8,128)(2,1)} %maximum_bitcast_fusion), calls=%async_computation | async-start | bytes 1572864 | tf_op jit(solution)/shard_map/all_to_all | solution.py:289
  11.9 0.9 convert_reduce_fusion
  13.9 18.6 %all-to-all-done.got_ref = bf16[16,2,96,128]{3,2,1,0:T(8,128)(2,1)S(1)} async-done(((bf16[16,2,96,128]{3,2,1,0:T(8,128)(2,1)}), bf16[16,2,96,128]{3,2,1,0:T(8,128)(2,1)S(1)}, u32[]{:S(2)}, u32[]{:S(2)}) %all-to-all-start) | async-done | bytes 786464 | tf_op jit(solution)/shard_map/all_to_all | solution.py:289
  33.4 2.2 %prepare.1.kv0 = bf16[2,12,128,128]{3,2,1,0:T(8,128)(2,1)} custom-call(bf16[16,2,96,128]{3,2,1,0:T(8,128)(2,1)} %copy-done.4), custom_call_target="tpu_custom_call" | custom-call | tf_op jit(solution)/shard_map/prepare/pallas_call | solution.py:43
  35.6 1.5 collective-permute-start.2
  37.9 5.1 %all-to-all-start.1 = ((bf16[16,96,128]{2,1,0:T(8,128)(2,1)}), bf16[16,96,128]{2,1,0:T(8,128)(2,1)S(1)}, u32[]{:S(2)}, u32[]{:S(2)}) async-start(bf16[16,96,128]{2,1,0:T(8,128)(2,1)} %bitcast_bitcast_fusion), calls=%async_computation.1 | async-start | bytes 786432 | tf_op jit(solution)/shard_map/all_to_all | solution.py:289
  43.0 1.8 %collective-permute-start.4 = (bf16[2,12,128,128]{3,2,1,0:T(8,128)(2,1)S(1)}, bf16[2,12,128,128]{3,2,1,0:T(8,128)(2,1)}, u32[]{:S(2)}, u32[]{:S(2)}) collective-permute-start(bf16[2,12,128,128]{3,2,1,0:T(8,128)(2,1)S(1)} %copy-done.5), channel_id=1, source_target_pairs={{0,192},{64,0},{128,64},{192,128},{1,193},{65,1},{129,65},{193,129... | collective-permute-start | bytes 2359304 | tf_op jit(solution)/shard_map/ppermute | solution.py:29
  44.9 11.9 %all-to-all-done.1 = bf16[16,96,128]{2,1,0:T(8,128)(2,1)S(1)} async-done(((bf16[16,96,128]{2,1,0:T(8,128)(2,1)}), bf16[16,96,128]{2,1,0:T(8,128)(2,1)S(1)}, u32[]{:S(2)}, u32[]{:S(2)}) %all-to-all-start.1) | async-done | bytes 393248 | tf_op jit(solution)/shard_map/all_to_all | solution.py:289
  57.2 1.6 collective-permute-start.1
  60.4 1.5 collective-permute-start.3
  61.9 1.2 collective-permute-done.4.kv1
  63.1 1.0 slice_bitcast_fusion
  64.1 3.0 %collective-permute-start.5 = (bf16[12,128,128]{2,1,0:T(8,128)(2,1)S(1)}, bf16[12,128,128]{2,1,0:T(8,128)(2,1)S(1)}, u32[]{:S(2)}, u32[]{:S(2)}) collective-permute-start(bf16[12,128,128]{2,1,0:T(8,128)(2,1)S(1)} %slice_bitcast_fusion), channel_id=1, source_target_pairs={{0,192},{64,0},{128,64},{192,128},{1,193},{65,1},{129,65},{193,129... | collective-permute-start | bytes 1179656 | tf_op jit(solution)/shard_map/ppermute | solution.py:29
  67.2 4.4 %pack.1 = (bf16[48,128,128]{2,1,0:T(8,128)(2,1)}, bf16[48,128,128]{2,1,0:T(8,128)(2,1)}) custom-call(bf16[2,12,128,128]{3,2,1,0:T(8,128)(2,1)} %prepare.1.kv0, bf16[2,12,128,128]{3,2,1,0:T(8,128)(2,1)} %collective-permute-done.4.kv1, bf16[2,12,128,128]{3,2,1,0:T(8,128)(2,1)} %copy-done.6), custom_call_target="tpu_custom_call" | custom-call | tf_op jit(solution)/shard_map/pack/pallas_call | solution.py:68
  71.6 1.4 collective-permute-start.7
  73.8 1.5 collective-permute-done.5.refs_3_
  75.3 1.4 copy-done.2
  76.7 1.4 copy-done.3
  78.1 14.5 %attend.3 = (bf16[48,128,128]{2,1,0:T(8,128)(2,1)S(1)}, bf16[48,128,128]{2,1,0:T(8,128)(2,1)S(1)}, bf16[12,144,128]{2,1,0:T(8,128)(2,1)S(1)}, bf16[12,144,128]{2,1,0:T(8,128)(2,1)S(1)}) custom-call(s32[48,48]{1,0:T(8,128)S(1)} %select_reduce_fusion.lists, s32[48]{0:T(128)S(1)} %get-tuple-element.16.counts, ...), custom_call_target="tpu_custom_call", output_to_operand_aliasing={{0}: (6, {}), {1}: (7, {})} | custom-call | flops 3019898880 | bytes 5242880 | tf_op jit(solution)/shard_map/attend/pallas_call | solution.py:219
  92.7 2.0 %collective-permute-start.6 = (bf16[12,144,128]{2,1,0:T(8,128)(2,1)S(1)}, bf16[12,144,128]{2,1,0:T(8,128)(2,1)S(1)}, u32[]{:S(2)}, u32[]{:S(2)}) collective-permute-start(bf16[12,144,128]{2,1,0:T(8,128)(2,1)S(1)} %get-tuple-element.24), channel_id=1, source_target_pairs={{0,4},{4,8},{8,12},{12,0},{1,5},{5,9},{9,13},{13,1},{2,6},{6,10},{... | collective-permute-start | bytes 1327112 | tf_op jit(solution)/shard_map/ppermute | solution.py:29
  94.8 7.1 %attend.5 = bf16[12,144,128]{2,1,0:T(8,128)(2,1)S(1)} custom-call(s32[48,48]{1,0:T(8,128)S(1)} %select_reduce_fusion.lists, s32[48]{0:T(128)S(1)} %get-tuple-element.16.counts, bf16[12,128,128]{2,1,0:T(8,128)(2,1)S(1)} %pad_maximum_fusion.refs_0_, bf16[48,128,128]{2,1,0:T(8,128)(2,1)S(1)} %get-tuple-element.22.refs_1_, ...), custom_call_target="tpu_custom_call" | custom-call | flops 1509949440 | bytes 5242880 | tf_op jit(solution)/shard_map/attend/pallas_call | solution.py:219
  101.9 3.0 %collective-permute-start.9 = (bf16[12,144,128]{2,1,0:T(8,128)(2,1)S(1)}, bf16[12,144,128]{2,1,0:T(8,128)(2,1)S(1)}, u32[]{:S(2)}, u32[]{:S(2)}) collective-permute-start(bf16[12,144,128]{2,1,0:T(8,128)(2,1)S(1)} %attend.5), channel_id=1, source_target_pairs={{0,8},{4,12},{8,0},{12,4},{1,9},{5,13},{9,1},{13,5},{2,10},{6,14},... | collective-permute-start | bytes 1327112 | tf_op jit(solution)/shard_map/ppermute | solution.py:29
  104.9 6.9 %attend.4.refs_0_ = bf16[12,144,128]{2,1,0:T(8,128)(2,1)S(1)} custom-call(s32[48,48]{1,0:T(8,128)S(1)} %select_reduce_fusion.lists, s32[48]{0:T(128)S(1)} %get-tuple-element.16.counts, bf16[12,128,128]{2,1,0:T(8,128)(2,1)S(1)} %bitcast.37, bf16[48,128,128]{2,1,0:T(8,128)(2,1)S(1)} %get-tuple-element.22.refs_1_, ...), custom_call_target="tpu_custom_call" | custom-call | flops 1509949440 | bytes 5242880 | tf_op jit(solution)/shard_map/attend/pallas_call | solution.py:219
  112.7 3.3 %collective-permute-done.9.refs_2_ = bf16[12,144,128]{2,1,0:T(8,128)(2,1)S(1)} collective-permute-done((bf16[12,144,128]{2,1,0:T(8,128)(2,1)S(1)}, bf16[12,144,128]{2,1,0:T(8,128)(2,1)S(1)}, u32[]{:S(2)}, u32[]{:S(2)}) %collective-permute-start.9) | collective-permute-done | bytes 442400 | tf_op jit(solution)/shard_map/ppermute | solution.py:29
  116.8 2.6 %combine.1 = (bf16[12,128,128]{2,1,0:T(8,128)(2,1)}, f32[12,128]{1,0:T(8,128)}) custom-call(bf16[12,144,128]{2,1,0:T(8,128)(2,1)} %copy-done.1, bf16[12,144,128]{2,1,0:T(8,128)(2,1)} %copy-done.8, bf16[12,144,128]{2,1,0:T(8,128)(2,1)} %copy-done.9, bf16[12,144,128]{2,1,0:T(8,128)(2,1)} %copy-done.7), custom_call_target="tpu_custom_call" | custom-call | tf_op jit(solution)/shard_map/combine/pallas_call | solution.py:262
  119.4 4.6 %all-to-all-start.2 = ((bf16[16,96,128]{2,1,0:T(8,128)(2,1)}), bf16[16,96,128]{2,1,0:T(8,128)(2,1)S(1)}, u32[]{:S(2)}, u32[]{:S(2)}) async-start(bf16[16,96,128]{2,1,0:T(8,128)(2,1)} %bitcast.42), calls=%async_computation.2 | async-start | bytes 786432 | tf_op jit(solution)/shard_map/all_to_all | solution.py:289
  124.1 12.0 %all-gather.2 = f32[4,12,128]{2,1,0:T(8,128)S(1)} all-gather(f32[1,12,128]{2,1,0:T(8,128)} %bitcast.43), channel_id=2, replica_groups=mesh['x'=4,'zh'=4,'y'=4,'zl'=2,'core'=2] {'y'}, dimensions={0}, use_global_device_ids=true | all-gather | bytes 30720 | tf_op jit(solution)/shard_map/all_gather | solution.py:315
  136.1 18.0 %all-gather.1 = f32[16,12,128]{2,1,0:T(8,128)S(1)} all-gather(f32[4,12,128]{2,1,0:T(8,128)S(1)} %all-gather.2), channel_id=3, replica_groups=mesh['x'=4,'zh'=4,'y'=4,'zl'=2,'core'=2] {'x'}, dimensions={0}, use_global_device_ids=true | all-gather | bytes 122880 | tf_op jit(solution)/shard_map/all_gather | solution.py:315
  154.8 9.2 %collective-permute-start.11 = (f32[1,1536]{1,0:T(1,128)S(1)}, f32[1,1536]{1,0:T(1,128)S(1)}, u32[]{:S(2)}, u32[]{:S(2)}) collective-permute-start(f32[1,1536]{1,0:T(1,128)S(1)} %bitcast.44), channel_id=1, source_target_pairs={{0,0},{16,4},{32,8},{48,12},{4,16},{20,20},{36,24},{52,28},{8,32},... | collective-permute-start | bytes 18440 | tf_op jit(solution)/shard_map/ppermute | solution.py:320
  164.0 2.6 %collective-permute-done.11 = f32[1,1536]{1,0:T(1,128)S(1)} collective-permute-done((f32[1,1536]{1,0:T(1,128)S(1)}, f32[1,1536]{1,0:T(1,128)S(1)}, u32[]{:S(2)}, u32[]{:S(2)}) %collective-permute-start.11) | collective-permute-done | bytes 6176 | tf_op jit(solution)/shard_map/ppermute | solution.py:320
  (55 shorter events, 10.0 us)
Async XLA Ops:
  0.6 36.4 %copy-start = (bf16[96,2048]{1,0:T(8,128)(2,1)S(1)}, bf16[96,2048]{1,0:T(8,128)(2,1)}, u32[]{:S(2)}) copy-start(bf16[96,2048]{1,0:T(8,128)(2,1)} %param.6) | copy-start | bytes 1179652
  0.6 1.3 copy-start.10
  3.1 8.7 %copy-start.12 = (s32[192]{0:T(256)S(1)}, s32[192]{0:T(256)}, u32[]{:S(2)}) copy-start(s32[192]{0:T(256)} %param.10) | copy-start | bytes 2308
  3.1 29.4 %all-to-all-start = ((bf16[16,2,96,128]{3,2,1,0:T(8,128)(2,1)}), bf16[16,2,96,128]{3,2,1,0:T(8,128)(2,1)S(1)}, u32[]{:S(2)}, u32[]{:S(2)}) async-start(bf16[16,2,96,128]{3,2,1,0:T(8,128)(2,1)} %maximum_bitcast_fusion), calls=%async_computation | async-start | bytes 1572864 | tf_op jit(solution)/shard_map/all_to_all | solution.py:289
  32.5 0.9 copy-start.4
  35.6 7.5 %copy-start.5 = (bf16[2,12,128,128]{3,2,1,0:T(8,128)(2,1)S(1)}, bf16[2,12,128,128]{3,2,1,0:T(8,128)(2,1)}, u32[]{:S(2)}) copy-start(bf16[2,12,128,128]{3,2,1,0:T(8,128)(2,1)} %prepare.1.kv0) | copy-start | bytes 2359300
  35.6 23.2 %collective-permute-start.2 = (bf16[2,12,128,128]{3,2,1,0:T(8,128)(2,1)}, bf16[2,12,128,128]{3,2,1,0:T(8,128)(2,1)S(1)}, u32[]{:S(2)}, u32[]{:S(2)}) collective-permute-start(bf16[2,12,128,128]{3,2,1,0:T(8,128)(2,1)} %prepare.1.kv0), channel_id=1, source_target_pairs={{0,64},{64,128},{128,192},{192,0},{1,65},{65,129},{129,193},{193,1... | collective-permute-start | bytes 2359304 | tf_op jit(solution)/shard_map/ppermute | solution.py:29
  37.9 18.8 %all-to-all-start.1 = ((bf16[16,96,128]{2,1,0:T(8,128)(2,1)}), bf16[16,96,128]{2,1,0:T(8,128)(2,1)S(1)}, u32[]{:S(2)}, u32[]{:S(2)}) async-start(bf16[16,96,128]{2,1,0:T(8,128)(2,1)} %bitcast_bitcast_fusion), calls=%async_computation.1 | async-start | bytes 786432 | tf_op jit(solution)/shard_map/all_to_all | solution.py:289
  43.0 20.1 %collective-permute-start.4 = (bf16[2,12,128,128]{3,2,1,0:T(8,128)(2,1)S(1)}, bf16[2,12,128,128]{3,2,1,0:T(8,128)(2,1)}, u32[]{:S(2)}, u32[]{:S(2)}) collective-permute-start(bf16[2,12,128,128]{3,2,1,0:T(8,128)(2,1)S(1)} %copy-done.5), channel_id=1, source_target_pairs={{0,192},{64,0},{128,64},{192,128},{1,193},{65,1},{129,65},{193,129... | collective-permute-start | bytes 2359304 | tf_op jit(solution)/shard_map/ppermute | solution.py:29
  56.7 16.3 %collective-permute-start = (bf16[12,128,128]{2,1,0:T(8,128)(2,1)S(1)}, bf16[12,128,128]{2,1,0:T(8,128)(2,1)S(1)}, u32[]{:S(2)}, u32[]{:S(2)}) collective-permute-start(bf16[12,128,128]{2,1,0:T(8,128)(2,1)S(1)} %bitcast.35), channel_id=1, source_target_pairs={{0,12},{4,0},{8,4},{12,8},{1,13},{5,1},{9,5},{13,9},{2,14},{6,2},{... | collective-permute-start | bytes 1179656 | tf_op jit(solution)/shard_map/ppermute | solution.py:29
  57.2 14.4 %collective-permute-start.1 = (bf16[12,128,128]{2,1,0:T(8,128)(2,1)S(1)}, bf16[12,128,128]{2,1,0:T(8,128)(2,1)S(1)}, u32[]{:S(2)}, u32[]{:S(2)}) collective-permute-start(bf16[12,128,128]{2,1,0:T(8,128)(2,1)S(1)} %bitcast.36), channel_id=1, source_target_pairs={{0,4},{4,8},{8,12},{12,0},{1,5},{5,9},{9,13},{13,1},{2,6},{6,10},{... | collective-permute-start | bytes 1179656 | tf_op jit(solution)/shard_map/ppermute | solution.py:29
  58.7 0.9 copy-start.6
  60.4 13.4 %collective-permute-start.3 = (bf16[12,128,128]{2,1,0:T(8,128)(2,1)}, bf16[12,128,128]{2,1,0:T(8,128)(2,1)S(1)}, u32[]{:S(2)}, u32[]{:S(2)}) collective-permute-start(bf16[12,128,128]{2,1,0:T(8,128)(2,1)} %slice_bitcast_fusion.1), channel_id=1, source_target_pairs={{0,64},{64,128},{128,192},{192,0},{1,65},{65,129},{129,193},{193,1... | collective-permute-start | bytes 1179656 | tf_op jit(solution)/shard_map/ppermute | solution.py:29
  64.1 11.2 %collective-permute-start.5 = (bf16[12,128,128]{2,1,0:T(8,128)(2,1)S(1)}, bf16[12,128,128]{2,1,0:T(8,128)(2,1)S(1)}, u32[]{:S(2)}, u32[]{:S(2)}) collective-permute-start(bf16[12,128,128]{2,1,0:T(8,128)(2,1)S(1)} %slice_bitcast_fusion), channel_id=1, source_target_pairs={{0,192},{64,0},{128,64},{192,128},{1,193},{65,1},{129,65},{193,129... | collective-permute-start | bytes 1179656 | tf_op jit(solution)/shard_map/ppermute | solution.py:29
  71.6 23.2 %collective-permute-start.7 = (bf16[6,128,128]{2,1,0:T(8,128)(2,1)S(1)}, bf16[6,128,128]{2,1,0:T(8,128)(2,1)S(1)}, u32[]{:S(2)}, u32[]{:S(2)}) collective-permute-start(bf16[6,128,128]{2,1,0:T(8,128)(2,1)S(1)} %slice.20), channel_id=1, source_target_pairs={{0,4},{4,8},{8,12},{12,0},{1,5},{5,9},{9,13},{13,1},{2,6},{6,10},{... | collective-permute-start | bytes 589832 | tf_op jit(solution)/shard_map/ppermute | solution.py:29
  73.0 21.8 %collective-permute-start.8 = (bf16[6,128,128]{2,1,0:T(8,128)(2,1)S(1)}, bf16[6,128,128]{2,1,0:T(8,128)(2,1)S(1)}, u32[]{:S(2)}, u32[]{:S(2)}) collective-permute-start(bf16[6,128,128]{2,1,0:T(8,128)(2,1)S(1)} %slice.21), channel_id=1, source_target_pairs={{0,12},{4,0},{8,4},{12,8},{1,13},{5,1},{9,5},{13,9},{2,14},{6,2},{... | collective-permute-start | bytes 589832 | tf_op jit(solution)/shard_map/ppermute | solution.py:29
  75.3 1.4 copy-start.2
  76.7 1.4 copy-start.3
  92.6 20.0 %collective-permute-start.10 = (bf16[12,144,128]{2,1,0:T(8,128)(2,1)S(1)}, bf16[12,144,128]{2,1,0:T(8,128)(2,1)S(1)}, u32[]{:S(2)}, u32[]{:S(2)}) collective-permute-start(bf16[12,144,128]{2,1,0:T(8,128)(2,1)S(1)} %get-tuple-element.25), channel_id=1, source_target_pairs={{0,12},{4,0},{8,4},{12,8},{1,13},{5,1},{9,5},{13,9},{2,14},{6,2},{... | collective-permute-start | bytes 1327112 | tf_op jit(solution)/shard_map/ppermute | solution.py:29
  92.7 19.9 %collective-permute-start.6 = (bf16[12,144,128]{2,1,0:T(8,128)(2,1)S(1)}, bf16[12,144,128]{2,1,0:T(8,128)(2,1)S(1)}, u32[]{:S(2)}, u32[]{:S(2)}) collective-permute-start(bf16[12,144,128]{2,1,0:T(8,128)(2,1)S(1)} %get-tuple-element.24), channel_id=1, source_target_pairs={{0,4},{4,8},{8,12},{12,0},{1,5},{5,9},{9,13},{13,1},{2,6},{6,10},{... | collective-permute-start | bytes 1327112 | tf_op jit(solution)/shard_map/ppermute | solution.py:29
  101.9 14.0 %collective-permute-start.9 = (bf16[12,144,128]{2,1,0:T(8,128)(2,1)S(1)}, bf16[12,144,128]{2,1,0:T(8,128)(2,1)S(1)}, u32[]{:S(2)}, u32[]{:S(2)}) collective-permute-start(bf16[12,144,128]{2,1,0:T(8,128)(2,1)S(1)} %attend.5), channel_id=1, source_target_pairs={{0,8},{4,12},{8,0},{12,4},{1,9},{5,13},{9,1},{13,5},{2,10},{6,14},... | collective-permute-start | bytes 1327112 | tf_op jit(solution)/shard_map/ppermute | solution.py:29
  111.9 0.8 copy-start.1
  112.6 11.4 %copy-start.11 = (s32[192]{0:T(256)S(1)}, s32[192]{0:T(256)}, u32[]{:S(2)}) copy-start(s32[192]{0:T(256)} %param.11) | copy-start | bytes 2308
  112.6 3.3 %copy-start.7 = (bf16[12,144,128]{2,1,0:T(8,128)(2,1)}, bf16[12,144,128]{2,1,0:T(8,128)(2,1)S(1)}, u32[]{:S(2)}) copy-start(bf16[12,144,128]{2,1,0:T(8,128)(2,1)S(1)} %collective-permute-done.10.refs_3_) | copy-start | bytes 1327108
  112.6 3.3 %copy-start.8 = (bf16[12,144,128]{2,1,0:T(8,128)(2,1)}, bf16[12,144,128]{2,1,0:T(8,128)(2,1)S(1)}, u32[]{:S(2)}) copy-start(bf16[12,144,128]{2,1,0:T(8,128)(2,1)S(1)} %collective-permute-done.6.refs_1_) | copy-start | bytes 1327108
  116.0 0.8 copy-start.9
  119.4 47.2 %all-to-all-start.2 = ((bf16[16,96,128]{2,1,0:T(8,128)(2,1)}), bf16[16,96,128]{2,1,0:T(8,128)(2,1)S(1)}, u32[]{:S(2)}, u32[]{:S(2)}) async-start(bf16[16,96,128]{2,1,0:T(8,128)(2,1)} %bitcast.42), calls=%async_computation.2 | async-start | bytes 786432 | tf_op jit(solution)/shard_map/all_to_all | solution.py:289
  154.8 11.8 %collective-permute-start.11 = (f32[1,1536]{1,0:T(1,128)S(1)}, f32[1,1536]{1,0:T(1,128)S(1)}, u32[]{:S(2)}, u32[]{:S(2)}) collective-permute-start(f32[1,1536]{1,0:T(1,128)S(1)} %bitcast.44), channel_id=1, source_target_pairs={{0,0},{16,4},{32,8},{48,12},{4,16},{20,20},{36,24},{52,28},{8,32},... | collective-permute-start | bytes 18440 | tf_op jit(solution)/shard_map/ppermute | solution.py:320

commit v4 on v3

--- a/solution.py
+++ b/solution.py
@@ -21,12 +21,16 @@
 LOG2E = 1.4426950408889634
 VMEM = pl.BlockSpec(memory_space=pltpu.VMEM)
 SMEM = pl.BlockSpec(memory_space=pltpu.SMEM)
-ANY = pl.BlockSpec(memory_space=pl.ANY)
+SPACE = pltpu.CompilerParams(vmem_limit_bytes=16 * 1024 * 1024)
 GROUP = ("zh", "zl", "core")
 
 
 def shift(array, axis, by):
     return lax.ppermute(array, axis, [(i, (i + by) % RING) for i in range(RING)])
+
+
+def around(array, axis):
+    return jnp.stack([array] + [shift(array, axis, -by) for by in range(1, RING)])
 
 
 def prepare_kernel(got_ref, kv_ref):
@@ -45,56 +49,34 @@
         out_shape=jax.ShapeDtypeStruct((2, OWN, BLK, HD), jnp.bfloat16),
         in_specs=[VMEM],
         out_specs=VMEM,
+        compiler_params=SPACE,
         name="prepare",
     )(got)
 
 
-def pack_kernel(kv0, kv1, kv3, ks, vs, sems):
-    copies = []
-    for b, kv in ((0, kv0), (1, kv1), (3, kv3)):
-        for which, held in enumerate((ks, vs)):
-            span = pl.ds(b * OWN, OWN)
-            copies.append(
-                pltpu.make_async_copy(kv.at[which], held.at[span], sems.at[len(copies)])
-            )
-    for copy in copies:
-        copy.start()
-    for copy in copies:
-        copy.wait()
-
-
-def pack(kv0, kv1, kv3):
-    tiles = jax.ShapeDtypeStruct((KEYS, BLK, HD), jnp.bfloat16)
-    return pl.pallas_call(
-        pack_kernel,
-        out_shape=(tiles, tiles),
-        in_specs=[VMEM] * 3,
-        out_specs=(VMEM, VMEM),
-        scratch_shapes=[pltpu.SemaphoreType.DMA((6,))],
-        name="pack",
-    )(kv0, kv1, kv3)
-
-
-def attend_kernel(blocks, last, lists, counts, *refs):
+def attend_kernel(blocks, first_call, lists, counts, *refs):
     tiles = len(blocks) * OWN
     queries, refs = refs[: len(blocks)], refs[len(blocks) :]
-    if last:
-        k2, v2, _, _, ks, vs = refs[:6]
-        o_out, refs = refs[6 : 6 + len(blocks)], refs[6 + len(blocks) :]
+    if first_call:
+        kv0, kv1, kv3, k2, v2, ks, vs = refs[:7]
+        refs = refs[7:]
     else:
         ks, vs = refs[:2]
-        o_out, refs = refs[2 : 2 + len(blocks)], refs[2 + len(blocks) :]
-    sems, rows, sizes, qs, m_ref, l_ref, acc_ref = refs[:7]
-    s_refs, top_refs = refs[7 : 7 + WIDTH], refs[7 + WIDTH :]
-    moves = [(q, qs, b * OWN) for b, q in enumerate(queries)]
-    if last:
-        moves += [(k2, ks, 2 * OWN), (v2, vs, 2 * OWN)]
-    copies = [
-        pltpu.make_async_copy(source, held.at[pl.ds(at, OWN)], sems.at[i])
-        for i, (source, held, at) in enumerate(moves)
-    ]
-    for copy in copies:
-        copy.start()
+        refs = refs[2:]
+    o_out, refs = refs[: len(blocks)], refs[len(blocks) :]
+    rows, sizes, qs, m_ref, l_ref, acc_ref = refs[:6]
+    s_refs, top_refs = refs[6 : 6 + WIDTH], refs[6 + WIDTH :]
+    for b, q in enumerate(queries):
+        qs[b * OWN : (b + 1) * OWN] = q[...]
+    if first_call:
+        for b, k, v in (
+            (0, kv0.at[0], kv0.at[1]),
+            (1, kv1.at[0], kv1.at[1]),
+            (2, k2, v2),
+            (3, kv3.at[0], kv3.at[1]),
+        ):
+            ks[b * OWN : (b + 1) * OWN] = k[...]
+            vs[b * OWN : (b + 1) * OWN] = v[...]
     m_ref[...] = jnp.full(m_ref.shape, NEG, jnp.float32)
     l_ref[...] = jnp.zeros(l_ref.shape, jnp.float32)
     acc_ref[...] = jnp.zeros(acc_ref.shape, jnp.float32)
@@ -121,25 +103,16 @@
     def score(lane, t, j):
         left = sizes[t] - j * CHUNK
         tile = listed(t, j)
-        q = qs[jnp.minimum(t, tiles - 1)]
-        none = jnp.zeros_like(q)
-        twice = jnp.concatenate(
-            [jnp.concatenate([q, none], axis=1), jnp.concatenate([none, q], axis=1)], axis=0
-        )
-        pairs = [
-            jnp.concatenate([ks[tile[u]], ks[tile[u + 1]]], axis=1) for u in range(0, CHUNK, 2)
-        ]
         s = lax.dot_general(
-            jnp.concatenate(pairs, axis=0),
-            twice,
+            jnp.concatenate([ks[u] for u in tile], axis=0),
+            qs[jnp.minimum(t, tiles - 1)],
             (((1,), (1,)), ((), ())),
             preferred_element_type=jnp.float32,
         )
         s_refs[lane][...] = s
         top = jnp.full((8, BLK), NEG, jnp.float32)
         for u in range(CHUNK):
-            part = s[u // 2 * BLK : (u // 2 + 1) * BLK, u % 2 * BLK : (u % 2 + 1) * BLK]
-            part = jnp.max(part.reshape(16, 8, BLK), axis=0)
+            part = jnp.max(s[u * BLK : (u + 1) * BLK].reshape(16, 8, BLK), axis=0)
             top = jnp.maximum(top, jnp.where(u < left, part, NEG))
         top_refs[lane][...] = jnp.max(top, axis=0, keepdims=True)
 
@@ -153,8 +126,8 @@
         total = jnp.zeros((8, BLK), jnp.float32)
         weights = []
         for u in range(CHUNK):
-            s = s_refs[lane][u // 2 * BLK : (u // 2 + 1) * BLK, u % 2 * BLK : (u % 2 + 1) * BLK]
-            w = jnp.exp2(s * (SCALE * LOG2E) - jnp.where(u < left, base, -NEG))
+            s = s_refs[lane][u * BLK : (u + 1) * BLK] * (SCALE * LOG2E)
+            w = jnp.exp2(s - jnp.where(u < left, base, -NEG))
             total = total + jnp.sum(w.reshape(16, 8, BLK), axis=0)
             weights.append(w.astype(jnp.bfloat16))
         vt = jnp.concatenate([vs[tile] for tile in listed(t, j)], axis=1)
@@ -169,8 +142,6 @@
             group += [t, j]
         return tuple(group)
 
-    for copy in copies:
-        copy.wait()
     first = [jnp.int32(0), jnp.int32(0)]
     for _ in range(WIDTH - 1):
         first += advance(*first[-2:])
@@ -210,20 +181,18 @@
         lax.fori_loop(0, OWN // 4, finish, 0)
 
 
-def attend(blocks, lists, counts, queries, keys, values, last=()):
+def attend(blocks, lists, counts, queries, keys_values, first_call=False):
     tiles = jax.ShapeDtypeStruct((OWN, HD + PAD, BLK), jnp.bfloat16)
-    held = jax.ShapeDtypeStruct((KEYS, BLK, HD), jnp.bfloat16)
+    held = (jax.ShapeDtypeStruct((KEYS, BLK, HD), jnp.bfloat16),) * 2 if first_call else ()
     count = len(blocks)
     slots = count * OWN + 1
     pairs = count * OWN * 15
     return pl.pallas_call(
-        functools.partial(attend_kernel, blocks, bool(last)),
-        out_shape=((held, held) if last else ()) + (tiles,) * count,
-        in_specs=[SMEM, SMEM] + [VMEM] * (count + len(last) + 2),
-        out_specs=(VMEM,) * (count + len(last)),
-        input_output_aliases={count + 4: 0, count + 5: 1} if last else {},
+        functools.partial(attend_kernel, blocks, first_call),
+        out_shape=held + (tiles,) * count,
+        in_specs=[SMEM, SMEM] + [VMEM] * (count + len(keys_values)),
+        out_specs=(VMEM,) * (count + len(held)),
         scratch_shapes=[
-            pltpu.SemaphoreType.DMA((count + len(last),)),
             pltpu.SMEM((slots,), jnp.int32),
             pltpu.SMEM((slots,), jnp.int32),
             pltpu.VMEM((count * OWN, BLK, HD), jnp.bfloat16),
@@ -231,16 +200,16 @@
             pltpu.VMEM((slots, 8, BLK), jnp.float32),
             pltpu.VMEM((slots, HD, BLK), jnp.float32),
         ]
-        + [pltpu.VMEM((CHUNK // 2 * BLK, 2 * BLK), jnp.float32)] * WIDTH
+        + [pltpu.VMEM((CHUNK * BLK, BLK), jnp.float32)] * WIDTH
         + [pltpu.VMEM((1, BLK), jnp.float32)] * WIDTH,
-        compiler_params=pltpu.CompilerParams(vmem_limit_bytes=32 * 1024 * 1024),
+        compiler_params=SPACE,
         cost_estimate=pl.CostEstimate(
             flops=pairs * 4 * BLK * BLK * HD,
             bytes_accessed=5 << 20,
             transcendentals=pairs * BLK * BLK,
         ),
         name="attend",
-    )(lists, counts, *queries, *last, keys, values)
+    )(lists, counts, *queries, *keys_values)
 
 
 def combine_kernel(*refs):
@@ -267,6 +236,7 @@
         ),
         in_specs=[VMEM] * RING,
         out_specs=(VMEM, VMEM),
+        compiler_params=SPACE,
         name="combine",
     )(*outs)
 
@@ -303,18 +273,18 @@
     q1, q3 = shift(q0, "y", -1), shift(q0, "y", 1)
     half = OWN // 2
     q2 = jnp.concatenate([shift(q3[:half], "y", 1), shift(q1[half:], "y", -1)])
-    some_keys, some_values = pack(kv0, kv1, kv3)
     all_keys, all_values, o1, o3 = attend(
-        (1, 3), lists, counts, (q1, q3), some_keys, some_values, (k2, v2)
+        (1, 3), lists, counts, (q1, q3), (kv0, kv1, kv3, k2, v2), first_call=True
     )
-    (o2,) = attend((2,), lists, counts, (q2,), all_keys, all_values)
-    (o0,) = attend((0,), lists, counts, (q0,), all_keys, all_values)
+    (o2,) = attend((2,), lists, counts, (q2,), (all_keys, all_values))
+    (o0,) = attend((0,), lists, counts, (q0,), (all_keys, all_values))
     blended, lse = combine((o0, shift(o1, "y", 1), shift(o2, "y", 2), shift(o3, "y", -1)))
     back = exchange(blended.reshape(16, 96, HD))
     attended = jnp.transpose(back, (1, 0, 2)).reshape(96, 16 * HD)
-    every = lax.all_gather(lax.all_gather(lse, "y"), "x").reshape(-1, BLK)
+    every = around(around(lse, "y"), "x").reshape(-1, BLK)
     tiles = lax.dynamic_slice_in_dim(assign, (xi * RING + yi) * OWN, OWN)
-    spots = tiles // KEYS * KEYS + tiles % OWN // 3 * OWN + tiles % KEYS // OWN * 3 + tiles % 3
+    spots = (tiles // KEYS - xi) % RING * KEYS + (tiles % OWN // 3 - yi) % RING * OWN
+    spots = spots + tiles % KEYS // OWN * 3 + tiles % 3
     chosen = jnp.take(every, spots, axis=0).reshape(1, OWN * BLK)
     turned = [(b * RING + a, a * RING + b) for a in range(RING) for b in range(RING)]
     return attended, lax.ppermute(chosen, ("zh", "y"), turned)

time: 169 us -> 149 us (0.88)
  blocking collectives: 30 us -> 0 us
  starting transfers between devices: 44.8 us -> 58 us
  waiting for transfers between devices: 39.1 us -> 49.3 us
  local copies, waits for them, and re-layouts: 12.3 us -> 4.36 us
  Pallas kernels: 37.7 us -> 30.9 us
    all_gather x2 -> x0, blocking collectives: 30 us -> none  [on_device(): every = lax.all_gather(lax.all_gather(lse, 'y'), 'x').reshape(-1, BLK)]
    ppermute x11 -> x17, starting transfers between devices: 17.1 us -> 29.8 us  [shift(): lax.ppermute(array, axis, [(i, (i + by) % RING) for i in range(RING)])]
    ppermute x11 -> x17, waiting for transfers between devices: 6.02 us -> 17.9 us  [shift(): lax.ppermute(array, axis, [(i, (i + by) % RING) for i in range(RING)])]
    unnamed x30 -> x14, local copies, waits for them, and re-layouts: 8.02 us -> 1.83 us
    pallas_call x4 -> x3, Pallas kernels: 33 us -> 29.6 us  [attend(): pl.pallas_call(functools.partial(attend_kernel, blocks, first_call), out_...]
    pallas_call x1, Pallas kernels: 2.17 us -> 0.15 us  [prepare(): pl.pallas_call(prepare_kernel, out_shape=jax.ShapeDtypeStruct((2, OWN, BL...]
    squeeze x2, local copies, waits for them, and re-layouts: 1.79 us -> 0.05 us  [on_device(): k2, v2 = (shift(kv3[0], 'x', 1), shift(kv1[1], 'x', -1))]
  transfers between devices with their start and end apart: 15 -> 21, of which waited for: 6 -> 11; matrix products, arithmetic and copies ran while one was open for 3% -> 3% of each run, Pallas kernels for 20% -> 20%
where the time goes in v4:
time: 149 us; the launch traced here: 147 us
  starting transfers between devices  58 us (39%)
  waiting for transfers between devices  49.3 us (33%)
  Pallas kernels  30.9 us (21%)
  local copies, waits for them, and re-layouts  4.36 us (3%)
  other arithmetic  3.66 us (2%)
    all_to_all x3, waiting for transfers between devices, exchange(): return lax.all_to_all(array, GROUP, split_axis=0, concat_axis=0, tiled=True)  29.9 us
    ppermute x17, starting transfers between devices, shift(): lax.ppermute(array, axis, [(i, (i + by) % RING) for i in range(RING)])  29.8 us
    pallas_call x3, Pallas kernels, attend(): pl.pallas_call(functools.partial(attend_kernel, blocks, first_call), out_...  29.6 us
    ppermute x17, waiting for transfers between devices, shift(): lax.ppermute(array, axis, [(i, (i + by) % RING) for i in range(RING)])  17.9 us
    all_to_all x3, starting transfers between devices, exchange(): return lax.all_to_all(array, GROUP, split_axis=0, concat_axis=0, tiled=True)  17.8 us
    ppermute x1, starting transfers between devices, on_device(): return (attended, lax.ppermute(chosen, ('zh', 'y'), turned))  10.3 us
  transfers between devices with their start and end apart: 21, of which 11 were waited for; matrix products, arithmetic and copies ran while one was open for 3% of the time, Pallas kernels for 20%

profile of v4, /device:TPU:16, one launch (start us, length us, event | category | flops | bytes accessed | tf_op | source)
XLA Modules:
  0.0 147.3 jit_solution(13236325152507755166)
XLA Ops:
  0.7 1.1 copy.20
  2.1 1.0 maximum_bitcast_fusion
  3.1 8.7 %all-to-all-start = ((bf16[16,2,96,128]{3,2,1,0:T(8,128)(2,1)}), bf16[16,2,96,128]{3,2,1,0:T(8,128)(2,1)S(1)}, u32[]{:S(2)}, u32[]{:S(2)}) async-start(bf16[16,2,96,128]{3,2,1,0:T(8,128)(2,1)} %maximum_bitcast_fusion), calls=%async_computation | async-start | bytes 1572864 | tf_op jit(solution)/shard_map/all_to_all | solution.py:259
  13.0 1.5 %select_reduce_fusion.lists = s32[48,48]{1,0:T(8,128)} fusion(s32[48,96]{1,0:T(8,128)S(1)} %get-tuple-element.28, s32[48,96]{1,0:T(8,128)S(1)} %convolution_convert_fusion, pred[48,96]{1,0:T(8,128)(4,1)S(1)} %get-tuple-element.27), kind=kLoop, calls=%fused_computation.1 | loop fusion | flops 882432 | bytes 50688 | tf_op jit(solution)/shard_map/reduce_sum | solution.py:254
  14.5 18.0 %all-to-all-done.got_ref = bf16[16,2,96,128]{3,2,1,0:T(8,128)(2,1)S(1)} async-done(((bf16[16,2,96,128]{3,2,1,0:T(8,128)(2,1)}), bf16[16,2,96,128]{3,2,1,0:T(8,128)(2,1)S(1)}, u32[]{:S(2)}, u32[]{:S(2)}) %all-to-all-start) | async-done | bytes 786464 | tf_op jit(solution)/shard_map/all_to_all | solution.py:259
  32.6 1.6 %collective-permute-start.3 = (bf16[2,12,128,128]{3,2,1,0:T(8,128)(2,1)S(1)}, bf16[2,12,128,128]{3,2,1,0:T(8,128)(2,1)S(1)}, u32[]{:S(2)}, u32[]{:S(2)}) collective-permute-start(bf16[2,12,128,128]{3,2,1,0:T(8,128)(2,1)S(1)} %prepare.1.refs_2_), channel_id=1, source_target_pairs={{0,64},{64,128},{128,192},{192,0},{1,65},{65,129},{129,193},{193,1... | collective-permute-start | bytes 2359304 | tf_op jit(solution)/shard_map/ppermute | solution.py:29
  35.0 5.1 %all-to-all-start.1 = ((bf16[16,96,128]{2,1,0:T(8,128)(2,1)}), bf16[16,96,128]{2,1,0:T(8,128)(2,1)S(1)}, u32[]{:S(2)}, u32[]{:S(2)}) async-start(bf16[16,96,128]{2,1,0:T(8,128)(2,1)} %bitcast_bitcast_fusion), calls=%async_computation.1 | async-start | bytes 786432 | tf_op jit(solution)/shard_map/all_to_all | solution.py:259
  40.2 1.8 %collective-permute-start.2 = (bf16[2,12,128,128]{3,2,1,0:T(8,128)(2,1)S(1)}, bf16[2,12,128,128]{3,2,1,0:T(8,128)(2,1)S(1)}, u32[]{:S(2)}, u32[]{:S(2)}) collective-permute-start(bf16[2,12,128,128]{3,2,1,0:T(8,128)(2,1)S(1)} %prepare.1.refs_2_), channel_id=1, source_target_pairs={{0,192},{64,0},{128,64},{192,128},{1,193},{65,1},{129,65},{193,129... | collective-permute-start | bytes 2359304 | tf_op jit(solution)/shard_map/ppermute | solution.py:29
  42.0 11.9 %all-to-all-done.1 = bf16[16,96,128]{2,1,0:T(8,128)(2,1)S(1)} async-done(((bf16[16,96,128]{2,1,0:T(8,128)(2,1)}), bf16[16,96,128]{2,1,0:T(8,128)(2,1)S(1)}, u32[]{:S(2)}, u32[]{:S(2)}) %all-to-all-start.1) | async-done | bytes 393248 | tf_op jit(solution)/shard_map/all_to_all | solution.py:259
  54.3 1.6 %collective-permute-start.1 = (bf16[12,128,128]{2,1,0:T(8,128)(2,1)S(1)}, bf16[12,128,128]{2,1,0:T(8,128)(2,1)S(1)}, u32[]{:S(2)}, u32[]{:S(2)}) collective-permute-start(bf16[12,128,128]{2,1,0:T(8,128)(2,1)S(1)} %bitcast.44), channel_id=1, source_target_pairs={{0,4},{4,8},{8,12},{12,0},{1,5},{5,9},{9,13},{13,1},{2,6},{6,10},{... | collective-permute-start | bytes 1179656 | tf_op jit(solution)/shard_map/ppermute | solution.py:29
  55.9 1.6 %collective-permute-start.4 = (bf16[12,128,128]{2,1,0:T(8,128)(2,1)S(1)}, bf16[12,128,128]{2,1,0:T(8,128)(2,1)S(1)}, u32[]{:S(2)}, u32[]{:S(2)}) collective-permute-start(bf16[12,128,128]{2,1,0:T(8,128)(2,1)S(1)} %slice_bitcast_fusion.1), channel_id=1, source_target_pairs={{0,64},{64,128},{128,192},{192,0},{1,65},{65,129},{129,193},{193,1... | collective-permute-start | bytes 1179656 | tf_op jit(solution)/shard_map/ppermute | solution.py:29
  57.5 2.6 %collective-permute-done.2.refs_3_ = bf16[2,12,128,128]{3,2,1,0:T(8,128)(2,1)S(1)} collective-permute-done((bf16[2,12,128,128]{3,2,1,0:T(8,128)(2,1)S(1)}, bf16[2,12,128,128]{3,2,1,0:T(8,128)(2,1)S(1)}, u32[]{:S(2)}, u32[]{:S(2)}) %collective-permute-start.2) | collective-permute-done | bytes 786464 | tf_op jit(solution)/shard_map/ppermute | solution.py:29
  60.2 3.0 %collective-permute-start.5 = (bf16[12,128,128]{2,1,0:T(8,128)(2,1)S(1)}, bf16[12,128,128]{2,1,0:T(8,128)(2,1)S(1)}, u32[]{:S(2)}, u32[]{:S(2)}) collective-permute-start(bf16[12,128,128]{2,1,0:T(8,128)(2,1)S(1)} %slice_bitcast_fusion), channel_id=1, source_target_pairs={{0,192},{64,0},{128,64},{192,128},{1,193},{65,1},{129,65},{193,129... | collective-permute-start | bytes 1179656 | tf_op jit(solution)/shard_map/ppermute | solution.py:29
  63.2 3.1 %collective-permute-done.1.refs_1_ = bf16[12,128,128]{2,1,0:T(8,128)(2,1)S(1)} collective-permute-done((bf16[12,128,128]{2,1,0:T(8,128)(2,1)S(1)}, bf16[12,128,128]{2,1,0:T(8,128)(2,1)S(1)}, u32[]{:S(2)}, u32[]{:S(2)}) %collective-permute-start.1) | collective-permute-done | bytes 393248 | tf_op jit(solution)/shard_map/ppermute | solution.py:29
  66.3 1.7 %collective-permute-start.7 = (bf16[6,128,128]{2,1,0:T(8,128)(2,1)S(1)}, bf16[6,128,128]{2,1,0:T(8,128)(2,1)S(1)}, u32[]{:S(2)}, u32[]{:S(2)}) collective-permute-start(bf16[6,128,128]{2,1,0:T(8,128)(2,1)S(1)} %slice.20), channel_id=1, source_target_pairs={{0,4},{4,8},{8,12},{12,0},{1,5},{5,9},{9,13},{13,1},{2,6},{6,10},{... | collective-permute-start | bytes 589832 | tf_op jit(solution)/shard_map/ppermute | solution.py:29
  68.9 2.4 %collective-permute-done.5.refs_6_ = bf16[12,128,128]{2,1,0:T(8,128)(2,1)S(1)} collective-permute-done((bf16[12,128,128]{2,1,0:T(8,128)(2,1)S(1)}, bf16[12,128,128]{2,1,0:T(8,128)(2,1)S(1)}, u32[]{:S(2)}, u32[]{:S(2)}) %collective-permute-start.5) | collective-permute-done | bytes 393248 | tf_op jit(solution)/shard_map/ppermute | solution.py:29
  71.4 13.9 %attend.3 = (bf16[48,128,128]{2,1,0:T(8,128)(2,1)S(1)}, bf16[48,128,128]{2,1,0:T(8,128)(2,1)S(1)}, bf16[12,144,128]{2,1,0:T(8,128)(2,1)S(1)}, bf16[12,144,128]{2,1,0:T(8,128)(2,1)S(1)}) custom-call(s32[48,48]{1,0:T(8,128)S(1)} %copy-done.1, s32[48]{0:T(128)S(1)} %get-tuple-element.14.counts, bf16[12,128,128]{2,1,0:T(8,128)(2,1)S(1)} %collective-permute-done.refs_0_, ...), custom_call_target="tpu_custom_call" | custom-call | flops 3019898880 | bytes 5242880 | tf_op jit(solution)/shard_map/attend/pallas_call | solution.py:190
  85.7 1.6 %collective-permute-start.6 = (bf16[12,144,128]{2,1,0:T(8,128)(2,1)S(1)}, bf16[12,144,128]{2,1,0:T(8,128)(2,1)S(1)}, u32[]{:S(2)}, u32[]{:S(2)}) collective-permute-start(bf16[12,144,128]{2,1,0:T(8,128)(2,1)S(1)} %get-tuple-element.20), channel_id=1, source_target_pairs={{0,4},{4,8},{8,12},{12,0},{1,5},{5,9},{9,13},{13,1},{2,6},{6,10},{... | collective-permute-start | bytes 1327112 | tf_op jit(solution)/shard_map/ppermute | solution.py:29
  87.4 8.3 %attend.5 = bf16[12,144,128]{2,1,0:T(8,128)(2,1)S(1)} custom-call(s32[48,48]{1,0:T(8,128)S(1)} %copy-done.1, s32[48]{0:T(128)S(1)} %get-tuple-element.14.counts, bf16[12,128,128]{2,1,0:T(8,128)(2,1)S(1)} %pad_maximum_fusion.refs_0_, bf16[48,128,128]{2,1,0:T(8,128)(2,1)S(1)} %get-tuple-element.18.refs_1_, bf16[48,128,128]{2,1,0:T(8,128)(2,1)S(1)} %get-tuple-element.19.refs_2_), custom_call_target="tpu_custom_call" | custom-call | flops 1509949440 | bytes 5242880 | tf_op jit(solution)/shard_map/attend/pallas_call | solution.py:190
  95.7 3.7 %collective-permute-start.9 = (bf16[12,144,128]{2,1,0:T(8,128)(2,1)S(1)}, bf16[12,144,128]{2,1,0:T(8,128)(2,1)S(1)}, u32[]{:S(2)}, u32[]{:S(2)}) collective-permute-start(bf16[12,144,128]{2,1,0:T(8,128)(2,1)S(1)} %attend.5), channel_id=1, source_target_pairs={{0,8},{4,12},{8,0},{12,4},{1,9},{5,13},{9,1},{13,5},{2,10},{6,14},... | collective-permute-start | bytes 1327112 | tf_op jit(solution)/shard_map/ppermute | solution.py:29
  99.5 7.4 %attend.4.refs_0_ = bf16[12,144,128]{2,1,0:T(8,128)(2,1)S(1)} custom-call(s32[48,48]{1,0:T(8,128)S(1)} %copy-done.1, s32[48]{0:T(128)S(1)} %get-tuple-element.14.counts, bf16[12,128,128]{2,1,0:T(8,128)(2,1)S(1)} %bitcast.45, bf16[48,128,128]{2,1,0:T(8,128)(2,1)S(1)} %get-tuple-element.18.refs_1_, bf16[48,128,128]{2,1,0:T(8,128)(2,1)S(1)} %get-tuple-element.19.refs_2_), custom_call_target="tpu_custom_call" | custom-call | flops 1509949440 | bytes 5242880 | tf_op jit(solution)/shard_map/attend/pallas_call | solution.py:190
  106.9 3.3 %collective-permute-done.9.refs_2_ = bf16[12,144,128]{2,1,0:T(8,128)(2,1)S(1)} collective-permute-done((bf16[12,144,128]{2,1,0:T(8,128)(2,1)S(1)}, bf16[12,144,128]{2,1,0:T(8,128)(2,1)S(1)}, u32[]{:S(2)}, u32[]{:S(2)}) %collective-permute-start.9) | collective-permute-done | bytes 442400 | tf_op jit(solution)/shard_map/ppermute | solution.py:29
  110.1 1.2 combine.1
  111.3 4.0 %all-to-all-start.2 = ((bf16[16,96,128]{2,1,0:T(8,128)(2,1)}), bf16[16,96,128]{2,1,0:T(8,128)(2,1)S(1)}, u32[]{:S(2)}, u32[]{:S(2)}) async-start(bf16[16,96,128]{2,1,0:T(8,128)(2,1)} %bitcast.5), calls=%async_computation.2 | async-start | bytes 786432 | tf_op jit(solution)/shard_map/all_to_all | solution.py:259
  115.3 1.5 %collective-permute-start.13 = (f32[12,128]{1,0:T(8,128)S(1)}, f32[12,128]{1,0:T(8,128)S(1)}, u32[]{:S(2)}, u32[]{:S(2)}) collective-permute-start(f32[12,128]{1,0:T(8,128)S(1)} %get-tuple-element.23), channel_id=1, source_target_pairs={{0,4},{4,8},{8,12},{12,0},{1,5},{5,9},{9,13},{13,1},{2,6},{6,10},{... | collective-permute-start | bytes 18440 | tf_op jit(solution)/shard_map/ppermute | solution.py:29
  117.4 3.7 %collective-permute-start.12 = (f32[12,128]{1,0:T(8,128)S(1)}, f32[12,128]{1,0:T(8,128)S(1)}, u32[]{:S(2)}, u32[]{:S(2)}) collective-permute-start(f32[12,128]{1,0:T(8,128)S(1)} %get-tuple-element.23), channel_id=1, source_target_pairs={{0,8},{4,12},{8,0},{12,4},{1,9},{5,13},{9,1},{13,5},{2,10},{6,14},... | collective-permute-start | bytes 18440 | tf_op jit(solution)/shard_map/ppermute | solution.py:29
  121.3 1.5 %collective-permute-done.12 = f32[12,128]{1,0:T(8,128)S(1)} collective-permute-done((f32[12,128]{1,0:T(8,128)S(1)}, f32[12,128]{1,0:T(8,128)S(1)}, u32[]{:S(2)}, u32[]{:S(2)}) %collective-permute-start.12) | collective-permute-done | bytes 6176 | tf_op jit(solution)/shard_map/ppermute | solution.py:29
  122.8 5.1 %collective-permute-start.14 = (f32[4,12,128]{2,1,0:T(8,128)S(1)}, f32[4,12,128]{2,1,0:T(8,128)S(1)}, u32[]{:S(2)}, u32[]{:S(2)}) collective-permute-start(f32[4,12,128]{2,1,0:T(8,128)S(1)} %get-tuple-element.30), channel_id=1, source_target_pairs={{0,192},{64,0},{128,64},{192,128},{1,193},{65,1},{129,65},{193,129... | collective-permute-start | bytes 73736 | tf_op jit(solution)/shard_map/ppermute | solution.py:29
  127.8 1.0 collective-permute-start.16
  129.4 3.9 %collective-permute-done.15 = f32[4,12,128]{2,1,0:T(8,128)S(1)} collective-permute-done((f32[4,12,128]{2,1,0:T(8,128)S(1)}, f32[4,12,128]{2,1,0:T(8,128)S(1)}, u32[]{:S(2)}, u32[]{:S(2)}) %collective-permute-start.15) | collective-permute-done | bytes 24608 | tf_op jit(solution)/shard_map/ppermute | solution.py:29
  134.0 10.3 %collective-permute-start.17 = (f32[1,1536]{1,0:T(1,128)S(1)}, f32[1,1536]{1,0:T(1,128)S(1)}, u32[]{:S(2)}, u32[]{:S(2)}) collective-permute-start(f32[1,1536]{1,0:T(1,128)S(1)} %bitcast.57), channel_id=1, source_target_pairs={{0,0},{16,4},{32,8},{48,12},{4,16},{20,20},{36,24},{52,28},{8,32},... | collective-permute-start | bytes 18440 | tf_op jit(solution)/shard_map/ppermute | solution.py:290
  144.3 1.6 %collective-permute-done.17 = f32[1,1536]{1,0:T(1,128)S(1)} collective-permute-done((f32[1,1536]{1,0:T(1,128)S(1)}, f32[1,1536]{1,0:T(1,128)S(1)}, u32[]{:S(2)}, u32[]{:S(2)}) %collective-permute-start.17) | collective-permute-done | bytes 6176 | tf_op jit(solution)/shard_map/ppermute | solution.py:290
  (50 shorter events, 7.9 us)
Async XLA Ops:
  0.6 33.6 %copy-start = (bf16[96,2048]{1,0:T(8,128)(2,1)S(1)}, bf16[96,2048]{1,0:T(8,128)(2,1)}, u32[]{:S(2)}) copy-start(bf16[96,2048]{1,0:T(8,128)(2,1)} %param.6) | copy-start | bytes 1179652
  0.6 1.3 copy-start.2
  3.1 8.7 %copy-start.4 = (s32[192]{0:T(256)S(1)}, s32[192]{0:T(256)}, u32[]{:S(2)}) copy-start(s32[192]{0:T(256)} %param.10) | copy-start | bytes 2308
  3.1 29.4 %all-to-all-start = ((bf16[16,2,96,128]{3,2,1,0:T(8,128)(2,1)}), bf16[16,2,96,128]{3,2,1,0:T(8,128)(2,1)S(1)}, u32[]{:S(2)}, u32[]{:S(2)}) async-start(bf16[16,2,96,128]{3,2,1,0:T(8,128)(2,1)} %maximum_bitcast_fusion), calls=%async_computation | async-start | bytes 1572864 | tf_op jit(solution)/shard_map/all_to_all | solution.py:259
  32.6 23.3 %collective-permute-start.3 = (bf16[2,12,128,128]{3,2,1,0:T(8,128)(2,1)S(1)}, bf16[2,12,128,128]{3,2,1,0:T(8,128)(2,1)S(1)}, u32[]{:S(2)}, u32[]{:S(2)}) collective-permute-start(bf16[2,12,128,128]{3,2,1,0:T(8,128)(2,1)S(1)} %prepare.1.refs_2_), channel_id=1, source_target_pairs={{0,64},{64,128},{128,192},{192,0},{1,65},{65,129},{129,193},{193,1... | collective-permute-start | bytes 2359304 | tf_op jit(solution)/shard_map/ppermute | solution.py:29
  35.0 18.8 %all-to-all-start.1 = ((bf16[16,96,128]{2,1,0:T(8,128)(2,1)}), bf16[16,96,128]{2,1,0:T(8,128)(2,1)S(1)}, u32[]{:S(2)}, u32[]{:S(2)}) async-start(bf16[16,96,128]{2,1,0:T(8,128)(2,1)} %bitcast_bitcast_fusion), calls=%async_computation.1 | async-start | bytes 786432 | tf_op jit(solution)/shard_map/all_to_all | solution.py:259
  40.2 20.0 %collective-permute-start.2 = (bf16[2,12,128,128]{3,2,1,0:T(8,128)(2,1)S(1)}, bf16[2,12,128,128]{3,2,1,0:T(8,128)(2,1)S(1)}, u32[]{:S(2)}, u32[]{:S(2)}) collective-permute-start(bf16[2,12,128,128]{3,2,1,0:T(8,128)(2,1)S(1)} %prepare.1.refs_2_), channel_id=1, source_target_pairs={{0,192},{64,0},{128,64},{192,128},{1,193},{65,1},{129,65},{193,129... | collective-permute-start | bytes 2359304 | tf_op jit(solution)/shard_map/ppermute | solution.py:29
  53.9 17.5 %copy-start.1 = (s32[48,48]{1,0:T(8,128)S(1)}, s32[48,48]{1,0:T(8,128)}, u32[]{:S(2)}) copy-start(s32[48,48]{1,0:T(8,128)} %select_reduce_fusion.lists) | copy-start | bytes 27652
  53.9 14.1 %collective-permute-start = (bf16[12,128,128]{2,1,0:T(8,128)(2,1)S(1)}, bf16[12,128,128]{2,1,0:T(8,128)(2,1)S(1)}, u32[]{:S(2)}, u32[]{:S(2)}) collective-permute-start(bf16[12,128,128]{2,1,0:T(8,128)(2,1)S(1)} %bitcast.43), channel_id=1, source_target_pairs={{0,12},{4,0},{8,4},{12,8},{1,13},{5,1},{9,5},{13,9},{2,14},{6,2},{... | collective-permute-start | bytes 1179656 | tf_op jit(solution)/shard_map/ppermute | solution.py:29
  54.3 12.0 %collective-permute-start.1 = (bf16[12,128,128]{2,1,0:T(8,128)(2,1)S(1)}, bf16[12,128,128]{2,1,0:T(8,128)(2,1)S(1)}, u32[]{:S(2)}, u32[]{:S(2)}) collective-permute-start(bf16[12,128,128]{2,1,0:T(8,128)(2,1)S(1)} %bitcast.44), channel_id=1, source_target_pairs={{0,4},{4,8},{8,12},{12,0},{1,5},{5,9},{9,13},{13,1},{2,6},{6,10},{... | collective-permute-start | bytes 1179656 | tf_op jit(solution)/shard_map/ppermute | solution.py:29
  55.9 13.0 %collective-permute-start.4 = (bf16[12,128,128]{2,1,0:T(8,128)(2,1)S(1)}, bf16[12,128,128]{2,1,0:T(8,128)(2,1)S(1)}, u32[]{:S(2)}, u32[]{:S(2)}) collective-permute-start(bf16[12,128,128]{2,1,0:T(8,128)(2,1)S(1)} %slice_bitcast_fusion.1), channel_id=1, source_target_pairs={{0,64},{64,128},{128,192},{192,0},{1,65},{65,129},{129,193},{193,1... | collective-permute-start | bytes 1179656 | tf_op jit(solution)/shard_map/ppermute | solution.py:29
  60.2 11.2 %collective-permute-start.5 = (bf16[12,128,128]{2,1,0:T(8,128)(2,1)S(1)}, bf16[12,128,128]{2,1,0:T(8,128)(2,1)S(1)}, u32[]{:S(2)}, u32[]{:S(2)}) collective-permute-start(bf16[12,128,128]{2,1,0:T(8,128)(2,1)S(1)} %slice_bitcast_fusion), channel_id=1, source_target_pairs={{0,192},{64,0},{128,64},{192,128},{1,193},{65,1},{129,65},{193,129... | collective-permute-start | bytes 1179656 | tf_op jit(solution)/shard_map/ppermute | solution.py:29
  66.3 21.0 %collective-permute-start.7 = (bf16[6,128,128]{2,1,0:T(8,128)(2,1)S(1)}, bf16[6,128,128]{2,1,0:T(8,128)(2,1)S(1)}, u32[]{:S(2)}, u32[]{:S(2)}) collective-permute-start(bf16[6,128,128]{2,1,0:T(8,128)(2,1)S(1)} %slice.20), channel_id=1, source_target_pairs={{0,4},{4,8},{8,12},{12,0},{1,5},{5,9},{9,13},{13,1},{2,6},{6,10},{... | collective-permute-start | bytes 589832 | tf_op jit(solution)/shard_map/ppermute | solution.py:29
  68.0 19.4 %collective-permute-start.8 = (bf16[6,128,128]{2,1,0:T(8,128)(2,1)S(1)}, bf16[6,128,128]{2,1,0:T(8,128)(2,1)S(1)}, u32[]{:S(2)}, u32[]{:S(2)}) collective-permute-start(bf16[6,128,128]{2,1,0:T(8,128)(2,1)S(1)} %slice.21), channel_id=1, source_target_pairs={{0,12},{4,0},{8,4},{12,8},{1,13},{5,1},{9,5},{13,9},{2,14},{6,2},{... | collective-permute-start | bytes 589832 | tf_op jit(solution)/shard_map/ppermute | solution.py:29
  85.2 21.6 %collective-permute-start.10 = (bf16[12,144,128]{2,1,0:T(8,128)(2,1)S(1)}, bf16[12,144,128]{2,1,0:T(8,128)(2,1)S(1)}, u32[]{:S(2)}, u32[]{:S(2)}) collective-permute-start(bf16[12,144,128]{2,1,0:T(8,128)(2,1)S(1)} %get-tuple-element.21), channel_id=1, source_target_pairs={{0,12},{4,0},{8,4},{12,8},{1,13},{5,1},{9,5},{13,9},{2,14},{6,2},{... | collective-permute-start | bytes 1327112 | tf_op jit(solution)/shard_map/ppermute | solution.py:29
  85.7 21.1 %collective-permute-start.6 = (bf16[12,144,128]{2,1,0:T(8,128)(2,1)S(1)}, bf16[12,144,128]{2,1,0:T(8,128)(2,1)S(1)}, u32[]{:S(2)}, u32[]{:S(2)}) collective-permute-start(bf16[12,144,128]{2,1,0:T(8,128)(2,1)S(1)} %get-tuple-element.20), channel_id=1, source_target_pairs={{0,4},{4,8},{8,12},{12,0},{1,5},{5,9},{9,13},{13,1},{2,6},{6,10},{... | collective-permute-start | bytes 1327112 | tf_op jit(solution)/shard_map/ppermute | solution.py:29
  95.7 14.4 %collective-permute-start.9 = (bf16[12,144,128]{2,1,0:T(8,128)(2,1)S(1)}, bf16[12,144,128]{2,1,0:T(8,128)(2,1)S(1)}, u32[]{:S(2)}, u32[]{:S(2)}) collective-permute-start(bf16[12,144,128]{2,1,0:T(8,128)(2,1)S(1)} %attend.5), channel_id=1, source_target_pairs={{0,8},{4,12},{8,0},{12,4},{1,9},{5,13},{9,1},{13,5},{2,10},{6,14},... | collective-permute-start | bytes 1327112 | tf_op jit(solution)/shard_map/ppermute | solution.py:29
  106.8 14.3 %copy-start.3 = (s32[192]{0:T(256)S(1)}, s32[192]{0:T(256)}, u32[]{:S(2)}) copy-start(s32[192]{0:T(256)} %param.11) | copy-start | bytes 2308
  111.3 34.6 %all-to-all-start.2 = ((bf16[16,96,128]{2,1,0:T(8,128)(2,1)}), bf16[16,96,128]{2,1,0:T(8,128)(2,1)S(1)}, u32[]{:S(2)}, u32[]{:S(2)}) async-start(bf16[16,96,128]{2,1,0:T(8,128)(2,1)} %bitcast.5), calls=%async_computation.2 | async-start | bytes 786432 | tf_op jit(solution)/shard_map/all_to_all | solution.py:259
  115.3 5.9 %collective-permute-start.13 = (f32[12,128]{1,0:T(8,128)S(1)}, f32[12,128]{1,0:T(8,128)S(1)}, u32[]{:S(2)}, u32[]{:S(2)}) collective-permute-start(f32[12,128]{1,0:T(8,128)S(1)} %get-tuple-element.23), channel_id=1, source_target_pairs={{0,4},{4,8},{8,12},{12,0},{1,5},{5,9},{9,13},{13,1},{2,6},{6,10},{... | collective-permute-start | bytes 18440 | tf_op jit(solution)/shard_map/ppermute | solution.py:29
  116.8 4.5 %collective-permute-start.11 = (f32[12,128]{1,0:T(8,128)S(1)}, f32[12,128]{1,0:T(8,128)S(1)}, u32[]{:S(2)}, u32[]{:S(2)}) collective-permute-start(f32[12,128]{1,0:T(8,128)S(1)} %get-tuple-element.23), channel_id=1, source_target_pairs={{0,12},{4,0},{8,4},{12,8},{1,13},{5,1},{9,5},{13,9},{2,14},{6,2},{... | collective-permute-start | bytes 18440 | tf_op jit(solution)/shard_map/ppermute | solution.py:29
  117.4 5.3 %collective-permute-start.12 = (f32[12,128]{1,0:T(8,128)S(1)}, f32[12,128]{1,0:T(8,128)S(1)}, u32[]{:S(2)}, u32[]{:S(2)}) collective-permute-start(f32[12,128]{1,0:T(8,128)S(1)} %get-tuple-element.23), channel_id=1, source_target_pairs={{0,8},{4,12},{8,0},{12,4},{1,9},{5,13},{9,1},{13,5},{2,10},{6,14},... | collective-permute-start | bytes 18440 | tf_op jit(solution)/shard_map/ppermute | solution.py:29
  122.8 6.7 %collective-permute-start.14 = (f32[4,12,128]{2,1,0:T(8,128)S(1)}, f32[4,12,128]{2,1,0:T(8,128)S(1)}, u32[]{:S(2)}, u32[]{:S(2)}) collective-permute-start(f32[4,12,128]{2,1,0:T(8,128)S(1)} %get-tuple-element.30), channel_id=1, source_target_pairs={{0,192},{64,0},{128,64},{192,128},{1,193},{65,1},{129,65},{193,129... | collective-permute-start | bytes 73736 | tf_op jit(solution)/shard_map/ppermute | solution.py:29
  127.8 5.5 %collective-permute-start.15 = (f32[4,12,128]{2,1,0:T(8,128)S(1)}, f32[4,12,128]{2,1,0:T(8,128)S(1)}, u32[]{:S(2)}, u32[]{:S(2)}) collective-permute-start(f32[4,12,128]{2,1,0:T(8,128)S(1)} %get-tuple-element.30), channel_id=1, source_target_pairs={{0,128},{64,192},{128,0},{192,64},{1,129},{65,193},{129,1},{193,65... | collective-permute-start | bytes 73736 | tf_op jit(solution)/shard_map/ppermute | solution.py:29
  127.8 5.5 %collective-permute-start.16 = (f32[4,12,128]{2,1,0:T(8,128)S(1)}, f32[4,12,128]{2,1,0:T(8,128)S(1)}, u32[]{:S(2)}, u32[]{:S(2)}) collective-permute-start(f32[4,12,128]{2,1,0:T(8,128)S(1)} %get-tuple-element.30), channel_id=1, source_target_pairs={{0,64},{64,128},{128,192},{192,0},{1,65},{65,129},{129,193},{193,1... | collective-permute-start | bytes 73736 | tf_op jit(solution)/shard_map/ppermute | solution.py:29
  134.0 11.9 %collective-permute-start.17 = (f32[1,1536]{1,0:T(1,128)S(1)}, f32[1,1536]{1,0:T(1,128)S(1)}, u32[]{:S(2)}, u32[]{:S(2)}) collective-permute-start(f32[1,1536]{1,0:T(1,128)S(1)} %bitcast.57), channel_id=1, source_target_pairs={{0,0},{16,4},{32,8},{48,12},{4,16},{20,20},{36,24},{52,28},{8,32},... | collective-permute-start | bytes 18440 | tf_op jit(solution)/shard_map/ppermute | solution.py:290

commit v5 on v4

--- a/solution.py
+++ b/solution.py
@@ -30,7 +30,33 @@
 
 
 def around(array, axis):
-    return jnp.stack([array] + [shift(array, axis, -by) for by in range(1, RING)])
+    return [array] + [shift(array, axis, -by) for by in range(1, RING)]
+
+
+def spread_kernel(keys, values, out, sems):
+    copies = [
+        pltpu.make_async_copy(
+            array.at[:, pl.ds(head * HD, HD)], out.at[head, which], sems.at[which, head]
+        )
+        for which, array in enumerate((keys, values))
+        for head in range(16)
+    ]
+    for copy in copies:
+        copy.start()
+    for copy in copies:
+        copy.wait()
+
+
+def spread(keys, values):
+    return pl.pallas_call(
+        spread_kernel,
+        out_shape=jax.ShapeDtypeStruct((16, 2, 96, HD), jnp.bfloat16),
+        in_specs=[pl.BlockSpec(memory_space=pl.ANY)] * 2,
+        out_specs=VMEM,
+        scratch_shapes=[pltpu.SemaphoreType.DMA((2, 16))],
+        compiler_params=SPACE,
+        name="spread",
+    )(keys, values)
 
 
 def prepare_kernel(got_ref, kv_ref):
@@ -64,6 +90,7 @@
         ks, vs = refs[:2]
         refs = refs[2:]
     o_out, refs = refs[: len(blocks)], refs[len(blocks) :]
+    e_out, refs = refs[: len(blocks)], refs[len(blocks) :]
     rows, sizes, qs, m_ref, l_ref, acc_ref = refs[:6]
     s_refs, top_refs = refs[6 : 6 + WIDTH], refs[6 + WIDTH :]
     for b, q in enumerate(queries):
@@ -98,7 +125,8 @@
 
     def listed(t, j):
         row = rows[t]
-        return [lists[row, j * CHUNK + u] for u in range(CHUNK)]
+        word = lists[row * (KEYS // CHUNK) + j]
+        return [(word >> (8 * u)) & 255 for u in range(CHUNK)]
 
     def score(lane, t, j):
         left = sizes[t] - j * CHUNK
@@ -167,6 +195,7 @@
                 safe = jnp.where(some, total, 1.0)
                 share = jnp.where(some, 1.0 / safe, 0.0)
                 lse = jnp.where(some, m_ref[b * OWN + t] * SCALE + jnp.log(safe), NEG)
+                e_out[b][pl.ds(t, 1)] = lse
                 high = lse.astype(jnp.bfloat16)
                 middle = (lse - high.astype(jnp.float32)).astype(jnp.bfloat16)
                 low = (lse - high.astype(jnp.float32) - middle.astype(jnp.float32)).astype(
@@ -183,15 +212,16 @@
 
 def attend(blocks, lists, counts, queries, keys_values, first_call=False):
     tiles = jax.ShapeDtypeStruct((OWN, HD + PAD, BLK), jnp.bfloat16)
+    logs = jax.ShapeDtypeStruct((OWN, BLK), jnp.float32)
     held = (jax.ShapeDtypeStruct((KEYS, BLK, HD), jnp.bfloat16),) * 2 if first_call else ()
     count = len(blocks)
     slots = count * OWN + 1
     pairs = count * OWN * 15
     return pl.pallas_call(
         functools.partial(attend_kernel, blocks, first_call),
-        out_shape=held + (tiles,) * count,
+        out_shape=held + (tiles,) * count + (logs,) * count,
         in_specs=[SMEM, SMEM] + [VMEM] * (count + len(keys_values)),
-        out_specs=(VMEM,) * (count + len(held)),
+        out_specs=(VMEM,) * (2 * count + len(held)),
         scratch_shapes=[
             pltpu.SMEM((slots,), jnp.int32),
             pltpu.SMEM((slots,), jnp.int32),
@@ -213,7 +243,7 @@
 
 
 def combine_kernel(*refs):
-    outs, (o_ref, lse_ref) = refs[:RING], refs[RING:]
+    outs, o_ref = refs[:-1], refs[-1]
     for t in range(OWN):
         parts = []
         for o in outs:
@@ -222,7 +252,6 @@
         top = jnp.maximum(jnp.maximum(parts[0], parts[1]), jnp.maximum(parts[2], parts[3]))
         shares = [jnp.exp(part - top) for part in parts]
         total = (shares[0] + shares[1]) + (shares[2] + shares[3])
-        lse_ref[t : t + 1] = top + jnp.log(total)
         mixed = sum(o[t, :HD].astype(jnp.float32) * (w / total) for o, w in zip(outs, shares))
         o_ref[t] = mixed.T.astype(jnp.bfloat16)
 
@@ -230,15 +259,59 @@
 def combine(outs):
     return pl.pallas_call(
         combine_kernel,
-        out_shape=(
-            jax.ShapeDtypeStruct((OWN, BLK, HD), jnp.bfloat16),
-            jax.ShapeDtypeStruct((OWN, BLK), jnp.float32),
-        ),
+        out_shape=jax.ShapeDtypeStruct((OWN, BLK, HD), jnp.bfloat16),
         in_specs=[VMEM] * RING,
-        out_specs=(VMEM, VMEM),
+        out_specs=VMEM,
         compiler_params=SPACE,
         name="combine",
     )(*outs)
+
+
+def settle_kernel(spots, e0, e1, e2, e3, *refs):
+    outs, merged = refs[:RING], refs[RING]
+    parts = (e0, e1, e2, e3)
+    for block in range(RING):
+        part = [
+            parts[s][(block - s) % RING * OWN : ((block - s) % RING + 1) * OWN] for s in range(RING)
+        ]
+        top = jnp.maximum(jnp.maximum(part[0], part[1]), jnp.maximum(part[2], part[3]))
+        total = sum(jnp.exp(p - top) for p in part)
+        merged[block * OWN : (block + 1) * OWN] = top + jnp.log(total)
+    merged[KEYS : KEYS + 8] = jnp.zeros((8, BLK), jnp.float32)
+    for away, out in enumerate(outs):
+        for slot in range(OWN):
+            out[slot : slot + 1] = merged[pl.ds(spots[away * OWN + slot], 1)]
+
+
+def settle(spots, parts):
+    return pl.pallas_call(
+        settle_kernel,
+        out_shape=(jax.ShapeDtypeStruct((OWN, BLK), jnp.float32),) * RING,
+        in_specs=[SMEM] + [VMEM] * RING,
+        out_specs=(VMEM,) * RING,
+        scratch_shapes=[pltpu.VMEM((KEYS + 8, BLK), jnp.float32)],
+        compiler_params=SPACE,
+        name="settle",
+    )(spots, *parts)
+
+
+def slot_spots(assign, xi, yi):
+    away = jnp.arange(RING * OWN, dtype=jnp.int32) // OWN
+    slots = ((xi + away) % RING * RING + yi) * OWN + jnp.arange(RING * OWN, dtype=jnp.int32) % OWN
+    match = slots[:, None] == jnp.arange(assign.shape[0], dtype=jnp.int32)[None, :]
+    tiles = jnp.sum(jnp.where(match, assign[None, :], 0), axis=1)
+    spots = (tiles % OWN // 3 - yi) % RING * OWN + tiles % KEYS // OWN * 3 + tiles % 3
+    return jnp.where(tiles // KEYS == xi, spots, KEYS)
+
+
+def deliver(array, away):
+    pairs = []
+    for x in range(RING):
+        for zh in range(RING):
+            for y in range(RING):
+                source = (x * RING + zh) * RING + y
+                pairs.append((source, ((x + away) % RING * RING + y) * RING + zh))
+    return lax.ppermute(array, ("x", "zh", "y"), pairs)
 
 
 def key_lists(kv_tiles, tile_count, xi, yi):
@@ -250,8 +323,10 @@
     rank = jnp.dot(
         here.astype(jnp.bfloat16), before.astype(jnp.bfloat16), preferred_element_type=jnp.float32
     ).astype(jnp.int32)
-    at = here[:, None, :] & (rank[:, None, :] == jnp.arange(KEYS, dtype=jnp.int32)[None, :, None])
-    lists = jnp.sum(jnp.where(at, place[:, None, :], 0), axis=2)
+    step = jnp.arange(KEYS // CHUNK, dtype=jnp.int32)[None, :, None]
+    at = here[:, None, :] & (rank[:, None, :] // CHUNK == step)
+    word = place << (8 * (rank % CHUNK))
+    lists = jnp.sum(jnp.where(at, word[:, None, :], 0), axis=2).reshape(-1)
     return lists, jnp.sum(here.astype(jnp.int32), axis=1)
 
 
@@ -262,32 +337,30 @@
 def on_device(queries, keys, values, kv_tiles, tile_count, assign):
     xi, yi = lax.axis_index("x"), lax.axis_index("y")
     lists, counts = key_lists(kv_tiles, tile_count, xi, yi)
-    sent = jnp.stack([a.reshape(96, 16, HD) for a in (keys, values)])
-    got = exchange(jnp.transpose(sent, (2, 0, 1, 3)))
-    got, lists, counts = lax.optimization_barrier((got, lists, counts))
+    spots = slot_spots(assign, xi, yi)
+    by_head = jnp.transpose(queries.reshape(96, 16, HD), (1, 0, 2))
+    got = exchange(spread(keys, values))
+    got, lists, counts, spots, by_head = lax.optimization_barrier(
+        (got, lists, counts, spots, by_head)
+    )
     kv0 = prepare(got)
     kv1, kv3 = shift(kv0, "x", -1), shift(kv0, "x", 1)
-    queries, kv0 = lax.optimization_barrier((queries, kv0))
-    q0 = exchange(jnp.transpose(queries.reshape(96, 16, HD), (1, 0, 2))).reshape(OWN, BLK, HD)
+    q0 = exchange(by_head).reshape(OWN, BLK, HD)
     k2, v2 = shift(kv3[0], "x", 1), shift(kv1[1], "x", -1)
     q1, q3 = shift(q0, "y", -1), shift(q0, "y", 1)
     half = OWN // 2
     q2 = jnp.concatenate([shift(q3[:half], "y", 1), shift(q1[half:], "y", -1)])
-    all_keys, all_values, o1, o3 = attend(
+    all_keys, all_values, o1, o3, e1, e3 = attend(
         (1, 3), lists, counts, (q1, q3), (kv0, kv1, kv3, k2, v2), first_call=True
     )
-    (o2,) = attend((2,), lists, counts, (q2,), (all_keys, all_values))
-    (o0,) = attend((0,), lists, counts, (q0,), (all_keys, all_values))
-    blended, lse = combine((o0, shift(o1, "y", 1), shift(o2, "y", 2), shift(o3, "y", -1)))
+    o2, e2 = attend((2,), lists, counts, (q2,), (all_keys, all_values))
+    o0, e0 = attend((0,), lists, counts, (q0,), (all_keys, all_values))
+    picked = settle(spots, around(jnp.concatenate([e0, e1, e2, e3]), "y"))
+    blended = combine((o0, shift(o1, "y", 1), shift(o2, "y", 2), shift(o3, "y", -1)))
     back = exchange(blended.reshape(16, 96, HD))
     attended = jnp.transpose(back, (1, 0, 2)).reshape(96, 16 * HD)
-    every = around(around(lse, "y"), "x").reshape(-1, BLK)
-    tiles = lax.dynamic_slice_in_dim(assign, (xi * RING + yi) * OWN, OWN)
-    spots = (tiles // KEYS - xi) % RING * KEYS + (tiles % OWN // 3 - yi) % RING * OWN
-    spots = spots + tiles % KEYS // OWN * 3 + tiles % 3
-    chosen = jnp.take(every, spots, axis=0).reshape(1, OWN * BLK)
-    turned = [(b * RING + a, a * RING + b) for a in range(RING) for b in range(RING)]
-    return attended, lax.ppermute(chosen, ("zh", "y"), turned)
+    slot_lse = sum(deliver(array, away) for away, array in enumerate(picked))
+    return attended, slot_lse.reshape(1, OWN * BLK)
 
 
 def solution(mesh):

time: 149 us -> 160 us (1.074)
  starting transfers between devices: 58 us -> 63.5 us
  waiting for transfers between devices: 49.3 us -> 53.9 us
  local copies, waits for them, and re-layouts: 4.36 us -> 6.58 us
  other arithmetic: 3.66 us -> 1.89 us
    ppermute x1 -> x4, starting transfers between devices: 10.3 us -> 22.6 us  [deliver(): return lax.ppermute(array, ('x', 'zh', 'y'), pairs)]
    ppermute x1 -> x4, waiting for transfers between devices: 1.59 us -> 10.9 us  [deliver(): return lax.ppermute(array, ('x', 'zh', 'y'), pairs)]
    ppermute x17 -> x14, starting transfers between devices: 29.8 us -> 21.2 us  [shift(): lax.ppermute(array, axis, [(i, (i + by) % RING) for i in range(RING)])]
    ppermute x17 -> x14, waiting for transfers between devices: 17.9 us -> 14.2 us  [shift(): lax.ppermute(array, axis, [(i, (i + by) % RING) for i in range(RING)])]
    unnamed x14 -> x19, local copies, waits for them, and re-layouts: 1.83 us -> 4.03 us
    pallas_call x1 -> x3, Pallas kernels: 1.21 us -> 3.28 us  [the longest x1 1.46 us: spread(): pl.pallas_call(spread_kernel, out_shape=jax.ShapeDtypeStruct((16, 2, 96,...]
    all_to_all x3, starting transfers between devices: 17.8 us -> 19.7 us  [exchange(): return lax.all_to_all(array, GROUP, split_axis=0, concat_axis=0, tiled=True)]
  transfers between devices with their start and end apart: 21 -> 21, of which waited for: 11 -> 11; matrix products, arithmetic and copies ran while one was open for 3% -> 3% of each run, Pallas kernels for 20% -> 18%
where the time goes in v5:
time: 160 us; the launch traced here: 159 us
  starting transfers between devices  63.5 us (40%)
  waiting for transfers between devices  53.9 us (34%)
  Pallas kernels  32 us (20%)
  local copies, waits for them, and re-layouts  6.58 us (4%)
  other arithmetic  1.89 us (1%)
    all_to_all x3, waiting for transfers between devices, exchange(): return lax.all_to_all(array, GROUP, split_axis=0, concat_axis=0, tiled=True)  28.8 us
    pallas_call x3, Pallas kernels, attend(): pl.pallas_call(functools.partial(attend_kernel, blocks, first_call), out_...  28.6 us
    ppermute x4, starting transfers between devices, deliver(): return lax.ppermute(array, ('x', 'zh', 'y'), pairs)  22.6 us
    ppermute x14, starting transfers between devices, shift(): lax.ppermute(array, axis, [(i, (i + by) % RING) for i in range(RING)])  21.2 us
    all_to_all x3, starting transfers between devices, exchange(): return lax.all_to_all(array, GROUP, split_axis=0, concat_axis=0, tiled=True)  19.7 us
    ppermute x14, waiting for transfers between devices, shift(): lax.ppermute(array, axis, [(i, (i + by) % RING) for i in range(RING)])  14.2 us
    ppermute x4, waiting for transfers between devices, deliver(): return lax.ppermute(array, ('x', 'zh', 'y'), pairs)  10.9 us
    unnamed x19, local copies, waits for them, and re-layouts  4.03 us
  transfers between devices with their start and end apart: 21, of which 11 were waited for; matrix products, arithmetic and copies ran while one was open for 3% of the time, Pallas kernels for 18%

profile of v5, /device:TPU:16, one launch (start us, length us, event | category | flops | bytes accessed | tf_op | source)
XLA Modules:
  0.0 158.9 jit_solution(4685398259930419314)
XLA Ops:
  0.7 1.0 copy-done.1
  1.7 1.0 copy-done.2
  2.7 1.5 spread.1
  4.2 8.6 %all-to-all-start = ((bf16[16,2,96,128]{3,2,1,0:T(8,128)(2,1)}), bf16[16,2,96,128]{3,2,1,0:T(8,128)(2,1)S(1)}, u32[]{:S(2)}, u32[]{:S(2)}) async-start(bf16[16,2,96,128]{3,2,1,0:T(8,128)(2,1)} %spread.1), calls=%async_computation | async-start | bytes 1572864 | tf_op jit(solution)/shard_map/all_to_all | solution.py:334
  16.5 17.0 %all-to-all-done.got_ref = bf16[16,2,96,128]{3,2,1,0:T(8,128)(2,1)S(1)} async-done(((bf16[16,2,96,128]{3,2,1,0:T(8,128)(2,1)}), bf16[16,2,96,128]{3,2,1,0:T(8,128)(2,1)S(1)}, u32[]{:S(2)}, u32[]{:S(2)}) %all-to-all-start) | async-done | bytes 786464 | tf_op jit(solution)/shard_map/all_to_all | solution.py:334
  33.6 1.6 collective-permute-start.3
  35.2 5.1 %all-to-all-start.1 = ((bf16[16,96,128]{2,1,0:T(8,128)(2,1)}), bf16[16,96,128]{2,1,0:T(8,128)(2,1)S(1)}, u32[]{:S(2)}, u32[]{:S(2)}) async-start(bf16[16,96,128]{2,1,0:T(8,128)(2,1)} %bitcast_bitcast_fusion), calls=%async_computation.1 | async-start | bytes 786432 | tf_op jit(solution)/shard_map/all_to_all | solution.py:334
  40.3 1.8 %collective-permute-start.2 = (bf16[2,12,128,128]{3,2,1,0:T(8,128)(2,1)S(1)}, bf16[2,12,128,128]{3,2,1,0:T(8,128)(2,1)S(1)}, u32[]{:S(2)}, u32[]{:S(2)}) collective-permute-start(bf16[2,12,128,128]{3,2,1,0:T(8,128)(2,1)S(1)} %prepare.1.refs_2_), channel_id=1, source_target_pairs={{0,192},{64,0},{128,64},{192,128},{1,193},{65,1},{129,65},{193,129... | collective-permute-start | bytes 2359304 | tf_op jit(solution)/shard_map/ppermute | solution.py:29
  42.2 11.9 %all-to-all-done.1 = bf16[16,96,128]{2,1,0:T(8,128)(2,1)S(1)} async-done(((bf16[16,96,128]{2,1,0:T(8,128)(2,1)}), bf16[16,96,128]{2,1,0:T(8,128)(2,1)S(1)}, u32[]{:S(2)}, u32[]{:S(2)}) %all-to-all-start.1) | async-done | bytes 393248 | tf_op jit(solution)/shard_map/all_to_all | solution.py:334
  54.5 1.6 collective-permute-start.1
  56.1 1.6 collective-permute-start.4
  57.6 2.6 %collective-permute-done.2.refs_3_ = bf16[2,12,128,128]{3,2,1,0:T(8,128)(2,1)S(1)} collective-permute-done((bf16[2,12,128,128]{3,2,1,0:T(8,128)(2,1)S(1)}, bf16[2,12,128,128]{3,2,1,0:T(8,128)(2,1)S(1)}, u32[]{:S(2)}, u32[]{:S(2)}) %collective-permute-start.2) | collective-permute-done | bytes 786464 | tf_op jit(solution)/shard_map/ppermute | solution.py:29
  60.3 3.0 %collective-permute-start.5 = (bf16[12,128,128]{2,1,0:T(8,128)(2,1)S(1)}, bf16[12,128,128]{2,1,0:T(8,128)(2,1)S(1)}, u32[]{:S(2)}, u32[]{:S(2)}) collective-permute-start(bf16[12,128,128]{2,1,0:T(8,128)(2,1)S(1)} %slice_bitcast_fusion), channel_id=1, source_target_pairs={{0,192},{64,0},{128,64},{192,128},{1,193},{65,1},{129,65},{193,129... | collective-permute-start | bytes 1179656 | tf_op jit(solution)/shard_map/ppermute | solution.py:29
  63.3 3.1 %collective-permute-done.1.refs_1_ = bf16[12,128,128]{2,1,0:T(8,128)(2,1)S(1)} collective-permute-done((bf16[12,128,128]{2,1,0:T(8,128)(2,1)S(1)}, bf16[12,128,128]{2,1,0:T(8,128)(2,1)S(1)}, u32[]{:S(2)}, u32[]{:S(2)}) %collective-permute-start.1) | collective-permute-done | bytes 393248 | tf_op jit(solution)/shard_map/ppermute | solution.py:29
  66.4 1.7 %collective-permute-start.7 = (bf16[6,128,128]{2,1,0:T(8,128)(2,1)S(1)}, bf16[6,128,128]{2,1,0:T(8,128)(2,1)S(1)}, u32[]{:S(2)}, u32[]{:S(2)}) collective-permute-start(bf16[6,128,128]{2,1,0:T(8,128)(2,1)S(1)} %slice.18), channel_id=1, source_target_pairs={{0,4},{4,8},{8,12},{12,0},{1,5},{5,9},{9,13},{13,1},{2,6},{6,10},{... | collective-permute-start | bytes 589832 | tf_op jit(solution)/shard_map/ppermute | solution.py:29
  69.1 2.4 %collective-permute-done.5.refs_6_ = bf16[12,128,128]{2,1,0:T(8,128)(2,1)S(1)} collective-permute-done((bf16[12,128,128]{2,1,0:T(8,128)(2,1)S(1)}, bf16[12,128,128]{2,1,0:T(8,128)(2,1)S(1)}, u32[]{:S(2)}, u32[]{:S(2)}) %collective-permute-start.5) | collective-permute-done | bytes 393248 | tf_op jit(solution)/shard_map/ppermute | solution.py:29
  72.9 13.2 %attend.3 = (bf16[48,128,128]{2,1,0:T(8,128)(2,1)S(1)}, bf16[48,128,128]{2,1,0:T(8,128)(2,1)S(1)}, bf16[12,144,128]{2,1,0:T(8,128)(2,1)S(1)}, bf16[12,144,128]{2...) custom-call(s32[576]{0:T(1024)S(1)} %copy-done.3, s32[48]{0:T(128)S(1)} %copy-done.5, ...), custom_call_target="tpu_custom_call" | custom-call | flops 3019898880 | bytes 5242880 | tf_op jit(solution)/shard_map/attend/pallas_call | solution.py:220
  86.1 1.5 collective-permute-start.10
  87.6 0.9 collective-permute-start.6
  88.6 8.2 %attend.5 = (bf16[12,144,128]{2,1,0:T(8,128)(2,1)S(1)}, f32[12,128]{1,0:T(8,128)S(1)}) custom-call(s32[576]{0:T(1024)S(1)} %copy-done.3, s32[48]{0:T(128)S(1)} %copy-done.5, bf16[12,128,128]{2,1,0:T(8,128)(2,1)S(1)} %pad_maximum_fusion.refs_0_, bf16[48,128,128]{2,1,0:T(8,128)(2,1)S(1)} %get-tuple-element.25.refs_1_, ...), custom_call_target="tpu_custom_call" | custom-call | flops 1509949440 | bytes 5242880 | tf_op jit(solution)/shard_map/attend/pallas_call | solution.py:220
  96.8 1.3 collective-permute-start.9
  98.0 7.2 %attend.4 = (bf16[12,144,128]{2,1,0:T(8,128)(2,1)S(1)}, f32[12,128]{1,0:T(8,128)S(1)}) custom-call(s32[576]{0:T(1024)S(1)} %copy-done.3, s32[48]{0:T(128)S(1)} %copy-done.5, bf16[12,128,128]{2,1,0:T(8,128)(2,1)S(1)} %bitcast.28, bf16[48,128,128]{2,1,0:T(8,128)(2,1)S(1)} %get-tuple-element.25.refs_1_, bf16[48,128,128]{2,1,0:T(8,128)(2,1)S(1)} %get-tuple-element.26.refs_2_), custom_call_target="tpu_custom_call" | custom-call | flops 1509949440 | bytes 5242880 | tf_op jit(solution)/shard_map/attend/pallas_call | solution.py:220
  105.3 4.1 %collective-permute-done.9.refs_2_ = bf16[12,144,128]{2,1,0:T(8,128)(2,1)S(1)} collective-permute-done((bf16[12,144,128]{2,1,0:T(8,128)(2,1)S(1)}, bf16[12,144,128]{2,1,0:T(8,128)(2,1)S(1)}, u32[]{:S(2)}, u32[]{:S(2)}) %collective-permute-start.9) | collective-permute-done | bytes 442400 | tf_op jit(solution)/shard_map/ppermute | solution.py:29
  109.4 1.2 combine.1
  110.6 5.9 %all-to-all-start.2 = ((bf16[16,96,128]{2,1,0:T(8,128)(2,1)}), bf16[16,96,128]{2,1,0:T(8,128)(2,1)S(1)}, u32[]{:S(2)}, u32[]{:S(2)}) async-start(bf16[16,96,128]{2,1,0:T(8,128)(2,1)} %bitcast.4), calls=%async_computation.2 | async-start | bytes 786432 | tf_op jit(solution)/shard_map/all_to_all | solution.py:334
  117.0 2.6 %collective-permute-start.12 = (f32[48,128]{1,0:T(8,128)S(1)}, f32[48,128]{1,0:T(8,128)S(1)}, u32[]{:S(2)}, u32[]{:S(2)}) collective-permute-start(f32[48,128]{1,0:T(8,128)S(1)} %pad_maximum_fusion.1.e0), channel_id=1, source_target_pairs={{0,8},{4,12},{8,0},{12,4},{1,9},{5,13},{9,1},{13,5},{2,10},{6,14},... | collective-permute-start | bytes 73736 | tf_op jit(solution)/shard_map/ppermute | solution.py:29
  119.5 2.3 %collective-permute-start.13 = (f32[48,128]{1,0:T(8,128)S(1)}, f32[48,128]{1,0:T(8,128)S(1)}, u32[]{:S(2)}, u32[]{:S(2)}) collective-permute-start(f32[48,128]{1,0:T(8,128)S(1)} %pad_maximum_fusion.1.e0), channel_id=1, source_target_pairs={{0,4},{4,8},{8,12},{12,0},{1,5},{5,9},{9,13},{13,1},{2,6},{6,10},{... | collective-permute-start | bytes 73736 | tf_op jit(solution)/shard_map/ppermute | solution.py:29
  124.0 9.5 %collective-permute-start.14 = (f32[12,128]{1,0:T(8,128)S(1)}, f32[12,128]{1,0:T(8,128)S(1)}, u32[]{:S(2)}, u32[]{:S(2)}) collective-permute-start(f32[12,128]{1,0:T(8,128)S(1)} %get-tuple-element.36), channel_id=1, source_target_pairs={{0,0},{4,16},{8,32},{12,48},{16,4},{20,20},{24,36},{28,52},{32,8},... | collective-permute-start | bytes 18440 | tf_op jit(solution)/shard_map/ppermute | solution.py:314
  133.6 3.2 %collective-permute-start.15 = (f32[12,128]{1,0:T(8,128)S(1)}, f32[12,128]{1,0:T(8,128)S(1)}, u32[]{:S(2)}, u32[]{:S(2)}) collective-permute-start(f32[12,128]{1,0:T(8,128)S(1)} %get-tuple-element.37), channel_id=1, source_target_pairs={{0,64},{4,80},{8,96},{12,112},{16,68},{20,84},{24,100},{28,116},{3... | collective-permute-start | bytes 18440 | tf_op jit(solution)/shard_map/ppermute | solution.py:314
  136.8 9.9 %collective-permute-start.16 = (f32[12,128]{1,0:T(8,128)S(1)}, f32[12,128]{1,0:T(8,128)S(1)}, u32[]{:S(2)}, u32[]{:S(2)}) collective-permute-start(f32[12,128]{1,0:T(8,128)S(1)} %get-tuple-element.38), channel_id=1, source_target_pairs={{0,128},{4,144},{8,160},{12,176},{16,132},{20,148},{24,164},{28,18... | collective-permute-start | bytes 18440 | tf_op jit(solution)/shard_map/ppermute | solution.py:314
  146.6 2.5 %collective-permute-done.16 = f32[12,128]{1,0:T(8,128)S(1)} collective-permute-done((f32[12,128]{1,0:T(8,128)S(1)}, f32[12,128]{1,0:T(8,128)S(1)}, u32[]{:S(2)}, u32[]{:S(2)}) %collective-permute-start.16) | collective-permute-done | bytes 6176 | tf_op jit(solution)/shard_map/ppermute | solution.py:314
  149.1 8.4 %collective-permute-done.17 = f32[12,128]{1,0:T(8,128)S(1)} collective-permute-done((f32[12,128]{1,0:T(8,128)S(1)}, f32[12,128]{1,0:T(8,128)S(1)}, u32[]{:S(2)}, u32[]{:S(2)}) %collective-permute-start.17) | collective-permute-done | bytes 6176 | tf_op jit(solution)/shard_map/ppermute | solution.py:314
  (54 shorter events, 10.7 us)
Async XLA Ops:
  0.6 15.0 %copy-start = (bf16[96,2048]{1,0:T(8,128)(2,1)S(1)}, bf16[96,2048]{1,0:T(8,128)(2,1)}, u32[]{:S(2)}) copy-start(bf16[96,2048]{1,0:T(8,128)(2,1)} %param.6) | copy-start | bytes 1179652
  0.6 1.0 copy-start.1
  1.7 1.0 copy-start.2
  2.7 10.1 %copy-start.8 = (s32[192]{0:T(256)S(1)}, s32[192]{0:T(256)}, u32[]{:S(2)}) copy-start(s32[192]{0:T(256)} %param.10) | copy-start | bytes 2308
  2.7 10.2 %copy-start.6 = (s32[192,96]{1,0:T(8,128)S(1)}, s32[192,96]{1,0:T(8,128)}, u32[]{:S(2)}) copy-start(s32[192,96]{1,0:T(8,128)} %param.9) | copy-start | bytes 221188
  4.2 10.7 %copy-start.7 = (s32[192]{0:T(256)S(1)}, s32[192]{0:T(256)}, u32[]{:S(2)}) copy-start(s32[192]{0:T(256)} %param.11) | copy-start | bytes 2308
  4.2 29.3 %all-to-all-start = ((bf16[16,2,96,128]{3,2,1,0:T(8,128)(2,1)}), bf16[16,2,96,128]{3,2,1,0:T(8,128)(2,1)S(1)}, u32[]{:S(2)}, u32[]{:S(2)}) async-start(bf16[16,2,96,128]{3,2,1,0:T(8,128)(2,1)} %spread.1), calls=%async_computation | async-start | bytes 1572864 | tf_op jit(solution)/shard_map/all_to_all | solution.py:334
  33.6 22.4 %collective-permute-start.3 = (bf16[2,12,128,128]{3,2,1,0:T(8,128)(2,1)S(1)}, bf16[2,12,128,128]{3,2,1,0:T(8,128)(2,1)S(1)}, u32[]{:S(2)}, u32[]{:S(2)}) collective-permute-start(bf16[2,12,128,128]{3,2,1,0:T(8,128)(2,1)S(1)} %prepare.1.refs_2_), channel_id=1, source_target_pairs={{0,64},{64,128},{128,192},{192,0},{1,65},{65,129},{129,193},{193,1... | collective-permute-start | bytes 2359304 | tf_op jit(solution)/shard_map/ppermute | solution.py:29
  35.2 18.8 %all-to-all-start.1 = ((bf16[16,96,128]{2,1,0:T(8,128)(2,1)}), bf16[16,96,128]{2,1,0:T(8,128)(2,1)S(1)}, u32[]{:S(2)}, u32[]{:S(2)}) async-start(bf16[16,96,128]{2,1,0:T(8,128)(2,1)} %bitcast_bitcast_fusion), calls=%async_computation.1 | async-start | bytes 786432 | tf_op jit(solution)/shard_map/all_to_all | solution.py:334
  40.3 20.0 %collective-permute-start.2 = (bf16[2,12,128,128]{3,2,1,0:T(8,128)(2,1)S(1)}, bf16[2,12,128,128]{3,2,1,0:T(8,128)(2,1)S(1)}, u32[]{:S(2)}, u32[]{:S(2)}) collective-permute-start(bf16[2,12,128,128]{3,2,1,0:T(8,128)(2,1)S(1)} %prepare.1.refs_2_), channel_id=1, source_target_pairs={{0,192},{64,0},{128,64},{192,128},{1,193},{65,1},{129,65},{193,129... | collective-permute-start | bytes 2359304 | tf_op jit(solution)/shard_map/ppermute | solution.py:29
  54.0 14.1 %collective-permute-start = (bf16[12,128,128]{2,1,0:T(8,128)(2,1)S(1)}, bf16[12,128,128]{2,1,0:T(8,128)(2,1)S(1)}, u32[]{:S(2)}, u32[]{:S(2)}) collective-permute-start(bf16[12,128,128]{2,1,0:T(8,128)(2,1)S(1)} %bitcast.26), channel_id=1, source_target_pairs={{0,12},{4,0},{8,4},{12,8},{1,13},{5,1},{9,5},{13,9},{2,14},{6,2},{... | collective-permute-start | bytes 1179656 | tf_op jit(solution)/shard_map/ppermute | solution.py:29
  54.5 12.0 %collective-permute-start.1 = (bf16[12,128,128]{2,1,0:T(8,128)(2,1)S(1)}, bf16[12,128,128]{2,1,0:T(8,128)(2,1)S(1)}, u32[]{:S(2)}, u32[]{:S(2)}) collective-permute-start(bf16[12,128,128]{2,1,0:T(8,128)(2,1)S(1)} %bitcast.27), channel_id=1, source_target_pairs={{0,4},{4,8},{8,12},{12,0},{1,5},{5,9},{9,13},{13,1},{2,6},{6,10},{... | collective-permute-start | bytes 1179656 | tf_op jit(solution)/shard_map/ppermute | solution.py:29
  56.1 13.0 %collective-permute-start.4 = (bf16[12,128,128]{2,1,0:T(8,128)(2,1)S(1)}, bf16[12,128,128]{2,1,0:T(8,128)(2,1)S(1)}, u32[]{:S(2)}, u32[]{:S(2)}) collective-permute-start(bf16[12,128,128]{2,1,0:T(8,128)(2,1)S(1)} %slice_bitcast_fusion.1), channel_id=1, source_target_pairs={{0,64},{64,128},{128,192},{192,0},{1,65},{65,129},{129,193},{193,1... | collective-permute-start | bytes 1179656 | tf_op jit(solution)/shard_map/ppermute | solution.py:29
  60.3 11.2 %collective-permute-start.5 = (bf16[12,128,128]{2,1,0:T(8,128)(2,1)S(1)}, bf16[12,128,128]{2,1,0:T(8,128)(2,1)S(1)}, u32[]{:S(2)}, u32[]{:S(2)}) collective-permute-start(bf16[12,128,128]{2,1,0:T(8,128)(2,1)S(1)} %slice_bitcast_fusion), channel_id=1, source_target_pairs={{0,192},{64,0},{128,64},{192,128},{1,193},{65,1},{129,65},{193,129... | collective-permute-start | bytes 1179656 | tf_op jit(solution)/shard_map/ppermute | solution.py:29
  66.4 22.1 %collective-permute-start.7 = (bf16[6,128,128]{2,1,0:T(8,128)(2,1)S(1)}, bf16[6,128,128]{2,1,0:T(8,128)(2,1)S(1)}, u32[]{:S(2)}, u32[]{:S(2)}) collective-permute-start(bf16[6,128,128]{2,1,0:T(8,128)(2,1)S(1)} %slice.18), channel_id=1, source_target_pairs={{0,4},{4,8},{8,12},{12,0},{1,5},{5,9},{9,13},{13,1},{2,6},{6,10},{... | collective-permute-start | bytes 589832 | tf_op jit(solution)/shard_map/ppermute | solution.py:29
  68.1 20.4 %collective-permute-start.8 = (bf16[6,128,128]{2,1,0:T(8,128)(2,1)S(1)}, bf16[6,128,128]{2,1,0:T(8,128)(2,1)S(1)}, u32[]{:S(2)}, u32[]{:S(2)}) collective-permute-start(bf16[6,128,128]{2,1,0:T(8,128)(2,1)S(1)} %slice.19), channel_id=1, source_target_pairs={{0,12},{4,0},{8,4},{12,8},{1,13},{5,1},{9,5},{13,9},{2,14},{6,2},{... | collective-permute-start | bytes 589832 | tf_op jit(solution)/shard_map/ppermute | solution.py:29
  71.5 0.7 copy-start.3
  72.2 0.7 copy-start.5
  86.1 19.2 %collective-permute-start.10 = (bf16[12,144,128]{2,1,0:T(8,128)(2,1)S(1)}, bf16[12,144,128]{2,1,0:T(8,128)(2,1)S(1)}, u32[]{:S(2)}, u32[]{:S(2)}) collective-permute-start(bf16[12,144,128]{2,1,0:T(8,128)(2,1)S(1)} %get-tuple-element.30), channel_id=1, source_target_pairs={{0,12},{4,0},{8,4},{12,8},{1,13},{5,1},{9,5},{13,9},{2,14},{6,2},{... | collective-permute-start | bytes 1327112 | tf_op jit(solution)/shard_map/ppermute | solution.py:29
  87.6 17.7 %collective-permute-start.6 = (bf16[12,144,128]{2,1,0:T(8,128)(2,1)S(1)}, bf16[12,144,128]{2,1,0:T(8,128)(2,1)S(1)}, u32[]{:S(2)}, u32[]{:S(2)}) collective-permute-start(bf16[12,144,128]{2,1,0:T(8,128)(2,1)S(1)} %get-tuple-element.28), channel_id=1, source_target_pairs={{0,4},{4,8},{8,12},{12,0},{1,5},{5,9},{9,13},{13,1},{2,6},{6,10},{... | collective-permute-start | bytes 1327112 | tf_op jit(solution)/shard_map/ppermute | solution.py:29
  96.8 12.6 %collective-permute-start.9 = (bf16[12,144,128]{2,1,0:T(8,128)(2,1)S(1)}, bf16[12,144,128]{2,1,0:T(8,128)(2,1)S(1)}, u32[]{:S(2)}, u32[]{:S(2)}) collective-permute-start(bf16[12,144,128]{2,1,0:T(8,128)(2,1)S(1)} %get-tuple-element.29), channel_id=1, source_target_pairs={{0,8},{4,12},{8,0},{12,4},{1,9},{5,13},{9,1},{13,5},{2,10},{6,14},... | collective-permute-start | bytes 1327112 | tf_op jit(solution)/shard_map/ppermute | solution.py:29
  105.2 18.2 %copy-start.4 = (s32[48]{0:T(128)S(1)}, s32[48]{0:T(128)}, u32[]{:S(2)}) copy-start(s32[48]{0:T(128)} %compare_select_fusion.4.spots) | copy-start | bytes 580
  110.6 47.5 %all-to-all-start.2 = ((bf16[16,96,128]{2,1,0:T(8,128)(2,1)}), bf16[16,96,128]{2,1,0:T(8,128)(2,1)S(1)}, u32[]{:S(2)}, u32[]{:S(2)}) async-start(bf16[16,96,128]{2,1,0:T(8,128)(2,1)} %bitcast.4), calls=%async_computation.2 | async-start | bytes 786432 | tf_op jit(solution)/shard_map/all_to_all | solution.py:334
  116.5 5.3 %collective-permute-start.11 = (f32[48,128]{1,0:T(8,128)S(1)}, f32[48,128]{1,0:T(8,128)S(1)}, u32[]{:S(2)}, u32[]{:S(2)}) collective-permute-start(f32[48,128]{1,0:T(8,128)S(1)} %pad_maximum_fusion.1.e0), channel_id=1, source_target_pairs={{0,12},{4,0},{8,4},{12,8},{1,13},{5,1},{9,5},{13,9},{2,14},{6,2},{... | collective-permute-start | bytes 73736 | tf_op jit(solution)/shard_map/ppermute | solution.py:29
  117.0 5.6 %collective-permute-start.12 = (f32[48,128]{1,0:T(8,128)S(1)}, f32[48,128]{1,0:T(8,128)S(1)}, u32[]{:S(2)}, u32[]{:S(2)}) collective-permute-start(f32[48,128]{1,0:T(8,128)S(1)} %pad_maximum_fusion.1.e0), channel_id=1, source_target_pairs={{0,8},{4,12},{8,0},{12,4},{1,9},{5,13},{9,1},{13,5},{2,10},{6,14},... | collective-permute-start | bytes 73736 | tf_op jit(solution)/shard_map/ppermute | solution.py:29
  119.5 3.9 %collective-permute-start.13 = (f32[48,128]{1,0:T(8,128)S(1)}, f32[48,128]{1,0:T(8,128)S(1)}, u32[]{:S(2)}, u32[]{:S(2)}) collective-permute-start(f32[48,128]{1,0:T(8,128)S(1)} %pad_maximum_fusion.1.e0), channel_id=1, source_target_pairs={{0,4},{4,8},{8,12},{12,0},{1,5},{5,9},{9,13},{13,1},{2,6},{6,10},{... | collective-permute-start | bytes 73736 | tf_op jit(solution)/shard_map/ppermute | solution.py:29
  124.0 22.6 %collective-permute-start.14 = (f32[12,128]{1,0:T(8,128)S(1)}, f32[12,128]{1,0:T(8,128)S(1)}, u32[]{:S(2)}, u32[]{:S(2)}) collective-permute-start(f32[12,128]{1,0:T(8,128)S(1)} %get-tuple-element.36), channel_id=1, source_target_pairs={{0,0},{4,16},{8,32},{12,48},{16,4},{20,20},{24,36},{28,52},{32,8},... | collective-permute-start | bytes 18440 | tf_op jit(solution)/shard_map/ppermute | solution.py:314
  133.6 13.1 %collective-permute-start.15 = (f32[12,128]{1,0:T(8,128)S(1)}, f32[12,128]{1,0:T(8,128)S(1)}, u32[]{:S(2)}, u32[]{:S(2)}) collective-permute-start(f32[12,128]{1,0:T(8,128)S(1)} %get-tuple-element.37), channel_id=1, source_target_pairs={{0,64},{4,80},{8,96},{12,112},{16,68},{20,84},{24,100},{28,116},{3... | collective-permute-start | bytes 18440 | tf_op jit(solution)/shard_map/ppermute | solution.py:314
  136.8 12.4 %collective-permute-start.16 = (f32[12,128]{1,0:T(8,128)S(1)}, f32[12,128]{1,0:T(8,128)S(1)}, u32[]{:S(2)}, u32[]{:S(2)}) collective-permute-start(f32[12,128]{1,0:T(8,128)S(1)} %get-tuple-element.38), channel_id=1, source_target_pairs={{0,128},{4,144},{8,160},{12,176},{16,132},{20,148},{24,164},{28,18... | collective-permute-start | bytes 18440 | tf_op jit(solution)/shard_map/ppermute | solution.py:314
  146.6 10.9 %collective-permute-start.17 = (f32[12,128]{1,0:T(8,128)S(1)}, f32[12,128]{1,0:T(8,128)S(1)}, u32[]{:S(2)}, u32[]{:S(2)}) collective-permute-start(f32[12,128]{1,0:T(8,128)S(1)} %get-tuple-element.39), channel_id=1, source_target_pairs={{0,192},{4,208},{8,224},{12,240},{16,196},{20,212},{24,228},{28,24... | collective-permute-start | bytes 18440 | tf_op jit(solution)/shard_map/ppermute | solution.py:314

commit v6 on v5

--- a/solution.py
+++ b/solution.py
@@ -51,7 +51,7 @@
     return pl.pallas_call(
         spread_kernel,
         out_shape=jax.ShapeDtypeStruct((16, 2, 96, HD), jnp.bfloat16),
-        in_specs=[pl.BlockSpec(memory_space=pl.ANY)] * 2,
+        in_specs=[pl.BlockSpec(memory_space=pltpu.HBM)] * 2,
         out_specs=VMEM,
         scratch_shapes=[pltpu.SemaphoreType.DMA((2, 16))],
         compiler_params=SPACE,
@@ -125,8 +125,7 @@
 
     def listed(t, j):
         row = rows[t]
-        word = lists[row * (KEYS // CHUNK) + j]
-        return [(word >> (8 * u)) & 255 for u in range(CHUNK)]
+        return [lists[row, j * CHUNK + u] for u in range(CHUNK)]
 
     def score(lane, t, j):
         left = sizes[t] - j * CHUNK
@@ -267,8 +266,7 @@
     )(*outs)
 
 
-def settle_kernel(spots, e0, e1, e2, e3, *refs):
-    outs, merged = refs[:RING], refs[RING]
+def settle_kernel(e0, e1, e2, e3, out):
     parts = (e0, e1, e2, e3)
     for block in range(RING):
         part = [
@@ -276,42 +274,48 @@
         ]
         top = jnp.maximum(jnp.maximum(part[0], part[1]), jnp.maximum(part[2], part[3]))
         total = sum(jnp.exp(p - top) for p in part)
-        merged[block * OWN : (block + 1) * OWN] = top + jnp.log(total)
-    merged[KEYS : KEYS + 8] = jnp.zeros((8, BLK), jnp.float32)
+        out[block * OWN : (block + 1) * OWN] = top + jnp.log(total)
+
+
+def settle(parts):
+    return pl.pallas_call(
+        settle_kernel,
+        out_shape=jax.ShapeDtypeStruct((KEYS, BLK), jnp.float32),
+        in_specs=[VMEM] * RING,
+        out_specs=VMEM,
+        compiler_params=SPACE,
+        name="settle",
+    )(*parts)
+
+
+def choose_kernel(spots, *refs):
+    logs, outs, every = refs[:RING], refs[RING : 2 * RING], refs[2 * RING]
+    for away, log in enumerate(logs):
+        every[away * KEYS : (away + 1) * KEYS] = log[...]
     for away, out in enumerate(outs):
         for slot in range(OWN):
-            out[slot : slot + 1] = merged[pl.ds(spots[away * OWN + slot], 1)]
-
-
-def settle(spots, parts):
-    return pl.pallas_call(
-        settle_kernel,
+            out[slot : slot + 1] = every[pl.ds(spots[away * OWN + slot], 1)]
+
+
+def choose(spots, logs):
+    return pl.pallas_call(
+        choose_kernel,
         out_shape=(jax.ShapeDtypeStruct((OWN, BLK), jnp.float32),) * RING,
         in_specs=[SMEM] + [VMEM] * RING,
         out_specs=(VMEM,) * RING,
-        scratch_shapes=[pltpu.VMEM((KEYS + 8, BLK), jnp.float32)],
-        compiler_params=SPACE,
-        name="settle",
-    )(spots, *parts)
-
-
-def slot_spots(assign, xi, yi):
+        scratch_shapes=[pltpu.VMEM((RING * KEYS, BLK), jnp.float32)],
+        compiler_params=SPACE,
+        name="choose",
+    )(spots, *logs)
+
+
+def slot_spots(assign, xi, yi, zi):
     away = jnp.arange(RING * OWN, dtype=jnp.int32) // OWN
-    slots = ((xi + away) % RING * RING + yi) * OWN + jnp.arange(RING * OWN, dtype=jnp.int32) % OWN
+    slots = (xi * RING + (zi + away) % RING) * OWN + jnp.arange(RING * OWN, dtype=jnp.int32) % OWN
     match = slots[:, None] == jnp.arange(assign.shape[0], dtype=jnp.int32)[None, :]
     tiles = jnp.sum(jnp.where(match, assign[None, :], 0), axis=1)
-    spots = (tiles % OWN // 3 - yi) % RING * OWN + tiles % KEYS // OWN * 3 + tiles % 3
-    return jnp.where(tiles // KEYS == xi, spots, KEYS)
-
-
-def deliver(array, away):
-    pairs = []
-    for x in range(RING):
-        for zh in range(RING):
-            for y in range(RING):
-                source = (x * RING + zh) * RING + y
-                pairs.append((source, ((x + away) % RING * RING + y) * RING + zh))
-    return lax.ppermute(array, ("x", "zh", "y"), pairs)
+    spots = (tiles // KEYS - xi) % RING * KEYS + (tiles % OWN // 3 - yi) % RING * OWN
+    return spots + tiles % KEYS // OWN * 3 + tiles % 3
 
 
 def key_lists(kv_tiles, tile_count, xi, yi):
@@ -323,10 +327,8 @@
     rank = jnp.dot(
         here.astype(jnp.bfloat16), before.astype(jnp.bfloat16), preferred_element_type=jnp.float32
     ).astype(jnp.int32)
-    step = jnp.arange(KEYS // CHUNK, dtype=jnp.int32)[None, :, None]
-    at = here[:, None, :] & (rank[:, None, :] // CHUNK == step)
-    word = place << (8 * (rank % CHUNK))
-    lists = jnp.sum(jnp.where(at, word[:, None, :], 0), axis=2).reshape(-1)
+    at = here[:, None, :] & (rank[:, None, :] == jnp.arange(KEYS, dtype=jnp.int32)[None, :, None])
+    lists = jnp.sum(jnp.where(at, place[:, None, :], 0), axis=2)
     return lists, jnp.sum(here.astype(jnp.int32), axis=1)
 
 
@@ -335,9 +337,9 @@
 
 
 def on_device(queries, keys, values, kv_tiles, tile_count, assign):
-    xi, yi = lax.axis_index("x"), lax.axis_index("y")
+    xi, yi, zi = lax.axis_index("x"), lax.axis_index("y"), lax.axis_index("zh")
     lists, counts = key_lists(kv_tiles, tile_count, xi, yi)
-    spots = slot_spots(assign, xi, yi)
+    spots = slot_spots(assign, xi, yi, zi)
     by_head = jnp.transpose(queries.reshape(96, 16, HD), (1, 0, 2))
     got = exchange(spread(keys, values))
     got, lists, counts, spots, by_head = lax.optimization_barrier(
@@ -348,18 +350,23 @@
     q0 = exchange(by_head).reshape(OWN, BLK, HD)
     k2, v2 = shift(kv3[0], "x", 1), shift(kv1[1], "x", -1)
     q1, q3 = shift(q0, "y", -1), shift(q0, "y", 1)
-    half = OWN // 2
-    q2 = jnp.concatenate([shift(q3[:half], "y", 1), shift(q1[half:], "y", -1)])
-    all_keys, all_values, o1, o3, e1, e3 = attend(
-        (1, 3), lists, counts, (q1, q3), (kv0, kv1, kv3, k2, v2), first_call=True
-    )
-    o2, e2 = attend((2,), lists, counts, (q2,), (all_keys, all_values))
+    q2 = shift(q0, "y", -2)
+    all_keys, all_values, o2, e2 = attend(
+        (2,), lists, counts, (q2,), (kv0, kv1, kv3, k2, v2), first_call=True
+    )
+    o1, o3, e1, e3 = attend((1, 3), lists, counts, (q1, q3), (all_keys, all_values))
+    q0, o1 = lax.optimization_barrier((q0, o1))
     o0, e0 = attend((0,), lists, counts, (q0,), (all_keys, all_values))
-    picked = settle(spots, around(jnp.concatenate([e0, e1, e2, e3]), "y"))
+    parts = around(jnp.concatenate([e0, e1, e2, e3]), "y")
+    *parts, o0 = lax.optimization_barrier((*parts, o0))
     blended = combine((o0, shift(o1, "y", 1), shift(o2, "y", 2), shift(o3, "y", -1)))
     back = exchange(blended.reshape(16, 96, HD))
     attended = jnp.transpose(back, (1, 0, 2)).reshape(96, 16 * HD)
-    slot_lse = sum(deliver(array, away) for away, array in enumerate(picked))
+    picked = choose(spots, around(settle(parts), "x"))
+    slot_lse = sum(
+        jnp.where((zi - yi) % RING == away, shift(array, "zh", away), 0.0)
+        for away, array in enumerate(picked)
+    )
     return attended, slot_lse.reshape(1, OWN * BLK)
 
 

time: 160 us -> 152 us (0.950)
  starting transfers between devices: 63.5 us -> 58.6 us
  local copies, waits for them, and re-layouts: 6.58 us -> 4.39 us
    ppermute x4 -> x0, starting transfers between devices: 22.6 us -> none  [deliver(): return lax.ppermute(array, ('x', 'zh', 'y'), pairs)]
    ppermute x14 -> x20, starting transfers between devices: 21.2 us -> 39 us  [shift(): lax.ppermute(array, axis, [(i, (i + by) % RING) for i in range(RING)])]
    ppermute x4 -> x0, waiting for transfers between devices: 10.9 us -> none  [deliver(): return lax.ppermute(array, ('x', 'zh', 'y'), pairs)]
    ppermute x14 -> x20, waiting for transfers between devices: 14.2 us -> 24.1 us  [shift(): lax.ppermute(array, axis, [(i, (i + by) % RING) for i in range(RING)])]
    unnamed x19 -> x13, local copies, waits for them, and re-layouts: 4.03 us -> 2.66 us
  transfers between devices with their start and end apart: 21 -> 23, of which waited for: 11 -> 12; matrix products, arithmetic and copies ran while one was open for 3% -> 3% of each run, Pallas kernels for 18% -> 11%
where the time goes in v6:
time: 152 us; the launch traced here: 151 us
  starting transfers between devices  58.6 us (39%)
  waiting for transfers between devices  52.9 us (35%)
  Pallas kernels  31.6 us (21%)
  local copies, waits for them, and re-layouts  4.39 us (3%)
  other arithmetic  2.7 us (2%)
    ppermute x20, starting transfers between devices, shift(): lax.ppermute(array, axis, [(i, (i + by) % RING) for i in range(RING)])  39 us
    all_to_all x3, waiting for transfers between devices, exchange(): return lax.all_to_all(array, GROUP, split_axis=0, concat_axis=0, tiled=True)  28.8 us
    pallas_call x3, Pallas kernels, attend(): pl.pallas_call(functools.partial(attend_kernel, blocks, first_call), out_...  28.2 us
    ppermute x20, waiting for transfers between devices, shift(): lax.ppermute(array, axis, [(i, (i + by) % RING) for i in range(RING)])  24.1 us
    all_to_all x3, starting transfers between devices, exchange(): return lax.all_to_all(array, GROUP, split_axis=0, concat_axis=0, tiled=True)  19.6 us
  transfers between devices with their start and end apart: 23, of which 12 were waited for; matrix products, arithmetic and copies ran while one was open for 3% of the time, Pallas kernels for 11%

profile of v6, /device:TPU:16, one launch (start us, length us, event | category | flops | bytes accessed | tf_op | source)
XLA Modules:
  0.0 151.2 jit_solution(16292721572286708673)
XLA Ops:
  0.7 1.0 copy-done.1
  1.7 1.0 copy-done.2
  2.7 1.5 spread.1
  4.2 8.6 %all-to-all-start = ((bf16[16,2,96,128]{3,2,1,0:T(8,128)(2,1)}), bf16[16,2,96,128]{3,2,1,0:T(8,128)(2,1)S(1)}, u32[]{:S(2)}, u32[]{:S(2)}) async-start(bf16[16,2,96,128]{3,2,1,0:T(8,128)(2,1)} %spread.1), calls=%async_computation | async-start | bytes 1572864 | tf_op jit(solution)/shard_map/all_to_all | solution.py:336
  14.1 1.5 %select_reduce_fusion.lists = s32[48,48]{1,0:T(8,128)} fusion(s32[48,96]{1,0:T(8,128)S(1)} %get-tuple-element.56, s32[48,96]{1,0:T(8,128)S(1)} %convolution_convert_fusion, pred[48,96]{1,0:T(8,128)(4,1)S(1)} %get-tuple-element.55), kind=kLoop, calls=%fused_computation | loop fusion | flops 882432 | bytes 50688 | tf_op jit(solution)/shard_map/reduce_sum | solution.py:331
  16.5 16.9 %all-to-all-done.got_ref = bf16[16,2,96,128]{3,2,1,0:T(8,128)(2,1)S(1)} async-done(((bf16[16,2,96,128]{3,2,1,0:T(8,128)(2,1)}), bf16[16,2,96,128]{3,2,1,0:T(8,128)(2,1)S(1)}, u32[]{:S(2)}, u32[]{:S(2)}) %all-to-all-start) | async-done | bytes 786464 | tf_op jit(solution)/shard_map/all_to_all | solution.py:336
  33.6 1.6 %collective-permute-start.4 = (bf16[2,12,128,128]{3,2,1,0:T(8,128)(2,1)S(1)}, bf16[2,12,128,128]{3,2,1,0:T(8,128)(2,1)S(1)}, u32[]{:S(2)}, u32[]{:S(2)}) collective-permute-start(bf16[2,12,128,128]{3,2,1,0:T(8,128)(2,1)S(1)} %prepare.1.refs_1_), channel_id=1, source_target_pairs={{0,64},{64,128},{128,192},{192,0},{1,65},{65,129},{129,193},{193,1... | collective-permute-start | bytes 2359304 | tf_op jit(solution)/shard_map/ppermute | solution.py:29
  35.2 5.1 %all-to-all-start.1 = ((bf16[16,96,128]{2,1,0:T(8,128)(2,1)}), bf16[16,96,128]{2,1,0:T(8,128)(2,1)S(1)}, u32[]{:S(2)}, u32[]{:S(2)}) async-start(bf16[16,96,128]{2,1,0:T(8,128)(2,1)} %bitcast_bitcast_fusion), calls=%async_computation.1 | async-start | bytes 786432 | tf_op jit(solution)/shard_map/all_to_all | solution.py:336
  40.3 1.8 %collective-permute-start.3 = (bf16[2,12,128,128]{3,2,1,0:T(8,128)(2,1)S(1)}, bf16[2,12,128,128]{3,2,1,0:T(8,128)(2,1)S(1)}, u32[]{:S(2)}, u32[]{:S(2)}) collective-permute-start(bf16[2,12,128,128]{3,2,1,0:T(8,128)(2,1)S(1)} %prepare.1.refs_1_), channel_id=1, source_target_pairs={{0,192},{64,0},{128,64},{192,128},{1,193},{65,1},{129,65},{193,129... | collective-permute-start | bytes 2359304 | tf_op jit(solution)/shard_map/ppermute | solution.py:29
  42.2 11.9 %all-to-all-done.1 = bf16[16,96,128]{2,1,0:T(8,128)(2,1)S(1)} async-done(((bf16[16,96,128]{2,1,0:T(8,128)(2,1)}), bf16[16,96,128]{2,1,0:T(8,128)(2,1)S(1)}, u32[]{:S(2)}, u32[]{:S(2)}) %all-to-all-start.1) | async-done | bytes 393248 | tf_op jit(solution)/shard_map/all_to_all | solution.py:336
  54.4 1.6 %collective-permute-start.5 = (bf16[12,128,128]{2,1,0:T(8,128)(2,1)S(1)}, bf16[12,128,128]{2,1,0:T(8,128)(2,1)S(1)}, u32[]{:S(2)}, u32[]{:S(2)}) collective-permute-start(bf16[12,128,128]{2,1,0:T(8,128)(2,1)S(1)} %slice_bitcast_fusion.1), channel_id=1, source_target_pairs={{0,64},{64,128},{128,192},{192,0},{1,65},{65,129},{129,193},{193,1... | collective-permute-start | bytes 1179656 | tf_op jit(solution)/shard_map/ppermute | solution.py:29
  56.0 4.3 %collective-permute-done.3.refs_2_ = bf16[2,12,128,128]{3,2,1,0:T(8,128)(2,1)S(1)} collective-permute-done((bf16[2,12,128,128]{3,2,1,0:T(8,128)(2,1)S(1)}, bf16[2,12,128,128]{3,2,1,0:T(8,128)(2,1)S(1)}, u32[]{:S(2)}, u32[]{:S(2)}) %collective-permute-start.3) | collective-permute-done | bytes 786464 | tf_op jit(solution)/shard_map/ppermute | solution.py:29
  60.3 3.0 %collective-permute-start.6 = (bf16[12,128,128]{2,1,0:T(8,128)(2,1)S(1)}, bf16[12,128,128]{2,1,0:T(8,128)(2,1)S(1)}, u32[]{:S(2)}, u32[]{:S(2)}) collective-permute-start(bf16[12,128,128]{2,1,0:T(8,128)(2,1)S(1)} %slice_bitcast_fusion), channel_id=1, source_target_pairs={{0,192},{64,0},{128,64},{192,128},{1,193},{65,1},{129,65},{193,129... | collective-permute-start | bytes 1179656 | tf_op jit(solution)/shard_map/ppermute | solution.py:29
  63.8 1.6 %collective-permute-start.1 = (bf16[12,128,128]{2,1,0:T(8,128)(2,1)S(1)}, bf16[12,128,128]{2,1,0:T(8,128)(2,1)S(1)}, u32[]{:S(2)}, u32[]{:S(2)}) collective-permute-start(bf16[12,128,128]{2,1,0:T(8,128)(2,1)S(1)} %bitcast.28), channel_id=1, source_target_pairs={{0,4},{4,8},{8,12},{12,0},{1,5},{5,9},{9,13},{13,1},{2,6},{6,10},{... | collective-permute-start | bytes 1179656 | tf_op jit(solution)/shard_map/ppermute | solution.py:29
  65.4 1.9 %collective-permute-done.2.refs_0_ = bf16[12,128,128]{2,1,0:T(8,128)(2,1)S(1)} collective-permute-done((bf16[12,128,128]{2,1,0:T(8,128)(2,1)S(1)}, bf16[12,128,128]{2,1,0:T(8,128)(2,1)S(1)}, u32[]{:S(2)}, u32[]{:S(2)}) %collective-permute-start.2) | collective-permute-done | bytes 393248 | tf_op jit(solution)/shard_map/ppermute | solution.py:29
  67.6 3.9 %collective-permute-done.6.refs_5_ = bf16[12,128,128]{2,1,0:T(8,128)(2,1)S(1)} collective-permute-done((bf16[12,128,128]{2,1,0:T(8,128)(2,1)S(1)}, bf16[12,128,128]{2,1,0:T(8,128)(2,1)S(1)}, u32[]{:S(2)}, u32[]{:S(2)}) %collective-permute-start.6) | collective-permute-done | bytes 393248 | tf_op jit(solution)/shard_map/ppermute | solution.py:29
  71.5 8.1 %attend.3 = (bf16[48,128,128]{2,1,0:T(8,128)(2,1)S(1)}, bf16[48,128,128]{2,1,0:T(8,128)(2,1)S(1)}, bf16[12,144,128]{2,1,0:T(8,128)(2,1)S(1)}, f32[12,128]{1,0:T(8,128)S(1)}) custom-call(s32[48,48]{1,0:T(8,128)S(1)} %copy-done.3, s32[48]{0:T(128)S(1)} %get-tuple-element.29.counts, bf16[12,128,128]{2,1,0:T(8,128)(2,1)S(1)} %collective-permute-done.2.refs_0_, ...), custom_call_target="tpu_custom_call" | custom-call | flops 1509949440 | bytes 5242880 | tf_op jit(solution)/shard_map/attend/pallas_call | solution.py:219
  79.7 12.5 %attend.4 = (bf16[12,144,128]{2,1,0:T(8,128)(2,1)S(1)}, bf16[12,144,128]{2,1,0:T(8,128)(2,1)S(1)}, f32[12,128]{1,0:T(8,128)S(1)}, f32[12,128]{1,0:T(8,128)S(1)}) custom-call(s32[48,48]{1,0:T(8,128)S(1)} %copy-done.3, s32[48]{0:T(128)S(1)} %get-tuple-element.29.counts, bf16[12,128,128]{2,1,0:T(8,128)(2,1)S(1)} %collective-permute-done.refs_0_, ...), custom_call_target="tpu_custom_call" | custom-call | flops 3019898880 | bytes 5242880 | tf_op jit(solution)/shard_map/attend/pallas_call | solution.py:219
  92.2 1.8 %collective-permute-start.10 = (bf16[12,144,128]{2,1,0:T(8,128)(2,1)S(1)}, bf16[12,144,128]{2,1,0:T(8,128)(2,1)S(1)}, u32[]{:S(2)}, u32[]{:S(2)}) collective-permute-start(bf16[12,144,128]{2,1,0:T(8,128)(2,1)S(1)} %get-tuple-element.42), channel_id=1, source_target_pairs={{0,4},{4,8},{8,12},{12,0},{1,5},{5,9},{9,13},{13,1},{2,6},{6,10},{... | collective-permute-start | bytes 1327112 | tf_op jit(solution)/shard_map/ppermute | solution.py:29
  94.3 3.0 %collective-permute-start.11 = (bf16[12,144,128]{2,1,0:T(8,128)(2,1)S(1)}, bf16[12,144,128]{2,1,0:T(8,128)(2,1)S(1)}, u32[]{:S(2)}, u32[]{:S(2)}) collective-permute-start(bf16[12,144,128]{2,1,0:T(8,128)(2,1)S(1)} %get-tuple-element.43), channel_id=1, source_target_pairs={{0,8},{4,12},{8,0},{12,4},{1,9},{5,13},{9,1},{13,5},{2,10},{6,14},... | collective-permute-start | bytes 1327112 | tf_op jit(solution)/shard_map/ppermute | solution.py:29
  97.3 7.6 %attend.5 = (bf16[12,144,128]{2,1,0:T(8,128)(2,1)S(1)}, f32[12,128]{1,0:T(8,128)S(1)}) custom-call(s32[48,48]{1,0:T(8,128)S(1)} %copy-done.3, s32[48]{0:T(128)S(1)} %get-tuple-element.29.counts, bf16[12,128,128]{2,1,0:T(8,128)(2,1)S(1)} %bitcast.29, bf16[48,128,128]{2,1,0:T(8,128)(2,1)S(1)} %get-tuple-element.32.refs_2_.refs_1_, ...), custom_call_target="tpu_custom_call" | custom-call | flops 1509949440 | bytes 5242880 | tf_op jit(solution)/shard_map/attend/pallas_call | solution.py:219
  105.6 2.9 %collective-permute-start.8 = (f32[48,128]{1,0:T(8,128)S(1)}, f32[48,128]{1,0:T(8,128)S(1)}, u32[]{:S(2)}, u32[]{:S(2)}) collective-permute-start(f32[48,128]{1,0:T(8,128)S(1)} %pad_maximum_fusion.e0), channel_id=1, source_target_pairs={{0,8},{4,12},{8,0},{12,4},{1,9},{5,13},{9,1},{13,5},{2,10},{6,14},... | collective-permute-start | bytes 73736 | tf_op jit(solution)/shard_map/ppermute | solution.py:29
  108.5 6.3 %collective-permute-done.7.e1 = f32[48,128]{1,0:T(8,128)S(1)} collective-permute-done((f32[48,128]{1,0:T(8,128)S(1)}, f32[48,128]{1,0:T(8,128)S(1)}, u32[]{:S(2)}, u32[]{:S(2)}) %collective-permute-start.7) | collective-permute-done | bytes 24608 | tf_op jit(solution)/shard_map/ppermute | solution.py:29
  114.8 3.0 %collective-permute-start.9 = (f32[48,128]{1,0:T(8,128)S(1)}, f32[48,128]{1,0:T(8,128)S(1)}, u32[]{:S(2)}, u32[]{:S(2)}) collective-permute-start(f32[48,128]{1,0:T(8,128)S(1)} %pad_maximum_fusion.e0), channel_id=1, source_target_pairs={{0,4},{4,8},{8,12},{12,0},{1,5},{5,9},{9,13},{13,1},{2,6},{6,10},{... | collective-permute-start | bytes 73736 | tf_op jit(solution)/shard_map/ppermute | solution.py:29
  117.9 1.5 %collective-permute-done.9.e3 = f32[48,128]{1,0:T(8,128)S(1)} collective-permute-done((f32[48,128]{1,0:T(8,128)S(1)}, f32[48,128]{1,0:T(8,128)S(1)}, u32[]{:S(2)}, u32[]{:S(2)}) %collective-permute-start.9) | collective-permute-done | bytes 24608 | tf_op jit(solution)/shard_map/ppermute | solution.py:29
  119.4 1.2 combine.1
  120.6 5.8 %all-to-all-start.2 = ((bf16[16,96,128]{2,1,0:T(8,128)(2,1)}), bf16[16,96,128]{2,1,0:T(8,128)(2,1)S(1)}, u32[]{:S(2)}, u32[]{:S(2)}) async-start(bf16[16,96,128]{2,1,0:T(8,128)(2,1)} %bitcast.4), calls=%async_computation.2 | async-start | bytes 786432 | tf_op jit(solution)/shard_map/all_to_all | solution.py:336
  126.5 5.9 %collective-permute-start.13 = (f32[48,128]{1,0:T(8,128)S(1)}, f32[48,128]{1,0:T(8,128)S(1)}, u32[]{:S(2)}, u32[]{:S(2)}) collective-permute-start(f32[48,128]{1,0:T(8,128)S(1)} %settle.1.refs_0_), channel_id=1, source_target_pairs={{0,192},{64,0},{128,64},{192,128},{1,193},{65,1},{129,65},{193,129... | collective-permute-start | bytes 73736 | tf_op jit(solution)/shard_map/ppermute | solution.py:29
  133.9 3.8 %collective-permute-done.14.refs_2_ = f32[48,128]{1,0:T(8,128)S(1)} collective-permute-done((f32[48,128]{1,0:T(8,128)S(1)}, f32[48,128]{1,0:T(8,128)S(1)}, u32[]{:S(2)}, u32[]{:S(2)}) %collective-permute-start.14) | collective-permute-done | bytes 24608 | tf_op jit(solution)/shard_map/ppermute | solution.py:29
  138.3 2.9 %collective-permute-start.17 = (f32[12,128]{1,0:T(8,128)S(1)}, f32[12,128]{1,0:T(8,128)S(1)}, u32[]{:S(2)}, u32[]{:S(2)}) collective-permute-start(f32[12,128]{1,0:T(8,128)S(1)} %get-tuple-element.51), channel_id=1, source_target_pairs={{0,16},{16,32},{32,48},{48,0},{1,17},{17,33},{33,49},{49,1},{2,18}... | collective-permute-start | bytes 18440 | tf_op jit(solution)/shard_map/ppermute | solution.py:29
  141.2 3.6 %collective-permute-start.18 = (f32[12,128]{1,0:T(8,128)S(1)}, f32[12,128]{1,0:T(8,128)S(1)}, u32[]{:S(2)}, u32[]{:S(2)}) collective-permute-start(f32[12,128]{1,0:T(8,128)S(1)} %get-tuple-element.52), channel_id=1, source_target_pairs={{0,32},{16,48},{32,0},{48,16},{1,33},{17,49},{33,1},{49,17},{2,34}... | collective-permute-start | bytes 18440 | tf_op jit(solution)/shard_map/ppermute | solution.py:29
  144.8 3.6 %collective-permute-start.19 = (f32[12,128]{1,0:T(8,128)S(1)}, f32[12,128]{1,0:T(8,128)S(1)}, u32[]{:S(2)}, u32[]{:S(2)}) collective-permute-start(f32[12,128]{1,0:T(8,128)S(1)} %get-tuple-element.53), channel_id=1, source_target_pairs={{0,48},{16,0},{32,16},{48,32},{1,49},{17,1},{33,17},{49,33},{2,50}... | collective-permute-start | bytes 18440 | tf_op jit(solution)/shard_map/ppermute | solution.py:29
  (48 shorter events, 9.6 us)
Async XLA Ops:
  0.6 15.1 %copy-start = (bf16[96,2048]{1,0:T(8,128)(2,1)S(1)}, bf16[96,2048]{1,0:T(8,128)(2,1)}, u32[]{:S(2)}) copy-start(bf16[96,2048]{1,0:T(8,128)(2,1)} %param.6) | copy-start | bytes 1179652
  0.6 1.0 copy-start.1
  1.7 1.0 copy-start.2
  4.1 8.6 %copy-start.5 = (s32[192]{0:T(256)S(1)}, s32[192]{0:T(256)}, u32[]{:S(2)}) copy-start(s32[192]{0:T(256)} %param.10) | copy-start | bytes 2308
  4.2 8.7 %copy-start.4 = (s32[192]{0:T(256)S(1)}, s32[192]{0:T(256)}, u32[]{:S(2)}) copy-start(s32[192]{0:T(256)} %param.11) | copy-start | bytes 2308
  4.2 29.3 %all-to-all-start = ((bf16[16,2,96,128]{3,2,1,0:T(8,128)(2,1)}), bf16[16,2,96,128]{3,2,1,0:T(8,128)(2,1)S(1)}, u32[]{:S(2)}, u32[]{:S(2)}) async-start(bf16[16,2,96,128]{3,2,1,0:T(8,128)(2,1)} %spread.1), calls=%async_computation | async-start | bytes 1572864 | tf_op jit(solution)/shard_map/all_to_all | solution.py:336
  33.6 37.9 %copy-start.3 = (s32[48,48]{1,0:T(8,128)S(1)}, s32[48,48]{1,0:T(8,128)}, u32[]{:S(2)}) copy-start(s32[48,48]{1,0:T(8,128)} %select_reduce_fusion.lists) | copy-start | bytes 27652
  33.6 20.7 %collective-permute-start.4 = (bf16[2,12,128,128]{3,2,1,0:T(8,128)(2,1)S(1)}, bf16[2,12,128,128]{3,2,1,0:T(8,128)(2,1)S(1)}, u32[]{:S(2)}, u32[]{:S(2)}) collective-permute-start(bf16[2,12,128,128]{3,2,1,0:T(8,128)(2,1)S(1)} %prepare.1.refs_1_), channel_id=1, source_target_pairs={{0,64},{64,128},{128,192},{192,0},{1,65},{65,129},{129,193},{193,1... | collective-permute-start | bytes 2359304 | tf_op jit(solution)/shard_map/ppermute | solution.py:29
  35.2 18.8 %all-to-all-start.1 = ((bf16[16,96,128]{2,1,0:T(8,128)(2,1)}), bf16[16,96,128]{2,1,0:T(8,128)(2,1)S(1)}, u32[]{:S(2)}, u32[]{:S(2)}) async-start(bf16[16,96,128]{2,1,0:T(8,128)(2,1)} %bitcast_bitcast_fusion), calls=%async_computation.1 | async-start | bytes 786432 | tf_op jit(solution)/shard_map/all_to_all | solution.py:336
  40.3 20.0 %collective-permute-start.3 = (bf16[2,12,128,128]{3,2,1,0:T(8,128)(2,1)S(1)}, bf16[2,12,128,128]{3,2,1,0:T(8,128)(2,1)S(1)}, u32[]{:S(2)}, u32[]{:S(2)}) collective-permute-start(bf16[2,12,128,128]{3,2,1,0:T(8,128)(2,1)S(1)} %prepare.1.refs_1_), channel_id=1, source_target_pairs={{0,192},{64,0},{128,64},{192,128},{1,193},{65,1},{129,65},{193,129... | collective-permute-start | bytes 2359304 | tf_op jit(solution)/shard_map/ppermute | solution.py:29
  54.0 13.3 %collective-permute-start.2 = (bf16[12,128,128]{2,1,0:T(8,128)(2,1)S(1)}, bf16[12,128,128]{2,1,0:T(8,128)(2,1)S(1)}, u32[]{:S(2)}, u32[]{:S(2)}) collective-permute-start(bf16[12,128,128]{2,1,0:T(8,128)(2,1)S(1)} %bitcast.26), channel_id=1, source_target_pairs={{0,8},{4,12},{8,0},{12,4},{1,9},{5,13},{9,1},{13,5},{2,10},{6,14},... | collective-permute-start | bytes 1179656 | tf_op jit(solution)/shard_map/ppermute | solution.py:29
  54.4 13.3 %collective-permute-start.5 = (bf16[12,128,128]{2,1,0:T(8,128)(2,1)S(1)}, bf16[12,128,128]{2,1,0:T(8,128)(2,1)S(1)}, u32[]{:S(2)}, u32[]{:S(2)}) collective-permute-start(bf16[12,128,128]{2,1,0:T(8,128)(2,1)S(1)} %slice_bitcast_fusion.1), channel_id=1, source_target_pairs={{0,64},{64,128},{128,192},{192,0},{1,65},{65,129},{129,193},{193,1... | collective-permute-start | bytes 1179656 | tf_op jit(solution)/shard_map/ppermute | solution.py:29
  60.3 11.2 %collective-permute-start.6 = (bf16[12,128,128]{2,1,0:T(8,128)(2,1)S(1)}, bf16[12,128,128]{2,1,0:T(8,128)(2,1)S(1)}, u32[]{:S(2)}, u32[]{:S(2)}) collective-permute-start(bf16[12,128,128]{2,1,0:T(8,128)(2,1)S(1)} %slice_bitcast_fusion), channel_id=1, source_target_pairs={{0,192},{64,0},{128,64},{192,128},{1,193},{65,1},{129,65},{193,129... | collective-permute-start | bytes 1179656 | tf_op jit(solution)/shard_map/ppermute | solution.py:29
  63.4 16.3 %collective-permute-start = (bf16[12,128,128]{2,1,0:T(8,128)(2,1)S(1)}, bf16[12,128,128]{2,1,0:T(8,128)(2,1)S(1)}, u32[]{:S(2)}, u32[]{:S(2)}) collective-permute-start(bf16[12,128,128]{2,1,0:T(8,128)(2,1)S(1)} %bitcast.27), channel_id=1, source_target_pairs={{0,12},{4,0},{8,4},{12,8},{1,13},{5,1},{9,5},{13,9},{2,14},{6,2},{... | collective-permute-start | bytes 1179656 | tf_op jit(solution)/shard_map/ppermute | solution.py:29
  63.8 15.9 %collective-permute-start.1 = (bf16[12,128,128]{2,1,0:T(8,128)(2,1)S(1)}, bf16[12,128,128]{2,1,0:T(8,128)(2,1)S(1)}, u32[]{:S(2)}, u32[]{:S(2)}) collective-permute-start(bf16[12,128,128]{2,1,0:T(8,128)(2,1)S(1)} %bitcast.28), channel_id=1, source_target_pairs={{0,4},{4,8},{8,12},{12,0},{1,5},{5,9},{9,13},{13,1},{2,6},{6,10},{... | collective-permute-start | bytes 1179656 | tf_op jit(solution)/shard_map/ppermute | solution.py:29
  92.2 27.2 %collective-permute-start.10 = (bf16[12,144,128]{2,1,0:T(8,128)(2,1)S(1)}, bf16[12,144,128]{2,1,0:T(8,128)(2,1)S(1)}, u32[]{:S(2)}, u32[]{:S(2)}) collective-permute-start(bf16[12,144,128]{2,1,0:T(8,128)(2,1)S(1)} %get-tuple-element.42), channel_id=1, source_target_pairs={{0,4},{4,8},{8,12},{12,0},{1,5},{5,9},{9,13},{13,1},{2,6},{6,10},{... | collective-permute-start | bytes 1327112 | tf_op jit(solution)/shard_map/ppermute | solution.py:29
  94.0 25.4 %collective-permute-start.12 = (bf16[12,144,128]{2,1,0:T(8,128)(2,1)S(1)}, bf16[12,144,128]{2,1,0:T(8,128)(2,1)S(1)}, u32[]{:S(2)}, u32[]{:S(2)}) collective-permute-start(bf16[12,144,128]{2,1,0:T(8,128)(2,1)S(1)} %get-tuple-element.44), channel_id=1, source_target_pairs={{0,12},{4,0},{8,4},{12,8},{1,13},{5,1},{9,5},{13,9},{2,14},{6,2},{... | collective-permute-start | bytes 1327112 | tf_op jit(solution)/shard_map/ppermute | solution.py:29
  94.3 25.1 %collective-permute-start.11 = (bf16[12,144,128]{2,1,0:T(8,128)(2,1)S(1)}, bf16[12,144,128]{2,1,0:T(8,128)(2,1)S(1)}, u32[]{:S(2)}, u32[]{:S(2)}) collective-permute-start(bf16[12,144,128]{2,1,0:T(8,128)(2,1)S(1)} %get-tuple-element.43), channel_id=1, source_target_pairs={{0,8},{4,12},{8,0},{12,4},{1,9},{5,13},{9,1},{13,5},{2,10},{6,14},... | collective-permute-start | bytes 1327112 | tf_op jit(solution)/shard_map/ppermute | solution.py:29
  104.9 10.0 %collective-permute-start.7 = (f32[48,128]{1,0:T(8,128)S(1)}, f32[48,128]{1,0:T(8,128)S(1)}, u32[]{:S(2)}, u32[]{:S(2)}) collective-permute-start(f32[48,128]{1,0:T(8,128)S(1)} %pad_maximum_fusion.e0), channel_id=1, source_target_pairs={{0,12},{4,0},{8,4},{12,8},{1,13},{5,1},{9,5},{13,9},{2,14},{6,2},{... | collective-permute-start | bytes 73736 | tf_op jit(solution)/shard_map/ppermute | solution.py:29
  105.6 12.2 %collective-permute-start.8 = (f32[48,128]{1,0:T(8,128)S(1)}, f32[48,128]{1,0:T(8,128)S(1)}, u32[]{:S(2)}, u32[]{:S(2)}) collective-permute-start(f32[48,128]{1,0:T(8,128)S(1)} %pad_maximum_fusion.e0), channel_id=1, source_target_pairs={{0,8},{4,12},{8,0},{12,4},{1,9},{5,13},{9,1},{13,5},{2,10},{6,14},... | collective-permute-start | bytes 73736 | tf_op jit(solution)/shard_map/ppermute | solution.py:29
  114.8 4.5 %collective-permute-start.9 = (f32[48,128]{1,0:T(8,128)S(1)}, f32[48,128]{1,0:T(8,128)S(1)}, u32[]{:S(2)}, u32[]{:S(2)}) collective-permute-start(f32[48,128]{1,0:T(8,128)S(1)} %pad_maximum_fusion.e0), channel_id=1, source_target_pairs={{0,4},{4,8},{8,12},{12,0},{1,5},{5,9},{9,13},{13,1},{2,6},{6,10},{... | collective-permute-start | bytes 73736 | tf_op jit(solution)/shard_map/ppermute | solution.py:29
  120.6 29.8 %all-to-all-start.2 = ((bf16[16,96,128]{2,1,0:T(8,128)(2,1)}), bf16[16,96,128]{2,1,0:T(8,128)(2,1)S(1)}, u32[]{:S(2)}, u32[]{:S(2)}) async-start(bf16[16,96,128]{2,1,0:T(8,128)(2,1)} %bitcast.4), calls=%async_computation.2 | async-start | bytes 786432 | tf_op jit(solution)/shard_map/all_to_all | solution.py:336
  126.5 7.4 %collective-permute-start.13 = (f32[48,128]{1,0:T(8,128)S(1)}, f32[48,128]{1,0:T(8,128)S(1)}, u32[]{:S(2)}, u32[]{:S(2)}) collective-permute-start(f32[48,128]{1,0:T(8,128)S(1)} %settle.1.refs_0_), channel_id=1, source_target_pairs={{0,192},{64,0},{128,64},{192,128},{1,193},{65,1},{129,65},{193,129... | collective-permute-start | bytes 73736 | tf_op jit(solution)/shard_map/ppermute | solution.py:29
  132.4 5.3 %collective-permute-start.14 = (f32[48,128]{1,0:T(8,128)S(1)}, f32[48,128]{1,0:T(8,128)S(1)}, u32[]{:S(2)}, u32[]{:S(2)}) collective-permute-start(f32[48,128]{1,0:T(8,128)S(1)} %settle.1.refs_0_), channel_id=1, source_target_pairs={{0,128},{64,192},{128,0},{192,64},{1,129},{65,193},{129,1},{193,65... | collective-permute-start | bytes 73736 | tf_op jit(solution)/shard_map/ppermute | solution.py:29
  132.4 5.3 %collective-permute-start.15 = (f32[48,128]{1,0:T(8,128)S(1)}, f32[48,128]{1,0:T(8,128)S(1)}, u32[]{:S(2)}, u32[]{:S(2)}) collective-permute-start(f32[48,128]{1,0:T(8,128)S(1)} %settle.1.refs_0_), channel_id=1, source_target_pairs={{0,64},{64,128},{128,192},{192,0},{1,65},{65,129},{129,193},{193,1... | collective-permute-start | bytes 73736 | tf_op jit(solution)/shard_map/ppermute | solution.py:29
  138.3 10.1 %collective-permute-start.16 = (f32[12,128]{1,0:T(8,128)S(1)}, f32[12,128]{1,0:T(8,128)S(1)}, u32[]{:S(2)}, u32[]{:S(2)}) collective-permute-start(f32[12,128]{1,0:T(8,128)S(1)} %get-tuple-element.50), channel_id=1, source_target_pairs={{0,0},{16,16},{32,32},{48,48},{1,1},{17,17},{33,33},{49,49},{2,2},... | collective-permute-start | bytes 18440 | tf_op jit(solution)/shard_map/ppermute | solution.py:29
  138.3 10.1 %collective-permute-start.17 = (f32[12,128]{1,0:T(8,128)S(1)}, f32[12,128]{1,0:T(8,128)S(1)}, u32[]{:S(2)}, u32[]{:S(2)}) collective-permute-start(f32[12,128]{1,0:T(8,128)S(1)} %get-tuple-element.51), channel_id=1, source_target_pairs={{0,16},{16,32},{32,48},{48,0},{1,17},{17,33},{33,49},{49,1},{2,18}... | collective-permute-start | bytes 18440 | tf_op jit(solution)/shard_map/ppermute | solution.py:29
  141.2 7.6 %collective-permute-start.18 = (f32[12,128]{1,0:T(8,128)S(1)}, f32[12,128]{1,0:T(8,128)S(1)}, u32[]{:S(2)}, u32[]{:S(2)}) collective-permute-start(f32[12,128]{1,0:T(8,128)S(1)} %get-tuple-element.52), channel_id=1, source_target_pairs={{0,32},{16,48},{32,0},{48,16},{1,33},{17,49},{33,1},{49,17},{2,34}... | collective-permute-start | bytes 18440 | tf_op jit(solution)/shard_map/ppermute | solution.py:29
  144.8 4.9 %collective-permute-start.19 = (f32[12,128]{1,0:T(8,128)S(1)}, f32[12,128]{1,0:T(8,128)S(1)}, u32[]{:S(2)}, u32[]{:S(2)}) collective-permute-start(f32[12,128]{1,0:T(8,128)S(1)} %get-tuple-element.53), channel_id=1, source_target_pairs={{0,48},{16,0},{32,16},{48,32},{1,49},{17,1},{33,17},{49,33},{2,50}... | collective-permute-start | bytes 18440 | tf_op jit(solution)/shard_map/ppermute | solution.py:29

commit v7 on v6

v7 whole, which is shorter than its diff:
```python
import functools

import jax
import jax.numpy as jnp
from jax import lax
from jax.experimental import pallas as pl
from jax.experimental.pallas import tpu as pltpu
from jax.sharding import PartitionSpec as P

HD = 128
BLK = 128
LIST = 96
RING = 4
OWN = 12
KEYS = RING * OWN
NEAR = 3 * OWN
CHUNK = 4
WIDTH = 4
PAD = 16
NEG = -1e30
SCALE = HD**-0.5
LOG2E = 1.4426950408889634
VMEM = pl.BlockSpec(memory_space=pltpu.VMEM)
SMEM = pl.BlockSpec(memory_space=pltpu.SMEM)
SPACE = pltpu.CompilerParams(vmem_limit_bytes=16 * 1024 * 1024)
GROUP = ("zh", "zl", "core")


def shift(array, axis, by):
    return lax.ppermute(array, axis, [(i, (i + by) % RING) for i in range(RING)])


def around(array, axis):
    return [array] + [shift(array, axis, -by) for by in range(1, RING)]


def spread_kernel(keys, values, out, sems):
    copies = [
        pltpu.make_async_copy(
            array.at[:, pl.ds(head * HD, HD)], out.at[head, which], sems.at[which, head]
        )
        for which, array in enumerate((keys, values))
        for head in range(16)
    ]
    for copy in copies:
        copy.start()
    for copy in copies:
        copy.wait()


def spread(keys, values):
    return pl.pallas_call(
        spread_kernel,
        out_shape=jax.ShapeDtypeStruct((16, 2, 96, HD), jnp.bfloat16),
        in_specs=[pl.BlockSpec(memory_space=pltpu.HBM)] * 2,
        out_specs=VMEM,
        scratch_shapes=[pltpu.SemaphoreType.DMA((2, 16))],
        compiler_params=SPACE,
        name="spread",
    )(keys, values)


def prepare_kernel(got_ref, kv_ref):
    for part in range(RING):
        k, v = (
            got_ref[4 * part : 4 * part + 4, which].reshape(3, BLK, HD) for which in range(2)
        )
        kv_ref[0, 3 * part : 3 * part + 3] = k
        for i in range(3):
            kv_ref[1, 3 * part + i] = v[i].T


def prepare(got):
    return pl.pallas_call(
        prepare_kernel,
        out_shape=jax.ShapeDtypeStruct((2, OWN, BLK, HD), jnp.bfloat16),
        in_specs=[VMEM],
        out_specs=VMEM,
        compiler_params=SPACE,
        name="prepare",
    )(got)


def split(log):
    high = log.astype(jnp.bfloat16)
    rest = log - high.astype(jnp.float32)
    middle = rest.astype(jnp.bfloat16)
    return [high, middle, (rest - middle.astype(jnp.float32)).astype(jnp.bfloat16)]


def joined(rows, block):
    parts = [rows[3 * block + i : 3 * block + i + 1] for i in range(3)]
    return parts[0] + parts[1] + parts[2]


def attend_kernel(blocks, mode, last, lists, nears, counts, *refs):
    count = len(blocks)
    tiles = count * OWN
    queries, refs = refs[:count], refs[count:]
    if mode != "far":
        for_near, refs = refs[:3], refs[3:]
    if mode != "near":
        (k2, v2), refs = refs[:2], refs[2:]
    if mode == "far":
        states, refs = refs[: 3 * count], refs[3 * count :]
    if last:
        (e0, e2), refs = refs[:2], refs[2:]
    size = (3 if mode == "near" else 2) * count + last
    outs, refs = refs[:size], refs[size:]
    rows, begins, sizes, qs, ks, vs, m_ref, l_ref, acc_ref = refs[:9]
    s_refs, top_refs = refs[9 : 9 + WIDTH], refs[9 + WIDTH :]
    for b, q in enumerate(queries):
        qs[b * OWN : (b + 1) * OWN] = q[...]
    if mode != "far":
        for b, kv in enumerate(for_near):
            ks[b * OWN : (b + 1) * OWN] = kv[0]
            vs[b * OWN : (b + 1) * OWN] = kv[1]
    if mode != "near":
        at = 0 if mode == "far" else NEAR
        ks[at : at + OWN] = k2[...]
        vs[at : at + OWN] = v2[...]
    m_ref[...] = jnp.full(m_ref.shape, NEG, jnp.float32)
    l_ref[...] = jnp.zeros(l_ref.shape, jnp.float32)
    acc_ref[...] = jnp.zeros(acc_ref.shape, jnp.float32)
    if mode == "far":
        for b in range(count):
            for held, state in zip((m_ref, l_ref, acc_ref), states[3 * b : 3 * b + 3]):
                held[b * OWN : (b + 1) * OWN] = state[...]
    yi = lax.axis_index("y")
    items = jnp.int32(0)
    for b, block in enumerate(blocks):
        owner = lax.rem(yi + block, RING) * 3
        for t in range(OWN):
            row = owner + (t // 3 * OWN + t % 3)
            begin = nears[row] if mode == "far" else jnp.int32(0)
            total = (nears[row] if mode == "near" else counts[row]) - begin
            rows[b * OWN + t] = row
            begins[b * OWN + t] = begin
            sizes[b * OWN + t] = total
            items += jnp.maximum((total + CHUNK - 1) // CHUNK, 1)
    rows[tiles] = 0
    begins[tiles] = 0
    sizes[tiles] = 0

    def advance(t, j):
        more = (j + 1) * CHUNK < sizes[t]
        return jnp.where(more, t, jnp.minimum(t + 1, tiles)), jnp.where(more, j + 1, 0)

    def listed(t, j):
        row = rows[t]
        at = begins[t] + j * CHUNK
        found = [lists[row, at + u] for u in range(CHUNK)]
        if mode == "near":
            return [jnp.minimum(u, NEAR - 1) for u in found]
        return [jnp.maximum(u - NEAR, 0) for u in found] if mode == "far" else found

    def score(lane, t, j):
        left = sizes[t] - j * CHUNK
        tile = listed(t, j)
        s = lax.dot_general(
            jnp.concatenate([ks[u] for u in tile], axis=0),
            qs[jnp.minimum(t, tiles - 1)],
            (((1,), (1,)), ((), ())),
            preferred_element_type=jnp.float32,
        )
        s_refs[lane][...] = s
        top = jnp.full((8, BLK), NEG, jnp.float32)
        for u in range(CHUNK):
            part = jnp.max(s[u * BLK : (u + 1) * BLK].reshape(16, 8, BLK), axis=0)
            top = jnp.maximum(top, jnp.where(u < left, part, NEG))
        top_refs[lane][...] = jnp.max(top, axis=0, keepdims=True)

    def blend(lane, t, j):
        left = sizes[t] - j * CHUNK
        m_old = m_ref[t]
        m_new = jnp.maximum(m_old, top_refs[lane][...])
        m_ref[t] = m_new
        alpha = jnp.exp2((m_old - m_new) * (SCALE * LOG2E))
        base = m_new * (SCALE * LOG2E)
        total = jnp.zeros((8, BLK), jnp.float32)
        weights = []
        for u in range(CHUNK):
            s = s_refs[lane][u * BLK : (u + 1) * BLK] * (SCALE * LOG2E)
            w = jnp.exp2(s - jnp.where(u < left, base, -NEG))
            total = total + jnp.sum(w.reshape(16, 8, BLK), axis=0)
            weights.append(w.astype(jnp.bfloat16))
        vt = jnp.concatenate([vs[tile] for tile in listed(t, j)], axis=1)
        mixed = jnp.dot(vt, jnp.concatenate(weights, axis=0), preferred_element_type=jnp.float32)
        l_ref[t] = l_ref[t] * alpha + total
        acc_ref[t] = acc_ref[t] * alpha + mixed

    def following(t, j):
        group = []
        for _ in range(WIDTH):
            t, j = advance(t, j)
            group += [t, j]
        return tuple(group)

    start = [jnp.int32(0), jnp.int32(0)]
    for _ in range(WIDTH - 1):
        start += advance(*start[-2:])
    for lane in range(WIDTH):
        score(lane, start[2 * lane], start[2 * lane + 1])

    def step(_, now):
        later = following(*now[-2:])
        for lane in range(WIDTH):
            blend(lane, now[2 * lane], now[2 * lane + 1])
            score(lane, later[2 * lane], later[2 * lane + 1])
        return later

    lax.fori_loop(0, (items + WIDTH - 1) // WIDTH, step, tuple(start))

    if mode == "near":
        for b in range(count):
            for held, out in zip((m_ref, l_ref, acc_ref), outs[3 * b : 3 * b + 3]):
                out[...] = held[b * OWN : (b + 1) * OWN]
        return

    def finish(i, _):
        for u in range(4):
            t = i * 4 + u
            logs = {}
            for b, block in enumerate(blocks):
                total = jnp.sum(l_ref[b * OWN + t], axis=0, keepdims=True)
                some = total > 0.0
                safe = jnp.where(some, total, 1.0)
                share = jnp.where(some, 1.0 / safe, 0.0)
                outs[b][t, :HD] = (acc_ref[b * OWN + t] * share).astype(jnp.bfloat16)
                logs[block] = jnp.where(some, m_ref[b * OWN + t] * SCALE + jnp.log(safe), NEG)
                outs[count + b][pl.ds(t, 1)] = logs[block]
            if last:
                logs[0], logs[2] = e0[pl.ds(t, 1)], e2[pl.ds(t, 1)]
                for block in range(RING):
                    outs[2 * count][pl.ds(block * OWN + t, 1)] = logs[block]
            none = [jnp.zeros((1, BLK), jnp.bfloat16)] * 3
            below = [row for b in range(RING) for row in (split(logs[b]) if b in logs else none)]
            below.append(jnp.zeros((PAD - 3 * RING, BLK), jnp.bfloat16))
            for b in range(count):
                outs[b][t, HD:] = jnp.concatenate(below, axis=0)
        return 0

    lax.fori_loop(0, OWN // 4, finish, 0)


def attend(blocks, mode, lists, queries, keys_values, states=(), logs=()):
    last = bool(logs)
    count = len(blocks)
    slots = count * OWN + 1
    keys = {"near": NEAR, "far": OWN, "full": KEYS}[mode]
    pairs = count * keys * 4
    shapes = ((1, BLK), (8, BLK), (HD, BLK))
    if mode == "near":
        out_shape = [jax.ShapeDtypeStruct((OWN, *shape), jnp.float32) for shape in shapes] * count
    else:
        out_shape = [jax.ShapeDtypeStruct((OWN, HD + PAD, BLK), jnp.bfloat16)] * count
        out_shape += [jax.ShapeDtypeStruct((OWN, BLK), jnp.float32)] * count
        out_shape += [jax.ShapeDtypeStruct((KEYS, BLK), jnp.float32)] * last
    operands = (*queries, *keys_values, *states, *logs)
    return pl.pallas_call(
        functools.partial(attend_kernel, blocks, mode, last),
        out_shape=tuple(out_shape),
        in_specs=[SMEM] * 3 + [VMEM] * len(operands),
        out_specs=(VMEM,) * len(out_shape),
        scratch_shapes=[pltpu.SMEM((slots,), jnp.int32)] * 3
        + [
            pltpu.VMEM((count * OWN, BLK, HD), jnp.bfloat16),
            pltpu.VMEM((keys, BLK, HD), jnp.bfloat16),
            pltpu.VMEM((keys, HD, BLK), jnp.bfloat16),
        ]
        + [pltpu.VMEM((slots, *shape), jnp.float32) for shape in shapes]
        + [pltpu.VMEM((CHUNK * BLK, BLK), jnp.float32)] * WIDTH
        + [pltpu.VMEM((1, BLK), jnp.float32)] * WIDTH,
        compiler_params=SPACE,
        cost_estimate=pl.CostEstimate(
            flops=pairs * 4 * BLK * BLK * HD,
            bytes_accessed=5 << 20,
            transcendentals=pairs * BLK * BLK,
        ),
        name=mode,
    )(*lists, *operands)


def combine_kernel(e0, *refs):
    outs, o_ref = refs[:-1], refs[-1]
    for t in range(OWN):
        parts = [e0[t : t + 1]]
        for block in range(1, RING):
            parts.append(joined(outs[block][t, HD:].astype(jnp.float32), block))
        top = jnp.maximum(jnp.maximum(parts[0], parts[1]), jnp.maximum(parts[2], parts[3]))
        shares = [jnp.exp(part - top) for part in parts]
        total = (shares[0] + shares[1]) + (shares[2] + shares[3])
        mixed = sum(o[t, :HD].astype(jnp.float32) * (w / total) for o, w in zip(outs, shares))
        o_ref[t] = mixed.T.astype(jnp.bfloat16)


def combine(e0, outs):
    return pl.pallas_call(
        combine_kernel,
        out_shape=jax.ShapeDtypeStruct((OWN, BLK, HD), jnp.bfloat16),
        in_specs=[VMEM] * (RING + 1),
        out_specs=VMEM,
        compiler_params=SPACE,
        name="combine",
    )(e0, *outs)


def settle_kernel(own, further, two, before, out, spread_out):
    for s, o in ((1, further), (3, before)):
        for t in range(OWN):
            rows = o[t, HD:].astype(jnp.float32)
            for block in range(RING):
                spread_out[s // 2, block * OWN + t : block * OWN + t + 1] = joined(rows, block)
    for block in range(RING):
        part = []
        for s, logs in enumerate((own, spread_out.at[0], two, spread_out.at[1])):
            at = (block - s) % RING * OWN
            part.append(logs[at : at + OWN])
        top = jnp.maximum(jnp.maximum(part[0], part[1]), jnp.maximum(part[2], part[3]))
        total = sum(jnp.exp(p - top) for p in part)
        out[block * OWN : (block + 1) * OWN] = top + jnp.log(total)


def settle(own, further, two, before):
    return pl.pallas_call(
        settle_kernel,
        out_shape=jax.ShapeDtypeStruct((KEYS, BLK), jnp.float32),
        in_specs=[VMEM] * 4,
        out_specs=VMEM,
        scratch_shapes=[pltpu.VMEM((2, KEYS, BLK), jnp.float32)],
        compiler_params=SPACE,
        name="settle",
    )(own, further, two, before)


def choose_kernel(spots, e0, e1, e2, e3, out, every):
    for away, log in enumerate((e0, e1, e2, e3)):
        every[away * KEYS : (away + 1) * KEYS] = log[...]
    for slot in range(OWN):
        out[slot : slot + 1] = every[pl.ds(spots[slot], 1)]


def choose(spots, logs):
    return pl.pallas_call(
        choose_kernel,
        out_shape=jax.ShapeDtypeStruct((OWN, BLK), jnp.float32),
        in_specs=[SMEM] + [VMEM] * RING,
        out_specs=VMEM,
        scratch_shapes=[pltpu.VMEM((RING * KEYS, BLK), jnp.float32)],
        compiler_params=SPACE,
        name="choose",
    )(spots, *logs)


def slot_spots(assign, xi, yi):
    tiles = lax.dynamic_slice_in_dim(assign, (xi * RING + yi) * OWN, OWN)
    spots = (tiles // KEYS - xi) % RING * KEYS + (tiles % OWN // 3 - yi) % RING * OWN
    return spots + tiles % KEYS // OWN * 3 + tiles % 3


def key_lists(kv_tiles, tile_count, xi, yi):
    rows = lax.dynamic_slice_in_dim(kv_tiles, xi * KEYS, KEYS)
    used = lax.dynamic_slice_in_dim(tile_count, xi * KEYS, KEYS)
    here = (rows % OWN // 3 == yi) & (jnp.arange(LIST, dtype=jnp.int32)[None, :] < used[:, None])
    away = (rows // KEYS - xi) % RING
    block = jnp.where(away == 2, 3, jnp.minimum(away, 2))
    place = block * OWN + rows % KEYS // OWN * 3 + rows % 3
    near, far = here & (away != 2), here & (away == 2)
    nears = jnp.sum(near.astype(jnp.int32), axis=1)
    before = (jnp.arange(LIST)[:, None] < jnp.arange(LIST)[None, :]).astype(jnp.bfloat16)
    rank_near = jnp.dot(near.astype(jnp.bfloat16), before, preferred_element_type=jnp.float32)
    rank_far = jnp.dot(far.astype(jnp.bfloat16), before, preferred_element_type=jnp.float32)
    rank = jnp.where(
        near, rank_near.astype(jnp.int32), nears[:, None] + rank_far.astype(jnp.int32)
    )
    spot = jnp.arange(KEYS + CHUNK, dtype=jnp.int32)[None, :, None]
    at = here[:, None, :] & (rank[:, None, :] == spot)
    lists = jnp.sum(jnp.where(at, place[:, None, :], 0), axis=2)
    return lists, nears, jnp.sum(here.astype(jnp.int32), axis=1)


def exchange(array):
    return lax.all_to_all(array, GROUP, split_axis=0, concat_axis=0, tiled=True)


def on_device(queries, keys, values, kv_tiles, tile_count, assign):
    xi, yi = lax.axis_index("x"), lax.axis_index("y")
    lists = key_lists(kv_tiles, tile_count, xi, yi)
    spots = slot_spots(assign, xi, yi)
    by_head = jnp.transpose(queries.reshape(96, 16, HD), (1, 0, 2))
    got = exchange(spread(keys, values))
    got, by_head, spots, *lists = lax.optimization_barrier((got, by_head, spots, *lists))
    kv0 = prepare(got)
    kv1, kv3 = shift(kv0, "x", -1), shift(kv0, "x", 1)
    q0 = exchange(by_head).reshape(OWN, BLK, HD)
    k2, v2 = shift(kv3[0], "x", 1), shift(kv1[1], "x", -1)
    q0, q1, q2, q3 = around(q0, "y")
    state = attend((0,), "near", lists, (q0,), (kv0, kv1, kv3))
    o0, e0 = attend((0,), "far", lists, (q0,), (k2, v2), state)
    q2, o0 = lax.optimization_barrier((q2, o0))
    kv = (kv0, kv1, kv3, k2, v2)
    o2, e2 = attend((2,), "full", lists, (q2,), kv)
    o1, o3, _, _, logs = attend((1, 3), "full", lists, (q1, q3), kv, logs=(e0, e2))
    o1, o2, o3, logs2 = (
        shift(o1, "y", 1),
        shift(o2, "y", 2),
        shift(o3, "y", -1),
        shift(logs, "y", 2),
    )
    o1, logs2 = lax.optimization_barrier((o1, logs2))
    blended = combine(e0, (o0, o1, o2, o3))
    back = exchange(blended.reshape(16, 96, HD))
    attended = jnp.transpose(back, (1, 0, 2)).reshape(96, 16 * HD)
    chosen = choose(spots, around(settle(logs, o3, logs2, o1), "x"))
    turned = [(b * RING + a, a * RING + b) for a in range(RING) for b in range(RING)]
    return attended, lax.ppermute(chosen.reshape(1, OWN * BLK), ("zh", "y"), turned)


def solution(mesh):
    split = jax.sharding.Mesh(
        mesh.devices.reshape(RING, RING, RING, 2, 2), ("x", "zh", "y", "zl", "core")
    )
    tokens = P(("x", "zh", "y", "zl", "core"), None)
    return jax.shard_map(
        on_device,
        mesh=split,
        in_specs=(tokens, tokens, tokens, P(), P(), P()),
        out_specs=(tokens, P(("y", "zl", "core"), ("x", "zh"))),
        check_vma=False,
    )
```

time: 152 us -> 150 us (0.987)
  starting transfers between devices: 58.6 us -> 47.4 us
  Pallas kernels: 31.6 us -> 37.4 us
  local copies, waits for them, and re-layouts: 4.39 us -> 7 us
  waiting for transfers between devices: 52.9 us -> 55.5 us
    ppermute x20 -> x14, starting transfers between devices: 39 us -> 21.5 us  [shift(): lax.ppermute(array, axis, [(i, (i + by) % RING) for i in range(RING)])]
    all_to_all x3, waiting for transfers between devices: 28.8 us -> 18 us  [exchange(): return lax.all_to_all(array, GROUP, split_axis=0, concat_axis=0, tiled=True)]
    ppermute x20 -> x14, waiting for transfers between devices: 24.1 us -> 34.1 us  [shift(): lax.ppermute(array, axis, [(i, (i + by) % RING) for i in range(RING)])]
    ppermute x0 -> x1, starting transfers between devices: none -> 8.46 us  [on_device(): lax.ppermute(chosen.reshape(1, OWN * BLK), ('zh', 'y'), turned)]
    pallas_call x4 -> x5, Pallas kernels: 28.8 us -> 34.5 us  [the longest x4 34 us: attend(): pl.pallas_call(functools.partial(attend_kernel, blocks, mode, last), out_...]
    ppermute x0 -> x1, waiting for transfers between devices: none -> 3.37 us  [on_device(): lax.ppermute(chosen.reshape(1, OWN * BLK), ('zh', 'y'), turned)]
    squeeze x2, local copies, waits for them, and re-layouts: 0.05 us -> 2.58 us  [on_device(): k2, v2 = (shift(kv3[0], 'x', 1), shift(kv1[1], 'x', -1))]
    all_to_all x3, starting transfers between devices: 19.6 us -> 17.4 us  [exchange(): return lax.all_to_all(array, GROUP, split_axis=0, concat_axis=0, tiled=True)]
  transfers between devices with their start and end apart: 23 -> 18, of which waited for: 12 -> 8; matrix products, arithmetic and copies ran while one was open for 3% -> 4% of each run, Pallas kernels for 11% -> 13%
where the time goes in v7:
time: 150 us
  waiting for transfers between devices  55.5 us (37%)
  starting transfers between devices  47.4 us (32%)
  Pallas kernels  37.4 us (25%)
  local copies, waits for them, and re-layouts  7 us (5%)
    ppermute x14, waiting for transfers between devices, shift(): lax.ppermute(array, axis, [(i, (i + by) % RING) for i in range(RING)])  34.1 us
    pallas_call x4, Pallas kernels, attend(): pl.pallas_call(functools.partial(attend_kernel, blocks, mode, last), out_...  34 us
    ppermute x14, starting transfers between devices, shift(): lax.ppermute(array, axis, [(i, (i + by) % RING) for i in range(RING)])  21.5 us
    all_to_all x3, waiting for transfers between devices, exchange(): return lax.all_to_all(array, GROUP, split_axis=0, concat_axis=0, tiled=True)  18 us
    all_to_all x3, starting transfers between devices, exchange(): return lax.all_to_all(array, GROUP, split_axis=0, concat_axis=0, tiled=True)  17.4 us
    ppermute x1, starting transfers between devices, on_device(): lax.ppermute(chosen.reshape(1, OWN * BLK), ('zh', 'y'), turned)  8.46 us
    ppermute x1, waiting for transfers between devices, on_device(): lax.ppermute(chosen.reshape(1, OWN * BLK), ('zh', 'y'), turned)  3.37 us
  transfers between devices with their start and end apart: 18, of which 8 were waited for; matrix products, arithmetic and copies ran while one was open for 4% of the time, Pallas kernels for 13%

profile of v7, /device:TPU:16, one launch (start us, length us, event | category | flops | bytes accessed | tf_op | source)
XLA Modules:
  0.0 149.9 jit_solution(13440628398534571733)
XLA Ops:
  0.7 1.0 copy-done.1
  1.7 1.0 copy-done.2
  2.7 1.4 spread.1
  4.2 8.7 %all-to-all-start = ((bf16[16,2,96,128]{3,2,1,0:T(8,128)(2,1)}), bf16[16,2,96,128]{3,2,1,0:T(8,128)(2,1)S(1)}, u32[]{:S(2)}, u32[]{:S(2)}) async-start(bf16[16,2,96,128]{3,2,1,0:T(8,128)(2,1)} %spread.1), calls=%async_computation | async-start | bytes 1572864 | tf_op jit(solution)/shard_map/all_to_all | solution.py:383
  13.8 1.0 select_reduce_fusion
  14.7 0.8 bitcast_bitcast_fusion
  15.6 18.0 %all-to-all-done.got_ref = bf16[16,2,96,128]{3,2,1,0:T(8,128)(2,1)S(1)} async-done(((bf16[16,2,96,128]{3,2,1,0:T(8,128)(2,1)}), bf16[16,2,96,128]{3,2,1,0:T(8,128)(2,1)S(1)}, u32[]{:S(2)}, u32[]{:S(2)}) %all-to-all-start) | async-done | bytes 786464 | tf_op jit(solution)/shard_map/all_to_all | solution.py:383
  33.7 1.6 %collective-permute-start = (bf16[2,12,128,128]{3,2,1,0:T(8,128)(2,1)S(1)}, bf16[2,12,128,128]{3,2,1,0:T(8,128)(2,1)S(1)}, u32[]{:S(2)}, u32[]{:S(2)}) collective-permute-start(bf16[2,12,128,128]{3,2,1,0:T(8,128)(2,1)S(1)} %prepare.1.refs_1_.refs_2_), channel_id=1, source_target_pairs={{0,64},{64,128},{128,192},{192,0},{1,65},{65,129},{129,193},{193,1... | collective-permute-start | bytes 2359304 | tf_op jit(solution)/shard_map/ppermute | solution.py:30
  35.3 1.7 %collective-permute-start.2 = (bf16[2,12,128,128]{3,2,1,0:T(8,128)(2,1)S(1)}, bf16[2,12,128,128]{3,2,1,0:T(8,128)(2,1)}, u32[]{:S(2)}, u32[]{:S(2)}) collective-permute-start(bf16[2,12,128,128]{3,2,1,0:T(8,128)(2,1)S(1)} %prepare.1.refs_1_.refs_2_), channel_id=1, source_target_pairs={{0,192},{64,0},{128,64},{192,128},{1,193},{65,1},{129,65},{193,129... | collective-permute-start | bytes 2359304 | tf_op jit(solution)/shard_map/ppermute | solution.py:30
  37.1 5.1 %all-to-all-start.1 = ((bf16[16,96,128]{2,1,0:T(8,128)(2,1)}), bf16[16,96,128]{2,1,0:T(8,128)(2,1)S(1)}, u32[]{:S(2)}, u32[]{:S(2)}) async-start(bf16[16,96,128]{2,1,0:T(8,128)(2,1)} %bitcast_bitcast_fusion), calls=%async_computation.1 | async-start | bytes 786432 | tf_op jit(solution)/shard_map/all_to_all | solution.py:383
  42.2 11.8 %collective-permute-done.refs_3_.refs_4_ = bf16[2,12,128,128]{3,2,1,0:T(8,128)(2,1)S(1)} collective-permute-done((bf16[2,12,128,128]{3,2,1,0:T(8,128)(2,1)S(1)}, bf16[2,12,128,128]{3,2,1,0:T(8,128)(2,1)S(1)}, u32[]{:S(2)}, u32[]{:S(2)}) %collective-permute-start) | collective-permute-done | bytes 786464 | tf_op jit(solution)/shard_map/ppermute | solution.py:30
  54.0 0.8 slice_bitcast_fusion.1
  55.1 1.8 %slice_bitcast_fusion = bf16[12,128,128]{2,1,0:T(8,128)(2,1)} fusion(bf16[2,12,128,128]{3,2,1,0:T(8,128)(2,1)} %collective-permute-done.2.refs_2_.refs_3_), kind=kLoop, calls=%fused_computation.9 | loop fusion | bytes 786432 | tf_op jit(solution)/shard_map/squeeze | solution.py:396
  56.8 3.0 %collective-permute-start.3 = (bf16[12,128,128]{2,1,0:T(8,128)(2,1)}, bf16[12,128,128]{2,1,0:T(8,128)(2,1)S(1)}, u32[]{:S(2)}, u32[]{:S(2)}) collective-permute-start(bf16[12,128,128]{2,1,0:T(8,128)(2,1)} %slice_bitcast_fusion), channel_id=1, source_target_pairs={{0,192},{64,0},{128,64},{192,128},{1,193},{65,1},{129,65},{193,129... | collective-permute-start | bytes 1179656 | tf_op jit(solution)/shard_map/ppermute | solution.py:30
  60.1 2.4 %collective-permute-start.5 = (bf16[12,128,128]{2,1,0:T(8,128)(2,1)S(1)}, bf16[12,128,128]{2,1,0:T(8,128)(2,1)}, u32[]{:S(2)}, u32[]{:S(2)}) collective-permute-start(bf16[12,128,128]{2,1,0:T(8,128)(2,1)S(1)} %bitcast.26), channel_id=1, source_target_pairs={{0,12},{4,0},{8,4},{12,8},{1,13},{5,1},{9,5},{13,9},{2,14},{6,2},{... | collective-permute-start | bytes 1179656 | tf_op jit(solution)/shard_map/ppermute | solution.py:30
  62.6 7.1 %near.1 = (f32[12,1,128]{2,1,0:T(1,128)S(1)}, f32[12,8,128]{2,1,0:T(8,128)S(1)}, f32[12,128,128]{2,1,0:T(8,128)S(1)}) custom-call(s32[48,52]{1,0:T(8,128)S(1)} %copy.12.lists, s32[48]{0:T(128)S(1)} %get-tuple-element.23.nears, s32[48]{0:T(128)S(1)} %get-tuple-element.24.counts, bf16[12,128,128]{2,1,0:T(8,128)(2,1)S(1)} %bitcast.28, ...), custom_call_target="tpu_custom_call" | custom-call | flops 1207959552 | bytes 5242880 | tf_op jit(solution)/shard_map/near/pallas_call | solution.py:260
  69.7 3.5 %far.1 = (bf16[12,144,128]{2,1,0:T(8,128)(2,1)S(1)}, f32[12,128]{1,0:T(8,128)S(1)}) custom-call(s32[48,52]{1,0:T(8,128)S(1)} %copy.12.lists, s32[48]{0:T(128)S(1)} %get-tuple-element.23.nears, s32[48]{0:T(128)S(1)} %get-tuple-element.24.counts, bf16[12,128,128]{2,1,0:T(8,128)(2,1)S(1)} %bitcast.29, ...), custom_call_target="tpu_custom_call" | custom-call | flops 402653184 | bytes 5242880 | tf_op jit(solution)/shard_map/far/pallas_call | solution.py:260
  73.4 8.3 %full.2 = (bf16[12,144,128]{2,1,0:T(8,128)(2,1)S(1)}, f32[12,128]{1,0:T(8,128)S(1)}) custom-call(s32[48,52]{1,0:T(8,128)S(1)} %copy.12.lists, s32[48]{0:T(128)S(1)} %get-tuple-element.23.nears, s32[48]{0:T(128)S(1)} %get-tuple-element.24.counts, bf16[12,128,128]{2,1,0:T(8,128)(2,1)} %collective-permute-done.4.refs_0_, ...), custom_call_target="tpu_custom_call" | custom-call | flops 1610612736 | bytes 5242880 | tf_op jit(solution)/shard_map/full/pallas_call | solution.py:260
  81.8 15.1 %full.3 = (bf16[12,144,128]{2,1,0:T(8,128)(2,1)S(1)}, bf16[12,144,128]{2,1,0:T(8,128)(2,1)S(1)}, f32[12,128]{1,0:T(8,128)}, f32[12,128]{1,0:T(8,128)}, f32[48,128]{1,0:T(8,128)S(1)}) custom-call(s32[48,52]{1,0:T(8,128)S(1)} %copy.12.lists, s32[48]{0:T(128)S(1)} %get-tuple-element.23.nears, s32[48]{0:T(128)S(1)} %get-tuple-element.24.counts, ...), custom_call_target="tpu_custom_call" | custom-call | flops 3221225472 | bytes 5242880 | tf_op jit(solution)/shard_map/full/pallas_call | solution.py:260
  96.9 1.3 collective-permute-start.7
  98.2 1.5 collective-permute-start.9
  99.7 1.5 collective-permute-start.10
  101.2 1.9 %collective-permute-start.8 = (f32[48,128]{1,0:T(8,128)S(1)}, f32[48,128]{1,0:T(8,128)S(1)}, u32[]{:S(2)}, u32[]{:S(2)}) collective-permute-start(f32[48,128]{1,0:T(8,128)S(1)} %get-tuple-element.36.own), channel_id=1, source_target_pairs={{0,8},{4,12},{8,0},{12,4},{1,9},{5,13},{9,1},{13,5},{2,10},{6,14},... | collective-permute-start | bytes 73736 | tf_op jit(solution)/shard_map/ppermute | solution.py:30
  103.0 16.9 %collective-permute-done.8.two = f32[48,128]{1,0:T(8,128)S(1)} collective-permute-done((f32[48,128]{1,0:T(8,128)S(1)}, f32[48,128]{1,0:T(8,128)S(1)}, u32[]{:S(2)}, u32[]{:S(2)}) %collective-permute-start.8) | collective-permute-done | bytes 24608 | tf_op jit(solution)/shard_map/ppermute | solution.py:30
  119.9 0.9 collective-permute-done.10.refs_3_.further
  120.8 1.2 combine.1
  122.1 3.6 %all-to-all-start.2 = ((bf16[16,96,128]{2,1,0:T(8,128)(2,1)}), bf16[16,96,128]{2,1,0:T(8,128)(2,1)S(1)}, u32[]{:S(2)}, u32[]{:S(2)}) async-start(bf16[16,96,128]{2,1,0:T(8,128)(2,1)} %bitcast.4), calls=%async_computation.2 | async-start | bytes 786432 | tf_op jit(solution)/shard_map/all_to_all | solution.py:383
  125.7 5.1 %collective-permute-start.11 = (f32[48,128]{1,0:T(8,128)S(1)}, f32[48,128]{1,0:T(8,128)S(1)}, u32[]{:S(2)}, u32[]{:S(2)}) collective-permute-start(f32[48,128]{1,0:T(8,128)S(1)} %settle.1.e0), channel_id=1, source_target_pairs={{0,192},{64,0},{128,64},{192,128},{1,193},{65,1},{129,65},{193,129... | collective-permute-start | bytes 73736 | tf_op jit(solution)/shard_map/ppermute | solution.py:30
  130.8 1.0 collective-permute-start.13
  132.3 3.8 %collective-permute-done.12.e2 = f32[48,128]{1,0:T(8,128)S(1)} collective-permute-done((f32[48,128]{1,0:T(8,128)S(1)}, f32[48,128]{1,0:T(8,128)S(1)}, u32[]{:S(2)}, u32[]{:S(2)}) %collective-permute-start.12) | collective-permute-done | bytes 24608 | tf_op jit(solution)/shard_map/ppermute | solution.py:30
  136.7 8.5 %collective-permute-start.14 = (f32[1,1536]{1,0:T(1,128)S(1)}, f32[1,1536]{1,0:T(1,128)S(1)}, u32[]{:S(2)}, u32[]{:S(2)}) collective-permute-start(f32[1,1536]{1,0:T(1,128)S(1)} %bitcast.31), channel_id=1, source_target_pairs={{0,0},{16,4},{32,8},{48,12},{4,16},{20,20},{36,24},{52,28},{8,32},... | collective-permute-start | bytes 18440 | tf_op jit(solution)/shard_map/ppermute | solution.py:416
  145.2 3.4 %collective-permute-done.14 = f32[1,1536]{1,0:T(1,128)S(1)} collective-permute-done((f32[1,1536]{1,0:T(1,128)S(1)}, f32[1,1536]{1,0:T(1,128)S(1)}, u32[]{:S(2)}, u32[]{:S(2)}) %collective-permute-start.14) | collective-permute-done | bytes 6176 | tf_op jit(solution)/shard_map/ppermute | solution.py:416
  (39 shorter events, 4.6 us)
Async XLA Ops:
  0.6 14.1 %copy-start = (bf16[96,2048]{1,0:T(8,128)(2,1)S(1)}, bf16[96,2048]{1,0:T(8,128)(2,1)}, u32[]{:S(2)}) copy-start(bf16[96,2048]{1,0:T(8,128)(2,1)} %param.6) | copy-start | bytes 1179652
  0.6 1.0 copy-start.1
  1.7 1.0 copy-start.2
  4.1 8.8 %copy-start.5 = (s32[192]{0:T(256)S(1)}, s32[192]{0:T(256)}, u32[]{:S(2)}) copy-start(s32[192]{0:T(256)} %param.10) | copy-start | bytes 2308
  4.1 8.8 %copy-start.4 = (s32[192]{0:T(256)S(1)}, s32[192]{0:T(256)}, u32[]{:S(2)}) copy-start(s32[192]{0:T(256)} %param.11) | copy-start | bytes 2308
  4.2 8.9 %copy-start.3 = (s32[192,96]{1,0:T(8,128)S(1)}, s32[192,96]{1,0:T(8,128)}, u32[]{:S(2)}) copy-start(s32[192,96]{1,0:T(8,128)} %param.9) | copy-start | bytes 221188
  4.2 29.4 %all-to-all-start = ((bf16[16,2,96,128]{3,2,1,0:T(8,128)(2,1)}), bf16[16,2,96,128]{3,2,1,0:T(8,128)(2,1)S(1)}, u32[]{:S(2)}, u32[]{:S(2)}) async-start(bf16[16,2,96,128]{3,2,1,0:T(8,128)(2,1)} %spread.1), calls=%async_computation | async-start | bytes 1572864 | tf_op jit(solution)/shard_map/all_to_all | solution.py:383
  33.7 20.2 %collective-permute-start = (bf16[2,12,128,128]{3,2,1,0:T(8,128)(2,1)S(1)}, bf16[2,12,128,128]{3,2,1,0:T(8,128)(2,1)S(1)}, u32[]{:S(2)}, u32[]{:S(2)}) collective-permute-start(bf16[2,12,128,128]{3,2,1,0:T(8,128)(2,1)S(1)} %prepare.1.refs_1_.refs_2_), channel_id=1, source_target_pairs={{0,64},{64,128},{128,192},{192,0},{1,65},{65,129},{129,193},{193,1... | collective-permute-start | bytes 2359304 | tf_op jit(solution)/shard_map/ppermute | solution.py:30
  35.3 19.8 %collective-permute-start.2 = (bf16[2,12,128,128]{3,2,1,0:T(8,128)(2,1)S(1)}, bf16[2,12,128,128]{3,2,1,0:T(8,128)(2,1)}, u32[]{:S(2)}, u32[]{:S(2)}) collective-permute-start(bf16[2,12,128,128]{3,2,1,0:T(8,128)(2,1)S(1)} %prepare.1.refs_1_.refs_2_), channel_id=1, source_target_pairs={{0,192},{64,0},{128,64},{192,128},{1,193},{65,1},{129,65},{193,129... | collective-permute-start | bytes 2359304 | tf_op jit(solution)/shard_map/ppermute | solution.py:30
  37.1 22.7 %all-to-all-start.1 = ((bf16[16,96,128]{2,1,0:T(8,128)(2,1)}), bf16[16,96,128]{2,1,0:T(8,128)(2,1)S(1)}, u32[]{:S(2)}, u32[]{:S(2)}) async-start(bf16[16,96,128]{2,1,0:T(8,128)(2,1)} %bitcast_bitcast_fusion), calls=%async_computation.1 | async-start | bytes 786432 | tf_op jit(solution)/shard_map/all_to_all | solution.py:383
  54.8 14.9 %collective-permute-start.1 = (bf16[12,128,128]{2,1,0:T(8,128)(2,1)}, bf16[12,128,128]{2,1,0:T(8,128)(2,1)S(1)}, u32[]{:S(2)}, u32[]{:S(2)}) collective-permute-start(bf16[12,128,128]{2,1,0:T(8,128)(2,1)} %slice_bitcast_fusion.1), channel_id=1, source_target_pairs={{0,64},{64,128},{128,192},{192,0},{1,65},{65,129},{129,193},{193,1... | collective-permute-start | bytes 1179656 | tf_op jit(solution)/shard_map/ppermute | solution.py:30
  56.8 12.9 %collective-permute-start.3 = (bf16[12,128,128]{2,1,0:T(8,128)(2,1)}, bf16[12,128,128]{2,1,0:T(8,128)(2,1)S(1)}, u32[]{:S(2)}, u32[]{:S(2)}) collective-permute-start(bf16[12,128,128]{2,1,0:T(8,128)(2,1)} %slice_bitcast_fusion), channel_id=1, source_target_pairs={{0,192},{64,0},{128,64},{192,128},{1,193},{65,1},{129,65},{193,129... | collective-permute-start | bytes 1179656 | tf_op jit(solution)/shard_map/ppermute | solution.py:30
  59.8 13.6 %collective-permute-start.4 = (bf16[12,128,128]{2,1,0:T(8,128)(2,1)S(1)}, bf16[12,128,128]{2,1,0:T(8,128)(2,1)}, u32[]{:S(2)}, u32[]{:S(2)}) collective-permute-start(bf16[12,128,128]{2,1,0:T(8,128)(2,1)S(1)} %bitcast.25), channel_id=1, source_target_pairs={{0,8},{4,12},{8,0},{12,4},{1,9},{5,13},{9,1},{13,5},{2,10},{6,14},... | collective-permute-start | bytes 1179656 | tf_op jit(solution)/shard_map/ppermute | solution.py:30
  60.1 21.6 %collective-permute-start.5 = (bf16[12,128,128]{2,1,0:T(8,128)(2,1)S(1)}, bf16[12,128,128]{2,1,0:T(8,128)(2,1)}, u32[]{:S(2)}, u32[]{:S(2)}) collective-permute-start(bf16[12,128,128]{2,1,0:T(8,128)(2,1)S(1)} %bitcast.26), channel_id=1, source_target_pairs={{0,12},{4,0},{8,4},{12,8},{1,13},{5,1},{9,5},{13,9},{2,14},{6,2},{... | collective-permute-start | bytes 1179656 | tf_op jit(solution)/shard_map/ppermute | solution.py:30
  62.5 19.3 %collective-permute-start.6 = (bf16[12,128,128]{2,1,0:T(8,128)(2,1)S(1)}, bf16[12,128,128]{2,1,0:T(8,128)(2,1)}, u32[]{:S(2)}, u32[]{:S(2)}) collective-permute-start(bf16[12,128,128]{2,1,0:T(8,128)(2,1)S(1)} %bitcast.27), channel_id=1, source_target_pairs={{0,4},{4,8},{8,12},{12,0},{1,5},{5,9},{9,13},{13,1},{2,6},{6,10},{... | collective-permute-start | bytes 1179656 | tf_op jit(solution)/shard_map/ppermute | solution.py:30
  96.9 23.0 %collective-permute-start.7 = (bf16[12,144,128]{2,1,0:T(8,128)(2,1)S(1)}, bf16[12,144,128]{2,1,0:T(8,128)(2,1)S(1)}, u32[]{:S(2)}, u32[]{:S(2)}) collective-permute-start(bf16[12,144,128]{2,1,0:T(8,128)(2,1)S(1)} %get-tuple-element.35), channel_id=1, source_target_pairs={{0,4},{4,8},{8,12},{12,0},{1,5},{5,9},{9,13},{13,1},{2,6},{6,10},{... | collective-permute-start | bytes 1327112 | tf_op jit(solution)/shard_map/ppermute | solution.py:30
  98.2 21.7 %collective-permute-start.9 = (bf16[12,144,128]{2,1,0:T(8,128)(2,1)S(1)}, bf16[12,144,128]{2,1,0:T(8,128)(2,1)S(1)}, u32[]{:S(2)}, u32[]{:S(2)}) collective-permute-start(bf16[12,144,128]{2,1,0:T(8,128)(2,1)S(1)} %get-tuple-element.38), channel_id=1, source_target_pairs={{0,8},{4,12},{8,0},{12,4},{1,9},{5,13},{9,1},{13,5},{2,10},{6,14},... | collective-permute-start | bytes 1327112 | tf_op jit(solution)/shard_map/ppermute | solution.py:30
  99.7 21.1 %collective-permute-start.10 = (bf16[12,144,128]{2,1,0:T(8,128)(2,1)S(1)}, bf16[12,144,128]{2,1,0:T(8,128)(2,1)S(1)}, u32[]{:S(2)}, u32[]{:S(2)}) collective-permute-start(bf16[12,144,128]{2,1,0:T(8,128)(2,1)S(1)} %get-tuple-element.39), channel_id=1, source_target_pairs={{0,12},{4,0},{8,4},{12,8},{1,13},{5,1},{9,5},{13,9},{2,14},{6,2},{... | collective-permute-start | bytes 1327112 | tf_op jit(solution)/shard_map/ppermute | solution.py:30
  101.2 18.8 %collective-permute-start.8 = (f32[48,128]{1,0:T(8,128)S(1)}, f32[48,128]{1,0:T(8,128)S(1)}, u32[]{:S(2)}, u32[]{:S(2)}) collective-permute-start(f32[48,128]{1,0:T(8,128)S(1)} %get-tuple-element.36.own), channel_id=1, source_target_pairs={{0,8},{4,12},{8,0},{12,4},{1,9},{5,13},{9,1},{13,5},{2,10},{6,14},... | collective-permute-start | bytes 73736 | tf_op jit(solution)/shard_map/ppermute | solution.py:30
  122.1 26.5 %all-to-all-start.2 = ((bf16[16,96,128]{2,1,0:T(8,128)(2,1)}), bf16[16,96,128]{2,1,0:T(8,128)(2,1)S(1)}, u32[]{:S(2)}, u32[]{:S(2)}) async-start(bf16[16,96,128]{2,1,0:T(8,128)(2,1)} %bitcast.4), calls=%async_computation.2 | async-start | bytes 786432 | tf_op jit(solution)/shard_map/all_to_all | solution.py:383
  125.7 6.6 %collective-permute-start.11 = (f32[48,128]{1,0:T(8,128)S(1)}, f32[48,128]{1,0:T(8,128)S(1)}, u32[]{:S(2)}, u32[]{:S(2)}) collective-permute-start(f32[48,128]{1,0:T(8,128)S(1)} %settle.1.e0), channel_id=1, source_target_pairs={{0,192},{64,0},{128,64},{192,128},{1,193},{65,1},{129,65},{193,129... | collective-permute-start | bytes 73736 | tf_op jit(solution)/shard_map/ppermute | solution.py:30
  130.8 5.3 %collective-permute-start.12 = (f32[48,128]{1,0:T(8,128)S(1)}, f32[48,128]{1,0:T(8,128)S(1)}, u32[]{:S(2)}, u32[]{:S(2)}) collective-permute-start(f32[48,128]{1,0:T(8,128)S(1)} %settle.1.e0), channel_id=1, source_target_pairs={{0,128},{64,192},{128,0},{192,64},{1,129},{65,193},{129,1},{193,65... | collective-permute-start | bytes 73736 | tf_op jit(solution)/shard_map/ppermute | solution.py:30
  130.8 5.3 %collective-permute-start.13 = (f32[48,128]{1,0:T(8,128)S(1)}, f32[48,128]{1,0:T(8,128)S(1)}, u32[]{:S(2)}, u32[]{:S(2)}) collective-permute-start(f32[48,128]{1,0:T(8,128)S(1)} %settle.1.e0), channel_id=1, source_target_pairs={{0,64},{64,128},{128,192},{192,0},{1,65},{65,129},{129,193},{193,1... | collective-permute-start | bytes 73736 | tf_op jit(solution)/shard_map/ppermute | solution.py:30
  136.7 11.8 %collective-permute-start.14 = (f32[1,1536]{1,0:T(1,128)S(1)}, f32[1,1536]{1,0:T(1,128)S(1)}, u32[]{:S(2)}, u32[]{:S(2)}) collective-permute-start(f32[1,1536]{1,0:T(1,128)S(1)} %bitcast.31), channel_id=1, source_target_pairs={{0,0},{16,4},{32,8},{48,12},{4,16},{20,20},{36,24},{52,28},{8,32},... | collective-permute-start | bytes 18440 | tf_op jit(solution)/shard_map/ppermute | solution.py:416

commit v8 on v7

--- a/solution.py
+++ b/solution.py
@@ -104,7 +104,7 @@
     if mode == "far":
         states, refs = refs[: 3 * count], refs[3 * count :]
     if last:
-        (e0, e2), refs = refs[:2], refs[2:]
+        known, refs = refs[:3], refs[3:]
     size = (3 if mode == "near" else 2) * count + last
     outs, refs = refs[:size], refs[size:]
     rows, begins, sizes, qs, ks, vs, m_ref, l_ref, acc_ref = refs[:9]
@@ -230,9 +230,8 @@
                 logs[block] = jnp.where(some, m_ref[b * OWN + t] * SCALE + jnp.log(safe), NEG)
                 outs[count + b][pl.ds(t, 1)] = logs[block]
             if last:
-                logs[0], logs[2] = e0[pl.ds(t, 1)], e2[pl.ds(t, 1)]
-                for block in range(RING):
-                    outs[2 * count][pl.ds(block * OWN + t, 1)] = logs[block]
+                for block, log in enumerate((*known, outs[count])):
+                    outs[2][pl.ds(block * OWN + t, 1)] = log[pl.ds(t, 1)]
             none = [jnp.zeros((1, BLK), jnp.bfloat16)] * 3
             below = [row for b in range(RING) for row in (split(logs[b]) if b in logs else none)]
             below.append(jnp.zeros((PAD - 3 * RING, BLK), jnp.bfloat16))
@@ -305,32 +304,26 @@
     )(e0, *outs)
 
 
-def settle_kernel(own, further, two, before, out, spread_out):
-    for s, o in ((1, further), (3, before)):
-        for t in range(OWN):
-            rows = o[t, HD:].astype(jnp.float32)
-            for block in range(RING):
-                spread_out[s // 2, block * OWN + t : block * OWN + t + 1] = joined(rows, block)
+def settle_kernel(e0, e1, e2, e3, out):
+    parts = (e0, e1, e2, e3)
     for block in range(RING):
-        part = []
-        for s, logs in enumerate((own, spread_out.at[0], two, spread_out.at[1])):
-            at = (block - s) % RING * OWN
-            part.append(logs[at : at + OWN])
+        part = [
+            parts[s][(block - s) % RING * OWN : ((block - s) % RING + 1) * OWN] for s in range(RING)
+        ]
         top = jnp.maximum(jnp.maximum(part[0], part[1]), jnp.maximum(part[2], part[3]))
         total = sum(jnp.exp(p - top) for p in part)
         out[block * OWN : (block + 1) * OWN] = top + jnp.log(total)
 
 
-def settle(own, further, two, before):
+def settle(parts):
     return pl.pallas_call(
         settle_kernel,
         out_shape=jax.ShapeDtypeStruct((KEYS, BLK), jnp.float32),
-        in_specs=[VMEM] * 4,
+        in_specs=[VMEM] * RING,
         out_specs=VMEM,
-        scratch_shapes=[pltpu.VMEM((2, KEYS, BLK), jnp.float32)],
         compiler_params=SPACE,
         name="settle",
-    )(own, further, two, before)
+    )(*parts)
 
 
 def choose_kernel(spots, e0, e1, e2, e3, out, every):
@@ -395,23 +388,23 @@
     q0 = exchange(by_head).reshape(OWN, BLK, HD)
     k2, v2 = shift(kv3[0], "x", 1), shift(kv1[1], "x", -1)
     q0, q1, q2, q3 = around(q0, "y")
+    kv = (kv0, kv1, kv3, k2, v2)
+    barrier = lax.optimization_barrier
     state = attend((0,), "near", lists, (q0,), (kv0, kv1, kv3))
+    q2, state = barrier((q2, state))
+    o2, e2 = attend((2,), "full", lists, (q2,), kv)
+    state, o2 = barrier((state, o2))
     o0, e0 = attend((0,), "far", lists, (q0,), (k2, v2), state)
-    q2, o0 = lax.optimization_barrier((q2, o0))
-    kv = (kv0, kv1, kv3, k2, v2)
-    o2, e2 = attend((2,), "full", lists, (q2,), kv)
-    o1, o3, _, _, logs = attend((1, 3), "full", lists, (q1, q3), kv, logs=(e0, e2))
-    o1, o2, o3, logs2 = (
-        shift(o1, "y", 1),
-        shift(o2, "y", 2),
-        shift(o3, "y", -1),
-        shift(logs, "y", 2),
-    )
-    o1, logs2 = lax.optimization_barrier((o1, logs2))
-    blended = combine(e0, (o0, o1, o2, o3))
+    q1, o0 = barrier((q1, o0))
+    o1, e1 = attend((1,), "full", lists, (q1,), kv)
+    q3, o1, o2 = barrier((q3, o1, shift(o2, "y", 2)))
+    o3, _, logs = attend((3,), "full", lists, (q3,), kv, logs=(e0, e1, e2))
+    every = around(settle(around(logs, "y")), "x")
+    o0, *every = barrier((o0, *every))
+    blended = combine(e0, (o0, shift(o1, "y", 1), o2, shift(o3, "y", -1)))
     back = exchange(blended.reshape(16, 96, HD))
     attended = jnp.transpose(back, (1, 0, 2)).reshape(96, 16 * HD)
-    chosen = choose(spots, around(settle(logs, o3, logs2, o1), "x"))
+    chosen = choose(spots, every)
     turned = [(b * RING + a, a * RING + b) for a in range(RING) for b in range(RING)]
     return attended, lax.ppermute(chosen.reshape(1, OWN * BLK), ("zh", "y"), turned)
 

time: 150 us -> 161 us (1.073)
  starting transfers between devices: 47.4 us -> 52.9 us
  waiting for transfers between devices: 55.5 us -> 58.3 us
    ppermute x14 -> x16, waiting for transfers between devices: 34.1 us -> 21.2 us  [shift(): lax.ppermute(array, axis, [(i, (i + by) % RING) for i in range(RING)])]
    all_to_all x3, waiting for transfers between devices: 18 us -> 29.9 us  [exchange(): return lax.all_to_all(array, GROUP, split_axis=0, concat_axis=0, tiled=True)]
    ppermute x1, waiting for transfers between devices: 3.37 us -> 7.26 us  [on_device(): lax.ppermute(chosen.reshape(1, OWN * BLK), ('zh', 'y'), turned)]
    all_to_all x3, starting transfers between devices: 17.4 us -> 20.4 us  [exchange(): return lax.all_to_all(array, GROUP, split_axis=0, concat_axis=0, tiled=True)]
    ppermute x14 -> x16, starting transfers between devices: 21.5 us -> 23.7 us  [shift(): lax.ppermute(array, axis, [(i, (i + by) % RING) for i in range(RING)])]
    pallas_call x4 -> x5, Pallas kernels: 34 us -> 35.6 us  [attend(): pl.pallas_call(functools.partial(attend_kernel, blocks, mode, last), out_...]
  transfers between devices with their start and end apart: 18 -> 20, of which waited for: 8 -> 9; matrix products, arithmetic and copies ran while one was open for 4% -> 3% of each run, Pallas kernels for 13% -> 23%
where the time goes in v8:
time: 161 us; the launch traced here: 160 us
  waiting for transfers between devices  58.3 us (36%)
  starting transfers between devices  52.9 us (33%)
  Pallas kernels  39 us (24%)
  local copies, waits for them, and re-layouts  6.96 us (4%)
    pallas_call x5, Pallas kernels, attend(): pl.pallas_call(functools.partial(attend_kernel, blocks, mode, last), out_...  35.6 us
    all_to_all x3, waiting for transfers between devices, exchange(): return lax.all_to_all(array, GROUP, split_axis=0, concat_axis=0, tiled=True)  29.9 us
    ppermute x16, starting transfers between devices, shift(): lax.ppermute(array, axis, [(i, (i + by) % RING) for i in range(RING)])  23.7 us
    ppermute x16, waiting for transfers between devices, shift(): lax.ppermute(array, axis, [(i, (i + by) % RING) for i in range(RING)])  21.2 us
    all_to_all x3, starting transfers between devices, exchange(): return lax.all_to_all(array, GROUP, split_axis=0, concat_axis=0, tiled=True)  20.4 us
    ppermute x1, starting transfers between devices, on_device(): lax.ppermute(chosen.reshape(1, OWN * BLK), ('zh', 'y'), turned)  8.77 us
    ppermute x1, waiting for transfers between devices, on_device(): lax.ppermute(chosen.reshape(1, OWN * BLK), ('zh', 'y'), turned)  7.26 us
  transfers between devices with their start and end apart: 20, of which 9 were waited for; matrix products, arithmetic and copies ran while one was open for 3% of the time, Pallas kernels for 23%

profile of v8, /device:TPU:16, one launch (start us, length us, event | category | flops | bytes accessed | tf_op | source)
XLA Modules:
  0.0 159.8 jit_solution(17612462826551167418)
XLA Ops:
  0.7 1.0 copy-done.1
  1.7 1.0 copy-done.2
  2.7 1.4 spread.1
  4.2 8.7 %all-to-all-start = ((bf16[16,2,96,128]{3,2,1,0:T(8,128)(2,1)}), bf16[16,2,96,128]{3,2,1,0:T(8,128)(2,1)S(1)}, u32[]{:S(2)}, u32[]{:S(2)}) async-start(bf16[16,2,96,128]{3,2,1,0:T(8,128)(2,1)} %spread.1), calls=%async_computation | async-start | bytes 1572864 | tf_op jit(solution)/shard_map/all_to_all | solution.py:376
  15.6 18.0 %all-to-all-done.got_ref = bf16[16,2,96,128]{3,2,1,0:T(8,128)(2,1)S(1)} async-done(((bf16[16,2,96,128]{3,2,1,0:T(8,128)(2,1)}), bf16[16,2,96,128]{3,2,1,0:T(8,128)(2,1)S(1)}, u32[]{:S(2)}, u32[]{:S(2)}) %all-to-all-start) | async-done | bytes 786464 | tf_op jit(solution)/shard_map/all_to_all | solution.py:376
  33.7 1.6 collective-permute-start
  35.3 5.1 %all-to-all-start.1 = ((bf16[16,96,128]{2,1,0:T(8,128)(2,1)}), bf16[16,96,128]{2,1,0:T(8,128)(2,1)S(1)}, u32[]{:S(2)}, u32[]{:S(2)}) async-start(bf16[16,96,128]{2,1,0:T(8,128)(2,1)} %bitcast_bitcast_fusion), calls=%async_computation.1 | async-start | bytes 786432 | tf_op jit(solution)/shard_map/all_to_all | solution.py:376
  40.5 1.8 %collective-permute-start.2 = (bf16[2,12,128,128]{3,2,1,0:T(8,128)(2,1)S(1)}, bf16[2,12,128,128]{3,2,1,0:T(8,128)(2,1)}, u32[]{:S(2)}, u32[]{:S(2)}) collective-permute-start(bf16[2,12,128,128]{3,2,1,0:T(8,128)(2,1)S(1)} %prepare.1.refs_1_), channel_id=1, source_target_pairs={{0,192},{64,0},{128,64},{192,128},{1,193},{65,1},{129,65},{193,129... | collective-permute-start | bytes 2359304 | tf_op jit(solution)/shard_map/ppermute | solution.py:30
  42.3 11.9 %all-to-all-done.1 = bf16[16,96,128]{2,1,0:T(8,128)(2,1)S(1)} async-done(((bf16[16,96,128]{2,1,0:T(8,128)(2,1)}), bf16[16,96,128]{2,1,0:T(8,128)(2,1)S(1)}, u32[]{:S(2)}, u32[]{:S(2)}) %all-to-all-start.1) | async-done | bytes 393248 | tf_op jit(solution)/shard_map/all_to_all | solution.py:376
  55.3 1.5 collective-permute-start.1
  56.8 3.8 %collective-permute-done.2.refs_2_ = bf16[2,12,128,128]{3,2,1,0:T(8,128)(2,1)} collective-permute-done((bf16[2,12,128,128]{3,2,1,0:T(8,128)(2,1)S(1)}, bf16[2,12,128,128]{3,2,1,0:T(8,128)(2,1)}, u32[]{:S(2)}, u32[]{:S(2)}) %collective-permute-start.2) | collective-permute-done | bytes 786464 | tf_op jit(solution)/shard_map/ppermute | solution.py:30
  60.5 1.8 %slice_bitcast_fusion = bf16[12,128,128]{2,1,0:T(8,128)(2,1)} fusion(bf16[2,12,128,128]{3,2,1,0:T(8,128)(2,1)} %collective-permute-done.2.refs_2_), kind=kLoop, calls=%fused_computation.9 | loop fusion | bytes 786432 | tf_op jit(solution)/shard_map/squeeze | solution.py:389
  62.3 3.0 %collective-permute-start.3 = (bf16[12,128,128]{2,1,0:T(8,128)(2,1)}, bf16[12,128,128]{2,1,0:T(8,128)(2,1)S(1)}, u32[]{:S(2)}, u32[]{:S(2)}) collective-permute-start(bf16[12,128,128]{2,1,0:T(8,128)(2,1)} %slice_bitcast_fusion), channel_id=1, source_target_pairs={{0,192},{64,0},{128,64},{192,128},{1,193},{65,1},{129,65},{193,129... | collective-permute-start | bytes 1179656 | tf_op jit(solution)/shard_map/ppermute | solution.py:30
  65.8 7.6 %near.1 = (f32[12,1,128]{2,1,0:T(1,128)S(1)}, f32[12,8,128]{2,1,0:T(8,128)S(1)}, f32[12,128,128]{2,1,0:T(8,128)S(1)}) custom-call(s32[48,52]{1,0:T(8,128)S(1)} %copy.13.lists, s32[48]{0:T(128)S(1)} %get-tuple-element.38.nears, s32[48]{0:T(128)S(1)} %get-tuple-element.39.counts, bf16[12,128,128]{2,1,0:T(8,128)(2,1)S(1)} %bitcast.27, ...), custom_call_target="tpu_custom_call" | custom-call | flops 1207959552 | bytes 5242880 | tf_op jit(solution)/shard_map/near/pallas_call | solution.py:259
  73.7 7.8 %full.3 = (bf16[12,144,128]{2,1,0:T(8,128)(2,1)S(1)}, f32[12,128]{1,0:T(8,128)S(1)}) custom-call(s32[48,52]{1,0:T(8,128)S(1)} %copy.13.lists, s32[48]{0:T(128)S(1)} %get-tuple-element.38.nears, s32[48]{0:T(128)S(1)} %get-tuple-element.39.counts, bf16[12,128,128]{2,1,0:T(8,128)(2,1)} %collective-permute-done.4.refs_0_, ...), custom_call_target="tpu_custom_call" | custom-call | flops 1610612736 | bytes 5242880 | tf_op jit(solution)/shard_map/full/pallas_call | solution.py:259
  81.6 3.2 %collective-permute-start.7 = (bf16[12,144,128]{2,1,0:T(8,128)(2,1)S(1)}, bf16[12,144,128]{2,1,0:T(8,128)(2,1)S(1)}, u32[]{:S(2)}, u32[]{:S(2)}) collective-permute-start(bf16[12,144,128]{2,1,0:T(8,128)(2,1)S(1)} %get-tuple-element.58), channel_id=1, source_target_pairs={{0,8},{4,12},{8,0},{12,4},{1,9},{5,13},{9,1},{13,5},{2,10},{6,14},... | collective-permute-start | bytes 1327112 | tf_op jit(solution)/shard_map/ppermute | solution.py:30
  84.7 3.5 %far.1 = (bf16[12,144,128]{2,1,0:T(8,128)(2,1)S(1)}, f32[12,128]{1,0:T(8,128)S(1)}) custom-call(s32[48,52]{1,0:T(8,128)S(1)} %copy.13.lists, s32[48]{0:T(128)S(1)} %get-tuple-element.38.nears, s32[48]{0:T(128)S(1)} %get-tuple-element.39.counts, bf16[12,128,128]{2,1,0:T(8,128)(2,1)S(1)} %bitcast.29, ...), custom_call_target="tpu_custom_call" | custom-call | flops 402653184 | bytes 5242880 | tf_op jit(solution)/shard_map/far/pallas_call | solution.py:259
  88.3 6.9 %full.4 = (bf16[12,144,128]{2,1,0:T(8,128)(2,1)S(1)}, f32[12,128]{1,0:T(8,128)S(1)}) custom-call(s32[48,52]{1,0:T(8,128)S(1)} %copy.13.lists, s32[48]{0:T(128)S(1)} %get-tuple-element.38.nears, s32[48]{0:T(128)S(1)} %get-tuple-element.39.counts, bf16[12,128,128]{2,1,0:T(8,128)(2,1)S(1)} %collective-permute-done.5.refs_0_, ...), custom_call_target="tpu_custom_call" | custom-call | flops 1610612736 | bytes 5242880 | tf_op jit(solution)/shard_map/full/pallas_call | solution.py:259
  95.2 7.4 %collective-permute-done.6.refs_0_ = bf16[12,128,128]{2,1,0:T(8,128)(2,1)S(1)} collective-permute-done((bf16[12,128,128]{2,1,0:T(8,128)(2,1)S(1)}, bf16[12,128,128]{2,1,0:T(8,128)(2,1)S(1)}, u32[]{:S(2)}, u32[]{:S(2)}) %collective-permute-start.6) | collective-permute-done | bytes 393248 | tf_op jit(solution)/shard_map/ppermute | solution.py:30
  102.6 1.8 %collective-permute-start.14 = (bf16[12,144,128]{2,1,0:T(8,128)(2,1)S(1)}, bf16[12,144,128]{2,1,0:T(8,128)(2,1)S(1)}, u32[]{:S(2)}, u32[]{:S(2)}) collective-permute-start(bf16[12,144,128]{2,1,0:T(8,128)(2,1)S(1)} %get-tuple-element.64), channel_id=1, source_target_pairs={{0,4},{4,8},{8,12},{12,0},{1,5},{5,9},{9,13},{13,1},{2,6},{6,10},{... | collective-permute-start | bytes 1327112 | tf_op jit(solution)/shard_map/ppermute | solution.py:30
  104.4 9.8 %full.5 = (bf16[12,144,128]{2,1,0:T(8,128)(2,1)S(1)}, f32[12,128]{1,0:T(8,128)}, f32[48,128]{1,0:T(8,128)S(1)}) custom-call(s32[48,52]{1,0:T(8,128)S(1)} %copy.13.lists, s32[48]{0:T(128)S(1)} %get-tuple-element.38.nears, s32[48]{0:T(128)S(1)} %get-tuple-element.39.counts, bf16[12,128,128]{2,1,0:T(8,128)(2,1)S(1)} %collective-permute-done.6.refs_0_, ...), custom_call_target="tpu_custom_call" | custom-call | flops 1610612736 | bytes 5242880 | tf_op jit(solution)/shard_map/full/pallas_call | solution.py:259
  114.2 4.1 %collective-permute-start.9 = (f32[48,128]{1,0:T(8,128)S(1)}, f32[48,128]{1,0:T(8,128)S(1)}, u32[]{:S(2)}, u32[]{:S(2)}) collective-permute-start(f32[48,128]{1,0:T(8,128)S(1)} %get-tuple-element.62.e0), channel_id=1, source_target_pairs={{0,8},{4,12},{8,0},{12,4},{1,9},{5,13},{9,1},{13,5},{2,10},{6,14},... | collective-permute-start | bytes 73736 | tf_op jit(solution)/shard_map/ppermute | solution.py:30
  118.2 2.1 %collective-permute-start.10 = (f32[48,128]{1,0:T(8,128)S(1)}, f32[48,128]{1,0:T(8,128)S(1)}, u32[]{:S(2)}, u32[]{:S(2)}) collective-permute-start(f32[48,128]{1,0:T(8,128)S(1)} %get-tuple-element.62.e0), channel_id=1, source_target_pairs={{0,4},{4,8},{8,12},{12,0},{1,5},{5,9},{9,13},{13,1},{2,6},{6,10},{... | collective-permute-start | bytes 73736 | tf_op jit(solution)/shard_map/ppermute | solution.py:30
  120.3 6.0 %collective-permute-done.8.e1 = f32[48,128]{1,0:T(8,128)S(1)} collective-permute-done((f32[48,128]{1,0:T(8,128)S(1)}, f32[48,128]{1,0:T(8,128)S(1)}, u32[]{:S(2)}, u32[]{:S(2)}) %collective-permute-start.8) | collective-permute-done | bytes 24608 | tf_op jit(solution)/shard_map/ppermute | solution.py:30
  127.3 1.7 %collective-permute-start.12 = (f32[48,128]{1,0:T(8,128)S(1)}, f32[48,128]{1,0:T(8,128)S(1)}, u32[]{:S(2)}, u32[]{:S(2)}) collective-permute-start(f32[48,128]{1,0:T(8,128)S(1)} %settle.1.e0), channel_id=1, source_target_pairs={{0,128},{64,192},{128,0},{192,64},{1,129},{65,193},{129,1},{193,65... | collective-permute-start | bytes 73736 | tf_op jit(solution)/shard_map/ppermute | solution.py:30
  128.9 1.3 collective-permute-start.13
  130.3 2.3 %collective-permute-done.12.e2 = f32[48,128]{1,0:T(8,128)S(1)} collective-permute-done((f32[48,128]{1,0:T(8,128)S(1)}, f32[48,128]{1,0:T(8,128)S(1)}, u32[]{:S(2)}, u32[]{:S(2)}) %collective-permute-start.12) | collective-permute-done | bytes 24608 | tf_op jit(solution)/shard_map/ppermute | solution.py:30
  132.6 1.4 collective-permute-done.13.e3
  134.0 1.2 combine.1
  135.2 6.5 %all-to-all-start.2 = ((bf16[16,96,128]{2,1,0:T(8,128)(2,1)}), bf16[16,96,128]{2,1,0:T(8,128)(2,1)S(1)}, u32[]{:S(2)}, u32[]{:S(2)}) async-start(bf16[16,96,128]{2,1,0:T(8,128)(2,1)} %bitcast.4), calls=%async_computation.2 | async-start | bytes 786432 | tf_op jit(solution)/shard_map/all_to_all | solution.py:376
  142.4 8.8 %collective-permute-start.16 = (f32[1,1536]{1,0:T(1,128)S(1)}, f32[1,1536]{1,0:T(1,128)S(1)}, u32[]{:S(2)}, u32[]{:S(2)}) collective-permute-start(f32[1,1536]{1,0:T(1,128)S(1)} %bitcast.31), channel_id=1, source_target_pairs={{0,0},{16,4},{32,8},{48,12},{4,16},{20,20},{36,24},{52,28},{8,32},... | collective-permute-start | bytes 18440 | tf_op jit(solution)/shard_map/ppermute | solution.py:409
  151.1 7.3 %collective-permute-done.16 = f32[1,1536]{1,0:T(1,128)S(1)} collective-permute-done((f32[1,1536]{1,0:T(1,128)S(1)}, f32[1,1536]{1,0:T(1,128)S(1)}, u32[]{:S(2)}, u32[]{:S(2)}) %collective-permute-start.16) | collective-permute-done | bytes 6176 | tf_op jit(solution)/shard_map/ppermute | solution.py:409
  (44 shorter events, 7.8 us)
Async XLA Ops:
  0.6 14.1 %copy-start = (bf16[96,2048]{1,0:T(8,128)(2,1)S(1)}, bf16[96,2048]{1,0:T(8,128)(2,1)}, u32[]{:S(2)}) copy-start(bf16[96,2048]{1,0:T(8,128)(2,1)} %param.6) | copy-start | bytes 1179652
  0.6 1.0 copy-start.1
  1.7 1.0 copy-start.2
  4.1 8.8 %copy-start.5 = (s32[192]{0:T(256)S(1)}, s32[192]{0:T(256)}, u32[]{:S(2)}) copy-start(s32[192]{0:T(256)} %param.10) | copy-start | bytes 2308
  4.1 8.8 %copy-start.4 = (s32[192]{0:T(256)S(1)}, s32[192]{0:T(256)}, u32[]{:S(2)}) copy-start(s32[192]{0:T(256)} %param.11) | copy-start | bytes 2308
  4.2 8.9 %copy-start.3 = (s32[192,96]{1,0:T(8,128)S(1)}, s32[192,96]{1,0:T(8,128)}, u32[]{:S(2)}) copy-start(s32[192,96]{1,0:T(8,128)} %param.9) | copy-start | bytes 221188
  4.2 29.4 %all-to-all-start = ((bf16[16,2,96,128]{3,2,1,0:T(8,128)(2,1)}), bf16[16,2,96,128]{3,2,1,0:T(8,128)(2,1)S(1)}, u32[]{:S(2)}, u32[]{:S(2)}) async-start(bf16[16,2,96,128]{3,2,1,0:T(8,128)(2,1)} %spread.1), calls=%async_computation | async-start | bytes 1572864 | tf_op jit(solution)/shard_map/all_to_all | solution.py:376
  33.7 20.7 %collective-permute-start = (bf16[2,12,128,128]{3,2,1,0:T(8,128)(2,1)S(1)}, bf16[2,12,128,128]{3,2,1,0:T(8,128)(2,1)S(1)}, u32[]{:S(2)}, u32[]{:S(2)}) collective-permute-start(bf16[2,12,128,128]{3,2,1,0:T(8,128)(2,1)S(1)} %prepare.1.refs_1_), channel_id=1, source_target_pairs={{0,64},{64,128},{128,192},{192,0},{1,65},{65,129},{129,193},{193,1... | collective-permute-start | bytes 2359304 | tf_op jit(solution)/shard_map/ppermute | solution.py:30
  35.3 18.8 %all-to-all-start.1 = ((bf16[16,96,128]{2,1,0:T(8,128)(2,1)}), bf16[16,96,128]{2,1,0:T(8,128)(2,1)S(1)}, u32[]{:S(2)}, u32[]{:S(2)}) async-start(bf16[16,96,128]{2,1,0:T(8,128)(2,1)} %bitcast_bitcast_fusion), calls=%async_computation.1 | async-start | bytes 786432 | tf_op jit(solution)/shard_map/all_to_all | solution.py:376
  40.5 20.1 %collective-permute-start.2 = (bf16[2,12,128,128]{3,2,1,0:T(8,128)(2,1)S(1)}, bf16[2,12,128,128]{3,2,1,0:T(8,128)(2,1)}, u32[]{:S(2)}, u32[]{:S(2)}) collective-permute-start(bf16[2,12,128,128]{3,2,1,0:T(8,128)(2,1)S(1)} %prepare.1.refs_1_), channel_id=1, source_target_pairs={{0,192},{64,0},{128,64},{192,128},{1,193},{65,1},{129,65},{193,129... | collective-permute-start | bytes 2359304 | tf_op jit(solution)/shard_map/ppermute | solution.py:30
  54.1 19.2 %collective-permute-start.4 = (bf16[12,128,128]{2,1,0:T(8,128)(2,1)S(1)}, bf16[12,128,128]{2,1,0:T(8,128)(2,1)}, u32[]{:S(2)}, u32[]{:S(2)}) collective-permute-start(bf16[12,128,128]{2,1,0:T(8,128)(2,1)S(1)} %bitcast.25), channel_id=1, source_target_pairs={{0,8},{4,12},{8,0},{12,4},{1,9},{5,13},{9,1},{13,5},{2,10},{6,14},... | collective-permute-start | bytes 1179656 | tf_op jit(solution)/shard_map/ppermute | solution.py:30
  55.3 18.1 %collective-permute-start.1 = (bf16[12,128,128]{2,1,0:T(8,128)(2,1)}, bf16[12,128,128]{2,1,0:T(8,128)(2,1)S(1)}, u32[]{:S(2)}, u32[]{:S(2)}) collective-permute-start(bf16[12,128,128]{2,1,0:T(8,128)(2,1)} %slice_bitcast_fusion.1), channel_id=1, source_target_pairs={{0,64},{64,128},{128,192},{192,0},{1,65},{65,129},{129,193},{193,1... | collective-permute-start | bytes 1179656 | tf_op jit(solution)/shard_map/ppermute | solution.py:30
  62.3 11.4 %collective-permute-start.3 = (bf16[12,128,128]{2,1,0:T(8,128)(2,1)}, bf16[12,128,128]{2,1,0:T(8,128)(2,1)S(1)}, u32[]{:S(2)}, u32[]{:S(2)}) collective-permute-start(bf16[12,128,128]{2,1,0:T(8,128)(2,1)} %slice_bitcast_fusion), channel_id=1, source_target_pairs={{0,192},{64,0},{128,64},{192,128},{1,193},{65,1},{129,65},{193,129... | collective-permute-start | bytes 1179656 | tf_op jit(solution)/shard_map/ppermute | solution.py:30
  65.3 22.9 %collective-permute-start.5 = (bf16[12,128,128]{2,1,0:T(8,128)(2,1)S(1)}, bf16[12,128,128]{2,1,0:T(8,128)(2,1)S(1)}, u32[]{:S(2)}, u32[]{:S(2)}) collective-permute-start(bf16[12,128,128]{2,1,0:T(8,128)(2,1)S(1)} %bitcast.26), channel_id=1, source_target_pairs={{0,12},{4,0},{8,4},{12,8},{1,13},{5,1},{9,5},{13,9},{2,14},{6,2},{... | collective-permute-start | bytes 1179656 | tf_op jit(solution)/shard_map/ppermute | solution.py:30
  81.6 21.0 %collective-permute-start.7 = (bf16[12,144,128]{2,1,0:T(8,128)(2,1)S(1)}, bf16[12,144,128]{2,1,0:T(8,128)(2,1)S(1)}, u32[]{:S(2)}, u32[]{:S(2)}) collective-permute-start(bf16[12,144,128]{2,1,0:T(8,128)(2,1)S(1)} %get-tuple-element.58), channel_id=1, source_target_pairs={{0,8},{4,12},{8,0},{12,4},{1,9},{5,13},{9,1},{13,5},{2,10},{6,14},... | collective-permute-start | bytes 1327112 | tf_op jit(solution)/shard_map/ppermute | solution.py:30
  84.7 17.8 %collective-permute-start.6 = (bf16[12,128,128]{2,1,0:T(8,128)(2,1)S(1)}, bf16[12,128,128]{2,1,0:T(8,128)(2,1)S(1)}, u32[]{:S(2)}, u32[]{:S(2)}) collective-permute-start(bf16[12,128,128]{2,1,0:T(8,128)(2,1)S(1)} %bitcast.28), channel_id=1, source_target_pairs={{0,4},{4,8},{8,12},{12,0},{1,5},{5,9},{9,13},{13,1},{2,6},{6,10},{... | collective-permute-start | bytes 1179656 | tf_op jit(solution)/shard_map/ppermute | solution.py:30
  102.6 31.4 %collective-permute-start.14 = (bf16[12,144,128]{2,1,0:T(8,128)(2,1)S(1)}, bf16[12,144,128]{2,1,0:T(8,128)(2,1)S(1)}, u32[]{:S(2)}, u32[]{:S(2)}) collective-permute-start(bf16[12,144,128]{2,1,0:T(8,128)(2,1)S(1)} %get-tuple-element.64), channel_id=1, source_target_pairs={{0,4},{4,8},{8,12},{12,0},{1,5},{5,9},{9,13},{13,1},{2,6},{6,10},{... | collective-permute-start | bytes 1327112 | tf_op jit(solution)/shard_map/ppermute | solution.py:30
  114.1 19.9 %collective-permute-start.15 = (bf16[12,144,128]{2,1,0:T(8,128)(2,1)S(1)}, bf16[12,144,128]{2,1,0:T(8,128)(2,1)S(1)}, u32[]{:S(2)}, u32[]{:S(2)}) collective-permute-start(bf16[12,144,128]{2,1,0:T(8,128)(2,1)S(1)} %get-tuple-element.66), channel_id=1, source_target_pairs={{0,12},{4,0},{8,4},{12,8},{1,13},{5,1},{9,5},{13,9},{2,14},{6,2},{... | collective-permute-start | bytes 1327112 | tf_op jit(solution)/shard_map/ppermute | solution.py:30
  114.1 12.1 %collective-permute-start.8 = (f32[48,128]{1,0:T(8,128)S(1)}, f32[48,128]{1,0:T(8,128)S(1)}, u32[]{:S(2)}, u32[]{:S(2)}) collective-permute-start(f32[48,128]{1,0:T(8,128)S(1)} %get-tuple-element.62.e0), channel_id=1, source_target_pairs={{0,12},{4,0},{8,4},{12,8},{1,13},{5,1},{9,5},{13,9},{2,14},{6,2},{... | collective-permute-start | bytes 73736 | tf_op jit(solution)/shard_map/ppermute | solution.py:30
  114.2 12.1 %collective-permute-start.9 = (f32[48,128]{1,0:T(8,128)S(1)}, f32[48,128]{1,0:T(8,128)S(1)}, u32[]{:S(2)}, u32[]{:S(2)}) collective-permute-start(f32[48,128]{1,0:T(8,128)S(1)} %get-tuple-element.62.e0), channel_id=1, source_target_pairs={{0,8},{4,12},{8,0},{12,4},{1,9},{5,13},{9,1},{13,5},{2,10},{6,14},... | collective-permute-start | bytes 73736 | tf_op jit(solution)/shard_map/ppermute | solution.py:30
  118.2 8.0 %collective-permute-start.10 = (f32[48,128]{1,0:T(8,128)S(1)}, f32[48,128]{1,0:T(8,128)S(1)}, u32[]{:S(2)}, u32[]{:S(2)}) collective-permute-start(f32[48,128]{1,0:T(8,128)S(1)} %get-tuple-element.62.e0), channel_id=1, source_target_pairs={{0,4},{4,8},{8,12},{12,0},{1,5},{5,9},{9,13},{13,1},{2,6},{6,10},{... | collective-permute-start | bytes 73736 | tf_op jit(solution)/shard_map/ppermute | solution.py:30
  126.3 4.0 %collective-permute-start.11 = (f32[48,128]{1,0:T(8,128)S(1)}, f32[48,128]{1,0:T(8,128)S(1)}, u32[]{:S(2)}, u32[]{:S(2)}) collective-permute-start(f32[48,128]{1,0:T(8,128)S(1)} %settle.1.e0), channel_id=1, source_target_pairs={{0,192},{64,0},{128,64},{192,128},{1,193},{65,1},{129,65},{193,129... | collective-permute-start | bytes 73736 | tf_op jit(solution)/shard_map/ppermute | solution.py:30
  127.3 5.3 %collective-permute-start.12 = (f32[48,128]{1,0:T(8,128)S(1)}, f32[48,128]{1,0:T(8,128)S(1)}, u32[]{:S(2)}, u32[]{:S(2)}) collective-permute-start(f32[48,128]{1,0:T(8,128)S(1)} %settle.1.e0), channel_id=1, source_target_pairs={{0,128},{64,192},{128,0},{192,64},{1,129},{65,193},{129,1},{193,65... | collective-permute-start | bytes 73736 | tf_op jit(solution)/shard_map/ppermute | solution.py:30
  128.9 5.0 %collective-permute-start.13 = (f32[48,128]{1,0:T(8,128)S(1)}, f32[48,128]{1,0:T(8,128)S(1)}, u32[]{:S(2)}, u32[]{:S(2)}) collective-permute-start(f32[48,128]{1,0:T(8,128)S(1)} %settle.1.e0), channel_id=1, source_target_pairs={{0,64},{64,128},{128,192},{192,0},{1,65},{65,129},{129,193},{193,1... | collective-permute-start | bytes 73736 | tf_op jit(solution)/shard_map/ppermute | solution.py:30
  135.2 23.2 %all-to-all-start.2 = ((bf16[16,96,128]{2,1,0:T(8,128)(2,1)}), bf16[16,96,128]{2,1,0:T(8,128)(2,1)S(1)}, u32[]{:S(2)}, u32[]{:S(2)}) async-start(bf16[16,96,128]{2,1,0:T(8,128)(2,1)} %bitcast.4), calls=%async_computation.2 | async-start | bytes 786432 | tf_op jit(solution)/shard_map/all_to_all | solution.py:376
  142.4 16.0 %collective-permute-start.16 = (f32[1,1536]{1,0:T(1,128)S(1)}, f32[1,1536]{1,0:T(1,128)S(1)}, u32[]{:S(2)}, u32[]{:S(2)}) collective-permute-start(f32[1,1536]{1,0:T(1,128)S(1)} %bitcast.31), channel_id=1, source_target_pairs={{0,0},{16,4},{32,8},{48,12},{4,16},{20,20},{36,24},{52,28},{8,32},... | collective-permute-start | bytes 18440 | tf_op jit(solution)/shard_map/ppermute | solution.py:409

commit v9 on v7

--- a/solution.py
+++ b/solution.py
@@ -93,7 +93,7 @@
     return parts[0] + parts[1] + parts[2]
 
 
-def attend_kernel(blocks, mode, last, lists, nears, counts, *refs):
+def attend_kernel(blocks, mode, lists, nears, counts, *refs):
     count = len(blocks)
     tiles = count * OWN
     queries, refs = refs[:count], refs[count:]
@@ -103,9 +103,7 @@
         (k2, v2), refs = refs[:2], refs[2:]
     if mode == "far":
         states, refs = refs[: 3 * count], refs[3 * count :]
-    if last:
-        (e0, e2), refs = refs[:2], refs[2:]
-    size = (3 if mode == "near" else 2) * count + last
+    size = (3 if mode == "near" else 2) * count
     outs, refs = refs[:size], refs[size:]
     rows, begins, sizes, qs, ks, vs, m_ref, l_ref, acc_ref = refs[:9]
     s_refs, top_refs = refs[9 : 9 + WIDTH], refs[9 + WIDTH :]
@@ -229,10 +227,6 @@
                 outs[b][t, :HD] = (acc_ref[b * OWN + t] * share).astype(jnp.bfloat16)
                 logs[block] = jnp.where(some, m_ref[b * OWN + t] * SCALE + jnp.log(safe), NEG)
                 outs[count + b][pl.ds(t, 1)] = logs[block]
-            if last:
-                logs[0], logs[2] = e0[pl.ds(t, 1)], e2[pl.ds(t, 1)]
-                for block in range(RING):
-                    outs[2 * count][pl.ds(block * OWN + t, 1)] = logs[block]
             none = [jnp.zeros((1, BLK), jnp.bfloat16)] * 3
             below = [row for b in range(RING) for row in (split(logs[b]) if b in logs else none)]
             below.append(jnp.zeros((PAD - 3 * RING, BLK), jnp.bfloat16))
@@ -243,8 +237,7 @@
     lax.fori_loop(0, OWN // 4, finish, 0)
 
 
-def attend(blocks, mode, lists, queries, keys_values, states=(), logs=()):
-    last = bool(logs)
+def attend(blocks, mode, lists, queries, keys_values, states=()):
     count = len(blocks)
     slots = count * OWN + 1
     keys = {"near": NEAR, "far": OWN, "full": KEYS}[mode]
@@ -255,10 +248,9 @@
     else:
         out_shape = [jax.ShapeDtypeStruct((OWN, HD + PAD, BLK), jnp.bfloat16)] * count
         out_shape += [jax.ShapeDtypeStruct((OWN, BLK), jnp.float32)] * count
-        out_shape += [jax.ShapeDtypeStruct((KEYS, BLK), jnp.float32)] * last
-    operands = (*queries, *keys_values, *states, *logs)
-    return pl.pallas_call(
-        functools.partial(attend_kernel, blocks, mode, last),
+    operands = (*queries, *keys_values, *states)
+    return pl.pallas_call(
+        functools.partial(attend_kernel, blocks, mode),
         out_shape=tuple(out_shape),
         in_specs=[SMEM] * 3 + [VMEM] * len(operands),
         out_specs=(VMEM,) * len(out_shape),
@@ -305,57 +297,46 @@
     )(e0, *outs)
 
 
-def settle_kernel(own, further, two, before, out, spread_out):
-    for s, o in ((1, further), (3, before)):
-        for t in range(OWN):
-            rows = o[t, HD:].astype(jnp.float32)
-            for block in range(RING):
-                spread_out[s // 2, block * OWN + t : block * OWN + t + 1] = joined(rows, block)
-    for block in range(RING):
-        part = []
-        for s, logs in enumerate((own, spread_out.at[0], two, spread_out.at[1])):
-            at = (block - s) % RING * OWN
-            part.append(logs[at : at + OWN])
-        top = jnp.maximum(jnp.maximum(part[0], part[1]), jnp.maximum(part[2], part[3]))
-        total = sum(jnp.exp(p - top) for p in part)
-        out[block * OWN : (block + 1) * OWN] = top + jnp.log(total)
-
-
-def settle(own, further, two, before):
-    return pl.pallas_call(
-        settle_kernel,
-        out_shape=jax.ShapeDtypeStruct((KEYS, BLK), jnp.float32),
-        in_specs=[VMEM] * 4,
-        out_specs=VMEM,
-        scratch_shapes=[pltpu.VMEM((2, KEYS, BLK), jnp.float32)],
-        compiler_params=SPACE,
-        name="settle",
-    )(own, further, two, before)
-
-
-def choose_kernel(spots, e0, e1, e2, e3, out, every):
-    for away, log in enumerate((e0, e1, e2, e3)):
-        every[away * KEYS : (away + 1) * KEYS] = log[...]
-    for slot in range(OWN):
-        out[slot : slot + 1] = every[pl.ds(spots[slot], 1)]
-
-
-def choose(spots, logs):
-    return pl.pallas_call(
-        choose_kernel,
-        out_shape=jax.ShapeDtypeStruct((OWN, BLK), jnp.float32),
+def pick_kernel(spots, e0, e1, e2, e3, out, every):
+    for block, log in enumerate((e0, e1, e2, e3)):
+        every[block * OWN : (block + 1) * OWN] = log[...]
+    every[KEYS : KEYS + 8] = jnp.full((8, BLK), NEG, jnp.float32)
+    for ctx in range(RING * RING):
+        for slot in range(OWN):
+            out[ctx, slot : slot + 1] = every[pl.ds(spots[ctx * OWN + slot], 1)]
+
+
+def pick(spots, logs):
+    return pl.pallas_call(
+        pick_kernel,
+        out_shape=jax.ShapeDtypeStruct((RING * RING, OWN, BLK), jnp.float32),
         in_specs=[SMEM] + [VMEM] * RING,
         out_specs=VMEM,
-        scratch_shapes=[pltpu.VMEM((RING * KEYS, BLK), jnp.float32)],
-        compiler_params=SPACE,
-        name="choose",
+        scratch_shapes=[pltpu.VMEM((KEYS + 8, BLK), jnp.float32)],
+        compiler_params=SPACE,
+        name="pick",
     )(spots, *logs)
 
 
+def merge_kernel(parts, out):
+    top = jnp.max(parts[...], axis=0)
+    out[...] = top + jnp.log(jnp.sum(jnp.exp(parts[...] - top[None]), axis=0))
+
+
+def merge(parts):
+    return pl.pallas_call(
+        merge_kernel,
+        out_shape=jax.ShapeDtypeStruct((OWN, BLK), jnp.float32),
+        in_specs=[VMEM],
+        out_specs=VMEM,
+        compiler_params=SPACE,
+        name="merge",
+    )(parts)
+
+
 def slot_spots(assign, xi, yi):
-    tiles = lax.dynamic_slice_in_dim(assign, (xi * RING + yi) * OWN, OWN)
-    spots = (tiles // KEYS - xi) % RING * KEYS + (tiles % OWN // 3 - yi) % RING * OWN
-    return spots + tiles % KEYS // OWN * 3 + tiles % 3
+    spots = (assign % OWN // 3 - yi) % RING * OWN + assign % KEYS // OWN * 3 + assign % 3
+    return jnp.where(assign // KEYS == xi, spots, KEYS)
 
 
 def key_lists(kv_tiles, tile_count, xi, yi):
@@ -400,20 +381,16 @@
     q2, o0 = lax.optimization_barrier((q2, o0))
     kv = (kv0, kv1, kv3, k2, v2)
     o2, e2 = attend((2,), "full", lists, (q2,), kv)
-    o1, o3, _, _, logs = attend((1, 3), "full", lists, (q1, q3), kv, logs=(e0, e2))
-    o1, o2, o3, logs2 = (
-        shift(o1, "y", 1),
-        shift(o2, "y", 2),
-        shift(o3, "y", -1),
-        shift(logs, "y", 2),
+    o1, o3, e1, e3 = attend((1, 3), "full", lists, (q1, q3), kv)
+    parts = lax.all_to_all(
+        pick(spots, (e0, e1, e2, e3)), ("x", "y"), split_axis=0, concat_axis=0, tiled=True
     )
-    o1, logs2 = lax.optimization_barrier((o1, logs2))
-    blended = combine(e0, (o0, o1, o2, o3))
+    o0, parts = lax.optimization_barrier((o0, parts))
+    blended = combine(e0, (o0, shift(o1, "y", 1), shift(o2, "y", 2), shift(o3, "y", -1)))
     back = exchange(blended.reshape(16, 96, HD))
     attended = jnp.transpose(back, (1, 0, 2)).reshape(96, 16 * HD)
-    chosen = choose(spots, around(settle(logs, o3, logs2, o1), "x"))
     turned = [(b * RING + a, a * RING + b) for a in range(RING) for b in range(RING)]
-    return attended, lax.ppermute(chosen.reshape(1, OWN * BLK), ("zh", "y"), turned)
+    return attended, lax.ppermute(merge(parts).reshape(1, OWN * BLK), ("zh", "y"), turned)
 
 
 def solution(mesh):

time: 150 us -> 152 us (1.013)
  blocking collectives: 0 us -> 19.2 us
  waiting for transfers between devices: 55.5 us -> 46.1 us
  starting transfers between devices: 47.4 us -> 41.7 us
  Pallas kernels: 37.4 us -> 34.2 us
    all_to_all x0 -> x1, blocking collectives: none -> 19.2 us  [on_device(): lax.all_to_all(pick(spots, (e0, e1, e2, e3)), ('x', 'y'), split_axis=0, c...]
    ppermute x14 -> x10, waiting for transfers between devices: 34.1 us -> 20.8 us  [shift(): lax.ppermute(array, axis, [(i, (i + by) % RING) for i in range(RING)])]
    ppermute x14 -> x10, starting transfers between devices: 21.5 us -> 14.7 us  [shift(): lax.ppermute(array, axis, [(i, (i + by) % RING) for i in range(RING)])]
    ppermute x1, waiting for transfers between devices: 3.37 us -> 7.78 us  [on_device(): lax.ppermute(merge(parts).reshape(1, OWN * BLK), ('zh', 'y'), turned)]
    pallas_call x6, Pallas kernels: 34.6 us -> 31.3 us  [the longest x4 30.6 us: attend(): pl.pallas_call(functools.partial(attend_kernel, blocks, mode), out_shape=...]
  transfers between devices with their start and end apart: 18 -> 14, of which waited for: 8 -> 6; matrix products, arithmetic and copies ran while one was open for 4% -> 4% of each run, Pallas kernels for 13% -> 13%
where the time goes in v9:
time: 152 us; the launch traced here: 151 us
  waiting for transfers between devices  46.1 us (30%)
  starting transfers between devices  41.7 us (27%)
  Pallas kernels  34.2 us (23%)
  blocking collectives  19.2 us (13%)
  local copies, waits for them, and re-layouts  6.97 us (5%)
  other arithmetic  1.96 us (1%)
    pallas_call x4, Pallas kernels, attend(): pl.pallas_call(functools.partial(attend_kernel, blocks, mode), out_shape=...  30.6 us
    ppermute x10, waiting for transfers between devices, shift(): lax.ppermute(array, axis, [(i, (i + by) % RING) for i in range(RING)])  20.8 us
    all_to_all x1, blocking collectives, on_device(): lax.all_to_all(pick(spots, (e0, e1, e2, e3)), ('x', 'y'), split_axis=0, c...  19.2 us
    all_to_all x3, waiting for transfers between devices, exchange(): return lax.all_to_all(array, GROUP, split_axis=0, concat_axis=0, tiled=True)  17.5 us
    all_to_all x3, starting transfers between devices, exchange(): return lax.all_to_all(array, GROUP, split_axis=0, concat_axis=0, tiled=True)  17.4 us
    ppermute x10, starting transfers between devices, shift(): lax.ppermute(array, axis, [(i, (i + by) % RING) for i in range(RING)])  14.7 us
    ppermute x1, starting transfers between devices, on_device(): lax.ppermute(merge(parts).reshape(1, OWN * BLK), ('zh', 'y'), turned)  9.65 us
    ppermute x1, waiting for transfers between devices, on_device(): lax.ppermute(merge(parts).reshape(1, OWN * BLK), ('zh', 'y'), turned)  7.78 us
  transfers between devices with their start and end apart: 14, of which 6 were waited for; matrix products, arithmetic and copies ran while one was open for 4% of the time, Pallas kernels for 13%

profile of v9, /device:TPU:16, one launch (start us, length us, event | category | flops | bytes accessed | tf_op | source)
XLA Modules:
  0.0 151.3 jit_solution(12311081030029674874)
XLA Ops:
  0.7 1.0 copy-done.1
  1.7 1.0 copy-done.2
  2.7 1.4 spread.1
  4.2 8.7 %all-to-all-start = ((bf16[16,2,96,128]{3,2,1,0:T(8,128)(2,1)}), bf16[16,2,96,128]{3,2,1,0:T(8,128)(2,1)S(1)}, u32[]{:S(2)}, u32[]{:S(2)}) async-start(bf16[16,2,96,128]{3,2,1,0:T(8,128)(2,1)} %spread.1), calls=%async_computation | async-start | bytes 1572864 | tf_op jit(solution)/shard_map/all_to_all | solution.py:364
  13.6 1.6 %select_reduce_fusion = s32[48,52]{0,1:T(8,128)} fusion(s32[48,96]{1,0:T(8,128)S(1)} %get-tuple-element.48, s32[48,96]{1,0:T(8,128)S(1)} %fusion.2, pred[48,96]{1,0:T(8,128)(4,1)S(1)} %get-tuple-element.45), kind=kLoop, calls=%fused_computation | loop fusion | flops 955968 | bytes 51456 | tf_op jit(solution)/shard_map/reduce_sum | solution.py:359
  15.3 0.8 bitcast_bitcast_fusion
  16.1 17.5 %all-to-all-done.got_ref = bf16[16,2,96,128]{3,2,1,0:T(8,128)(2,1)S(1)} async-done(((bf16[16,2,96,128]{3,2,1,0:T(8,128)(2,1)}), bf16[16,2,96,128]{3,2,1,0:T(8,128)(2,1)S(1)}, u32[]{:S(2)}, u32[]{:S(2)}) %all-to-all-start) | async-done | bytes 786464 | tf_op jit(solution)/shard_map/all_to_all | solution.py:364
  33.7 1.6 %collective-permute-start = (bf16[2,12,128,128]{3,2,1,0:T(8,128)(2,1)S(1)}, bf16[2,12,128,128]{3,2,1,0:T(8,128)(2,1)S(1)}, u32[]{:S(2)}, u32[]{:S(2)}) collective-permute-start(bf16[2,12,128,128]{3,2,1,0:T(8,128)(2,1)S(1)} %prepare.1.refs_1_.refs_2_), channel_id=1, source_target_pairs={{0,64},{64,128},{128,192},{192,0},{1,65},{65,129},{129,193},{193,1... | collective-permute-start | bytes 2359304 | tf_op jit(solution)/shard_map/ppermute | solution.py:30
  35.3 1.7 %collective-permute-start.2 = (bf16[2,12,128,128]{3,2,1,0:T(8,128)(2,1)S(1)}, bf16[2,12,128,128]{3,2,1,0:T(8,128)(2,1)}, u32[]{:S(2)}, u32[]{:S(2)}) collective-permute-start(bf16[2,12,128,128]{3,2,1,0:T(8,128)(2,1)S(1)} %prepare.1.refs_1_.refs_2_), channel_id=1, source_target_pairs={{0,192},{64,0},{128,64},{192,128},{1,193},{65,1},{129,65},{193,129... | collective-permute-start | bytes 2359304 | tf_op jit(solution)/shard_map/ppermute | solution.py:30
  37.0 5.1 %all-to-all-start.1 = ((bf16[16,96,128]{2,1,0:T(8,128)(2,1)}), bf16[16,96,128]{2,1,0:T(8,128)(2,1)S(1)}, u32[]{:S(2)}, u32[]{:S(2)}) async-start(bf16[16,96,128]{2,1,0:T(8,128)(2,1)} %bitcast_bitcast_fusion), calls=%async_computation.1 | async-start | bytes 786432 | tf_op jit(solution)/shard_map/all_to_all | solution.py:364
  42.2 11.8 %collective-permute-done.refs_3_.refs_4_ = bf16[2,12,128,128]{3,2,1,0:T(8,128)(2,1)S(1)} collective-permute-done((bf16[2,12,128,128]{3,2,1,0:T(8,128)(2,1)S(1)}, bf16[2,12,128,128]{3,2,1,0:T(8,128)(2,1)S(1)}, u32[]{:S(2)}, u32[]{:S(2)}) %collective-permute-start) | collective-permute-done | bytes 786464 | tf_op jit(solution)/shard_map/ppermute | solution.py:30
  54.0 0.8 slice_bitcast_fusion.1
  55.0 1.8 %slice_bitcast_fusion = bf16[12,128,128]{2,1,0:T(8,128)(2,1)} fusion(bf16[2,12,128,128]{3,2,1,0:T(8,128)(2,1)} %collective-permute-done.2.refs_2_.refs_3_), kind=kLoop, calls=%fused_computation.9 | loop fusion | bytes 786432 | tf_op jit(solution)/shard_map/squeeze | solution.py:377
  56.8 3.0 %collective-permute-start.3 = (bf16[12,128,128]{2,1,0:T(8,128)(2,1)}, bf16[12,128,128]{2,1,0:T(8,128)(2,1)S(1)}, u32[]{:S(2)}, u32[]{:S(2)}) collective-permute-start(bf16[12,128,128]{2,1,0:T(8,128)(2,1)} %slice_bitcast_fusion), channel_id=1, source_target_pairs={{0,192},{64,0},{128,64},{192,128},{1,193},{65,1},{129,65},{193,129... | collective-permute-start | bytes 1179656 | tf_op jit(solution)/shard_map/ppermute | solution.py:30
  60.1 2.4 %collective-permute-start.5 = (bf16[12,128,128]{2,1,0:T(8,128)(2,1)S(1)}, bf16[12,128,128]{2,1,0:T(8,128)(2,1)}, u32[]{:S(2)}, u32[]{:S(2)}) collective-permute-start(bf16[12,128,128]{2,1,0:T(8,128)(2,1)S(1)} %bitcast.26), channel_id=1, source_target_pairs={{0,12},{4,0},{8,4},{12,8},{1,13},{5,1},{9,5},{13,9},{2,14},{6,2},{... | collective-permute-start | bytes 1179656 | tf_op jit(solution)/shard_map/ppermute | solution.py:30
  62.6 6.6 %near.1 = (f32[12,1,128]{2,1,0:T(1,128)S(1)}, f32[12,8,128]{2,1,0:T(8,128)S(1)}, f32[12,128,128]{2,1,0:T(8,128)S(1)}) custom-call(s32[48,52]{1,0:T(8,128)S(1)} %copy.12.lists, s32[48]{0:T(128)S(1)} %get-tuple-element.24.nears, s32[48]{0:T(128)S(1)} %get-tuple-element.25.counts, bf16[12,128,128]{2,1,0:T(8,128)(2,1)S(1)} %bitcast.28, ...), custom_call_target="tpu_custom_call" | custom-call | flops 1207959552 | bytes 5242880 | tf_op jit(solution)/shard_map/near/pallas_call | solution.py:252
  69.2 3.5 %far.1 = (bf16[12,144,128]{2,1,0:T(8,128)(2,1)S(1)}, f32[12,128]{1,0:T(8,128)S(1)}) custom-call(s32[48,52]{1,0:T(8,128)S(1)} %copy.12.lists, s32[48]{0:T(128)S(1)} %get-tuple-element.24.nears, s32[48]{0:T(128)S(1)} %get-tuple-element.25.counts, bf16[12,128,128]{2,1,0:T(8,128)(2,1)S(1)} %bitcast.29, ...), custom_call_target="tpu_custom_call" | custom-call | flops 402653184 | bytes 5242880 | tf_op jit(solution)/shard_map/far/pallas_call | solution.py:252
  72.7 0.7 collective-permute-done.4.refs_0_
  73.4 7.4 %collective-permute-done.5.refs_0_ = bf16[12,128,128]{2,1,0:T(8,128)(2,1)} collective-permute-done((bf16[12,128,128]{2,1,0:T(8,128)(2,1)S(1)}, bf16[12,128,128]{2,1,0:T(8,128)(2,1)}, u32[]{:S(2)}, u32[]{:S(2)}) %collective-permute-start.5) | collective-permute-done | bytes 393248 | tf_op jit(solution)/shard_map/ppermute | solution.py:30
  80.8 1.0 collective-permute-done.6.refs_1_
  81.8 12.0 %full.2 = (bf16[12,144,128]{2,1,0:T(8,128)(2,1)S(1)}, bf16[12,144,128]{2,1,0:T(8,128)(2,1)S(1)}, f32[12,128]{1,0:T(8,128)S(1)}, f32[12,128]{1,0:T(8,128)S(1)}) custom-call(s32[48,52]{1,0:T(8,128)S(1)} %copy.12.lists, s32[48]{0:T(128)S(1)} %get-tuple-element.24.nears, s32[48]{0:T(128)S(1)} %get-tuple-element.25.counts, ...), custom_call_target="tpu_custom_call" | custom-call | flops 3221225472 | bytes 5242880 | tf_op jit(solution)/shard_map/full/pallas_call | solution.py:252
  93.8 3.8 %collective-permute-start.7 = (bf16[12,144,128]{2,1,0:T(8,128)(2,1)S(1)}, bf16[12,144,128]{2,1,0:T(8,128)(2,1)S(1)}, u32[]{:S(2)}, u32[]{:S(2)}) collective-permute-start(bf16[12,144,128]{2,1,0:T(8,128)(2,1)S(1)} %get-tuple-element.40), channel_id=1, source_target_pairs={{0,4},{4,8},{8,12},{12,0},{1,5},{5,9},{9,13},{13,1},{2,6},{6,10},{... | collective-permute-start | bytes 1327112 | tf_op jit(solution)/shard_map/ppermute | solution.py:30
  97.6 8.5 %full.3 = (bf16[12,144,128]{2,1,0:T(8,128)(2,1)S(1)}, f32[12,128]{1,0:T(8,128)S(1)}) custom-call(s32[48,52]{1,0:T(8,128)S(1)} %copy.12.lists, s32[48]{0:T(128)S(1)} %get-tuple-element.24.nears, s32[48]{0:T(128)S(1)} %get-tuple-element.25.counts, bf16[12,128,128]{2,1,0:T(8,128)(2,1)} %collective-permute-done.4.refs_0_, ...), custom_call_target="tpu_custom_call" | custom-call | flops 1610612736 | bytes 5242880 | tf_op jit(solution)/shard_map/full/pallas_call | solution.py:252
  106.2 1.5 collective-permute-start.9
  107.7 0.7 pick.1
  108.3 19.2 %all_to_all.20.parts = f32[16,12,128]{2,1,0:T(8,128)S(1)} all-to-all(f32[16,12,128]{2,1,0:T(8,128)S(1)} %pick.1), channel_id=1, replica_groups=mesh['x'=4,'zh'=4,'y'=4,'zl'=2,'core'=2] {'x','y'}, dimensions={0} | all-to-all | bytes 196608 | tf_op jit(solution)/shard_map/all_to_all | solution.py:385
  127.6 1.2 combine.1
  128.8 3.6 %all-to-all-start.3 = ((bf16[16,96,128]{2,1,0:T(8,128)(2,1)}), bf16[16,96,128]{2,1,0:T(8,128)(2,1)S(1)}, u32[]{:S(2)}, u32[]{:S(2)}) async-start(bf16[16,96,128]{2,1,0:T(8,128)(2,1)} %bitcast.4), calls=%async_computation.3 | async-start | bytes 786432 | tf_op jit(solution)/shard_map/all_to_all | solution.py:364
  132.5 9.7 %collective-permute-start.10 = (f32[1,1536]{1,0:T(1,128)S(1)}, f32[1,1536]{1,0:T(1,128)S(1)}, u32[]{:S(2)}, u32[]{:S(2)}) collective-permute-start(f32[1,1536]{1,0:T(1,128)S(1)} %bitcast.31), channel_id=1, source_target_pairs={{0,0},{16,4},{32,8},{48,12},{4,16},{20,20},{36,24},{52,28},{8,32},... | collective-permute-start | bytes 18440 | tf_op jit(solution)/shard_map/ppermute | solution.py:393
  142.1 7.8 %collective-permute-done.10 = f32[1,1536]{1,0:T(1,128)S(1)} collective-permute-done((f32[1,1536]{1,0:T(1,128)S(1)}, f32[1,1536]{1,0:T(1,128)S(1)}, u32[]{:S(2)}, u32[]{:S(2)}) %collective-permute-start.10) | collective-permute-done | bytes 6176 | tf_op jit(solution)/shard_map/ppermute | solution.py:393
  149.9 0.8 copy_bitcast_fusion
  150.7 0.6 copy.24
  (34 shorter events, 1.8 us)
Async XLA Ops:
  0.6 14.6 %copy-start = (bf16[96,2048]{1,0:T(8,128)(2,1)S(1)}, bf16[96,2048]{1,0:T(8,128)(2,1)}, u32[]{:S(2)}) copy-start(bf16[96,2048]{1,0:T(8,128)(2,1)} %param.6) | copy-start | bytes 1179652
  0.6 1.0 copy-start.1
  1.7 1.0 copy-start.2
  4.1 8.8 %copy-start.6 = (s32[192]{0:T(256)S(1)}, s32[192]{0:T(256)}, u32[]{:S(2)}) copy-start(s32[192]{0:T(256)} %param.10) | copy-start | bytes 2308
  4.1 8.8 %copy-start.4 = (s32[192,96]{1,0:T(8,128)S(1)}, s32[192,96]{1,0:T(8,128)}, u32[]{:S(2)}) copy-start(s32[192,96]{1,0:T(8,128)} %param.9) | copy-start | bytes 221188
  4.2 11.1 %copy-start.5 = (s32[192]{0:T(256)S(1)}, s32[192]{0:T(256)}, u32[]{:S(2)}) copy-start(s32[192]{0:T(256)} %param.11) | copy-start | bytes 2308
  4.2 29.4 %all-to-all-start = ((bf16[16,2,96,128]{3,2,1,0:T(8,128)(2,1)}), bf16[16,2,96,128]{3,2,1,0:T(8,128)(2,1)S(1)}, u32[]{:S(2)}, u32[]{:S(2)}) async-start(bf16[16,2,96,128]{3,2,1,0:T(8,128)(2,1)} %spread.1), calls=%async_computation | async-start | bytes 1572864 | tf_op jit(solution)/shard_map/all_to_all | solution.py:364
  33.7 20.2 %collective-permute-start = (bf16[2,12,128,128]{3,2,1,0:T(8,128)(2,1)S(1)}, bf16[2,12,128,128]{3,2,1,0:T(8,128)(2,1)S(1)}, u32[]{:S(2)}, u32[]{:S(2)}) collective-permute-start(bf16[2,12,128,128]{3,2,1,0:T(8,128)(2,1)S(1)} %prepare.1.refs_1_.refs_2_), channel_id=1, source_target_pairs={{0,64},{64,128},{128,192},{192,0},{1,65},{65,129},{129,193},{193,1... | collective-permute-start | bytes 2359304 | tf_op jit(solution)/shard_map/ppermute | solution.py:30
  35.3 19.7 %collective-permute-start.2 = (bf16[2,12,128,128]{3,2,1,0:T(8,128)(2,1)S(1)}, bf16[2,12,128,128]{3,2,1,0:T(8,128)(2,1)}, u32[]{:S(2)}, u32[]{:S(2)}) collective-permute-start(bf16[2,12,128,128]{3,2,1,0:T(8,128)(2,1)S(1)} %prepare.1.refs_1_.refs_2_), channel_id=1, source_target_pairs={{0,192},{64,0},{128,64},{192,128},{1,193},{65,1},{129,65},{193,129... | collective-permute-start | bytes 2359304 | tf_op jit(solution)/shard_map/ppermute | solution.py:30
  37.0 22.7 %all-to-all-start.1 = ((bf16[16,96,128]{2,1,0:T(8,128)(2,1)}), bf16[16,96,128]{2,1,0:T(8,128)(2,1)S(1)}, u32[]{:S(2)}, u32[]{:S(2)}) async-start(bf16[16,96,128]{2,1,0:T(8,128)(2,1)} %bitcast_bitcast_fusion), calls=%async_computation.1 | async-start | bytes 786432 | tf_op jit(solution)/shard_map/all_to_all | solution.py:364
  42.2 20.3 %copy-start.3 = (s32[48,52]{0,1:T(8,128)S(1)}, s32[48,52]{0,1:T(8,128)}, u32[]{:S(2)}) copy-start(s32[48,52]{0,1:T(8,128)} %select_reduce_fusion) | copy-start | bytes 29956
  54.7 14.5 %collective-permute-start.1 = (bf16[12,128,128]{2,1,0:T(8,128)(2,1)}, bf16[12,128,128]{2,1,0:T(8,128)(2,1)S(1)}, u32[]{:S(2)}, u32[]{:S(2)}) collective-permute-start(bf16[12,128,128]{2,1,0:T(8,128)(2,1)} %slice_bitcast_fusion.1), channel_id=1, source_target_pairs={{0,64},{64,128},{128,192},{192,0},{1,65},{65,129},{129,193},{193,1... | collective-permute-start | bytes 1179656 | tf_op jit(solution)/shard_map/ppermute | solution.py:30
  56.8 12.4 %collective-permute-start.3 = (bf16[12,128,128]{2,1,0:T(8,128)(2,1)}, bf16[12,128,128]{2,1,0:T(8,128)(2,1)S(1)}, u32[]{:S(2)}, u32[]{:S(2)}) collective-permute-start(bf16[12,128,128]{2,1,0:T(8,128)(2,1)} %slice_bitcast_fusion), channel_id=1, source_target_pairs={{0,192},{64,0},{128,64},{192,128},{1,193},{65,1},{129,65},{193,129... | collective-permute-start | bytes 1179656 | tf_op jit(solution)/shard_map/ppermute | solution.py:30
  59.8 13.6 %collective-permute-start.4 = (bf16[12,128,128]{2,1,0:T(8,128)(2,1)S(1)}, bf16[12,128,128]{2,1,0:T(8,128)(2,1)}, u32[]{:S(2)}, u32[]{:S(2)}) collective-permute-start(bf16[12,128,128]{2,1,0:T(8,128)(2,1)S(1)} %bitcast.25), channel_id=1, source_target_pairs={{0,8},{4,12},{8,0},{12,4},{1,9},{5,13},{9,1},{13,5},{2,10},{6,14},... | collective-permute-start | bytes 1179656 | tf_op jit(solution)/shard_map/ppermute | solution.py:30
  60.1 20.7 %collective-permute-start.5 = (bf16[12,128,128]{2,1,0:T(8,128)(2,1)S(1)}, bf16[12,128,128]{2,1,0:T(8,128)(2,1)}, u32[]{:S(2)}, u32[]{:S(2)}) collective-permute-start(bf16[12,128,128]{2,1,0:T(8,128)(2,1)S(1)} %bitcast.26), channel_id=1, source_target_pairs={{0,12},{4,0},{8,4},{12,8},{1,13},{5,1},{9,5},{13,9},{2,14},{6,2},{... | collective-permute-start | bytes 1179656 | tf_op jit(solution)/shard_map/ppermute | solution.py:30
  62.5 19.3 %collective-permute-start.6 = (bf16[12,128,128]{2,1,0:T(8,128)(2,1)S(1)}, bf16[12,128,128]{2,1,0:T(8,128)(2,1)}, u32[]{:S(2)}, u32[]{:S(2)}) collective-permute-start(bf16[12,128,128]{2,1,0:T(8,128)(2,1)S(1)} %bitcast.27), channel_id=1, source_target_pairs={{0,4},{4,8},{8,12},{12,0},{1,5},{5,9},{9,13},{13,1},{2,6},{6,10},{... | collective-permute-start | bytes 1179656 | tf_op jit(solution)/shard_map/ppermute | solution.py:30
  93.8 33.8 %collective-permute-start.7 = (bf16[12,144,128]{2,1,0:T(8,128)(2,1)S(1)}, bf16[12,144,128]{2,1,0:T(8,128)(2,1)S(1)}, u32[]{:S(2)}, u32[]{:S(2)}) collective-permute-start(bf16[12,144,128]{2,1,0:T(8,128)(2,1)S(1)} %get-tuple-element.40), channel_id=1, source_target_pairs={{0,4},{4,8},{8,12},{12,0},{1,5},{5,9},{9,13},{13,1},{2,6},{6,10},{... | collective-permute-start | bytes 1327112 | tf_op jit(solution)/shard_map/ppermute | solution.py:30
  106.1 21.5 %collective-permute-start.8 = (bf16[12,144,128]{2,1,0:T(8,128)(2,1)S(1)}, bf16[12,144,128]{2,1,0:T(8,128)(2,1)S(1)}, u32[]{:S(2)}, u32[]{:S(2)}) collective-permute-start(bf16[12,144,128]{2,1,0:T(8,128)(2,1)S(1)} %get-tuple-element.41), channel_id=1, source_target_pairs={{0,8},{4,12},{8,0},{12,4},{1,9},{5,13},{9,1},{13,5},{2,10},{6,14},... | collective-permute-start | bytes 1327112 | tf_op jit(solution)/shard_map/ppermute | solution.py:30
  106.2 21.4 %collective-permute-start.9 = (bf16[12,144,128]{2,1,0:T(8,128)(2,1)S(1)}, bf16[12,144,128]{2,1,0:T(8,128)(2,1)S(1)}, u32[]{:S(2)}, u32[]{:S(2)}) collective-permute-start(bf16[12,144,128]{2,1,0:T(8,128)(2,1)S(1)} %get-tuple-element.42), channel_id=1, source_target_pairs={{0,12},{4,0},{8,4},{12,8},{1,13},{5,1},{9,5},{13,9},{2,14},{6,2},{... | collective-permute-start | bytes 1327112 | tf_op jit(solution)/shard_map/ppermute | solution.py:30
  128.8 21.1 %all-to-all-start.3 = ((bf16[16,96,128]{2,1,0:T(8,128)(2,1)}), bf16[16,96,128]{2,1,0:T(8,128)(2,1)S(1)}, u32[]{:S(2)}, u32[]{:S(2)}) async-start(bf16[16,96,128]{2,1,0:T(8,128)(2,1)} %bitcast.4), calls=%async_computation.3 | async-start | bytes 786432 | tf_op jit(solution)/shard_map/all_to_all | solution.py:364
  132.5 17.4 %collective-permute-start.10 = (f32[1,1536]{1,0:T(1,128)S(1)}, f32[1,1536]{1,0:T(1,128)S(1)}, u32[]{:S(2)}, u32[]{:S(2)}) collective-permute-start(f32[1,1536]{1,0:T(1,128)S(1)} %bitcast.31), channel_id=1, source_target_pairs={{0,0},{16,4},{32,8},{48,12},{4,16},{20,20},{36,24},{52,28},{8,32},... | collective-permute-start | bytes 18440 | tf_op jit(solution)/shard_map/ppermute | solution.py:393

commit v10 on v9

--- a/solution.py
+++ b/solution.py
@@ -32,32 +32,6 @@
 
 def around(array, axis):
     return [array] + [shift(array, axis, -by) for by in range(1, RING)]
-
-
-def spread_kernel(keys, values, out, sems):
-    copies = [
-        pltpu.make_async_copy(
-            array.at[:, pl.ds(head * HD, HD)], out.at[head, which], sems.at[which, head]
-        )
-        for which, array in enumerate((keys, values))
-        for head in range(16)
-    ]
-    for copy in copies:
-        copy.start()
-    for copy in copies:
-        copy.wait()
-
-
-def spread(keys, values):
-    return pl.pallas_call(
-        spread_kernel,
-        out_shape=jax.ShapeDtypeStruct((16, 2, 96, HD), jnp.bfloat16),
-        in_specs=[pl.BlockSpec(memory_space=pltpu.HBM)] * 2,
-        out_specs=VMEM,
-        scratch_shapes=[pltpu.SemaphoreType.DMA((2, 16))],
-        compiler_params=SPACE,
-        name="spread",
-    )(keys, values)
 
 
 def prepare_kernel(got_ref, kv_ref):
@@ -369,7 +343,8 @@
     lists = key_lists(kv_tiles, tile_count, xi, yi)
     spots = slot_spots(assign, xi, yi)
     by_head = jnp.transpose(queries.reshape(96, 16, HD), (1, 0, 2))
-    got = exchange(spread(keys, values))
+    sent = jnp.stack([a.reshape(96, 16, HD) for a in (keys, values)])
+    got = exchange(jnp.transpose(sent, (2, 0, 1, 3)))
     got, by_head, spots, *lists = lax.optimization_barrier((got, by_head, spots, *lists))
     kv0 = prepare(got)
     kv1, kv3 = shift(kv0, "x", -1), shift(kv0, "x", 1)
@@ -381,12 +356,15 @@
     q2, o0 = lax.optimization_barrier((q2, o0))
     kv = (kv0, kv1, kv3, k2, v2)
     o2, e2 = attend((2,), "full", lists, (q2,), kv)
+    q1, o2 = lax.optimization_barrier((q1, o2))
+    o2 = shift(o2, "y", 2)
     o1, o3, e1, e3 = attend((1, 3), "full", lists, (q1, q3), kv)
+    e1, o2 = lax.optimization_barrier((e1, o2))
     parts = lax.all_to_all(
         pick(spots, (e0, e1, e2, e3)), ("x", "y"), split_axis=0, concat_axis=0, tiled=True
     )
     o0, parts = lax.optimization_barrier((o0, parts))
-    blended = combine(e0, (o0, shift(o1, "y", 1), shift(o2, "y", 2), shift(o3, "y", -1)))
+    blended = combine(e0, (o0, shift(o1, "y", 1), o2, shift(o3, "y", -1)))
     back = exchange(blended.reshape(16, 96, HD))
     attended = jnp.transpose(back, (1, 0, 2)).reshape(96, 16 * HD)
     turned = [(b * RING + a, a * RING + b) for a in range(RING) for b in range(RING)]

time: 152 us -> 140 us (0.921)
  waiting for transfers between devices: 46.1 us -> 37.8 us
  blocking collectives: 19.2 us -> 13.3 us
    ppermute x10, waiting for transfers between devices: 20.8 us -> 12 us  [shift(): lax.ppermute(array, axis, [(i, (i + by) % RING) for i in range(RING)])]
    all_to_all x1, blocking collectives: 19.2 us -> 13.3 us  [on_device(): lax.all_to_all(pick(spots, (e0, e1, e2, e3)), ('x', 'y'), split_axis=0, c...]
    pallas_call x4, Pallas kernels: 30.6 us -> 33 us  [attend(): pl.pallas_call(functools.partial(attend_kernel, blocks, mode), out_shape=...]
    all_to_all x3, starting transfers between devices: 17.4 us -> 19.3 us  [exchange(): return lax.all_to_all(array, GROUP, split_axis=0, concat_axis=0, tiled=True)]
  transfers between devices with their start and end apart: 14 -> 14, of which waited for: 6 -> 4; matrix products, arithmetic and copies ran while one was open for 4% -> 4% of each run, Pallas kernels for 13% -> 24%
where the time goes in v10:
time: 140 us; the launch traced here: 139 us
  starting transfers between devices  42.6 us (30%)
  waiting for transfers between devices  37.8 us (27%)
  Pallas kernels  35.1 us (25%)
  blocking collectives  13.3 us (10%)
  local copies, waits for them, and re-layouts  6.34 us (5%)
  other arithmetic  2.32 us (2%)
    pallas_call x4, Pallas kernels, attend(): pl.pallas_call(functools.partial(attend_kernel, blocks, mode), out_shape=...  33 us
    all_to_all x3, starting transfers between devices, exchange(): return lax.all_to_all(array, GROUP, split_axis=0, concat_axis=0, tiled=True)  19.3 us
    all_to_all x3, waiting for transfers between devices, exchange(): return lax.all_to_all(array, GROUP, split_axis=0, concat_axis=0, tiled=True)  18.1 us
    ppermute x10, starting transfers between devices, shift(): lax.ppermute(array, axis, [(i, (i + by) % RING) for i in range(RING)])  14.1 us
    all_to_all x1, blocking collectives, on_device(): lax.all_to_all(pick(spots, (e0, e1, e2, e3)), ('x', 'y'), split_axis=0, c...  13.3 us
    ppermute x10, waiting for transfers between devices, shift(): lax.ppermute(array, axis, [(i, (i + by) % RING) for i in range(RING)])  12 us
    ppermute x1, starting transfers between devices, on_device(): lax.ppermute(merge(parts).reshape(1, OWN * BLK), ('zh', 'y'), turned)  9.19 us
    ppermute x1, waiting for transfers between devices, on_device(): lax.ppermute(merge(parts).reshape(1, OWN * BLK), ('zh', 'y'), turned)  7.78 us
  transfers between devices with their start and end apart: 14, of which 4 were waited for; matrix products, arithmetic and copies ran while one was open for 4% of the time, Pallas kernels for 24%

profile of v10, /device:TPU:16, one launch (start us, length us, event | category | flops | bytes accessed | tf_op | source)
XLA Modules:
  0.0 138.7 jit_solution(17177722679997441688)
XLA Ops:
  0.7 1.1 copy.25
  2.1 1.0 maximum_bitcast_fusion
  3.1 8.7 %all-to-all-start = ((bf16[16,2,96,128]{3,2,1,0:T(8,128)(2,1)}), bf16[16,2,96,128]{3,2,1,0:T(8,128)(2,1)S(1)}, u32[]{:S(2)}, u32[]{:S(2)}) async-start(bf16[16,2,96,128]{3,2,1,0:T(8,128)(2,1)} %maximum_bitcast_fusion), calls=%async_computation | async-start | bytes 1572864 | tf_op jit(solution)/shard_map/all_to_all | solution.py:338
  12.1 0.2 convert_reduce_fusion.1
  12.5 1.0 select_reduce_fusion
  13.6 0.8 bitcast_bitcast_fusion
  14.4 18.1 %all-to-all-done.got_ref = bf16[16,2,96,128]{3,2,1,0:T(8,128)(2,1)S(1)} async-done(((bf16[16,2,96,128]{3,2,1,0:T(8,128)(2,1)}), bf16[16,2,96,128]{3,2,1,0:T(8,128)(2,1)S(1)}, u32[]{:S(2)}, u32[]{:S(2)}) %all-to-all-start) | async-done | bytes 786464 | tf_op jit(solution)/shard_map/all_to_all | solution.py:338
  32.6 1.6 %collective-permute-start = (bf16[2,12,128,128]{3,2,1,0:T(8,128)(2,1)S(1)}, bf16[2,12,128,128]{3,2,1,0:T(8,128)(2,1)S(1)}, u32[]{:S(2)}, u32[]{:S(2)}) collective-permute-start(bf16[2,12,128,128]{3,2,1,0:T(8,128)(2,1)S(1)} %prepare.1.refs_1_.refs_2_), channel_id=1, source_target_pairs={{0,64},{64,128},{128,192},{192,0},{1,65},{65,129},{129,193},{193,1... | collective-permute-start | bytes 2359304 | tf_op jit(solution)/shard_map/ppermute | solution.py:30
  34.2 1.7 %collective-permute-start.2 = (bf16[2,12,128,128]{3,2,1,0:T(8,128)(2,1)S(1)}, bf16[2,12,128,128]{3,2,1,0:T(8,128)(2,1)}, u32[]{:S(2)}, u32[]{:S(2)}) collective-permute-start(bf16[2,12,128,128]{3,2,1,0:T(8,128)(2,1)S(1)} %prepare.1.refs_1_.refs_2_), channel_id=1, source_target_pairs={{0,192},{64,0},{128,64},{192,128},{1,193},{65,1},{129,65},{193,129... | collective-permute-start | bytes 2359304 | tf_op jit(solution)/shard_map/ppermute | solution.py:30
  35.9 5.1 %all-to-all-start.1 = ((bf16[16,96,128]{2,1,0:T(8,128)(2,1)}), bf16[16,96,128]{2,1,0:T(8,128)(2,1)S(1)}, u32[]{:S(2)}, u32[]{:S(2)}) async-start(bf16[16,96,128]{2,1,0:T(8,128)(2,1)} %bitcast_bitcast_fusion), calls=%async_computation.1 | async-start | bytes 786432 | tf_op jit(solution)/shard_map/all_to_all | solution.py:338
  41.1 11.8 %collective-permute-done.refs_3_.refs_4_ = bf16[2,12,128,128]{3,2,1,0:T(8,128)(2,1)S(1)} collective-permute-done((bf16[2,12,128,128]{3,2,1,0:T(8,128)(2,1)S(1)}, bf16[2,12,128,128]{3,2,1,0:T(8,128)(2,1)S(1)}, u32[]{:S(2)}, u32[]{:S(2)}) %collective-permute-start) | collective-permute-done | bytes 786464 | tf_op jit(solution)/shard_map/ppermute | solution.py:30
  52.9 0.8 slice_bitcast_fusion.1
  53.6 0.3 collective-permute-start.1
  53.9 1.8 %slice_bitcast_fusion = bf16[12,128,128]{2,1,0:T(8,128)(2,1)} fusion(bf16[2,12,128,128]{3,2,1,0:T(8,128)(2,1)} %collective-permute-done.2.refs_2_.refs_3_), kind=kLoop, calls=%fused_computation.10 | loop fusion | bytes 786432 | tf_op jit(solution)/shard_map/squeeze | solution.py:352
  55.7 3.0 %collective-permute-start.3 = (bf16[12,128,128]{2,1,0:T(8,128)(2,1)}, bf16[12,128,128]{2,1,0:T(8,128)(2,1)S(1)}, u32[]{:S(2)}, u32[]{:S(2)}) collective-permute-start(bf16[12,128,128]{2,1,0:T(8,128)(2,1)} %slice_bitcast_fusion), channel_id=1, source_target_pairs={{0,192},{64,0},{128,64},{192,128},{1,193},{65,1},{129,65},{193,129... | collective-permute-start | bytes 1179656 | tf_op jit(solution)/shard_map/ppermute | solution.py:30
  58.7 0.3 collective-permute-start.4
  59.0 2.4 %collective-permute-start.5 = (bf16[12,128,128]{2,1,0:T(8,128)(2,1)S(1)}, bf16[12,128,128]{2,1,0:T(8,128)(2,1)}, u32[]{:S(2)}, u32[]{:S(2)}) collective-permute-start(bf16[12,128,128]{2,1,0:T(8,128)(2,1)S(1)} %bitcast.34), channel_id=1, source_target_pairs={{0,12},{4,0},{8,4},{12,8},{1,13},{5,1},{9,5},{13,9},{2,14},{6,2},{... | collective-permute-start | bytes 1179656 | tf_op jit(solution)/shard_map/ppermute | solution.py:30
  61.5 7.6 %near.1 = (f32[12,1,128]{2,1,0:T(1,128)S(1)}, f32[12,8,128]{2,1,0:T(8,128)S(1)}, f32[12,128,128]{2,1,0:T(8,128)S(1)}) custom-call(s32[48,52]{1,0:T(8,128)S(1)} %copy.18.lists, s32[48]{0:T(128)S(1)} %get-tuple-element.28.nears, s32[48]{0:T(128)S(1)} %get-tuple-element.29.counts, bf16[12,128,128]{2,1,0:T(8,128)(2,1)S(1)} %bitcast.36, ...), custom_call_target="tpu_custom_call" | custom-call | flops 1207959552 | bytes 5242880 | tf_op jit(solution)/shard_map/near/pallas_call | solution.py:226
  69.1 3.0 %far.1 = (bf16[12,144,128]{2,1,0:T(8,128)(2,1)S(1)}, f32[12,128]{1,0:T(8,128)S(1)}) custom-call(s32[48,52]{1,0:T(8,128)S(1)} %copy.18.lists, s32[48]{0:T(128)S(1)} %get-tuple-element.28.nears, s32[48]{0:T(128)S(1)} %get-tuple-element.29.counts, bf16[12,128,128]{2,1,0:T(8,128)(2,1)S(1)} %bitcast.37, ...), custom_call_target="tpu_custom_call" | custom-call | flops 402653184 | bytes 5242880 | tf_op jit(solution)/shard_map/far/pallas_call | solution.py:226
  72.3 8.8 %full.2 = (bf16[12,144,128]{2,1,0:T(8,128)(2,1)S(1)}, f32[12,128]{1,0:T(8,128)S(1)}) custom-call(s32[48,52]{1,0:T(8,128)S(1)} %copy.18.lists, s32[48]{0:T(128)S(1)} %get-tuple-element.28.nears, s32[48]{0:T(128)S(1)} %get-tuple-element.29.counts, bf16[12,128,128]{2,1,0:T(8,128)(2,1)} %collective-permute-done.4.refs_0_, ...), custom_call_target="tpu_custom_call" | custom-call | flops 1610612736 | bytes 5242880 | tf_op jit(solution)/shard_map/full/pallas_call | solution.py:226
  81.1 2.7 %collective-permute-start.7 = (bf16[12,144,128]{2,1,0:T(8,128)(2,1)S(1)}, bf16[12,144,128]{2,1,0:T(8,128)(2,1)S(1)}, u32[]{:S(2)}, u32[]{:S(2)}) collective-permute-start(bf16[12,144,128]{2,1,0:T(8,128)(2,1)S(1)} %get-tuple-element.43), channel_id=1, source_target_pairs={{0,8},{4,12},{8,0},{12,4},{1,9},{5,13},{9,1},{13,5},{2,10},{6,14},... | collective-permute-start | bytes 1327112 | tf_op jit(solution)/shard_map/ppermute | solution.py:30
  83.9 13.6 %full.3 = (bf16[12,144,128]{2,1,0:T(8,128)(2,1)S(1)}, bf16[12,144,128]{2,1,0:T(8,128)(2,1)S(1)}, f32[12,128]{1,0:T(8,128)S(1)}, f32[12,128]{1,0:T(8,128)S(1)}) custom-call(s32[48,52]{1,0:T(8,128)S(1)} %copy.18.lists, s32[48]{0:T(128)S(1)} %get-tuple-element.28.nears, s32[48]{0:T(128)S(1)} %get-tuple-element.29.counts, ...), custom_call_target="tpu_custom_call" | custom-call | flops 3221225472 | bytes 5242880 | tf_op jit(solution)/shard_map/full/pallas_call | solution.py:226
  97.5 0.9 collective-permute-start.8
  98.4 1.2 collective-permute-start.9
  99.6 0.7 pick.1
  100.3 13.3 %all_to_all.20.parts = f32[16,12,128]{2,1,0:T(8,128)S(1)} all-to-all(f32[16,12,128]{2,1,0:T(8,128)S(1)} %pick.1), channel_id=1, replica_groups=mesh['x'=4,'zh'=4,'y'=4,'zl'=2,'core'=2] {'x','y'}, dimensions={0} | all-to-all | bytes 196608 | tf_op jit(solution)/shard_map/all_to_all | solution.py:363
  113.5 1.2 combine.1
  114.8 5.4 %all-to-all-start.3 = ((bf16[16,96,128]{2,1,0:T(8,128)(2,1)}), bf16[16,96,128]{2,1,0:T(8,128)(2,1)S(1)}, u32[]{:S(2)}, u32[]{:S(2)}) async-start(bf16[16,96,128]{2,1,0:T(8,128)(2,1)} %bitcast.5), calls=%async_computation.3 | async-start | bytes 786432 | tf_op jit(solution)/shard_map/all_to_all | solution.py:338
  120.3 9.2 %collective-permute-start.10 = (f32[1,1536]{1,0:T(1,128)S(1)}, f32[1,1536]{1,0:T(1,128)S(1)}, u32[]{:S(2)}, u32[]{:S(2)}) collective-permute-start(f32[1,1536]{1,0:T(1,128)S(1)} %bitcast.43), channel_id=1, source_target_pairs={{0,0},{16,4},{32,8},{48,12},{4,16},{20,20},{36,24},{52,28},{8,32},... | collective-permute-start | bytes 18440 | tf_op jit(solution)/shard_map/ppermute | solution.py:371
  129.5 7.8 %collective-permute-done.10 = f32[1,1536]{1,0:T(1,128)S(1)} collective-permute-done((f32[1,1536]{1,0:T(1,128)S(1)}, f32[1,1536]{1,0:T(1,128)S(1)}, u32[]{:S(2)}, u32[]{:S(2)}) %collective-permute-start.10) | collective-permute-done | bytes 6176 | tf_op jit(solution)/shard_map/ppermute | solution.py:371
  137.3 0.8 copy_bitcast_fusion
  138.1 0.6 copy.32
  (34 shorter events, 1.4 us)
Async XLA Ops:
  0.6 12.9 %copy-start = (bf16[96,2048]{1,0:T(8,128)(2,1)S(1)}, bf16[96,2048]{1,0:T(8,128)(2,1)}, u32[]{:S(2)}) copy-start(bf16[96,2048]{1,0:T(8,128)(2,1)} %param.6) | copy-start | bytes 1179652
  0.6 1.3 copy-start.1
  3.1 8.7 %copy-start.4 = (s32[192]{0:T(256)S(1)}, s32[192]{0:T(256)}, u32[]{:S(2)}) copy-start(s32[192]{0:T(256)} %param.10) | copy-start | bytes 2308
  3.1 8.8 %copy-start.2 = (s32[192,96]{1,0:T(8,128)S(1)}, s32[192,96]{1,0:T(8,128)}, u32[]{:S(2)}) copy-start(s32[192,96]{1,0:T(8,128)} %param.9) | copy-start | bytes 221188
  3.1 10.4 %copy-start.3 = (s32[192]{0:T(256)S(1)}, s32[192]{0:T(256)}, u32[]{:S(2)}) copy-start(s32[192]{0:T(256)} %param.11) | copy-start | bytes 2308
  3.1 29.4 %all-to-all-start = ((bf16[16,2,96,128]{3,2,1,0:T(8,128)(2,1)}), bf16[16,2,96,128]{3,2,1,0:T(8,128)(2,1)S(1)}, u32[]{:S(2)}, u32[]{:S(2)}) async-start(bf16[16,2,96,128]{3,2,1,0:T(8,128)(2,1)} %maximum_bitcast_fusion), calls=%async_computation | async-start | bytes 1572864 | tf_op jit(solution)/shard_map/all_to_all | solution.py:338
  32.6 20.2 %collective-permute-start = (bf16[2,12,128,128]{3,2,1,0:T(8,128)(2,1)S(1)}, bf16[2,12,128,128]{3,2,1,0:T(8,128)(2,1)S(1)}, u32[]{:S(2)}, u32[]{:S(2)}) collective-permute-start(bf16[2,12,128,128]{3,2,1,0:T(8,128)(2,1)S(1)} %prepare.1.refs_1_.refs_2_), channel_id=1, source_target_pairs={{0,64},{64,128},{128,192},{192,0},{1,65},{65,129},{129,193},{193,1... | collective-permute-start | bytes 2359304 | tf_op jit(solution)/shard_map/ppermute | solution.py:30
  34.2 19.7 %collective-permute-start.2 = (bf16[2,12,128,128]{3,2,1,0:T(8,128)(2,1)S(1)}, bf16[2,12,128,128]{3,2,1,0:T(8,128)(2,1)}, u32[]{:S(2)}, u32[]{:S(2)}) collective-permute-start(bf16[2,12,128,128]{3,2,1,0:T(8,128)(2,1)S(1)} %prepare.1.refs_1_.refs_2_), channel_id=1, source_target_pairs={{0,192},{64,0},{128,64},{192,128},{1,193},{65,1},{129,65},{193,129... | collective-permute-start | bytes 2359304 | tf_op jit(solution)/shard_map/ppermute | solution.py:30
  35.9 22.7 %all-to-all-start.1 = ((bf16[16,96,128]{2,1,0:T(8,128)(2,1)}), bf16[16,96,128]{2,1,0:T(8,128)(2,1)S(1)}, u32[]{:S(2)}, u32[]{:S(2)}) async-start(bf16[16,96,128]{2,1,0:T(8,128)(2,1)} %bitcast_bitcast_fusion), calls=%async_computation.1 | async-start | bytes 786432 | tf_op jit(solution)/shard_map/all_to_all | solution.py:338
  53.6 15.4 %collective-permute-start.1 = (bf16[12,128,128]{2,1,0:T(8,128)(2,1)}, bf16[12,128,128]{2,1,0:T(8,128)(2,1)S(1)}, u32[]{:S(2)}, u32[]{:S(2)}) collective-permute-start(bf16[12,128,128]{2,1,0:T(8,128)(2,1)} %slice_bitcast_fusion.1), channel_id=1, source_target_pairs={{0,64},{64,128},{128,192},{192,0},{1,65},{65,129},{129,193},{193,1... | collective-permute-start | bytes 1179656 | tf_op jit(solution)/shard_map/ppermute | solution.py:30
  55.7 13.4 %collective-permute-start.3 = (bf16[12,128,128]{2,1,0:T(8,128)(2,1)}, bf16[12,128,128]{2,1,0:T(8,128)(2,1)S(1)}, u32[]{:S(2)}, u32[]{:S(2)}) collective-permute-start(bf16[12,128,128]{2,1,0:T(8,128)(2,1)} %slice_bitcast_fusion), channel_id=1, source_target_pairs={{0,192},{64,0},{128,64},{192,128},{1,193},{65,1},{129,65},{193,129... | collective-permute-start | bytes 1179656 | tf_op jit(solution)/shard_map/ppermute | solution.py:30
  58.7 13.6 %collective-permute-start.4 = (bf16[12,128,128]{2,1,0:T(8,128)(2,1)S(1)}, bf16[12,128,128]{2,1,0:T(8,128)(2,1)}, u32[]{:S(2)}, u32[]{:S(2)}) collective-permute-start(bf16[12,128,128]{2,1,0:T(8,128)(2,1)S(1)} %bitcast.33), channel_id=1, source_target_pairs={{0,8},{4,12},{8,0},{12,4},{1,9},{5,13},{9,1},{13,5},{2,10},{6,14},... | collective-permute-start | bytes 1179656 | tf_op jit(solution)/shard_map/ppermute | solution.py:30
  59.0 22.1 %collective-permute-start.5 = (bf16[12,128,128]{2,1,0:T(8,128)(2,1)S(1)}, bf16[12,128,128]{2,1,0:T(8,128)(2,1)}, u32[]{:S(2)}, u32[]{:S(2)}) collective-permute-start(bf16[12,128,128]{2,1,0:T(8,128)(2,1)S(1)} %bitcast.34), channel_id=1, source_target_pairs={{0,12},{4,0},{8,4},{12,8},{1,13},{5,1},{9,5},{13,9},{2,14},{6,2},{... | collective-permute-start | bytes 1179656 | tf_op jit(solution)/shard_map/ppermute | solution.py:30
  61.4 22.4 %collective-permute-start.6 = (bf16[12,128,128]{2,1,0:T(8,128)(2,1)S(1)}, bf16[12,128,128]{2,1,0:T(8,128)(2,1)}, u32[]{:S(2)}, u32[]{:S(2)}) collective-permute-start(bf16[12,128,128]{2,1,0:T(8,128)(2,1)S(1)} %bitcast.35), channel_id=1, source_target_pairs={{0,4},{4,8},{8,12},{12,0},{1,5},{5,9},{9,13},{13,1},{2,6},{6,10},{... | collective-permute-start | bytes 1179656 | tf_op jit(solution)/shard_map/ppermute | solution.py:30
  81.1 18.5 %collective-permute-start.7 = (bf16[12,144,128]{2,1,0:T(8,128)(2,1)S(1)}, bf16[12,144,128]{2,1,0:T(8,128)(2,1)S(1)}, u32[]{:S(2)}, u32[]{:S(2)}) collective-permute-start(bf16[12,144,128]{2,1,0:T(8,128)(2,1)S(1)} %get-tuple-element.43), channel_id=1, source_target_pairs={{0,8},{4,12},{8,0},{12,4},{1,9},{5,13},{9,1},{13,5},{2,10},{6,14},... | collective-permute-start | bytes 1327112 | tf_op jit(solution)/shard_map/ppermute | solution.py:30
  97.5 16.0 %collective-permute-start.8 = (bf16[12,144,128]{2,1,0:T(8,128)(2,1)S(1)}, bf16[12,144,128]{2,1,0:T(8,128)(2,1)S(1)}, u32[]{:S(2)}, u32[]{:S(2)}) collective-permute-start(bf16[12,144,128]{2,1,0:T(8,128)(2,1)S(1)} %get-tuple-element.48), channel_id=1, source_target_pairs={{0,4},{4,8},{8,12},{12,0},{1,5},{5,9},{9,13},{13,1},{2,6},{6,10},{... | collective-permute-start | bytes 1327112 | tf_op jit(solution)/shard_map/ppermute | solution.py:30
  98.4 15.1 %collective-permute-start.9 = (bf16[12,144,128]{2,1,0:T(8,128)(2,1)S(1)}, bf16[12,144,128]{2,1,0:T(8,128)(2,1)S(1)}, u32[]{:S(2)}, u32[]{:S(2)}) collective-permute-start(bf16[12,144,128]{2,1,0:T(8,128)(2,1)S(1)} %get-tuple-element.50), channel_id=1, source_target_pairs={{0,12},{4,0},{8,4},{12,8},{1,13},{5,1},{9,5},{13,9},{2,14},{6,2},{... | collective-permute-start | bytes 1327112 | tf_op jit(solution)/shard_map/ppermute | solution.py:30
  114.8 22.5 %all-to-all-start.3 = ((bf16[16,96,128]{2,1,0:T(8,128)(2,1)}), bf16[16,96,128]{2,1,0:T(8,128)(2,1)S(1)}, u32[]{:S(2)}, u32[]{:S(2)}) async-start(bf16[16,96,128]{2,1,0:T(8,128)(2,1)} %bitcast.5), calls=%async_computation.3 | async-start | bytes 786432 | tf_op jit(solution)/shard_map/all_to_all | solution.py:338
  120.3 17.0 %collective-permute-start.10 = (f32[1,1536]{1,0:T(1,128)S(1)}, f32[1,1536]{1,0:T(1,128)S(1)}, u32[]{:S(2)}, u32[]{:S(2)}) collective-permute-start(f32[1,1536]{1,0:T(1,128)S(1)} %bitcast.43), channel_id=1, source_target_pairs={{0,0},{16,4},{32,8},{48,12},{4,16},{20,20},{36,24},{52,28},{8,32},... | collective-permute-start | bytes 18440 | tf_op jit(solution)/shard_map/ppermute | solution.py:371

commit v11 on v10

--- a/solution.py
+++ b/solution.py
@@ -34,22 +34,22 @@
     return [array] + [shift(array, axis, -by) for by in range(1, RING)]
 
 
-def prepare_kernel(got_ref, kv_ref):
+def prepare_kernel(got_ref, k_ref, vt_ref):
     for part in range(RING):
         k, v = (
             got_ref[4 * part : 4 * part + 4, which].reshape(3, BLK, HD) for which in range(2)
         )
-        kv_ref[0, 3 * part : 3 * part + 3] = k
+        k_ref[3 * part : 3 * part + 3] = k
         for i in range(3):
-            kv_ref[1, 3 * part + i] = v[i].T
+            vt_ref[3 * part + i] = v[i].T
 
 
 def prepare(got):
     return pl.pallas_call(
         prepare_kernel,
-        out_shape=jax.ShapeDtypeStruct((2, OWN, BLK, HD), jnp.bfloat16),
+        out_shape=(jax.ShapeDtypeStruct((OWN, BLK, HD), jnp.bfloat16),) * 2,
         in_specs=[VMEM],
-        out_specs=VMEM,
+        out_specs=(VMEM, VMEM),
         compiler_params=SPACE,
         name="prepare",
     )(got)
@@ -72,7 +72,7 @@
     tiles = count * OWN
     queries, refs = refs[:count], refs[count:]
     if mode != "far":
-        for_near, refs = refs[:3], refs[3:]
+        for_near, refs = refs[:6], refs[6:]
     if mode != "near":
         (k2, v2), refs = refs[:2], refs[2:]
     if mode == "far":
@@ -84,9 +84,9 @@
     for b, q in enumerate(queries):
         qs[b * OWN : (b + 1) * OWN] = q[...]
     if mode != "far":
-        for b, kv in enumerate(for_near):
-            ks[b * OWN : (b + 1) * OWN] = kv[0]
-            vs[b * OWN : (b + 1) * OWN] = kv[1]
+        for b in range(3):
+            ks[b * OWN : (b + 1) * OWN] = for_near[2 * b][...]
+            vs[b * OWN : (b + 1) * OWN] = for_near[2 * b + 1][...]
     if mode != "near":
         at = 0 if mode == "far" else NEAR
         ks[at : at + OWN] = k2[...]
@@ -346,15 +346,17 @@
     sent = jnp.stack([a.reshape(96, 16, HD) for a in (keys, values)])
     got = exchange(jnp.transpose(sent, (2, 0, 1, 3)))
     got, by_head, spots, *lists = lax.optimization_barrier((got, by_head, spots, *lists))
-    kv0 = prepare(got)
-    kv1, kv3 = shift(kv0, "x", -1), shift(kv0, "x", 1)
+    k0, v0 = prepare(got)
+    k3, v1 = shift(k0, "x", 1), shift(v0, "x", -1)
+    k1, v3 = shift(k0, "x", -1), shift(v0, "x", 1)
     q0 = exchange(by_head).reshape(OWN, BLK, HD)
-    k2, v2 = shift(kv3[0], "x", 1), shift(kv1[1], "x", -1)
+    k2, v2 = shift(k3, "x", 1), shift(v1, "x", -1)
     q0, q1, q2, q3 = around(q0, "y")
-    state = attend((0,), "near", lists, (q0,), (kv0, kv1, kv3))
+    near = (k0, v0, k1, v1, k3, v3)
+    state = attend((0,), "near", lists, (q0,), near)
     o0, e0 = attend((0,), "far", lists, (q0,), (k2, v2), state)
     q2, o0 = lax.optimization_barrier((q2, o0))
-    kv = (kv0, kv1, kv3, k2, v2)
+    kv = (*near, k2, v2)
     o2, e2 = attend((2,), "full", lists, (q2,), kv)
     q1, o2 = lax.optimization_barrier((q1, o2))
     o2 = shift(o2, "y", 2)

time: 140 us -> 146 us (1.043)
  starting transfers between devices: 42.6 us -> 46 us
    unnamed x14 -> x26, local copies, waits for them, and re-layouts: 1.83 us -> 5.33 us
    squeeze x2 -> x0, local copies, waits for them, and re-layouts: 2.56 us -> none  [on_device(): k2, v2 = (shift(kv3[0], 'x', 1), shift(kv1[1], 'x', -1))]
    all_to_all x3, starting transfers between devices: 19.3 us -> 21.1 us  [exchange(): return lax.all_to_all(array, GROUP, split_axis=0, concat_axis=0, tiled=True)]
    ppermute x10 -> x12, starting transfers between devices: 14.1 us -> 15.6 us  [shift(): lax.ppermute(array, axis, [(i, (i + by) % RING) for i in range(RING)])]
    ppermute x10 -> x12, waiting for transfers between devices: 12 us -> 13 us  [shift(): lax.ppermute(array, axis, [(i, (i + by) % RING) for i in range(RING)])]
  transfers between devices with their start and end apart: 14 -> 16, of which waited for: 4 -> 4; matrix products, arithmetic and copies ran while one was open for 4% -> 2% of each run, Pallas kernels for 24% -> 23%
where the time goes in v11:
time: 146 us; the launch traced here: 145 us
  starting transfers between devices  46 us (32%)
  waiting for transfers between devices  38.9 us (27%)
  Pallas kernels  35.1 us (24%)
  blocking collectives  13.9 us (10%)
  local copies, waits for them, and re-layouts  7.3 us (5%)
  other arithmetic  2.33 us (2%)
    pallas_call x4, Pallas kernels, attend(): pl.pallas_call(functools.partial(attend_kernel, blocks, mode), out_shape=...  33 us
    all_to_all x3, starting transfers between devices, exchange(): return lax.all_to_all(array, GROUP, split_axis=0, concat_axis=0, tiled=True)  21.1 us
    all_to_all x3, waiting for transfers between devices, exchange(): return lax.all_to_all(array, GROUP, split_axis=0, concat_axis=0, tiled=True)  18.1 us
    ppermute x12, starting transfers between devices, shift(): lax.ppermute(array, axis, [(i, (i + by) % RING) for i in range(RING)])  15.6 us
    all_to_all x1, blocking collectives, on_device(): lax.all_to_all(pick(spots, (e0, e1, e2, e3)), ('x', 'y'), split_axis=0, c...  13.9 us
    ppermute x12, waiting for transfers between devices, shift(): lax.ppermute(array, axis, [(i, (i + by) % RING) for i in range(RING)])  13 us
    ppermute x1, starting transfers between devices, on_device(): lax.ppermute(merge(parts).reshape(1, OWN * BLK), ('zh', 'y'), turned)  9.19 us
    ppermute x1, waiting for transfers between devices, on_device(): lax.ppermute(merge(parts).reshape(1, OWN * BLK), ('zh', 'y'), turned)  7.78 us
  transfers between devices with their start and end apart: 16, of which 4 were waited for; matrix products, arithmetic and copies ran while one was open for 2% of the time, Pallas kernels for 23%

profile of v11, /device:TPU:16, one launch (start us, length us, event | category | flops | bytes accessed | tf_op | source)
XLA Modules:
  0.0 144.7 jit_solution(14475961128246945538)
XLA Ops:
  0.7 1.1 copy.25
  2.1 1.0 maximum_bitcast_fusion
  3.1 8.7 %all-to-all-start = ((bf16[16,2,96,128]{3,2,1,0:T(8,128)(2,1)}), bf16[16,2,96,128]{3,2,1,0:T(8,128)(2,1)S(1)}, u32[]{:S(2)}, u32[]{:S(2)}) async-start(bf16[16,2,96,128]{3,2,1,0:T(8,128)(2,1)} %maximum_bitcast_fusion), calls=%async_computation | async-start | bytes 1572864 | tf_op jit(solution)/shard_map/all_to_all | solution.py:338
  12.6 1.0 select_reduce_fusion
  13.6 0.8 bitcast_bitcast_fusion
  14.4 18.1 %all-to-all-done.got_ref = bf16[16,2,96,128]{3,2,1,0:T(8,128)(2,1)S(1)} async-done(((bf16[16,2,96,128]{3,2,1,0:T(8,128)(2,1)}), bf16[16,2,96,128]{3,2,1,0:T(8,128)(2,1)S(1)}, u32[]{:S(2)}, u32[]{:S(2)}) %all-to-all-start) | async-done | bytes 786464 | tf_op jit(solution)/shard_map/all_to_all | solution.py:338
  32.5 5.1 %all-to-all-start.1 = ((bf16[16,96,128]{2,1,0:T(8,128)(2,1)}), bf16[16,96,128]{2,1,0:T(8,128)(2,1)S(1)}, u32[]{:S(2)}, u32[]{:S(2)}) async-start(bf16[16,96,128]{2,1,0:T(8,128)(2,1)} %bitcast_bitcast_fusion), calls=%async_computation.1 | async-start | bytes 786432 | tf_op jit(solution)/shard_map/all_to_all | solution.py:338
  37.8 1.6 %collective-permute-start = (bf16[12,128,128]{2,1,0:T(8,128)(2,1)S(1)}, bf16[12,128,128]{2,1,0:T(8,128)(2,1)}, u32[]{:S(2)}, u32[]{:S(2)}) collective-permute-start(bf16[12,128,128]{2,1,0:T(8,128)(2,1)S(1)} %get-tuple-element.34.refs_1_.refs_2_), channel_id=1, source_target_pairs={{0,64},{64,128},{128,192},{192,0},{1,65},{65,129},{129,193},{193,1... | collective-permute-start | bytes 1179656 | tf_op jit(solution)/shard_map/ppermute | solution.py:30
  39.4 1.7 %collective-permute-start.2 = (bf16[12,128,128]{2,1,0:T(8,128)(2,1)S(1)}, bf16[12,128,128]{2,1,0:T(8,128)(2,1)}, u32[]{:S(2)}, u32[]{:S(2)}) collective-permute-start(bf16[12,128,128]{2,1,0:T(8,128)(2,1)S(1)} %get-tuple-element.35.refs_2_.refs_3_), channel_id=1, source_target_pairs={{0,192},{64,0},{128,64},{192,128},{1,193},{65,1},{129,65},{193,129... | collective-permute-start | bytes 1179656 | tf_op jit(solution)/shard_map/ppermute | solution.py:30
  41.1 1.5 %collective-permute-start.4 = (bf16[12,128,128]{2,1,0:T(8,128)(2,1)S(1)}, bf16[12,128,128]{2,1,0:T(8,128)(2,1)S(1)}, u32[]{:S(2)}, u32[]{:S(2)}) collective-permute-start(bf16[12,128,128]{2,1,0:T(8,128)(2,1)S(1)} %get-tuple-element.34.refs_1_.refs_2_), channel_id=1, source_target_pairs={{0,192},{64,0},{128,64},{192,128},{1,193},{65,1},{129,65},{193,129... | collective-permute-start | bytes 1179656 | tf_op jit(solution)/shard_map/ppermute | solution.py:30
  43.1 8.0 %collective-permute-done.refs_5_.refs_6_ = bf16[12,128,128]{2,1,0:T(8,128)(2,1)} collective-permute-done((bf16[12,128,128]{2,1,0:T(8,128)(2,1)S(1)}, bf16[12,128,128]{2,1,0:T(8,128)(2,1)}, u32[]{:S(2)}, u32[]{:S(2)}) %collective-permute-start) | collective-permute-done | bytes 393248 | tf_op jit(solution)/shard_map/ppermute | solution.py:30
  51.5 3.0 %collective-permute-start.3 = (bf16[12,128,128]{2,1,0:T(8,128)(2,1)}, bf16[12,128,128]{2,1,0:T(8,128)(2,1)S(1)}, u32[]{:S(2)}, u32[]{:S(2)}) collective-permute-start(bf16[12,128,128]{2,1,0:T(8,128)(2,1)} %collective-permute-done.2.refs_4_.refs_5_), channel_id=1, source_target_pairs={{0,192},{64,0},{128,64},{192,128},{1,193},{65,1},{129,65},{193,129... | collective-permute-start | bytes 1179656 | tf_op jit(solution)/shard_map/ppermute | solution.py:30
  54.8 5.0 %collective-permute-done.4.refs_3_.refs_4_ = bf16[12,128,128]{2,1,0:T(8,128)(2,1)S(1)} collective-permute-done((bf16[12,128,128]{2,1,0:T(8,128)(2,1)S(1)}, bf16[12,128,128]{2,1,0:T(8,128)(2,1)S(1)}, u32[]{:S(2)}, u32[]{:S(2)}) %collective-permute-start.4) | collective-permute-done | bytes 393248 | tf_op jit(solution)/shard_map/ppermute | solution.py:30
  59.7 0.7 copy-done.1
  60.9 0.8 copy-done.4
  61.7 1.6 %collective-permute-start.8 = (bf16[12,128,128]{2,1,0:T(8,128)(2,1)S(1)}, bf16[12,128,128]{2,1,0:T(8,128)(2,1)}, u32[]{:S(2)}, u32[]{:S(2)}) collective-permute-start(bf16[12,128,128]{2,1,0:T(8,128)(2,1)S(1)} %bitcast.31), channel_id=1, source_target_pairs={{0,4},{4,8},{8,12},{12,0},{1,5},{5,9},{9,13},{13,1},{2,6},{6,10},{... | collective-permute-start | bytes 1179656 | tf_op jit(solution)/shard_map/ppermute | solution.py:30
  63.3 1.0 copy-done.2
  64.3 1.0 copy-done.5
  65.3 7.6 %near.1 = (f32[12,1,128]{2,1,0:T(1,128)S(1)}, f32[12,8,128]{2,1,0:T(8,128)S(1)}, f32[12,128,128]{2,1,0:T(8,128)S(1)}) custom-call(s32[48,52]{1,0:T(8,128)S(1)} %copy.18.lists, s32[48]{0:T(128)S(1)} %get-tuple-element.30.nears, s32[48]{0:T(128)S(1)} %get-tuple-element.31.counts, bf16[12,128,128]{2,1,0:T(8,128)(2,1)S(1)} %bitcast.32, ...), custom_call_target="tpu_custom_call" | custom-call | flops 1207959552 | bytes 5242880 | tf_op jit(solution)/shard_map/near/pallas_call | solution.py:226
  72.9 3.5 %far.1 = (bf16[12,144,128]{2,1,0:T(8,128)(2,1)S(1)}, f32[12,128]{1,0:T(8,128)S(1)}) custom-call(s32[48,52]{1,0:T(8,128)S(1)} %copy.18.lists, s32[48]{0:T(128)S(1)} %get-tuple-element.30.nears, s32[48]{0:T(128)S(1)} %get-tuple-element.31.counts, bf16[12,128,128]{2,1,0:T(8,128)(2,1)S(1)} %bitcast.33, ...), custom_call_target="tpu_custom_call" | custom-call | flops 402653184 | bytes 5242880 | tf_op jit(solution)/shard_map/far/pallas_call | solution.py:226
  76.5 8.5 %full.2 = (bf16[12,144,128]{2,1,0:T(8,128)(2,1)S(1)}, f32[12,128]{1,0:T(8,128)S(1)}) custom-call(s32[48,52]{1,0:T(8,128)S(1)} %copy.18.lists, s32[48]{0:T(128)S(1)} %get-tuple-element.30.nears, s32[48]{0:T(128)S(1)} %get-tuple-element.31.counts, bf16[12,128,128]{2,1,0:T(8,128)(2,1)} %collective-permute-done.6.refs_0_, ...), custom_call_target="tpu_custom_call" | custom-call | flops 1610612736 | bytes 5242880 | tf_op jit(solution)/shard_map/full/pallas_call | solution.py:226
  85.0 1.9 %collective-permute-start.9 = (bf16[12,144,128]{2,1,0:T(8,128)(2,1)S(1)}, bf16[12,144,128]{2,1,0:T(8,128)(2,1)S(1)}, u32[]{:S(2)}, u32[]{:S(2)}) collective-permute-start(bf16[12,144,128]{2,1,0:T(8,128)(2,1)S(1)} %get-tuple-element.47), channel_id=1, source_target_pairs={{0,8},{4,12},{8,0},{12,4},{1,9},{5,13},{9,1},{13,5},{2,10},{6,14},... | collective-permute-start | bytes 1327112 | tf_op jit(solution)/shard_map/ppermute | solution.py:30
  86.9 13.4 %full.3 = (bf16[12,144,128]{2,1,0:T(8,128)(2,1)S(1)}, bf16[12,144,128]{2,1,0:T(8,128)(2,1)S(1)}, f32[12,128]{1,0:T(8,128)S(1)}, f32[12,128]{1,0:T(8,128)S(1)}) custom-call(s32[48,52]{1,0:T(8,128)S(1)} %copy.18.lists, s32[48]{0:T(128)S(1)} %get-tuple-element.30.nears, s32[48]{0:T(128)S(1)} %get-tuple-element.31.counts, ...), custom_call_target="tpu_custom_call" | custom-call | flops 3221225472 | bytes 5242880 | tf_op jit(solution)/shard_map/full/pallas_call | solution.py:226
  100.3 0.8 collective-permute-start.10
  101.1 2.0 %collective-permute-start.11 = (bf16[12,144,128]{2,1,0:T(8,128)(2,1)S(1)}, bf16[12,144,128]{2,1,0:T(8,128)(2,1)S(1)}, u32[]{:S(2)}, u32[]{:S(2)}) collective-permute-start(bf16[12,144,128]{2,1,0:T(8,128)(2,1)S(1)} %get-tuple-element.54), channel_id=1, source_target_pairs={{0,12},{4,0},{8,4},{12,8},{1,13},{5,1},{9,5},{13,9},{2,14},{6,2},{... | collective-permute-start | bytes 1327112 | tf_op jit(solution)/shard_map/ppermute | solution.py:30
  103.1 0.7 pick.1
  103.8 13.9 %all_to_all.20.parts = f32[16,12,128]{2,1,0:T(8,128)S(1)} all-to-all(f32[16,12,128]{2,1,0:T(8,128)S(1)} %pick.1), channel_id=1, replica_groups=mesh['x'=4,'zh'=4,'y'=4,'zl'=2,'core'=2] {'x','y'}, dimensions={0} | all-to-all | bytes 196608 | tf_op jit(solution)/shard_map/all_to_all | solution.py:365
  117.7 1.2 combine.1
  119.0 7.3 %all-to-all-start.3 = ((bf16[16,96,128]{2,1,0:T(8,128)(2,1)}), bf16[16,96,128]{2,1,0:T(8,128)(2,1)S(1)}, u32[]{:S(2)}, u32[]{:S(2)}) async-start(bf16[16,96,128]{2,1,0:T(8,128)(2,1)} %bitcast.3), calls=%async_computation.3 | async-start | bytes 786432 | tf_op jit(solution)/shard_map/all_to_all | solution.py:338
  126.4 9.2 %collective-permute-start.12 = (f32[1,1536]{1,0:T(1,128)S(1)}, f32[1,1536]{1,0:T(1,128)S(1)}, u32[]{:S(2)}, u32[]{:S(2)}) collective-permute-start(f32[1,1536]{1,0:T(1,128)S(1)} %bitcast.39), channel_id=1, source_target_pairs={{0,0},{16,4},{32,8},{48,12},{4,16},{20,20},{36,24},{52,28},{8,32},... | collective-permute-start | bytes 18440 | tf_op jit(solution)/shard_map/ppermute | solution.py:373
  135.5 7.8 %collective-permute-done.12 = f32[1,1536]{1,0:T(1,128)S(1)} collective-permute-done((f32[1,1536]{1,0:T(1,128)S(1)}, f32[1,1536]{1,0:T(1,128)S(1)}, u32[]{:S(2)}, u32[]{:S(2)}) %collective-permute-start.12) | collective-permute-done | bytes 6176 | tf_op jit(solution)/shard_map/ppermute | solution.py:373
  143.3 0.8 copy_bitcast_fusion
  (48 shorter events, 3.5 us)
Async XLA Ops:
  0.6 12.9 %copy-start = (bf16[96,2048]{1,0:T(8,128)(2,1)S(1)}, bf16[96,2048]{1,0:T(8,128)(2,1)}, u32[]{:S(2)}) copy-start(bf16[96,2048]{1,0:T(8,128)(2,1)} %param.6) | copy-start | bytes 1179652
  0.6 1.3 copy-start.7
  3.1 8.7 %copy-start.10 = (s32[192]{0:T(256)S(1)}, s32[192]{0:T(256)}, u32[]{:S(2)}) copy-start(s32[192]{0:T(256)} %param.10) | copy-start | bytes 2308
  3.1 8.8 %copy-start.8 = (s32[192,96]{1,0:T(8,128)S(1)}, s32[192,96]{1,0:T(8,128)}, u32[]{:S(2)}) copy-start(s32[192,96]{1,0:T(8,128)} %param.9) | copy-start | bytes 221188
  3.1 10.4 %copy-start.9 = (s32[192]{0:T(256)S(1)}, s32[192]{0:T(256)}, u32[]{:S(2)}) copy-start(s32[192]{0:T(256)} %param.11) | copy-start | bytes 2308
  3.1 29.4 %all-to-all-start = ((bf16[16,2,96,128]{3,2,1,0:T(8,128)(2,1)}), bf16[16,2,96,128]{3,2,1,0:T(8,128)(2,1)S(1)}, u32[]{:S(2)}, u32[]{:S(2)}) async-start(bf16[16,2,96,128]{3,2,1,0:T(8,128)(2,1)} %maximum_bitcast_fusion), calls=%async_computation | async-start | bytes 1572864 | tf_op jit(solution)/shard_map/all_to_all | solution.py:338
  32.5 21.9 %all-to-all-start.1 = ((bf16[16,96,128]{2,1,0:T(8,128)(2,1)}), bf16[16,96,128]{2,1,0:T(8,128)(2,1)S(1)}, u32[]{:S(2)}, u32[]{:S(2)}) async-start(bf16[16,96,128]{2,1,0:T(8,128)(2,1)} %bitcast_bitcast_fusion), calls=%async_computation.1 | async-start | bytes 786432 | tf_op jit(solution)/shard_map/all_to_all | solution.py:338
  37.8 13.4 %collective-permute-start = (bf16[12,128,128]{2,1,0:T(8,128)(2,1)S(1)}, bf16[12,128,128]{2,1,0:T(8,128)(2,1)}, u32[]{:S(2)}, u32[]{:S(2)}) collective-permute-start(bf16[12,128,128]{2,1,0:T(8,128)(2,1)S(1)} %get-tuple-element.34.refs_1_.refs_2_), channel_id=1, source_target_pairs={{0,64},{64,128},{128,192},{192,0},{1,65},{65,129},{129,193},{193,1... | collective-permute-start | bytes 1179656 | tf_op jit(solution)/shard_map/ppermute | solution.py:30
  39.4 12.1 %collective-permute-start.2 = (bf16[12,128,128]{2,1,0:T(8,128)(2,1)S(1)}, bf16[12,128,128]{2,1,0:T(8,128)(2,1)}, u32[]{:S(2)}, u32[]{:S(2)}) collective-permute-start(bf16[12,128,128]{2,1,0:T(8,128)(2,1)S(1)} %get-tuple-element.35.refs_2_.refs_3_), channel_id=1, source_target_pairs={{0,192},{64,0},{128,64},{192,128},{1,193},{65,1},{129,65},{193,129... | collective-permute-start | bytes 1179656 | tf_op jit(solution)/shard_map/ppermute | solution.py:30
  41.1 18.6 %collective-permute-start.4 = (bf16[12,128,128]{2,1,0:T(8,128)(2,1)S(1)}, bf16[12,128,128]{2,1,0:T(8,128)(2,1)S(1)}, u32[]{:S(2)}, u32[]{:S(2)}) collective-permute-start(bf16[12,128,128]{2,1,0:T(8,128)(2,1)S(1)} %get-tuple-element.34.refs_1_.refs_2_), channel_id=1, source_target_pairs={{0,192},{64,0},{128,64},{192,128},{1,193},{65,1},{129,65},{193,129... | collective-permute-start | bytes 1179656 | tf_op jit(solution)/shard_map/ppermute | solution.py:30
  42.7 18.3 %collective-permute-start.5 = (bf16[12,128,128]{2,1,0:T(8,128)(2,1)S(1)}, bf16[12,128,128]{2,1,0:T(8,128)(2,1)S(1)}, u32[]{:S(2)}, u32[]{:S(2)}) collective-permute-start(bf16[12,128,128]{2,1,0:T(8,128)(2,1)S(1)} %get-tuple-element.35.refs_2_.refs_3_), channel_id=1, source_target_pairs={{0,64},{64,128},{128,192},{192,0},{1,65},{65,129},{129,193},{193,1... | collective-permute-start | bytes 1179656 | tf_op jit(solution)/shard_map/ppermute | solution.py:30
  51.2 21.7 %collective-permute-start.1 = (bf16[12,128,128]{2,1,0:T(8,128)(2,1)}, bf16[12,128,128]{2,1,0:T(8,128)(2,1)S(1)}, u32[]{:S(2)}, u32[]{:S(2)}) collective-permute-start(bf16[12,128,128]{2,1,0:T(8,128)(2,1)} %collective-permute-done.refs_5_.refs_6_), channel_id=1, source_target_pairs={{0,64},{64,128},{128,192},{192,0},{1,65},{65,129},{129,193},{193,1... | collective-permute-start | bytes 1179656 | tf_op jit(solution)/shard_map/ppermute | solution.py:30
  51.5 21.4 %collective-permute-start.3 = (bf16[12,128,128]{2,1,0:T(8,128)(2,1)}, bf16[12,128,128]{2,1,0:T(8,128)(2,1)S(1)}, u32[]{:S(2)}, u32[]{:S(2)}) collective-permute-start(bf16[12,128,128]{2,1,0:T(8,128)(2,1)} %collective-permute-done.2.refs_4_.refs_5_), channel_id=1, source_target_pairs={{0,192},{64,0},{128,64},{192,128},{1,193},{65,1},{129,65},{193,129... | collective-permute-start | bytes 1179656 | tf_op jit(solution)/shard_map/ppermute | solution.py:30
  54.4 22.0 %collective-permute-start.6 = (bf16[12,128,128]{2,1,0:T(8,128)(2,1)S(1)}, bf16[12,128,128]{2,1,0:T(8,128)(2,1)}, u32[]{:S(2)}, u32[]{:S(2)}) collective-permute-start(bf16[12,128,128]{2,1,0:T(8,128)(2,1)S(1)} %bitcast.29), channel_id=1, source_target_pairs={{0,8},{4,12},{8,0},{12,4},{1,9},{5,13},{9,1},{13,5},{2,10},{6,14},... | collective-permute-start | bytes 1179656 | tf_op jit(solution)/shard_map/ppermute | solution.py:30
  59.7 0.7 copy-start.1
  60.5 24.5 %collective-permute-start.7 = (bf16[12,128,128]{2,1,0:T(8,128)(2,1)S(1)}, bf16[12,128,128]{2,1,0:T(8,128)(2,1)}, u32[]{:S(2)}, u32[]{:S(2)}) collective-permute-start(bf16[12,128,128]{2,1,0:T(8,128)(2,1)S(1)} %bitcast.30), channel_id=1, source_target_pairs={{0,12},{4,0},{8,4},{12,8},{1,13},{5,1},{9,5},{13,9},{2,14},{6,2},{... | collective-permute-start | bytes 1179656 | tf_op jit(solution)/shard_map/ppermute | solution.py:30
  60.9 0.8 copy-start.4
  61.7 25.2 %collective-permute-start.8 = (bf16[12,128,128]{2,1,0:T(8,128)(2,1)S(1)}, bf16[12,128,128]{2,1,0:T(8,128)(2,1)}, u32[]{:S(2)}, u32[]{:S(2)}) collective-permute-start(bf16[12,128,128]{2,1,0:T(8,128)(2,1)S(1)} %bitcast.31), channel_id=1, source_target_pairs={{0,4},{4,8},{8,12},{12,0},{1,5},{5,9},{9,13},{13,1},{2,6},{6,10},{... | collective-permute-start | bytes 1179656 | tf_op jit(solution)/shard_map/ppermute | solution.py:30
  63.3 1.0 copy-start.2
  64.3 1.0 copy-start.5
  72.9 3.5 %copy-start.3 = (bf16[12,128,128]{2,1,0:T(8,128)(2,1)S(1)}, bf16[12,128,128]{2,1,0:T(8,128)(2,1)}, u32[]{:S(2)}) copy-start(bf16[12,128,128]{2,1,0:T(8,128)(2,1)} %copy-done.1) | copy-start | bytes 1179652
  72.9 3.5 %copy-start.6 = (bf16[12,128,128]{2,1,0:T(8,128)(2,1)S(1)}, bf16[12,128,128]{2,1,0:T(8,128)(2,1)}, u32[]{:S(2)}) copy-start(bf16[12,128,128]{2,1,0:T(8,128)(2,1)} %copy-done.4) | copy-start | bytes 1179652
  85.0 18.1 %collective-permute-start.9 = (bf16[12,144,128]{2,1,0:T(8,128)(2,1)S(1)}, bf16[12,144,128]{2,1,0:T(8,128)(2,1)S(1)}, u32[]{:S(2)}, u32[]{:S(2)}) collective-permute-start(bf16[12,144,128]{2,1,0:T(8,128)(2,1)S(1)} %get-tuple-element.47), channel_id=1, source_target_pairs={{0,8},{4,12},{8,0},{12,4},{1,9},{5,13},{9,1},{13,5},{2,10},{6,14},... | collective-permute-start | bytes 1327112 | tf_op jit(solution)/shard_map/ppermute | solution.py:30
  100.3 17.4 %collective-permute-start.10 = (bf16[12,144,128]{2,1,0:T(8,128)(2,1)S(1)}, bf16[12,144,128]{2,1,0:T(8,128)(2,1)S(1)}, u32[]{:S(2)}, u32[]{:S(2)}) collective-permute-start(bf16[12,144,128]{2,1,0:T(8,128)(2,1)S(1)} %get-tuple-element.52), channel_id=1, source_target_pairs={{0,4},{4,8},{8,12},{12,0},{1,5},{5,9},{9,13},{13,1},{2,6},{6,10},{... | collective-permute-start | bytes 1327112 | tf_op jit(solution)/shard_map/ppermute | solution.py:30
  101.1 16.6 %collective-permute-start.11 = (bf16[12,144,128]{2,1,0:T(8,128)(2,1)S(1)}, bf16[12,144,128]{2,1,0:T(8,128)(2,1)S(1)}, u32[]{:S(2)}, u32[]{:S(2)}) collective-permute-start(bf16[12,144,128]{2,1,0:T(8,128)(2,1)S(1)} %get-tuple-element.54), channel_id=1, source_target_pairs={{0,12},{4,0},{8,4},{12,8},{1,13},{5,1},{9,5},{13,9},{2,14},{6,2},{... | collective-permute-start | bytes 1327112 | tf_op jit(solution)/shard_map/ppermute | solution.py:30
  119.0 24.4 %all-to-all-start.3 = ((bf16[16,96,128]{2,1,0:T(8,128)(2,1)}), bf16[16,96,128]{2,1,0:T(8,128)(2,1)S(1)}, u32[]{:S(2)}, u32[]{:S(2)}) async-start(bf16[16,96,128]{2,1,0:T(8,128)(2,1)} %bitcast.3), calls=%async_computation.3 | async-start | bytes 786432 | tf_op jit(solution)/shard_map/all_to_all | solution.py:338
  126.4 17.0 %collective-permute-start.12 = (f32[1,1536]{1,0:T(1,128)S(1)}, f32[1,1536]{1,0:T(1,128)S(1)}, u32[]{:S(2)}, u32[]{:S(2)}) collective-permute-start(f32[1,1536]{1,0:T(1,128)S(1)} %bitcast.39), channel_id=1, source_target_pairs={{0,0},{16,4},{32,8},{48,12},{4,16},{20,20},{36,24},{52,28},{8,32},... | collective-permute-start | bytes 18440 | tf_op jit(solution)/shard_map/ppermute | solution.py:373

commit v12 on v10

--- a/solution.py
+++ b/solution.py
@@ -15,7 +15,7 @@
 KEYS = RING * OWN
 NEAR = 3 * OWN
 CHUNK = 4
-WIDTH = 4
+WIDTH = 8
 PAD = 16
 NEG = -1e30
 SCALE = HD**-0.5

time: 140 us -> 136 us (0.971)
  Pallas kernels: 35.1 us -> 30.4 us
    pallas_call x4, Pallas kernels: 33 us -> 28.3 us  [attend(): pl.pallas_call(functools.partial(attend_kernel, blocks, mode), out_shape=...]
  transfers between devices with their start and end apart: 14 -> 14, of which waited for: 4 -> 6; matrix products, arithmetic and copies ran while one was open for 4% -> 4% of each run, Pallas kernels for 24% -> 22%
where the time goes in v12:
time: 136 us; the launch traced here: 134 us
  starting transfers between devices  42 us (31%)
  waiting for transfers between devices  39.1 us (29%)
  Pallas kernels  30.4 us (22%)
  blocking collectives  12.7 us (9%)
  local copies, waits for them, and re-layouts  6.34 us (5%)
  other arithmetic  2.32 us (2%)
    pallas_call x4, Pallas kernels, attend(): pl.pallas_call(functools.partial(attend_kernel, blocks, mode), out_shape=...  28.3 us
    all_to_all x3, starting transfers between devices, exchange(): return lax.all_to_all(array, GROUP, split_axis=0, concat_axis=0, tiled=True)  19 us
    all_to_all x3, waiting for transfers between devices, exchange(): return lax.all_to_all(array, GROUP, split_axis=0, concat_axis=0, tiled=True)  18.1 us
    ppermute x10, starting transfers between devices, shift(): lax.ppermute(array, axis, [(i, (i + by) % RING) for i in range(RING)])  13.8 us
    ppermute x10, waiting for transfers between devices, shift(): lax.ppermute(array, axis, [(i, (i + by) % RING) for i in range(RING)])  13.3 us
    all_to_all x1, blocking collectives, on_device(): lax.all_to_all(pick(spots, (e0, e1, e2, e3)), ('x', 'y'), split_axis=0, c...  12.7 us
    ppermute x1, starting transfers between devices, on_device(): lax.ppermute(merge(parts).reshape(1, OWN * BLK), ('zh', 'y'), turned)  9.19 us
    ppermute x1, waiting for transfers between devices, on_device(): lax.ppermute(merge(parts).reshape(1, OWN * BLK), ('zh', 'y'), turned)  7.78 us
  transfers between devices with their start and end apart: 14, of which 6 were waited for; matrix products, arithmetic and copies ran while one was open for 4% of the time, Pallas kernels for 22%

profile of v12, /device:TPU:16, one launch (start us, length us, event | category | flops | bytes accessed | tf_op | source)
XLA Modules:
  0.0 134.1 jit_solution(17567854273440550346)
XLA Ops:
  0.7 1.1 copy.25
  2.1 1.0 maximum_bitcast_fusion
  3.1 8.7 %all-to-all-start = ((bf16[16,2,96,128]{3,2,1,0:T(8,128)(2,1)}), bf16[16,2,96,128]{3,2,1,0:T(8,128)(2,1)S(1)}, u32[]{:S(2)}, u32[]{:S(2)}) async-start(bf16[16,2,96,128]{3,2,1,0:T(8,128)(2,1)} %maximum_bitcast_fusion), calls=%async_computation | async-start | bytes 1572864 | tf_op jit(solution)/shard_map/all_to_all | solution.py:338
  12.5 1.0 select_reduce_fusion
  13.6 0.8 bitcast_bitcast_fusion
  14.4 18.1 %all-to-all-done.got_ref = bf16[16,2,96,128]{3,2,1,0:T(8,128)(2,1)S(1)} async-done(((bf16[16,2,96,128]{3,2,1,0:T(8,128)(2,1)}), bf16[16,2,96,128]{3,2,1,0:T(8,128)(2,1)S(1)}, u32[]{:S(2)}, u32[]{:S(2)}) %all-to-all-start) | async-done | bytes 786464 | tf_op jit(solution)/shard_map/all_to_all | solution.py:338
  32.6 1.6 %collective-permute-start = (bf16[2,12,128,128]{3,2,1,0:T(8,128)(2,1)S(1)}, bf16[2,12,128,128]{3,2,1,0:T(8,128)(2,1)S(1)}, u32[]{:S(2)}, u32[]{:S(2)}) collective-permute-start(bf16[2,12,128,128]{3,2,1,0:T(8,128)(2,1)S(1)} %prepare.1.refs_1_.refs_2_), channel_id=1, source_target_pairs={{0,64},{64,128},{128,192},{192,0},{1,65},{65,129},{129,193},{193,1... | collective-permute-start | bytes 2359304 | tf_op jit(solution)/shard_map/ppermute | solution.py:30
  34.2 1.7 %collective-permute-start.2 = (bf16[2,12,128,128]{3,2,1,0:T(8,128)(2,1)S(1)}, bf16[2,12,128,128]{3,2,1,0:T(8,128)(2,1)}, u32[]{:S(2)}, u32[]{:S(2)}) collective-permute-start(bf16[2,12,128,128]{3,2,1,0:T(8,128)(2,1)S(1)} %prepare.1.refs_1_.refs_2_), channel_id=1, source_target_pairs={{0,192},{64,0},{128,64},{192,128},{1,193},{65,1},{129,65},{193,129... | collective-permute-start | bytes 2359304 | tf_op jit(solution)/shard_map/ppermute | solution.py:30
  35.9 5.1 %all-to-all-start.1 = ((bf16[16,96,128]{2,1,0:T(8,128)(2,1)}), bf16[16,96,128]{2,1,0:T(8,128)(2,1)S(1)}, u32[]{:S(2)}, u32[]{:S(2)}) async-start(bf16[16,96,128]{2,1,0:T(8,128)(2,1)} %bitcast_bitcast_fusion), calls=%async_computation.1 | async-start | bytes 786432 | tf_op jit(solution)/shard_map/all_to_all | solution.py:338
  41.1 11.8 %collective-permute-done.refs_3_.refs_4_ = bf16[2,12,128,128]{3,2,1,0:T(8,128)(2,1)S(1)} collective-permute-done((bf16[2,12,128,128]{3,2,1,0:T(8,128)(2,1)S(1)}, bf16[2,12,128,128]{3,2,1,0:T(8,128)(2,1)S(1)}, u32[]{:S(2)}, u32[]{:S(2)}) %collective-permute-start) | collective-permute-done | bytes 786464 | tf_op jit(solution)/shard_map/ppermute | solution.py:30
  52.9 0.8 slice_bitcast_fusion.1
  53.9 1.8 %slice_bitcast_fusion = bf16[12,128,128]{2,1,0:T(8,128)(2,1)} fusion(bf16[2,12,128,128]{3,2,1,0:T(8,128)(2,1)} %collective-permute-done.2.refs_2_.refs_3_), kind=kLoop, calls=%fused_computation.10 | loop fusion | bytes 786432 | tf_op jit(solution)/shard_map/squeeze | solution.py:352
  55.7 3.0 %collective-permute-start.3 = (bf16[12,128,128]{2,1,0:T(8,128)(2,1)}, bf16[12,128,128]{2,1,0:T(8,128)(2,1)S(1)}, u32[]{:S(2)}, u32[]{:S(2)}) collective-permute-start(bf16[12,128,128]{2,1,0:T(8,128)(2,1)} %slice_bitcast_fusion), channel_id=1, source_target_pairs={{0,192},{64,0},{128,64},{192,128},{1,193},{65,1},{129,65},{193,129... | collective-permute-start | bytes 1179656 | tf_op jit(solution)/shard_map/ppermute | solution.py:30
  58.7 0.3 collective-permute-start.4
  59.0 2.4 %collective-permute-start.5 = (bf16[12,128,128]{2,1,0:T(8,128)(2,1)S(1)}, bf16[12,128,128]{2,1,0:T(8,128)(2,1)}, u32[]{:S(2)}, u32[]{:S(2)}) collective-permute-start(bf16[12,128,128]{2,1,0:T(8,128)(2,1)S(1)} %bitcast.34), channel_id=1, source_target_pairs={{0,12},{4,0},{8,4},{12,8},{1,13},{5,1},{9,5},{13,9},{2,14},{6,2},{... | collective-permute-start | bytes 1179656 | tf_op jit(solution)/shard_map/ppermute | solution.py:30
  61.5 6.5 %near.1 = (f32[12,1,128]{2,1,0:T(1,128)S(1)}, f32[12,8,128]{2,1,0:T(8,128)S(1)}, f32[12,128,128]{2,1,0:T(8,128)S(1)}) custom-call(s32[48,52]{1,0:T(8,128)S(1)} %copy.18.lists, s32[48]{0:T(128)S(1)} %get-tuple-element.28.nears, s32[48]{0:T(128)S(1)} %get-tuple-element.29.counts, bf16[12,128,128]{2,1,0:T(8,128)(2,1)S(1)} %bitcast.36, ...), custom_call_target="tpu_custom_call" | custom-call | flops 1207959552 | bytes 5242880 | tf_op jit(solution)/shard_map/near/pallas_call | solution.py:226
  68.1 3.3 %far.1 = (bf16[12,144,128]{2,1,0:T(8,128)(2,1)S(1)}, f32[12,128]{1,0:T(8,128)S(1)}) custom-call(s32[48,52]{1,0:T(8,128)S(1)} %copy.18.lists, s32[48]{0:T(128)S(1)} %get-tuple-element.28.nears, s32[48]{0:T(128)S(1)} %get-tuple-element.29.counts, bf16[12,128,128]{2,1,0:T(8,128)(2,1)S(1)} %bitcast.37, ...), custom_call_target="tpu_custom_call" | custom-call | flops 402653184 | bytes 5242880 | tf_op jit(solution)/shard_map/far/pallas_call | solution.py:226
  71.4 0.9 collective-permute-done.4.refs_0_
  72.3 6.8 %full.2 = (bf16[12,144,128]{2,1,0:T(8,128)(2,1)S(1)}, f32[12,128]{1,0:T(8,128)S(1)}) custom-call(s32[48,52]{1,0:T(8,128)S(1)} %copy.18.lists, s32[48]{0:T(128)S(1)} %get-tuple-element.28.nears, s32[48]{0:T(128)S(1)} %get-tuple-element.29.counts, bf16[12,128,128]{2,1,0:T(8,128)(2,1)} %collective-permute-done.4.refs_0_, ...), custom_call_target="tpu_custom_call" | custom-call | flops 1610612736 | bytes 5242880 | tf_op jit(solution)/shard_map/full/pallas_call | solution.py:226
  79.1 0.5 collective-permute-done.5.refs_0_
  79.7 2.4 %collective-permute-start.7 = (bf16[12,144,128]{2,1,0:T(8,128)(2,1)S(1)}, bf16[12,144,128]{2,1,0:T(8,128)(2,1)S(1)}, u32[]{:S(2)}, u32[]{:S(2)}) collective-permute-start(bf16[12,144,128]{2,1,0:T(8,128)(2,1)S(1)} %get-tuple-element.43), channel_id=1, source_target_pairs={{0,8},{4,12},{8,0},{12,4},{1,9},{5,13},{9,1},{13,5},{2,10},{6,14},... | collective-permute-start | bytes 1327112 | tf_op jit(solution)/shard_map/ppermute | solution.py:30
  82.1 11.7 %full.3 = (bf16[12,144,128]{2,1,0:T(8,128)(2,1)S(1)}, bf16[12,144,128]{2,1,0:T(8,128)(2,1)S(1)}, f32[12,128]{1,0:T(8,128)S(1)}, f32[12,128]{1,0:T(8,128)S(1)}) custom-call(s32[48,52]{1,0:T(8,128)S(1)} %copy.18.lists, s32[48]{0:T(128)S(1)} %get-tuple-element.28.nears, s32[48]{0:T(128)S(1)} %get-tuple-element.29.counts, ...), custom_call_target="tpu_custom_call" | custom-call | flops 3221225472 | bytes 5242880 | tf_op jit(solution)/shard_map/full/pallas_call | solution.py:226
  93.8 0.4 collective-permute-start.8
  94.2 1.7 %collective-permute-start.9 = (bf16[12,144,128]{2,1,0:T(8,128)(2,1)S(1)}, bf16[12,144,128]{2,1,0:T(8,128)(2,1)S(1)}, u32[]{:S(2)}, u32[]{:S(2)}) collective-permute-start(bf16[12,144,128]{2,1,0:T(8,128)(2,1)S(1)} %get-tuple-element.50), channel_id=1, source_target_pairs={{0,12},{4,0},{8,4},{12,8},{1,13},{5,1},{9,5},{13,9},{2,14},{6,2},{... | collective-permute-start | bytes 1327112 | tf_op jit(solution)/shard_map/ppermute | solution.py:30
  95.9 0.7 pick.1
  96.5 12.7 %all_to_all.20.parts = f32[16,12,128]{2,1,0:T(8,128)S(1)} all-to-all(f32[16,12,128]{2,1,0:T(8,128)S(1)} %pick.1), channel_id=1, replica_groups=mesh['x'=4,'zh'=4,'y'=4,'zl'=2,'core'=2] {'x','y'}, dimensions={0} | all-to-all | bytes 196608 | tf_op jit(solution)/shard_map/all_to_all | solution.py:363
  109.2 1.2 combine.1
  110.5 5.2 %all-to-all-start.3 = ((bf16[16,96,128]{2,1,0:T(8,128)(2,1)}), bf16[16,96,128]{2,1,0:T(8,128)(2,1)S(1)}, u32[]{:S(2)}, u32[]{:S(2)}) async-start(bf16[16,96,128]{2,1,0:T(8,128)(2,1)} %bitcast.5), calls=%async_computation.3 | async-start | bytes 786432 | tf_op jit(solution)/shard_map/all_to_all | solution.py:338
  115.8 9.2 %collective-permute-start.10 = (f32[1,1536]{1,0:T(1,128)S(1)}, f32[1,1536]{1,0:T(1,128)S(1)}, u32[]{:S(2)}, u32[]{:S(2)}) collective-permute-start(f32[1,1536]{1,0:T(1,128)S(1)} %bitcast.43), channel_id=1, source_target_pairs={{0,0},{16,4},{32,8},{48,12},{4,16},{20,20},{36,24},{52,28},{8,32},... | collective-permute-start | bytes 18440 | tf_op jit(solution)/shard_map/ppermute | solution.py:371
  125.0 7.8 %collective-permute-done.10 = f32[1,1536]{1,0:T(1,128)S(1)} collective-permute-done((f32[1,1536]{1,0:T(1,128)S(1)}, f32[1,1536]{1,0:T(1,128)S(1)}, u32[]{:S(2)}, u32[]{:S(2)}) %collective-permute-start.10) | collective-permute-done | bytes 6176 | tf_op jit(solution)/shard_map/ppermute | solution.py:371
  132.7 0.8 copy_bitcast_fusion
  133.5 0.6 copy.32
  (34 shorter events, 1.8 us)
Async XLA Ops:
  0.6 12.9 %copy-start = (bf16[96,2048]{1,0:T(8,128)(2,1)S(1)}, bf16[96,2048]{1,0:T(8,128)(2,1)}, u32[]{:S(2)}) copy-start(bf16[96,2048]{1,0:T(8,128)(2,1)} %param.6) | copy-start | bytes 1179652
  0.6 1.3 copy-start.1
  3.1 8.7 %copy-start.4 = (s32[192]{0:T(256)S(1)}, s32[192]{0:T(256)}, u32[]{:S(2)}) copy-start(s32[192]{0:T(256)} %param.10) | copy-start | bytes 2308
  3.1 8.8 %copy-start.2 = (s32[192,96]{1,0:T(8,128)S(1)}, s32[192,96]{1,0:T(8,128)}, u32[]{:S(2)}) copy-start(s32[192,96]{1,0:T(8,128)} %param.9) | copy-start | bytes 221188
  3.1 10.4 %copy-start.3 = (s32[192]{0:T(256)S(1)}, s32[192]{0:T(256)}, u32[]{:S(2)}) copy-start(s32[192]{0:T(256)} %param.11) | copy-start | bytes 2308
  3.1 29.4 %all-to-all-start = ((bf16[16,2,96,128]{3,2,1,0:T(8,128)(2,1)}), bf16[16,2,96,128]{3,2,1,0:T(8,128)(2,1)S(1)}, u32[]{:S(2)}, u32[]{:S(2)}) async-start(bf16[16,2,96,128]{3,2,1,0:T(8,128)(2,1)} %maximum_bitcast_fusion), calls=%async_computation | async-start | bytes 1572864 | tf_op jit(solution)/shard_map/all_to_all | solution.py:338
  32.6 20.2 %collective-permute-start = (bf16[2,12,128,128]{3,2,1,0:T(8,128)(2,1)S(1)}, bf16[2,12,128,128]{3,2,1,0:T(8,128)(2,1)S(1)}, u32[]{:S(2)}, u32[]{:S(2)}) collective-permute-start(bf16[2,12,128,128]{3,2,1,0:T(8,128)(2,1)S(1)} %prepare.1.refs_1_.refs_2_), channel_id=1, source_target_pairs={{0,64},{64,128},{128,192},{192,0},{1,65},{65,129},{129,193},{193,1... | collective-permute-start | bytes 2359304 | tf_op jit(solution)/shard_map/ppermute | solution.py:30
  34.2 19.7 %collective-permute-start.2 = (bf16[2,12,128,128]{3,2,1,0:T(8,128)(2,1)S(1)}, bf16[2,12,128,128]{3,2,1,0:T(8,128)(2,1)}, u32[]{:S(2)}, u32[]{:S(2)}) collective-permute-start(bf16[2,12,128,128]{3,2,1,0:T(8,128)(2,1)S(1)} %prepare.1.refs_1_.refs_2_), channel_id=1, source_target_pairs={{0,192},{64,0},{128,64},{192,128},{1,193},{65,1},{129,65},{193,129... | collective-permute-start | bytes 2359304 | tf_op jit(solution)/shard_map/ppermute | solution.py:30
  35.9 22.7 %all-to-all-start.1 = ((bf16[16,96,128]{2,1,0:T(8,128)(2,1)}), bf16[16,96,128]{2,1,0:T(8,128)(2,1)S(1)}, u32[]{:S(2)}, u32[]{:S(2)}) async-start(bf16[16,96,128]{2,1,0:T(8,128)(2,1)} %bitcast_bitcast_fusion), calls=%async_computation.1 | async-start | bytes 786432 | tf_op jit(solution)/shard_map/all_to_all | solution.py:338
  53.6 14.4 %collective-permute-start.1 = (bf16[12,128,128]{2,1,0:T(8,128)(2,1)}, bf16[12,128,128]{2,1,0:T(8,128)(2,1)S(1)}, u32[]{:S(2)}, u32[]{:S(2)}) collective-permute-start(bf16[12,128,128]{2,1,0:T(8,128)(2,1)} %slice_bitcast_fusion.1), channel_id=1, source_target_pairs={{0,64},{64,128},{128,192},{192,0},{1,65},{65,129},{129,193},{193,1... | collective-permute-start | bytes 1179656 | tf_op jit(solution)/shard_map/ppermute | solution.py:30
  55.7 12.4 %collective-permute-start.3 = (bf16[12,128,128]{2,1,0:T(8,128)(2,1)}, bf16[12,128,128]{2,1,0:T(8,128)(2,1)S(1)}, u32[]{:S(2)}, u32[]{:S(2)}) collective-permute-start(bf16[12,128,128]{2,1,0:T(8,128)(2,1)} %slice_bitcast_fusion), channel_id=1, source_target_pairs={{0,192},{64,0},{128,64},{192,128},{1,193},{65,1},{129,65},{193,129... | collective-permute-start | bytes 1179656 | tf_op jit(solution)/shard_map/ppermute | solution.py:30
  58.7 13.6 %collective-permute-start.4 = (bf16[12,128,128]{2,1,0:T(8,128)(2,1)S(1)}, bf16[12,128,128]{2,1,0:T(8,128)(2,1)}, u32[]{:S(2)}, u32[]{:S(2)}) collective-permute-start(bf16[12,128,128]{2,1,0:T(8,128)(2,1)S(1)} %bitcast.33), channel_id=1, source_target_pairs={{0,8},{4,12},{8,0},{12,4},{1,9},{5,13},{9,1},{13,5},{2,10},{6,14},... | collective-permute-start | bytes 1179656 | tf_op jit(solution)/shard_map/ppermute | solution.py:30
  59.0 20.7 %collective-permute-start.5 = (bf16[12,128,128]{2,1,0:T(8,128)(2,1)S(1)}, bf16[12,128,128]{2,1,0:T(8,128)(2,1)}, u32[]{:S(2)}, u32[]{:S(2)}) collective-permute-start(bf16[12,128,128]{2,1,0:T(8,128)(2,1)S(1)} %bitcast.34), channel_id=1, source_target_pairs={{0,12},{4,0},{8,4},{12,8},{1,13},{5,1},{9,5},{13,9},{2,14},{6,2},{... | collective-permute-start | bytes 1179656 | tf_op jit(solution)/shard_map/ppermute | solution.py:30
  61.4 20.7 %collective-permute-start.6 = (bf16[12,128,128]{2,1,0:T(8,128)(2,1)S(1)}, bf16[12,128,128]{2,1,0:T(8,128)(2,1)}, u32[]{:S(2)}, u32[]{:S(2)}) collective-permute-start(bf16[12,128,128]{2,1,0:T(8,128)(2,1)S(1)} %bitcast.35), channel_id=1, source_target_pairs={{0,4},{4,8},{8,12},{12,0},{1,5},{5,9},{9,13},{13,1},{2,6},{6,10},{... | collective-permute-start | bytes 1179656 | tf_op jit(solution)/shard_map/ppermute | solution.py:30
  79.7 16.2 %collective-permute-start.7 = (bf16[12,144,128]{2,1,0:T(8,128)(2,1)S(1)}, bf16[12,144,128]{2,1,0:T(8,128)(2,1)S(1)}, u32[]{:S(2)}, u32[]{:S(2)}) collective-permute-start(bf16[12,144,128]{2,1,0:T(8,128)(2,1)S(1)} %get-tuple-element.43), channel_id=1, source_target_pairs={{0,8},{4,12},{8,0},{12,4},{1,9},{5,13},{9,1},{13,5},{2,10},{6,14},... | collective-permute-start | bytes 1327112 | tf_op jit(solution)/shard_map/ppermute | solution.py:30
  93.8 15.5 %collective-permute-start.8 = (bf16[12,144,128]{2,1,0:T(8,128)(2,1)S(1)}, bf16[12,144,128]{2,1,0:T(8,128)(2,1)S(1)}, u32[]{:S(2)}, u32[]{:S(2)}) collective-permute-start(bf16[12,144,128]{2,1,0:T(8,128)(2,1)S(1)} %get-tuple-element.48), channel_id=1, source_target_pairs={{0,4},{4,8},{8,12},{12,0},{1,5},{5,9},{9,13},{13,1},{2,6},{6,10},{... | collective-permute-start | bytes 1327112 | tf_op jit(solution)/shard_map/ppermute | solution.py:30
  94.2 15.0 %collective-permute-start.9 = (bf16[12,144,128]{2,1,0:T(8,128)(2,1)S(1)}, bf16[12,144,128]{2,1,0:T(8,128)(2,1)S(1)}, u32[]{:S(2)}, u32[]{:S(2)}) collective-permute-start(bf16[12,144,128]{2,1,0:T(8,128)(2,1)S(1)} %get-tuple-element.50), channel_id=1, source_target_pairs={{0,12},{4,0},{8,4},{12,8},{1,13},{5,1},{9,5},{13,9},{2,14},{6,2},{... | collective-permute-start | bytes 1327112 | tf_op jit(solution)/shard_map/ppermute | solution.py:30
  110.5 22.2 %all-to-all-start.3 = ((bf16[16,96,128]{2,1,0:T(8,128)(2,1)}), bf16[16,96,128]{2,1,0:T(8,128)(2,1)S(1)}, u32[]{:S(2)}, u32[]{:S(2)}) async-start(bf16[16,96,128]{2,1,0:T(8,128)(2,1)} %bitcast.5), calls=%async_computation.3 | async-start | bytes 786432 | tf_op jit(solution)/shard_map/all_to_all | solution.py:338
  115.8 17.0 %collective-permute-start.10 = (f32[1,1536]{1,0:T(1,128)S(1)}, f32[1,1536]{1,0:T(1,128)S(1)}, u32[]{:S(2)}, u32[]{:S(2)}) collective-permute-start(f32[1,1536]{1,0:T(1,128)S(1)} %bitcast.43), channel_id=1, source_target_pairs={{0,0},{16,4},{32,8},{48,12},{4,16},{20,20},{36,24},{52,28},{8,32},... | collective-permute-start | bytes 18440 | tf_op jit(solution)/shard_map/ppermute | solution.py:371

commit v13 on v12

--- a/solution.py
+++ b/solution.py
@@ -15,7 +15,7 @@
 KEYS = RING * OWN
 NEAR = 3 * OWN
 CHUNK = 4
-WIDTH = 8
+WIDTHS = {1: 8, 2: 12}
 PAD = 16
 NEG = -1e30
 SCALE = HD**-0.5
@@ -70,6 +70,7 @@
 def attend_kernel(blocks, mode, lists, nears, counts, *refs):
     count = len(blocks)
     tiles = count * OWN
+    width = WIDTHS[count]
     queries, refs = refs[:count], refs[count:]
     if mode != "far":
         for_near, refs = refs[:3], refs[3:]
@@ -80,7 +81,7 @@
     size = (3 if mode == "near" else 2) * count
     outs, refs = refs[:size], refs[size:]
     rows, begins, sizes, qs, ks, vs, m_ref, l_ref, acc_ref = refs[:9]
-    s_refs, top_refs = refs[9 : 9 + WIDTH], refs[9 + WIDTH :]
+    s_refs, top_refs = refs[9 : 9 + width], refs[9 + width :]
     for b, q in enumerate(queries):
         qs[b * OWN : (b + 1) * OWN] = q[...]
     if mode != "far":
@@ -163,25 +164,27 @@
 
     def following(t, j):
         group = []
-        for _ in range(WIDTH):
+        for _ in range(width):
             t, j = advance(t, j)
             group += [t, j]
         return tuple(group)
 
     start = [jnp.int32(0), jnp.int32(0)]
-    for _ in range(WIDTH - 1):
+    for _ in range(width - 1):
         start += advance(*start[-2:])
-    for lane in range(WIDTH):
+    for lane in range(width):
         score(lane, start[2 * lane], start[2 * lane + 1])
 
     def step(_, now):
         later = following(*now[-2:])
-        for lane in range(WIDTH):
+        for lane in range(width):
             blend(lane, now[2 * lane], now[2 * lane + 1])
             score(lane, later[2 * lane], later[2 * lane + 1])
         return later
 
-    lax.fori_loop(0, (items + WIDTH - 1) // WIDTH, step, tuple(start))
+    end = lax.fori_loop(0, (items + width - 1) // width - 1, step, tuple(start))
+    for lane in range(width):
+        blend(lane, end[2 * lane], end[2 * lane + 1])
 
     if mode == "near":
         for b in range(count):
@@ -235,8 +238,8 @@
             pltpu.VMEM((keys, HD, BLK), jnp.bfloat16),
         ]
         + [pltpu.VMEM((slots, *shape), jnp.float32) for shape in shapes]
-        + [pltpu.VMEM((CHUNK * BLK, BLK), jnp.float32)] * WIDTH
-        + [pltpu.VMEM((1, BLK), jnp.float32)] * WIDTH,
+        + [pltpu.VMEM((CHUNK * BLK, BLK), jnp.float32)] * WIDTHS[count]
+        + [pltpu.VMEM((1, BLK), jnp.float32)] * WIDTHS[count],
         compiler_params=SPACE,
         cost_estimate=pl.CostEstimate(
             flops=pairs * 4 * BLK * BLK * HD,

time: 136 us -> 135 us (level)
  transfers between devices with their start and end apart: 14 -> 14, of which waited for: 6 -> 5; matrix products, arithmetic and copies ran while one was open for 4% -> 4% of each run, Pallas kernels for 22% -> 22%
where the time goes in v13:
time: 135 us; the launch traced here: 134 us
  starting transfers between devices  41.2 us (31%)
  waiting for transfers between devices  38.8 us (29%)
  Pallas kernels  31.1 us (23%)
  blocking collectives  13.3 us (10%)
  local copies, waits for them, and re-layouts  6.34 us (5%)
  other arithmetic  2.32 us (2%)
    pallas_call x4, Pallas kernels, attend(): pl.pallas_call(functools.partial(attend_kernel, blocks, mode), out_shape=...  29 us
    all_to_all x3, starting transfers between devices, exchange(): return lax.all_to_all(array, GROUP, split_axis=0, concat_axis=0, tiled=True)  18.3 us
    all_to_all x3, waiting for transfers between devices, exchange(): return lax.all_to_all(array, GROUP, split_axis=0, concat_axis=0, tiled=True)  18.1 us
    ppermute x10, starting transfers between devices, shift(): lax.ppermute(array, axis, [(i, (i + by) % RING) for i in range(RING)])  13.8 us
    all_to_all x1, blocking collectives, on_device(): lax.all_to_all(pick(spots, (e0, e1, e2, e3)), ('x', 'y'), split_axis=0, c...  13.3 us
    ppermute x10, waiting for transfers between devices, shift(): lax.ppermute(array, axis, [(i, (i + by) % RING) for i in range(RING)])  12.9 us
    ppermute x1, starting transfers between devices, on_device(): lax.ppermute(merge(parts).reshape(1, OWN * BLK), ('zh', 'y'), turned)  9.18 us
    ppermute x1, waiting for transfers between devices, on_device(): lax.ppermute(merge(parts).reshape(1, OWN * BLK), ('zh', 'y'), turned)  7.78 us
  transfers between devices with their start and end apart: 14, of which 5 were waited for; matrix products, arithmetic and copies ran while one was open for 4% of the time, Pallas kernels for 22%

profile of v13, /device:TPU:16, one launch (start us, length us, event | category | flops | bytes accessed | tf_op | source)
XLA Modules:
  0.0 134.2 jit_solution(16076520143034043353)
XLA Ops:
  0.7 1.1 copy.25
  2.1 1.0 maximum_bitcast_fusion
  3.1 8.7 %all-to-all-start = ((bf16[16,2,96,128]{3,2,1,0:T(8,128)(2,1)}), bf16[16,2,96,128]{3,2,1,0:T(8,128)(2,1)S(1)}, u32[]{:S(2)}, u32[]{:S(2)}) async-start(bf16[16,2,96,128]{3,2,1,0:T(8,128)(2,1)} %maximum_bitcast_fusion), calls=%async_computation | async-start | bytes 1572864 | tf_op jit(solution)/shard_map/all_to_all | solution.py:341
  12.5 1.0 select_reduce_fusion
  13.6 0.8 bitcast_bitcast_fusion
  14.4 18.1 %all-to-all-done.got_ref = bf16[16,2,96,128]{3,2,1,0:T(8,128)(2,1)S(1)} async-done(((bf16[16,2,96,128]{3,2,1,0:T(8,128)(2,1)}), bf16[16,2,96,128]{3,2,1,0:T(8,128)(2,1)S(1)}, u32[]{:S(2)}, u32[]{:S(2)}) %all-to-all-start) | async-done | bytes 786464 | tf_op jit(solution)/shard_map/all_to_all | solution.py:341
  32.6 1.6 %collective-permute-start = (bf16[2,12,128,128]{3,2,1,0:T(8,128)(2,1)S(1)}, bf16[2,12,128,128]{3,2,1,0:T(8,128)(2,1)S(1)}, u32[]{:S(2)}, u32[]{:S(2)}) collective-permute-start(bf16[2,12,128,128]{3,2,1,0:T(8,128)(2,1)S(1)} %prepare.1.refs_1_.refs_2_), channel_id=1, source_target_pairs={{0,64},{64,128},{128,192},{192,0},{1,65},{65,129},{129,193},{193,1... | collective-permute-start | bytes 2359304 | tf_op jit(solution)/shard_map/ppermute | solution.py:30
  34.2 1.7 %collective-permute-start.2 = (bf16[2,12,128,128]{3,2,1,0:T(8,128)(2,1)S(1)}, bf16[2,12,128,128]{3,2,1,0:T(8,128)(2,1)}, u32[]{:S(2)}, u32[]{:S(2)}) collective-permute-start(bf16[2,12,128,128]{3,2,1,0:T(8,128)(2,1)S(1)} %prepare.1.refs_1_.refs_2_), channel_id=1, source_target_pairs={{0,192},{64,0},{128,64},{192,128},{1,193},{65,1},{129,65},{193,129... | collective-permute-start | bytes 2359304 | tf_op jit(solution)/shard_map/ppermute | solution.py:30
  35.9 5.1 %all-to-all-start.1 = ((bf16[16,96,128]{2,1,0:T(8,128)(2,1)}), bf16[16,96,128]{2,1,0:T(8,128)(2,1)S(1)}, u32[]{:S(2)}, u32[]{:S(2)}) async-start(bf16[16,96,128]{2,1,0:T(8,128)(2,1)} %bitcast_bitcast_fusion), calls=%async_computation.1 | async-start | bytes 786432 | tf_op jit(solution)/shard_map/all_to_all | solution.py:341
  41.1 11.8 %collective-permute-done.refs_3_.refs_4_ = bf16[2,12,128,128]{3,2,1,0:T(8,128)(2,1)S(1)} collective-permute-done((bf16[2,12,128,128]{3,2,1,0:T(8,128)(2,1)S(1)}, bf16[2,12,128,128]{3,2,1,0:T(8,128)(2,1)S(1)}, u32[]{:S(2)}, u32[]{:S(2)}) %collective-permute-start) | collective-permute-done | bytes 786464 | tf_op jit(solution)/shard_map/ppermute | solution.py:30
  52.9 0.8 slice_bitcast_fusion.1
  53.6 0.3 collective-permute-start.1
  53.9 1.8 %slice_bitcast_fusion = bf16[12,128,128]{2,1,0:T(8,128)(2,1)} fusion(bf16[2,12,128,128]{3,2,1,0:T(8,128)(2,1)} %collective-permute-done.2.refs_2_.refs_3_), kind=kLoop, calls=%fused_computation.10 | loop fusion | bytes 786432 | tf_op jit(solution)/shard_map/squeeze | solution.py:355
  55.7 3.0 %collective-permute-start.3 = (bf16[12,128,128]{2,1,0:T(8,128)(2,1)}, bf16[12,128,128]{2,1,0:T(8,128)(2,1)S(1)}, u32[]{:S(2)}, u32[]{:S(2)}) collective-permute-start(bf16[12,128,128]{2,1,0:T(8,128)(2,1)} %slice_bitcast_fusion), channel_id=1, source_target_pairs={{0,192},{64,0},{128,64},{192,128},{1,193},{65,1},{129,65},{193,129... | collective-permute-start | bytes 1179656 | tf_op jit(solution)/shard_map/ppermute | solution.py:30
  58.7 0.3 collective-permute-start.4
  59.0 2.4 %collective-permute-start.5 = (bf16[12,128,128]{2,1,0:T(8,128)(2,1)S(1)}, bf16[12,128,128]{2,1,0:T(8,128)(2,1)}, u32[]{:S(2)}, u32[]{:S(2)}) collective-permute-start(bf16[12,128,128]{2,1,0:T(8,128)(2,1)S(1)} %bitcast.34), channel_id=1, source_target_pairs={{0,12},{4,0},{8,4},{12,8},{1,13},{5,1},{9,5},{13,9},{2,14},{6,2},{... | collective-permute-start | bytes 1179656 | tf_op jit(solution)/shard_map/ppermute | solution.py:30
  61.5 6.4 %near.1 = (f32[12,1,128]{2,1,0:T(1,128)S(1)}, f32[12,8,128]{2,1,0:T(8,128)S(1)}, f32[12,128,128]{2,1,0:T(8,128)S(1)}) custom-call(s32[48,52]{1,0:T(8,128)S(1)} %copy.18.lists, s32[48]{0:T(128)S(1)} %get-tuple-element.28.nears, s32[48]{0:T(128)S(1)} %get-tuple-element.29.counts, bf16[12,128,128]{2,1,0:T(8,128)(2,1)S(1)} %bitcast.36, ...), custom_call_target="tpu_custom_call" | custom-call | flops 1207959552 | bytes 5242880 | tf_op jit(solution)/shard_map/near/pallas_call | solution.py:229
  68.1 3.3 %far.1 = (bf16[12,144,128]{2,1,0:T(8,128)(2,1)S(1)}, f32[12,128]{1,0:T(8,128)S(1)}) custom-call(s32[48,52]{1,0:T(8,128)S(1)} %copy.18.lists, s32[48]{0:T(128)S(1)} %get-tuple-element.28.nears, s32[48]{0:T(128)S(1)} %get-tuple-element.29.counts, bf16[12,128,128]{2,1,0:T(8,128)(2,1)S(1)} %bitcast.37, ...), custom_call_target="tpu_custom_call" | custom-call | flops 402653184 | bytes 5242880 | tf_op jit(solution)/shard_map/far/pallas_call | solution.py:229
  71.4 0.9 collective-permute-done.4.refs_0_
  72.3 7.5 %full.2 = (bf16[12,144,128]{2,1,0:T(8,128)(2,1)S(1)}, f32[12,128]{1,0:T(8,128)S(1)}) custom-call(s32[48,52]{1,0:T(8,128)S(1)} %copy.18.lists, s32[48]{0:T(128)S(1)} %get-tuple-element.28.nears, s32[48]{0:T(128)S(1)} %get-tuple-element.29.counts, bf16[12,128,128]{2,1,0:T(8,128)(2,1)} %collective-permute-done.4.refs_0_, ...), custom_call_target="tpu_custom_call" | custom-call | flops 1610612736 | bytes 5242880 | tf_op jit(solution)/shard_map/full/pallas_call | solution.py:229
  79.8 1.8 %collective-permute-start.7 = (bf16[12,144,128]{2,1,0:T(8,128)(2,1)S(1)}, bf16[12,144,128]{2,1,0:T(8,128)(2,1)S(1)}, u32[]{:S(2)}, u32[]{:S(2)}) collective-permute-start(bf16[12,144,128]{2,1,0:T(8,128)(2,1)S(1)} %get-tuple-element.43), channel_id=1, source_target_pairs={{0,8},{4,12},{8,0},{12,4},{1,9},{5,13},{9,1},{13,5},{2,10},{6,14},... | collective-permute-start | bytes 1327112 | tf_op jit(solution)/shard_map/ppermute | solution.py:30
  81.6 11.9 %full.3 = (bf16[12,144,128]{2,1,0:T(8,128)(2,1)S(1)}, bf16[12,144,128]{2,1,0:T(8,128)(2,1)S(1)}, f32[12,128]{1,0:T(8,128)S(1)}, f32[12,128]{1,0:T(8,128)S(1)}) custom-call(s32[48,52]{1,0:T(8,128)S(1)} %copy.18.lists, s32[48]{0:T(128)S(1)} %get-tuple-element.28.nears, s32[48]{0:T(128)S(1)} %get-tuple-element.29.counts, ...), custom_call_target="tpu_custom_call" | custom-call | flops 3221225472 | bytes 5242880 | tf_op jit(solution)/shard_map/full/pallas_call | solution.py:229
  93.5 2.1 %collective-permute-start.8 = (bf16[12,144,128]{2,1,0:T(8,128)(2,1)S(1)}, bf16[12,144,128]{2,1,0:T(8,128)(2,1)S(1)}, u32[]{:S(2)}, u32[]{:S(2)}) collective-permute-start(bf16[12,144,128]{2,1,0:T(8,128)(2,1)S(1)} %get-tuple-element.48), channel_id=1, source_target_pairs={{0,4},{4,8},{8,12},{12,0},{1,5},{5,9},{9,13},{13,1},{2,6},{6,10},{... | collective-permute-start | bytes 1327112 | tf_op jit(solution)/shard_map/ppermute | solution.py:30
  95.7 0.5 collective-permute-start.9
  96.2 0.7 pick.1
  96.8 13.3 %all_to_all.20.parts = f32[16,12,128]{2,1,0:T(8,128)S(1)} all-to-all(f32[16,12,128]{2,1,0:T(8,128)S(1)} %pick.1), channel_id=1, replica_groups=mesh['x'=4,'zh'=4,'y'=4,'zl'=2,'core'=2] {'x','y'}, dimensions={0} | all-to-all | bytes 196608 | tf_op jit(solution)/shard_map/all_to_all | solution.py:366
  110.1 1.2 combine.1
  111.3 4.4 %all-to-all-start.3 = ((bf16[16,96,128]{2,1,0:T(8,128)(2,1)}), bf16[16,96,128]{2,1,0:T(8,128)(2,1)S(1)}, u32[]{:S(2)}, u32[]{:S(2)}) async-start(bf16[16,96,128]{2,1,0:T(8,128)(2,1)} %bitcast.5), calls=%async_computation.3 | async-start | bytes 786432 | tf_op jit(solution)/shard_map/all_to_all | solution.py:341
  115.9 9.2 %collective-permute-start.10 = (f32[1,1536]{1,0:T(1,128)S(1)}, f32[1,1536]{1,0:T(1,128)S(1)}, u32[]{:S(2)}, u32[]{:S(2)}) collective-permute-start(f32[1,1536]{1,0:T(1,128)S(1)} %bitcast.43), channel_id=1, source_target_pairs={{0,0},{16,4},{32,8},{48,12},{4,16},{20,20},{36,24},{52,28},{8,32},... | collective-permute-start | bytes 18440 | tf_op jit(solution)/shard_map/ppermute | solution.py:374
  125.0 7.8 %collective-permute-done.10 = f32[1,1536]{1,0:T(1,128)S(1)} collective-permute-done((f32[1,1536]{1,0:T(1,128)S(1)}, f32[1,1536]{1,0:T(1,128)S(1)}, u32[]{:S(2)}, u32[]{:S(2)}) %collective-permute-start.10) | collective-permute-done | bytes 6176 | tf_op jit(solution)/shard_map/ppermute | solution.py:374
  132.8 0.8 copy_bitcast_fusion
  133.6 0.6 copy.32
  (34 shorter events, 1.6 us)
Async XLA Ops:
  0.6 12.9 %copy-start = (bf16[96,2048]{1,0:T(8,128)(2,1)S(1)}, bf16[96,2048]{1,0:T(8,128)(2,1)}, u32[]{:S(2)}) copy-start(bf16[96,2048]{1,0:T(8,128)(2,1)} %param.6) | copy-start | bytes 1179652
  0.6 1.3 copy-start.1
  3.1 8.7 %copy-start.4 = (s32[192]{0:T(256)S(1)}, s32[192]{0:T(256)}, u32[]{:S(2)}) copy-start(s32[192]{0:T(256)} %param.10) | copy-start | bytes 2308
  3.1 8.8 %copy-start.2 = (s32[192,96]{1,0:T(8,128)S(1)}, s32[192,96]{1,0:T(8,128)}, u32[]{:S(2)}) copy-start(s32[192,96]{1,0:T(8,128)} %param.9) | copy-start | bytes 221188
  3.1 10.4 %copy-start.3 = (s32[192]{0:T(256)S(1)}, s32[192]{0:T(256)}, u32[]{:S(2)}) copy-start(s32[192]{0:T(256)} %param.11) | copy-start | bytes 2308
  3.1 29.4 %all-to-all-start = ((bf16[16,2,96,128]{3,2,1,0:T(8,128)(2,1)}), bf16[16,2,96,128]{3,2,1,0:T(8,128)(2,1)S(1)}, u32[]{:S(2)}, u32[]{:S(2)}) async-start(bf16[16,2,96,128]{3,2,1,0:T(8,128)(2,1)} %maximum_bitcast_fusion), calls=%async_computation | async-start | bytes 1572864 | tf_op jit(solution)/shard_map/all_to_all | solution.py:341
  32.6 20.2 %collective-permute-start = (bf16[2,12,128,128]{3,2,1,0:T(8,128)(2,1)S(1)}, bf16[2,12,128,128]{3,2,1,0:T(8,128)(2,1)S(1)}, u32[]{:S(2)}, u32[]{:S(2)}) collective-permute-start(bf16[2,12,128,128]{3,2,1,0:T(8,128)(2,1)S(1)} %prepare.1.refs_1_.refs_2_), channel_id=1, source_target_pairs={{0,64},{64,128},{128,192},{192,0},{1,65},{65,129},{129,193},{193,1... | collective-permute-start | bytes 2359304 | tf_op jit(solution)/shard_map/ppermute | solution.py:30
  34.2 19.7 %collective-permute-start.2 = (bf16[2,12,128,128]{3,2,1,0:T(8,128)(2,1)S(1)}, bf16[2,12,128,128]{3,2,1,0:T(8,128)(2,1)}, u32[]{:S(2)}, u32[]{:S(2)}) collective-permute-start(bf16[2,12,128,128]{3,2,1,0:T(8,128)(2,1)S(1)} %prepare.1.refs_1_.refs_2_), channel_id=1, source_target_pairs={{0,192},{64,0},{128,64},{192,128},{1,193},{65,1},{129,65},{193,129... | collective-permute-start | bytes 2359304 | tf_op jit(solution)/shard_map/ppermute | solution.py:30
  35.9 22.7 %all-to-all-start.1 = ((bf16[16,96,128]{2,1,0:T(8,128)(2,1)}), bf16[16,96,128]{2,1,0:T(8,128)(2,1)S(1)}, u32[]{:S(2)}, u32[]{:S(2)}) async-start(bf16[16,96,128]{2,1,0:T(8,128)(2,1)} %bitcast_bitcast_fusion), calls=%async_computation.1 | async-start | bytes 786432 | tf_op jit(solution)/shard_map/all_to_all | solution.py:341
  53.6 14.3 %collective-permute-start.1 = (bf16[12,128,128]{2,1,0:T(8,128)(2,1)}, bf16[12,128,128]{2,1,0:T(8,128)(2,1)S(1)}, u32[]{:S(2)}, u32[]{:S(2)}) collective-permute-start(bf16[12,128,128]{2,1,0:T(8,128)(2,1)} %slice_bitcast_fusion.1), channel_id=1, source_target_pairs={{0,64},{64,128},{128,192},{192,0},{1,65},{65,129},{129,193},{193,1... | collective-permute-start | bytes 1179656 | tf_op jit(solution)/shard_map/ppermute | solution.py:30
  55.7 12.4 %collective-permute-start.3 = (bf16[12,128,128]{2,1,0:T(8,128)(2,1)}, bf16[12,128,128]{2,1,0:T(8,128)(2,1)S(1)}, u32[]{:S(2)}, u32[]{:S(2)}) collective-permute-start(bf16[12,128,128]{2,1,0:T(8,128)(2,1)} %slice_bitcast_fusion), channel_id=1, source_target_pairs={{0,192},{64,0},{128,64},{192,128},{1,193},{65,1},{129,65},{193,129... | collective-permute-start | bytes 1179656 | tf_op jit(solution)/shard_map/ppermute | solution.py:30
  58.7 13.6 %collective-permute-start.4 = (bf16[12,128,128]{2,1,0:T(8,128)(2,1)S(1)}, bf16[12,128,128]{2,1,0:T(8,128)(2,1)}, u32[]{:S(2)}, u32[]{:S(2)}) collective-permute-start(bf16[12,128,128]{2,1,0:T(8,128)(2,1)S(1)} %bitcast.33), channel_id=1, source_target_pairs={{0,8},{4,12},{8,0},{12,4},{1,9},{5,13},{9,1},{13,5},{2,10},{6,14},... | collective-permute-start | bytes 1179656 | tf_op jit(solution)/shard_map/ppermute | solution.py:30
  59.0 20.8 %collective-permute-start.5 = (bf16[12,128,128]{2,1,0:T(8,128)(2,1)S(1)}, bf16[12,128,128]{2,1,0:T(8,128)(2,1)}, u32[]{:S(2)}, u32[]{:S(2)}) collective-permute-start(bf16[12,128,128]{2,1,0:T(8,128)(2,1)S(1)} %bitcast.34), channel_id=1, source_target_pairs={{0,12},{4,0},{8,4},{12,8},{1,13},{5,1},{9,5},{13,9},{2,14},{6,2},{... | collective-permute-start | bytes 1179656 | tf_op jit(solution)/shard_map/ppermute | solution.py:30
  61.4 20.2 %collective-permute-start.6 = (bf16[12,128,128]{2,1,0:T(8,128)(2,1)S(1)}, bf16[12,128,128]{2,1,0:T(8,128)(2,1)}, u32[]{:S(2)}, u32[]{:S(2)}) collective-permute-start(bf16[12,128,128]{2,1,0:T(8,128)(2,1)S(1)} %bitcast.35), channel_id=1, source_target_pairs={{0,4},{4,8},{8,12},{12,0},{1,5},{5,9},{9,13},{13,1},{2,6},{6,10},{... | collective-permute-start | bytes 1179656 | tf_op jit(solution)/shard_map/ppermute | solution.py:30
  79.8 16.4 %collective-permute-start.7 = (bf16[12,144,128]{2,1,0:T(8,128)(2,1)S(1)}, bf16[12,144,128]{2,1,0:T(8,128)(2,1)S(1)}, u32[]{:S(2)}, u32[]{:S(2)}) collective-permute-start(bf16[12,144,128]{2,1,0:T(8,128)(2,1)S(1)} %get-tuple-element.43), channel_id=1, source_target_pairs={{0,8},{4,12},{8,0},{12,4},{1,9},{5,13},{9,1},{13,5},{2,10},{6,14},... | collective-permute-start | bytes 1327112 | tf_op jit(solution)/shard_map/ppermute | solution.py:30
  93.5 16.6 %collective-permute-start.8 = (bf16[12,144,128]{2,1,0:T(8,128)(2,1)S(1)}, bf16[12,144,128]{2,1,0:T(8,128)(2,1)S(1)}, u32[]{:S(2)}, u32[]{:S(2)}) collective-permute-start(bf16[12,144,128]{2,1,0:T(8,128)(2,1)S(1)} %get-tuple-element.48), channel_id=1, source_target_pairs={{0,4},{4,8},{8,12},{12,0},{1,5},{5,9},{9,13},{13,1},{2,6},{6,10},{... | collective-permute-start | bytes 1327112 | tf_op jit(solution)/shard_map/ppermute | solution.py:30
  95.7 14.4 %collective-permute-start.9 = (bf16[12,144,128]{2,1,0:T(8,128)(2,1)S(1)}, bf16[12,144,128]{2,1,0:T(8,128)(2,1)S(1)}, u32[]{:S(2)}, u32[]{:S(2)}) collective-permute-start(bf16[12,144,128]{2,1,0:T(8,128)(2,1)S(1)} %get-tuple-element.50), channel_id=1, source_target_pairs={{0,12},{4,0},{8,4},{12,8},{1,13},{5,1},{9,5},{13,9},{2,14},{6,2},{... | collective-permute-start | bytes 1327112 | tf_op jit(solution)/shard_map/ppermute | solution.py:30
  111.3 21.5 %all-to-all-start.3 = ((bf16[16,96,128]{2,1,0:T(8,128)(2,1)}), bf16[16,96,128]{2,1,0:T(8,128)(2,1)S(1)}, u32[]{:S(2)}, u32[]{:S(2)}) async-start(bf16[16,96,128]{2,1,0:T(8,128)(2,1)} %bitcast.5), calls=%async_computation.3 | async-start | bytes 786432 | tf_op jit(solution)/shard_map/all_to_all | solution.py:341
  115.9 17.0 %collective-permute-start.10 = (f32[1,1536]{1,0:T(1,128)S(1)}, f32[1,1536]{1,0:T(1,128)S(1)}, u32[]{:S(2)}, u32[]{:S(2)}) collective-permute-start(f32[1,1536]{1,0:T(1,128)S(1)} %bitcast.43), channel_id=1, source_target_pairs={{0,0},{16,4},{32,8},{48,12},{4,16},{20,20},{36,24},{52,28},{8,32},... | collective-permute-start | bytes 18440 | tf_op jit(solution)/shard_map/ppermute | solution.py:374

commit v14 on v13

--- a/solution.py
+++ b/solution.py
@@ -72,40 +72,36 @@
     tiles = count * OWN
     width = WIDTHS[count]
     queries, refs = refs[:count], refs[count:]
-    if mode != "far":
-        for_near, refs = refs[:3], refs[3:]
+    for_near, refs = refs[:3], refs[3:]
     if mode != "near":
         (k2, v2), refs = refs[:2], refs[2:]
-    if mode == "far":
-        states, refs = refs[: 3 * count], refs[3 * count :]
+    if mode == "rest":
+        state, refs = refs[:3], refs[3:]
     size = (3 if mode == "near" else 2) * count
     outs, refs = refs[:size], refs[size:]
     rows, begins, sizes, qs, ks, vs, m_ref, l_ref, acc_ref = refs[:9]
     s_refs, top_refs = refs[9 : 9 + width], refs[9 + width :]
     for b, q in enumerate(queries):
         qs[b * OWN : (b + 1) * OWN] = q[...]
-    if mode != "far":
-        for b, kv in enumerate(for_near):
-            ks[b * OWN : (b + 1) * OWN] = kv[0]
-            vs[b * OWN : (b + 1) * OWN] = kv[1]
+    for b, kv in enumerate(for_near):
+        ks[b * OWN : (b + 1) * OWN] = kv[0]
+        vs[b * OWN : (b + 1) * OWN] = kv[1]
     if mode != "near":
-        at = 0 if mode == "far" else NEAR
-        ks[at : at + OWN] = k2[...]
-        vs[at : at + OWN] = v2[...]
+        ks[NEAR:KEYS] = k2[...]
+        vs[NEAR:KEYS] = v2[...]
     m_ref[...] = jnp.full(m_ref.shape, NEG, jnp.float32)
     l_ref[...] = jnp.zeros(l_ref.shape, jnp.float32)
     acc_ref[...] = jnp.zeros(acc_ref.shape, jnp.float32)
-    if mode == "far":
-        for b in range(count):
-            for held, state in zip((m_ref, l_ref, acc_ref), states[3 * b : 3 * b + 3]):
-                held[b * OWN : (b + 1) * OWN] = state[...]
+    if mode == "rest":
+        for held, part in zip((m_ref, l_ref, acc_ref), state):
+            held[:OWN] = part[...]
     yi = lax.axis_index("y")
     items = jnp.int32(0)
     for b, block in enumerate(blocks):
         owner = lax.rem(yi + block, RING) * 3
         for t in range(OWN):
             row = owner + (t // 3 * OWN + t % 3)
-            begin = nears[row] if mode == "far" else jnp.int32(0)
+            begin = nears[row] if mode == "rest" and b == 0 else jnp.int32(0)
             total = (nears[row] if mode == "near" else counts[row]) - begin
             rows[b * OWN + t] = row
             begins[b * OWN + t] = begin
@@ -123,9 +119,7 @@
         row = rows[t]
         at = begins[t] + j * CHUNK
         found = [lists[row, at + u] for u in range(CHUNK)]
-        if mode == "near":
-            return [jnp.minimum(u, NEAR - 1) for u in found]
-        return [jnp.maximum(u - NEAR, 0) for u in found] if mode == "far" else found
+        return [jnp.minimum(u, NEAR - 1) for u in found] if mode == "near" else found
 
     def score(lane, t, j):
         left = sizes[t] - j * CHUNK
@@ -217,7 +211,7 @@
 def attend(blocks, mode, lists, queries, keys_values, states=()):
     count = len(blocks)
     slots = count * OWN + 1
-    keys = {"near": NEAR, "far": OWN, "full": KEYS}[mode]
+    keys = NEAR if mode == "near" else KEYS
     pairs = count * keys * 4
     shapes = ((1, BLK), (8, BLK), (HD, BLK))
     if mode == "near":
@@ -355,10 +349,8 @@
     k2, v2 = shift(kv3[0], "x", 1), shift(kv1[1], "x", -1)
     q0, q1, q2, q3 = around(q0, "y")
     state = attend((0,), "near", lists, (q0,), (kv0, kv1, kv3))
-    o0, e0 = attend((0,), "far", lists, (q0,), (k2, v2), state)
-    q2, o0 = lax.optimization_barrier((q2, o0))
     kv = (kv0, kv1, kv3, k2, v2)
-    o2, e2 = attend((2,), "full", lists, (q2,), kv)
+    o0, o2, e0, e2 = attend((0, 2), "rest", lists, (q0, q2), kv, state)
     q1, o2 = lax.optimization_barrier((q1, o2))
     o2 = shift(o2, "y", 2)
     o1, o3, e1, e3 = attend((1, 3), "full", lists, (q1, q3), kv)

time: 135 us -> 138 us (1.022)
  starting transfers between devices: 41.2 us -> 44 us
  waiting for transfers between devices: 38.8 us -> 41.5 us
  Pallas kernels: 31.1 us -> 28.7 us
    all_to_all x3, waiting for transfers between devices: 18.1 us -> 30 us  [exchange(): return lax.all_to_all(array, GROUP, split_axis=0, concat_axis=0, tiled=True)]
    ppermute x10, waiting for transfers between devices: 12.9 us -> 3.81 us  [shift(): lax.ppermute(array, axis, [(i, (i + by) % RING) for i in range(RING)])]
    pallas_call x4 -> x3, Pallas kernels: 29 us -> 26.6 us  [attend(): pl.pallas_call(functools.partial(attend_kernel, blocks, mode), out_shape=...]
    all_to_all x3, starting transfers between devices: 18.3 us -> 20.4 us  [exchange(): return lax.all_to_all(array, GROUP, split_axis=0, concat_axis=0, tiled=True)]
    unnamed x14 -> x18, local copies, waits for them, and re-layouts: 1.83 us -> 2.96 us
  transfers between devices with their start and end apart: 14 -> 14, of which waited for: 5 -> 5; matrix products, arithmetic and copies ran while one was open for 4% -> 3% of each run, Pallas kernels for 22% -> 20%
where the time goes in v14:
time: 138 us; the launch traced here: 136 us
  starting transfers between devices  44 us (32%)
  waiting for transfers between devices  41.5 us (30%)
  Pallas kernels  28.7 us (21%)
  blocking collectives  12.1 us (9%)
  local copies, waits for them, and re-layouts  6.53 us (5%)
  other arithmetic  2.32 us (2%)
    all_to_all x3, waiting for transfers between devices, exchange(): return lax.all_to_all(array, GROUP, split_axis=0, concat_axis=0, tiled=True)  30 us
    pallas_call x3, Pallas kernels, attend(): pl.pallas_call(functools.partial(attend_kernel, blocks, mode), out_shape=...  26.6 us
    all_to_all x3, starting transfers between devices, exchange(): return lax.all_to_all(array, GROUP, split_axis=0, concat_axis=0, tiled=True)  20.4 us
    ppermute x10, starting transfers between devices, shift(): lax.ppermute(array, axis, [(i, (i + by) % RING) for i in range(RING)])  14.4 us
    all_to_all x1, blocking collectives, on_device(): lax.all_to_all(pick(spots, (e0, e1, e2, e3)), ('x', 'y'), split_axis=0, c...  12.1 us
    ppermute x1, starting transfers between devices, on_device(): lax.ppermute(merge(parts).reshape(1, OWN * BLK), ('zh', 'y'), turned)  9.19 us
    ppermute x1, waiting for transfers between devices, on_device(): lax.ppermute(merge(parts).reshape(1, OWN * BLK), ('zh', 'y'), turned)  7.78 us
    ppermute x10, waiting for transfers between devices, shift(): lax.ppermute(array, axis, [(i, (i + by) % RING) for i in range(RING)])  3.81 us
  transfers between devices with their start and end apart: 14, of which 5 were waited for; matrix products, arithmetic and copies ran while one was open for 3% of the time, Pallas kernels for 20%

profile of v14, /device:TPU:16, one launch (start us, length us, event | category | flops | bytes accessed | tf_op | source)
XLA Modules:
  0.0 136.3 jit_solution(15667480293889042283)
XLA Ops:
  0.7 1.1 copy.24
  2.1 1.0 maximum_bitcast_fusion
  3.1 8.7 %all-to-all-start = ((bf16[16,2,96,128]{3,2,1,0:T(8,128)(2,1)}), bf16[16,2,96,128]{3,2,1,0:T(8,128)(2,1)S(1)}, u32[]{:S(2)}, u32[]{:S(2)}) async-start(bf16[16,2,96,128]{3,2,1,0:T(8,128)(2,1)} %maximum_bitcast_fusion), calls=%async_computation | async-start | bytes 1572864 | tf_op jit(solution)/shard_map/all_to_all | solution.py:335
  12.5 1.0 select_reduce_fusion
  13.6 0.8 bitcast_bitcast_fusion
  14.4 18.1 %all-to-all-done.got_ref = bf16[16,2,96,128]{3,2,1,0:T(8,128)(2,1)S(1)} async-done(((bf16[16,2,96,128]{3,2,1,0:T(8,128)(2,1)}), bf16[16,2,96,128]{3,2,1,0:T(8,128)(2,1)S(1)}, u32[]{:S(2)}, u32[]{:S(2)}) %all-to-all-start) | async-done | bytes 786464 | tf_op jit(solution)/shard_map/all_to_all | solution.py:335
  32.6 1.6 %collective-permute-start.2 = (bf16[2,12,128,128]{3,2,1,0:T(8,128)(2,1)S(1)}, bf16[2,12,128,128]{3,2,1,0:T(8,128)(2,1)S(1)}, u32[]{:S(2)}, u32[]{:S(2)}) collective-permute-start(bf16[2,12,128,128]{3,2,1,0:T(8,128)(2,1)S(1)} %prepare.1.refs_1_.refs_2_), channel_id=1, source_target_pairs={{0,64},{64,128},{128,192},{192,0},{1,65},{65,129},{129,193},{193,1... | collective-permute-start | bytes 2359304 | tf_op jit(solution)/shard_map/ppermute | solution.py:30
  34.2 5.1 %all-to-all-start.1 = ((bf16[16,96,128]{2,1,0:T(8,128)(2,1)}), bf16[16,96,128]{2,1,0:T(8,128)(2,1)S(1)}, u32[]{:S(2)}, u32[]{:S(2)}) async-start(bf16[16,96,128]{2,1,0:T(8,128)(2,1)} %bitcast_bitcast_fusion), calls=%async_computation.1 | async-start | bytes 786432 | tf_op jit(solution)/shard_map/all_to_all | solution.py:335
  39.3 1.8 %collective-permute-start.1 = (bf16[2,12,128,128]{3,2,1,0:T(8,128)(2,1)S(1)}, bf16[2,12,128,128]{3,2,1,0:T(8,128)(2,1)S(1)}, u32[]{:S(2)}, u32[]{:S(2)}) collective-permute-start(bf16[2,12,128,128]{3,2,1,0:T(8,128)(2,1)S(1)} %prepare.1.refs_1_.refs_2_), channel_id=1, source_target_pairs={{0,192},{64,0},{128,64},{192,128},{1,193},{65,1},{129,65},{193,129... | collective-permute-start | bytes 2359304 | tf_op jit(solution)/shard_map/ppermute | solution.py:30
  41.2 11.9 %all-to-all-done.1 = bf16[16,96,128]{2,1,0:T(8,128)(2,1)S(1)} async-done(((bf16[16,96,128]{2,1,0:T(8,128)(2,1)}), bf16[16,96,128]{2,1,0:T(8,128)(2,1)S(1)}, u32[]{:S(2)}, u32[]{:S(2)}) %all-to-all-start.1) | async-done | bytes 393248 | tf_op jit(solution)/shard_map/all_to_all | solution.py:335
  53.0 0.3 collective-permute-start
  53.4 0.8 slice_bitcast_fusion.1
  54.1 1.5 %collective-permute-start.3 = (bf16[12,128,128]{2,1,0:T(8,128)(2,1)}, bf16[12,128,128]{2,1,0:T(8,128)(2,1)}, u32[]{:S(2)}, u32[]{:S(2)}) collective-permute-start(bf16[12,128,128]{2,1,0:T(8,128)(2,1)} %slice_bitcast_fusion.1), channel_id=1, source_target_pairs={{0,64},{64,128},{128,192},{192,0},{1,65},{65,129},{129,193},{193,1... | collective-permute-start | bytes 1179656 | tf_op jit(solution)/shard_map/ppermute | solution.py:30
  55.6 3.7 %collective-permute-done.1.refs_2_.refs_3_ = bf16[2,12,128,128]{3,2,1,0:T(8,128)(2,1)S(1)} collective-permute-done((bf16[2,12,128,128]{3,2,1,0:T(8,128)(2,1)S(1)}, bf16[2,12,128,128]{3,2,1,0:T(8,128)(2,1)S(1)}, u32[]{:S(2)}, u32[]{:S(2)}) %collective-permute-start.1) | collective-permute-done | bytes 786464 | tf_op jit(solution)/shard_map/ppermute | solution.py:30
  59.3 0.8 slice_bitcast_fusion
  60.1 3.0 %collective-permute-start.4 = (bf16[12,128,128]{2,1,0:T(8,128)(2,1)}, bf16[12,128,128]{2,1,0:T(8,128)(2,1)}, u32[]{:S(2)}, u32[]{:S(2)}) collective-permute-start(bf16[12,128,128]{2,1,0:T(8,128)(2,1)} %slice_bitcast_fusion), channel_id=1, source_target_pairs={{0,192},{64,0},{128,64},{192,128},{1,193},{65,1},{129,65},{193,129... | collective-permute-start | bytes 1179656 | tf_op jit(solution)/shard_map/ppermute | solution.py:30
  63.2 0.5 collective-permute-start.5
  63.6 1.6 %collective-permute-start.6 = (bf16[12,128,128]{2,1,0:T(8,128)(2,1)S(1)}, bf16[12,128,128]{2,1,0:T(8,128)(2,1)S(1)}, u32[]{:S(2)}, u32[]{:S(2)}) collective-permute-start(bf16[12,128,128]{2,1,0:T(8,128)(2,1)S(1)} %bitcast.35), channel_id=1, source_target_pairs={{0,4},{4,8},{8,12},{12,0},{1,5},{5,9},{9,13},{13,1},{2,6},{6,10},{... | collective-permute-start | bytes 1179656 | tf_op jit(solution)/shard_map/ppermute | solution.py:30
  65.2 6.2 %near.1 = (f32[12,1,128]{2,1,0:T(1,128)S(1)}, f32[12,8,128]{2,1,0:T(8,128)S(1)}, f32[12,128,128]{2,1,0:T(8,128)S(1)}) custom-call(s32[48,52]{1,0:T(8,128)S(1)} %copy.18.lists, s32[48]{0:T(128)S(1)} %get-tuple-element.26.nears, s32[48]{0:T(128)S(1)} %get-tuple-element.27.counts, bf16[12,128,128]{2,1,0:T(8,128)(2,1)S(1)} %bitcast.36, ...), custom_call_target="tpu_custom_call" | custom-call | flops 1207959552 | bytes 5242880 | tf_op jit(solution)/shard_map/near/pallas_call | solution.py:223
  71.6 1.1 copy-done.2
  72.7 8.8 %rest.1 = (bf16[12,144,128]{2,1,0:T(8,128)(2,1)S(1)}, bf16[12,144,128]{2,1,0:T(8,128)(2,1)S(1)}, f32[12,128]{1,0:T(8,128)S(1)}, f32[12,128]{1,0:T(8,128)S(1)}) custom-call(s32[48,52]{1,0:T(8,128)S(1)} %copy.18.lists, s32[48]{0:T(128)S(1)} %get-tuple-element.26.nears, s32[48]{0:T(128)S(1)} %get-tuple-element.27.counts, bf16[12,128,128]{2,1,0:T(8,128)(2,1)S(1)} %bitcast.37, ...), custom_call_target="tpu_custom_call" | custom-call | flops 3221225472 | bytes 5242880 | tf_op jit(solution)/shard_map/rest/pallas_call | solution.py:223
  81.5 2.1 %collective-permute-start.7 = (bf16[12,144,128]{2,1,0:T(8,128)(2,1)S(1)}, bf16[12,144,128]{2,1,0:T(8,128)(2,1)S(1)}, u32[]{:S(2)}, u32[]{:S(2)}) collective-permute-start(bf16[12,144,128]{2,1,0:T(8,128)(2,1)S(1)} %get-tuple-element.39), channel_id=1, source_target_pairs={{0,8},{4,12},{8,0},{12,4},{1,9},{5,13},{9,1},{13,5},{2,10},{6,14},... | collective-permute-start | bytes 1327112 | tf_op jit(solution)/shard_map/ppermute | solution.py:30
  83.6 11.6 %full.1 = (bf16[12,144,128]{2,1,0:T(8,128)(2,1)S(1)}, bf16[12,144,128]{2,1,0:T(8,128)(2,1)S(1)}, f32[12,128]{1,0:T(8,128)S(1)}, f32[12,128]{1,0:T(8,128)S(1)}) custom-call(s32[48,52]{1,0:T(8,128)S(1)} %copy.18.lists, s32[48]{0:T(128)S(1)} %get-tuple-element.26.nears, s32[48]{0:T(128)S(1)} %get-tuple-element.27.counts, ...), custom_call_target="tpu_custom_call" | custom-call | flops 3221225472 | bytes 5242880 | tf_op jit(solution)/shard_map/full/pallas_call | solution.py:223
  95.3 2.0 %collective-permute-start.9 = (bf16[12,144,128]{2,1,0:T(8,128)(2,1)S(1)}, bf16[12,144,128]{2,1,0:T(8,128)(2,1)S(1)}, u32[]{:S(2)}, u32[]{:S(2)}) collective-permute-start(bf16[12,144,128]{2,1,0:T(8,128)(2,1)S(1)} %get-tuple-element.46), channel_id=1, source_target_pairs={{0,12},{4,0},{8,4},{12,8},{1,13},{5,1},{9,5},{13,9},{2,14},{6,2},{... | collective-permute-start | bytes 1327112 | tf_op jit(solution)/shard_map/ppermute | solution.py:30
  97.4 0.7 pick.1
  98.0 12.1 %all_to_all.20.parts = f32[16,12,128]{2,1,0:T(8,128)S(1)} all-to-all(f32[16,12,128]{2,1,0:T(8,128)S(1)} %pick.1), channel_id=1, replica_groups=mesh['x'=4,'zh'=4,'y'=4,'zl'=2,'core'=2] {'x','y'}, dimensions={0} | all-to-all | bytes 196608 | tf_op jit(solution)/shard_map/all_to_all | solution.py:358
  110.1 1.2 combine.1
  111.4 6.5 %all-to-all-start.3 = ((bf16[16,96,128]{2,1,0:T(8,128)(2,1)}), bf16[16,96,128]{2,1,0:T(8,128)(2,1)S(1)}, u32[]{:S(2)}, u32[]{:S(2)}) async-start(bf16[16,96,128]{2,1,0:T(8,128)(2,1)} %bitcast.5), calls=%async_computation.3 | async-start | bytes 786432 | tf_op jit(solution)/shard_map/all_to_all | solution.py:335
  118.0 9.2 %collective-permute-start.10 = (f32[1,1536]{1,0:T(1,128)S(1)}, f32[1,1536]{1,0:T(1,128)S(1)}, u32[]{:S(2)}, u32[]{:S(2)}) collective-permute-start(f32[1,1536]{1,0:T(1,128)S(1)} %bitcast.43), channel_id=1, source_target_pairs={{0,0},{16,4},{32,8},{48,12},{4,16},{20,20},{36,24},{52,28},{8,32},... | collective-permute-start | bytes 18440 | tf_op jit(solution)/shard_map/ppermute | solution.py:366
  127.2 7.8 %collective-permute-done.10 = f32[1,1536]{1,0:T(1,128)S(1)} collective-permute-done((f32[1,1536]{1,0:T(1,128)S(1)}, f32[1,1536]{1,0:T(1,128)S(1)}, u32[]{:S(2)}, u32[]{:S(2)}) %collective-permute-start.10) | collective-permute-done | bytes 6176 | tf_op jit(solution)/shard_map/ppermute | solution.py:366
  134.9 0.8 copy_bitcast_fusion
  135.7 0.6 copy.31
  (37 shorter events, 1.6 us)
Async XLA Ops:
  0.6 12.9 %copy-start = (bf16[96,2048]{1,0:T(8,128)(2,1)S(1)}, bf16[96,2048]{1,0:T(8,128)(2,1)}, u32[]{:S(2)}) copy-start(bf16[96,2048]{1,0:T(8,128)(2,1)} %param.6) | copy-start | bytes 1179652
  0.6 1.3 copy-start.3
  3.1 8.7 %copy-start.6 = (s32[192]{0:T(256)S(1)}, s32[192]{0:T(256)}, u32[]{:S(2)}) copy-start(s32[192]{0:T(256)} %param.10) | copy-start | bytes 2308
  3.1 8.8 %copy-start.4 = (s32[192,96]{1,0:T(8,128)S(1)}, s32[192,96]{1,0:T(8,128)}, u32[]{:S(2)}) copy-start(s32[192,96]{1,0:T(8,128)} %param.9) | copy-start | bytes 221188
  3.1 10.4 %copy-start.5 = (s32[192]{0:T(256)S(1)}, s32[192]{0:T(256)}, u32[]{:S(2)}) copy-start(s32[192]{0:T(256)} %param.11) | copy-start | bytes 2308
  3.1 29.4 %all-to-all-start = ((bf16[16,2,96,128]{3,2,1,0:T(8,128)(2,1)}), bf16[16,2,96,128]{3,2,1,0:T(8,128)(2,1)S(1)}, u32[]{:S(2)}, u32[]{:S(2)}) async-start(bf16[16,2,96,128]{3,2,1,0:T(8,128)(2,1)} %maximum_bitcast_fusion), calls=%async_computation | async-start | bytes 1572864 | tf_op jit(solution)/shard_map/all_to_all | solution.py:335
  32.6 20.7 %collective-permute-start.2 = (bf16[2,12,128,128]{3,2,1,0:T(8,128)(2,1)S(1)}, bf16[2,12,128,128]{3,2,1,0:T(8,128)(2,1)S(1)}, u32[]{:S(2)}, u32[]{:S(2)}) collective-permute-start(bf16[2,12,128,128]{3,2,1,0:T(8,128)(2,1)S(1)} %prepare.1.refs_1_.refs_2_), channel_id=1, source_target_pairs={{0,64},{64,128},{128,192},{192,0},{1,65},{65,129},{129,193},{193,1... | collective-permute-start | bytes 2359304 | tf_op jit(solution)/shard_map/ppermute | solution.py:30
  34.2 18.8 %all-to-all-start.1 = ((bf16[16,96,128]{2,1,0:T(8,128)(2,1)}), bf16[16,96,128]{2,1,0:T(8,128)(2,1)S(1)}, u32[]{:S(2)}, u32[]{:S(2)}) async-start(bf16[16,96,128]{2,1,0:T(8,128)(2,1)} %bitcast_bitcast_fusion), calls=%async_computation.1 | async-start | bytes 786432 | tf_op jit(solution)/shard_map/all_to_all | solution.py:335
  39.3 20.0 %collective-permute-start.1 = (bf16[2,12,128,128]{3,2,1,0:T(8,128)(2,1)S(1)}, bf16[2,12,128,128]{3,2,1,0:T(8,128)(2,1)S(1)}, u32[]{:S(2)}, u32[]{:S(2)}) collective-permute-start(bf16[2,12,128,128]{3,2,1,0:T(8,128)(2,1)S(1)} %prepare.1.refs_1_.refs_2_), channel_id=1, source_target_pairs={{0,192},{64,0},{128,64},{192,128},{1,193},{65,1},{129,65},{193,129... | collective-permute-start | bytes 2359304 | tf_op jit(solution)/shard_map/ppermute | solution.py:30
  53.0 18.4 %collective-permute-start = (bf16[12,128,128]{2,1,0:T(8,128)(2,1)S(1)}, bf16[12,128,128]{2,1,0:T(8,128)(2,1)}, u32[]{:S(2)}, u32[]{:S(2)}) collective-permute-start(bf16[12,128,128]{2,1,0:T(8,128)(2,1)S(1)} %bitcast.33), channel_id=1, source_target_pairs={{0,8},{4,12},{8,0},{12,4},{1,9},{5,13},{9,1},{13,5},{2,10},{6,14},... | collective-permute-start | bytes 1179656 | tf_op jit(solution)/shard_map/ppermute | solution.py:30
  54.1 17.3 %collective-permute-start.3 = (bf16[12,128,128]{2,1,0:T(8,128)(2,1)}, bf16[12,128,128]{2,1,0:T(8,128)(2,1)}, u32[]{:S(2)}, u32[]{:S(2)}) collective-permute-start(bf16[12,128,128]{2,1,0:T(8,128)(2,1)} %slice_bitcast_fusion.1), channel_id=1, source_target_pairs={{0,64},{64,128},{128,192},{192,0},{1,65},{65,129},{129,193},{193,1... | collective-permute-start | bytes 1179656 | tf_op jit(solution)/shard_map/ppermute | solution.py:30
  59.3 12.1 %copy-start.1 = (bf16[2,12,128,128]{3,2,1,0:T(8,128)(2,1)}, bf16[2,12,128,128]{3,2,1,0:T(8,128)(2,1)S(1)}, u32[]{:S(2)}) copy-start(bf16[2,12,128,128]{3,2,1,0:T(8,128)(2,1)S(1)} %collective-permute-done.1.refs_2_.refs_3_) | copy-start | bytes 2359300
  60.1 11.4 %collective-permute-start.4 = (bf16[12,128,128]{2,1,0:T(8,128)(2,1)}, bf16[12,128,128]{2,1,0:T(8,128)(2,1)}, u32[]{:S(2)}, u32[]{:S(2)}) collective-permute-start(bf16[12,128,128]{2,1,0:T(8,128)(2,1)} %slice_bitcast_fusion), channel_id=1, source_target_pairs={{0,192},{64,0},{128,64},{192,128},{1,193},{65,1},{129,65},{193,129... | collective-permute-start | bytes 1179656 | tf_op jit(solution)/shard_map/ppermute | solution.py:30
  63.2 18.3 %collective-permute-start.5 = (bf16[12,128,128]{2,1,0:T(8,128)(2,1)S(1)}, bf16[12,128,128]{2,1,0:T(8,128)(2,1)S(1)}, u32[]{:S(2)}, u32[]{:S(2)}) collective-permute-start(bf16[12,128,128]{2,1,0:T(8,128)(2,1)S(1)} %bitcast.34), channel_id=1, source_target_pairs={{0,12},{4,0},{8,4},{12,8},{1,13},{5,1},{9,5},{13,9},{2,14},{6,2},{... | collective-permute-start | bytes 1179656 | tf_op jit(solution)/shard_map/ppermute | solution.py:30
  63.6 20.0 %collective-permute-start.6 = (bf16[12,128,128]{2,1,0:T(8,128)(2,1)S(1)}, bf16[12,128,128]{2,1,0:T(8,128)(2,1)S(1)}, u32[]{:S(2)}, u32[]{:S(2)}) collective-permute-start(bf16[12,128,128]{2,1,0:T(8,128)(2,1)S(1)} %bitcast.35), channel_id=1, source_target_pairs={{0,4},{4,8},{8,12},{12,0},{1,5},{5,9},{9,13},{13,1},{2,6},{6,10},{... | collective-permute-start | bytes 1179656 | tf_op jit(solution)/shard_map/ppermute | solution.py:30
  71.6 1.1 copy-start.2
  81.5 15.9 %collective-permute-start.7 = (bf16[12,144,128]{2,1,0:T(8,128)(2,1)S(1)}, bf16[12,144,128]{2,1,0:T(8,128)(2,1)S(1)}, u32[]{:S(2)}, u32[]{:S(2)}) collective-permute-start(bf16[12,144,128]{2,1,0:T(8,128)(2,1)S(1)} %get-tuple-element.39), channel_id=1, source_target_pairs={{0,8},{4,12},{8,0},{12,4},{1,9},{5,13},{9,1},{13,5},{2,10},{6,14},... | collective-permute-start | bytes 1327112 | tf_op jit(solution)/shard_map/ppermute | solution.py:30
  95.2 14.9 %collective-permute-start.8 = (bf16[12,144,128]{2,1,0:T(8,128)(2,1)S(1)}, bf16[12,144,128]{2,1,0:T(8,128)(2,1)S(1)}, u32[]{:S(2)}, u32[]{:S(2)}) collective-permute-start(bf16[12,144,128]{2,1,0:T(8,128)(2,1)S(1)} %get-tuple-element.44), channel_id=1, source_target_pairs={{0,4},{4,8},{8,12},{12,0},{1,5},{5,9},{9,13},{13,1},{2,6},{6,10},{... | collective-permute-start | bytes 1327112 | tf_op jit(solution)/shard_map/ppermute | solution.py:30
  95.3 14.8 %collective-permute-start.9 = (bf16[12,144,128]{2,1,0:T(8,128)(2,1)S(1)}, bf16[12,144,128]{2,1,0:T(8,128)(2,1)S(1)}, u32[]{:S(2)}, u32[]{:S(2)}) collective-permute-start(bf16[12,144,128]{2,1,0:T(8,128)(2,1)S(1)} %get-tuple-element.46), channel_id=1, source_target_pairs={{0,12},{4,0},{8,4},{12,8},{1,13},{5,1},{9,5},{13,9},{2,14},{6,2},{... | collective-permute-start | bytes 1327112 | tf_op jit(solution)/shard_map/ppermute | solution.py:30
  111.4 23.6 %all-to-all-start.3 = ((bf16[16,96,128]{2,1,0:T(8,128)(2,1)}), bf16[16,96,128]{2,1,0:T(8,128)(2,1)S(1)}, u32[]{:S(2)}, u32[]{:S(2)}) async-start(bf16[16,96,128]{2,1,0:T(8,128)(2,1)} %bitcast.5), calls=%async_computation.3 | async-start | bytes 786432 | tf_op jit(solution)/shard_map/all_to_all | solution.py:335
  118.0 17.0 %collective-permute-start.10 = (f32[1,1536]{1,0:T(1,128)S(1)}, f32[1,1536]{1,0:T(1,128)S(1)}, u32[]{:S(2)}, u32[]{:S(2)}) collective-permute-start(f32[1,1536]{1,0:T(1,128)S(1)} %bitcast.43), channel_id=1, source_target_pairs={{0,0},{16,4},{32,8},{48,12},{4,16},{20,20},{36,24},{52,28},{8,32},... | collective-permute-start | bytes 18440 | tf_op jit(solution)/shard_map/ppermute | solution.py:366

commit v15 on v13

--- a/solution.py
+++ b/solution.py
@@ -15,7 +15,7 @@
 KEYS = RING * OWN
 NEAR = 3 * OWN
 CHUNK = 4
-WIDTHS = {1: 8, 2: 12}
+WIDTHS = {1: 8, 2: 16}
 PAD = 16
 NEG = -1e30
 SCALE = HD**-0.5

time: 135 us -> 135 us (level)
  starting transfers between devices: 41.2 us -> 42.8 us
  transfers between devices with their start and end apart: 14 -> 14, of which waited for: 5 -> 5; matrix products, arithmetic and copies ran while one was open for 4% -> 4% of each run, Pallas kernels for 22% -> 21%
where the time goes in v15:
time: 135 us; the launch traced here: 133 us
  starting transfers between devices  42.8 us (32%)
  waiting for transfers between devices  38.8 us (29%)
  Pallas kernels  30 us (22%)
  blocking collectives  12 us (9%)
  local copies, waits for them, and re-layouts  6.34 us (5%)
  other arithmetic  2.32 us (2%)
    pallas_call x4, Pallas kernels, attend(): pl.pallas_call(functools.partial(attend_kernel, blocks, mode), out_shape=...  27.9 us
    all_to_all x3, starting transfers between devices, exchange(): return lax.all_to_all(array, GROUP, split_axis=0, concat_axis=0, tiled=True)  19.1 us
    all_to_all x3, waiting for transfers between devices, exchange(): return lax.all_to_all(array, GROUP, split_axis=0, concat_axis=0, tiled=True)  18.1 us
    ppermute x10, starting transfers between devices, shift(): lax.ppermute(array, axis, [(i, (i + by) % RING) for i in range(RING)])  14.5 us
    ppermute x10, waiting for transfers between devices, shift(): lax.ppermute(array, axis, [(i, (i + by) % RING) for i in range(RING)])  12.9 us
    all_to_all x1, blocking collectives, on_device(): lax.all_to_all(pick(spots, (e0, e1, e2, e3)), ('x', 'y'), split_axis=0, c...  12 us
    ppermute x1, starting transfers between devices, on_device(): lax.ppermute(merge(parts).reshape(1, OWN * BLK), ('zh', 'y'), turned)  9.18 us
    ppermute x1, waiting for transfers between devices, on_device(): lax.ppermute(merge(parts).reshape(1, OWN * BLK), ('zh', 'y'), turned)  7.78 us
  transfers between devices with their start and end apart: 14, of which 5 were waited for; matrix products, arithmetic and copies ran while one was open for 4% of the time, Pallas kernels for 21%

profile of v15, /device:TPU:16, one launch (start us, length us, event | category | flops | bytes accessed | tf_op | source)
XLA Modules:
  0.0 133.4 jit_solution(14550295256548834799)
XLA Ops:
  0.7 1.1 copy.25
  2.1 1.0 maximum_bitcast_fusion
  3.1 8.7 %all-to-all-start = ((bf16[16,2,96,128]{3,2,1,0:T(8,128)(2,1)}), bf16[16,2,96,128]{3,2,1,0:T(8,128)(2,1)S(1)}, u32[]{:S(2)}, u32[]{:S(2)}) async-start(bf16[16,2,96,128]{3,2,1,0:T(8,128)(2,1)} %maximum_bitcast_fusion), calls=%async_computation | async-start | bytes 1572864 | tf_op jit(solution)/shard_map/all_to_all | solution.py:341
  12.5 1.0 select_reduce_fusion
  13.6 0.8 bitcast_bitcast_fusion
  14.4 18.1 %all-to-all-done.got_ref = bf16[16,2,96,128]{3,2,1,0:T(8,128)(2,1)S(1)} async-done(((bf16[16,2,96,128]{3,2,1,0:T(8,128)(2,1)}), bf16[16,2,96,128]{3,2,1,0:T(8,128)(2,1)S(1)}, u32[]{:S(2)}, u32[]{:S(2)}) %all-to-all-start) | async-done | bytes 786464 | tf_op jit(solution)/shard_map/all_to_all | solution.py:341
  32.6 1.6 %collective-permute-start = (bf16[2,12,128,128]{3,2,1,0:T(8,128)(2,1)S(1)}, bf16[2,12,128,128]{3,2,1,0:T(8,128)(2,1)S(1)}, u32[]{:S(2)}, u32[]{:S(2)}) collective-permute-start(bf16[2,12,128,128]{3,2,1,0:T(8,128)(2,1)S(1)} %prepare.1.refs_1_.refs_2_), channel_id=1, source_target_pairs={{0,64},{64,128},{128,192},{192,0},{1,65},{65,129},{129,193},{193,1... | collective-permute-start | bytes 2359304 | tf_op jit(solution)/shard_map/ppermute | solution.py:30
  34.2 1.7 %collective-permute-start.2 = (bf16[2,12,128,128]{3,2,1,0:T(8,128)(2,1)S(1)}, bf16[2,12,128,128]{3,2,1,0:T(8,128)(2,1)}, u32[]{:S(2)}, u32[]{:S(2)}) collective-permute-start(bf16[2,12,128,128]{3,2,1,0:T(8,128)(2,1)S(1)} %prepare.1.refs_1_.refs_2_), channel_id=1, source_target_pairs={{0,192},{64,0},{128,64},{192,128},{1,193},{65,1},{129,65},{193,129... | collective-permute-start | bytes 2359304 | tf_op jit(solution)/shard_map/ppermute | solution.py:30
  35.9 5.1 %all-to-all-start.1 = ((bf16[16,96,128]{2,1,0:T(8,128)(2,1)}), bf16[16,96,128]{2,1,0:T(8,128)(2,1)S(1)}, u32[]{:S(2)}, u32[]{:S(2)}) async-start(bf16[16,96,128]{2,1,0:T(8,128)(2,1)} %bitcast_bitcast_fusion), calls=%async_computation.1 | async-start | bytes 786432 | tf_op jit(solution)/shard_map/all_to_all | solution.py:341
  41.1 11.8 %collective-permute-done.refs_3_.refs_4_ = bf16[2,12,128,128]{3,2,1,0:T(8,128)(2,1)S(1)} collective-permute-done((bf16[2,12,128,128]{3,2,1,0:T(8,128)(2,1)S(1)}, bf16[2,12,128,128]{3,2,1,0:T(8,128)(2,1)S(1)}, u32[]{:S(2)}, u32[]{:S(2)}) %collective-permute-start) | collective-permute-done | bytes 786464 | tf_op jit(solution)/shard_map/ppermute | solution.py:30
  52.9 0.8 slice_bitcast_fusion.1
  53.6 0.3 collective-permute-start.1
  53.9 1.8 %slice_bitcast_fusion = bf16[12,128,128]{2,1,0:T(8,128)(2,1)} fusion(bf16[2,12,128,128]{3,2,1,0:T(8,128)(2,1)} %collective-permute-done.2.refs_2_.refs_3_), kind=kLoop, calls=%fused_computation.10 | loop fusion | bytes 786432 | tf_op jit(solution)/shard_map/squeeze | solution.py:355
  55.7 3.0 %collective-permute-start.3 = (bf16[12,128,128]{2,1,0:T(8,128)(2,1)}, bf16[12,128,128]{2,1,0:T(8,128)(2,1)S(1)}, u32[]{:S(2)}, u32[]{:S(2)}) collective-permute-start(bf16[12,128,128]{2,1,0:T(8,128)(2,1)} %slice_bitcast_fusion), channel_id=1, source_target_pairs={{0,192},{64,0},{128,64},{192,128},{1,193},{65,1},{129,65},{193,129... | collective-permute-start | bytes 1179656 | tf_op jit(solution)/shard_map/ppermute | solution.py:30
  58.7 0.3 collective-permute-start.4
  59.0 2.4 %collective-permute-start.5 = (bf16[12,128,128]{2,1,0:T(8,128)(2,1)S(1)}, bf16[12,128,128]{2,1,0:T(8,128)(2,1)}, u32[]{:S(2)}, u32[]{:S(2)}) collective-permute-start(bf16[12,128,128]{2,1,0:T(8,128)(2,1)S(1)} %bitcast.34), channel_id=1, source_target_pairs={{0,12},{4,0},{8,4},{12,8},{1,13},{5,1},{9,5},{13,9},{2,14},{6,2},{... | collective-permute-start | bytes 1179656 | tf_op jit(solution)/shard_map/ppermute | solution.py:30
  61.5 6.4 %near.1 = (f32[12,1,128]{2,1,0:T(1,128)S(1)}, f32[12,8,128]{2,1,0:T(8,128)S(1)}, f32[12,128,128]{2,1,0:T(8,128)S(1)}) custom-call(s32[48,52]{1,0:T(8,128)S(1)} %copy.18.lists, s32[48]{0:T(128)S(1)} %get-tuple-element.28.nears, s32[48]{0:T(128)S(1)} %get-tuple-element.29.counts, bf16[12,128,128]{2,1,0:T(8,128)(2,1)S(1)} %bitcast.36, ...), custom_call_target="tpu_custom_call" | custom-call | flops 1207959552 | bytes 5242880 | tf_op jit(solution)/shard_map/near/pallas_call | solution.py:229
  68.1 3.3 %far.1 = (bf16[12,144,128]{2,1,0:T(8,128)(2,1)S(1)}, f32[12,128]{1,0:T(8,128)S(1)}) custom-call(s32[48,52]{1,0:T(8,128)S(1)} %copy.18.lists, s32[48]{0:T(128)S(1)} %get-tuple-element.28.nears, s32[48]{0:T(128)S(1)} %get-tuple-element.29.counts, bf16[12,128,128]{2,1,0:T(8,128)(2,1)S(1)} %bitcast.37, ...), custom_call_target="tpu_custom_call" | custom-call | flops 402653184 | bytes 5242880 | tf_op jit(solution)/shard_map/far/pallas_call | solution.py:229
  71.5 0.9 collective-permute-done.4.refs_0_
  72.3 7.5 %full.2 = (bf16[12,144,128]{2,1,0:T(8,128)(2,1)S(1)}, f32[12,128]{1,0:T(8,128)S(1)}) custom-call(s32[48,52]{1,0:T(8,128)S(1)} %copy.18.lists, s32[48]{0:T(128)S(1)} %get-tuple-element.28.nears, s32[48]{0:T(128)S(1)} %get-tuple-element.29.counts, bf16[12,128,128]{2,1,0:T(8,128)(2,1)} %collective-permute-done.4.refs_0_, ...), custom_call_target="tpu_custom_call" | custom-call | flops 1610612736 | bytes 5242880 | tf_op jit(solution)/shard_map/full/pallas_call | solution.py:229
  79.8 2.6 %collective-permute-start.7 = (bf16[12,144,128]{2,1,0:T(8,128)(2,1)S(1)}, bf16[12,144,128]{2,1,0:T(8,128)(2,1)S(1)}, u32[]{:S(2)}, u32[]{:S(2)}) collective-permute-start(bf16[12,144,128]{2,1,0:T(8,128)(2,1)S(1)} %get-tuple-element.43), channel_id=1, source_target_pairs={{0,8},{4,12},{8,0},{12,4},{1,9},{5,13},{9,1},{13,5},{2,10},{6,14},... | collective-permute-start | bytes 1327112 | tf_op jit(solution)/shard_map/ppermute | solution.py:30
  82.4 10.7 %full.3 = (bf16[12,144,128]{2,1,0:T(8,128)(2,1)S(1)}, bf16[12,144,128]{2,1,0:T(8,128)(2,1)S(1)}, f32[12,128]{1,0:T(8,128)S(1)}, f32[12,128]{1,0:T(8,128)S(1)}) custom-call(s32[48,52]{1,0:T(8,128)S(1)} %copy.18.lists, s32[48]{0:T(128)S(1)} %get-tuple-element.28.nears, s32[48]{0:T(128)S(1)} %get-tuple-element.29.counts, ...), custom_call_target="tpu_custom_call" | custom-call | flops 3221225472 | bytes 5242880 | tf_op jit(solution)/shard_map/full/pallas_call | solution.py:229
  93.1 2.2 %collective-permute-start.8 = (bf16[12,144,128]{2,1,0:T(8,128)(2,1)S(1)}, bf16[12,144,128]{2,1,0:T(8,128)(2,1)S(1)}, u32[]{:S(2)}, u32[]{:S(2)}) collective-permute-start(bf16[12,144,128]{2,1,0:T(8,128)(2,1)S(1)} %get-tuple-element.48), channel_id=1, source_target_pairs={{0,4},{4,8},{8,12},{12,0},{1,5},{5,9},{9,13},{13,1},{2,6},{6,10},{... | collective-permute-start | bytes 1327112 | tf_op jit(solution)/shard_map/ppermute | solution.py:30
  95.4 0.3 collective-permute-start.9
  95.7 0.7 pick.1
  96.4 12.0 %all_to_all.20.parts = f32[16,12,128]{2,1,0:T(8,128)S(1)} all-to-all(f32[16,12,128]{2,1,0:T(8,128)S(1)} %pick.1), channel_id=1, replica_groups=mesh['x'=4,'zh'=4,'y'=4,'zl'=2,'core'=2] {'x','y'}, dimensions={0} | all-to-all | bytes 196608 | tf_op jit(solution)/shard_map/all_to_all | solution.py:366
  108.4 1.2 combine.1
  109.6 5.3 %all-to-all-start.3 = ((bf16[16,96,128]{2,1,0:T(8,128)(2,1)}), bf16[16,96,128]{2,1,0:T(8,128)(2,1)S(1)}, u32[]{:S(2)}, u32[]{:S(2)}) async-start(bf16[16,96,128]{2,1,0:T(8,128)(2,1)} %bitcast.5), calls=%async_computation.3 | async-start | bytes 786432 | tf_op jit(solution)/shard_map/all_to_all | solution.py:341
  115.0 9.2 %collective-permute-start.10 = (f32[1,1536]{1,0:T(1,128)S(1)}, f32[1,1536]{1,0:T(1,128)S(1)}, u32[]{:S(2)}, u32[]{:S(2)}) collective-permute-start(f32[1,1536]{1,0:T(1,128)S(1)} %bitcast.43), channel_id=1, source_target_pairs={{0,0},{16,4},{32,8},{48,12},{4,16},{20,20},{36,24},{52,28},{8,32},... | collective-permute-start | bytes 18440 | tf_op jit(solution)/shard_map/ppermute | solution.py:374
  124.2 7.8 %collective-permute-done.10 = f32[1,1536]{1,0:T(1,128)S(1)} collective-permute-done((f32[1,1536]{1,0:T(1,128)S(1)}, f32[1,1536]{1,0:T(1,128)S(1)}, u32[]{:S(2)}, u32[]{:S(2)}) %collective-permute-start.10) | collective-permute-done | bytes 6176 | tf_op jit(solution)/shard_map/ppermute | solution.py:374
  132.0 0.8 copy_bitcast_fusion
  132.8 0.6 copy.32
  (34 shorter events, 1.6 us)
Async XLA Ops:
  0.6 12.9 %copy-start = (bf16[96,2048]{1,0:T(8,128)(2,1)S(1)}, bf16[96,2048]{1,0:T(8,128)(2,1)}, u32[]{:S(2)}) copy-start(bf16[96,2048]{1,0:T(8,128)(2,1)} %param.6) | copy-start | bytes 1179652
  0.6 1.3 copy-start.1
  3.1 8.7 %copy-start.4 = (s32[192]{0:T(256)S(1)}, s32[192]{0:T(256)}, u32[]{:S(2)}) copy-start(s32[192]{0:T(256)} %param.10) | copy-start | bytes 2308
  3.1 8.8 %copy-start.2 = (s32[192,96]{1,0:T(8,128)S(1)}, s32[192,96]{1,0:T(8,128)}, u32[]{:S(2)}) copy-start(s32[192,96]{1,0:T(8,128)} %param.9) | copy-start | bytes 221188
  3.1 10.4 %copy-start.3 = (s32[192]{0:T(256)S(1)}, s32[192]{0:T(256)}, u32[]{:S(2)}) copy-start(s32[192]{0:T(256)} %param.11) | copy-start | bytes 2308
  3.1 29.4 %all-to-all-start = ((bf16[16,2,96,128]{3,2,1,0:T(8,128)(2,1)}), bf16[16,2,96,128]{3,2,1,0:T(8,128)(2,1)S(1)}, u32[]{:S(2)}, u32[]{:S(2)}) async-start(bf16[16,2,96,128]{3,2,1,0:T(8,128)(2,1)} %maximum_bitcast_fusion), calls=%async_computation | async-start | bytes 1572864 | tf_op jit(solution)/shard_map/all_to_all | solution.py:341
  32.6 20.2 %collective-permute-start = (bf16[2,12,128,128]{3,2,1,0:T(8,128)(2,1)S(1)}, bf16[2,12,128,128]{3,2,1,0:T(8,128)(2,1)S(1)}, u32[]{:S(2)}, u32[]{:S(2)}) collective-permute-start(bf16[2,12,128,128]{3,2,1,0:T(8,128)(2,1)S(1)} %prepare.1.refs_1_.refs_2_), channel_id=1, source_target_pairs={{0,64},{64,128},{128,192},{192,0},{1,65},{65,129},{129,193},{193,1... | collective-permute-start | bytes 2359304 | tf_op jit(solution)/shard_map/ppermute | solution.py:30
  34.2 19.7 %collective-permute-start.2 = (bf16[2,12,128,128]{3,2,1,0:T(8,128)(2,1)S(1)}, bf16[2,12,128,128]{3,2,1,0:T(8,128)(2,1)}, u32[]{:S(2)}, u32[]{:S(2)}) collective-permute-start(bf16[2,12,128,128]{3,2,1,0:T(8,128)(2,1)S(1)} %prepare.1.refs_1_.refs_2_), channel_id=1, source_target_pairs={{0,192},{64,0},{128,64},{192,128},{1,193},{65,1},{129,65},{193,129... | collective-permute-start | bytes 2359304 | tf_op jit(solution)/shard_map/ppermute | solution.py:30
  35.9 22.7 %all-to-all-start.1 = ((bf16[16,96,128]{2,1,0:T(8,128)(2,1)}), bf16[16,96,128]{2,1,0:T(8,128)(2,1)S(1)}, u32[]{:S(2)}, u32[]{:S(2)}) async-start(bf16[16,96,128]{2,1,0:T(8,128)(2,1)} %bitcast_bitcast_fusion), calls=%async_computation.1 | async-start | bytes 786432 | tf_op jit(solution)/shard_map/all_to_all | solution.py:341
  53.6 14.2 %collective-permute-start.1 = (bf16[12,128,128]{2,1,0:T(8,128)(2,1)}, bf16[12,128,128]{2,1,0:T(8,128)(2,1)S(1)}, u32[]{:S(2)}, u32[]{:S(2)}) collective-permute-start(bf16[12,128,128]{2,1,0:T(8,128)(2,1)} %slice_bitcast_fusion.1), channel_id=1, source_target_pairs={{0,64},{64,128},{128,192},{192,0},{1,65},{65,129},{129,193},{193,1... | collective-permute-start | bytes 1179656 | tf_op jit(solution)/shard_map/ppermute | solution.py:30
  55.7 12.4 %collective-permute-start.3 = (bf16[12,128,128]{2,1,0:T(8,128)(2,1)}, bf16[12,128,128]{2,1,0:T(8,128)(2,1)S(1)}, u32[]{:S(2)}, u32[]{:S(2)}) collective-permute-start(bf16[12,128,128]{2,1,0:T(8,128)(2,1)} %slice_bitcast_fusion), channel_id=1, source_target_pairs={{0,192},{64,0},{128,64},{192,128},{1,193},{65,1},{129,65},{193,129... | collective-permute-start | bytes 1179656 | tf_op jit(solution)/shard_map/ppermute | solution.py:30
  58.7 13.6 %collective-permute-start.4 = (bf16[12,128,128]{2,1,0:T(8,128)(2,1)S(1)}, bf16[12,128,128]{2,1,0:T(8,128)(2,1)}, u32[]{:S(2)}, u32[]{:S(2)}) collective-permute-start(bf16[12,128,128]{2,1,0:T(8,128)(2,1)S(1)} %bitcast.33), channel_id=1, source_target_pairs={{0,8},{4,12},{8,0},{12,4},{1,9},{5,13},{9,1},{13,5},{2,10},{6,14},... | collective-permute-start | bytes 1179656 | tf_op jit(solution)/shard_map/ppermute | solution.py:30
  59.0 20.8 %collective-permute-start.5 = (bf16[12,128,128]{2,1,0:T(8,128)(2,1)S(1)}, bf16[12,128,128]{2,1,0:T(8,128)(2,1)}, u32[]{:S(2)}, u32[]{:S(2)}) collective-permute-start(bf16[12,128,128]{2,1,0:T(8,128)(2,1)S(1)} %bitcast.34), channel_id=1, source_target_pairs={{0,12},{4,0},{8,4},{12,8},{1,13},{5,1},{9,5},{13,9},{2,14},{6,2},{... | collective-permute-start | bytes 1179656 | tf_op jit(solution)/shard_map/ppermute | solution.py:30
  61.4 21.0 %collective-permute-start.6 = (bf16[12,128,128]{2,1,0:T(8,128)(2,1)S(1)}, bf16[12,128,128]{2,1,0:T(8,128)(2,1)}, u32[]{:S(2)}, u32[]{:S(2)}) collective-permute-start(bf16[12,128,128]{2,1,0:T(8,128)(2,1)S(1)} %bitcast.35), channel_id=1, source_target_pairs={{0,4},{4,8},{8,12},{12,0},{1,5},{5,9},{9,13},{13,1},{2,6},{6,10},{... | collective-permute-start | bytes 1179656 | tf_op jit(solution)/shard_map/ppermute | solution.py:30
  79.8 15.9 %collective-permute-start.7 = (bf16[12,144,128]{2,1,0:T(8,128)(2,1)S(1)}, bf16[12,144,128]{2,1,0:T(8,128)(2,1)S(1)}, u32[]{:S(2)}, u32[]{:S(2)}) collective-permute-start(bf16[12,144,128]{2,1,0:T(8,128)(2,1)S(1)} %get-tuple-element.43), channel_id=1, source_target_pairs={{0,8},{4,12},{8,0},{12,4},{1,9},{5,13},{9,1},{13,5},{2,10},{6,14},... | collective-permute-start | bytes 1327112 | tf_op jit(solution)/shard_map/ppermute | solution.py:30
  93.1 15.2 %collective-permute-start.8 = (bf16[12,144,128]{2,1,0:T(8,128)(2,1)S(1)}, bf16[12,144,128]{2,1,0:T(8,128)(2,1)S(1)}, u32[]{:S(2)}, u32[]{:S(2)}) collective-permute-start(bf16[12,144,128]{2,1,0:T(8,128)(2,1)S(1)} %get-tuple-element.48), channel_id=1, source_target_pairs={{0,4},{4,8},{8,12},{12,0},{1,5},{5,9},{9,13},{13,1},{2,6},{6,10},{... | collective-permute-start | bytes 1327112 | tf_op jit(solution)/shard_map/ppermute | solution.py:30
  95.4 13.0 %collective-permute-start.9 = (bf16[12,144,128]{2,1,0:T(8,128)(2,1)S(1)}, bf16[12,144,128]{2,1,0:T(8,128)(2,1)S(1)}, u32[]{:S(2)}, u32[]{:S(2)}) collective-permute-start(bf16[12,144,128]{2,1,0:T(8,128)(2,1)S(1)} %get-tuple-element.50), channel_id=1, source_target_pairs={{0,12},{4,0},{8,4},{12,8},{1,13},{5,1},{9,5},{13,9},{2,14},{6,2},{... | collective-permute-start | bytes 1327112 | tf_op jit(solution)/shard_map/ppermute | solution.py:30
  109.6 22.3 %all-to-all-start.3 = ((bf16[16,96,128]{2,1,0:T(8,128)(2,1)}), bf16[16,96,128]{2,1,0:T(8,128)(2,1)S(1)}, u32[]{:S(2)}, u32[]{:S(2)}) async-start(bf16[16,96,128]{2,1,0:T(8,128)(2,1)} %bitcast.5), calls=%async_computation.3 | async-start | bytes 786432 | tf_op jit(solution)/shard_map/all_to_all | solution.py:341
  115.0 17.0 %collective-permute-start.10 = (f32[1,1536]{1,0:T(1,128)S(1)}, f32[1,1536]{1,0:T(1,128)S(1)}, u32[]{:S(2)}, u32[]{:S(2)}) collective-permute-start(f32[1,1536]{1,0:T(1,128)S(1)} %bitcast.43), channel_id=1, source_target_pairs={{0,0},{16,4},{32,8},{48,12},{4,16},{20,20},{36,24},{52,28},{8,32},... | collective-permute-start | bytes 18440 | tf_op jit(solution)/shard_map/ppermute | solution.py:374
